TPU v7x, 32 devices: a whole 2x2x4 slice. The times are simulated.
32 devices in a mesh: replica: 4 (over y, x), shard: 8 (over z, core).
Axes of the slice: x: 2, y: 2, z: 4, core: 2. Of those that a mesh axis runs over, the one named last changes fastest.
Arguments:
- queries: bfloat16 [16384, 2048], P(('replica', 'shard')), may hold values from -20 to 20
- keys: bfloat16 [16384, 1024], P(('replica', 'shard')), may hold values from -20 to 20
- values: bfloat16 [16384, 1024], P(('replica', 'shard')), may hold values from -6 to 6
- segments: int32 [32, 512], P(('replica', 'shard')), may hold values from 0 to 7, never falling along the last dimension, each value on 1 to 384 neighbouring positions
- out_weight: bfloat16 [2048, 4608], P('shard'), may hold values from -0.125 to 0.125
- upstream: bfloat16 [16384, 4608], P(('replica', 'shard')), may hold values from -6 to 6
- first_moment: float32 [2048, 4608], P('shard'), may hold values from -0.0034179688 to 0.0034179688
- second_moment: float32 [2048, 4608], P('shard'), may hold values from 1.2207032e-07 to 3.0517579e-06
Outputs:
- grad_queries: bfloat16 [16384, 2048], P(('replica', 'shard'))
- grad_keys: bfloat16 [16384, 1024], P(('replica', 'shard'))
- grad_values: bfloat16 [16384, 1024], P(('replica', 'shard'))
- adam_step: float32 [2048, 4608], P('shard')
Inputs may be any that keep to these rules, and one draw needn't show every extreme that they name: `segments`: within each block the document numbers never fall; every document holds 1 to 384 tokens.
All inputs are finite; a program needn't handle non-finite values.
Results may differ from a plain program's by a relative error of at most 0.014.
Values may be sent and summed in bfloat16 or wider, within the bound.
No kernel may reach another device: no remote copies, remote signals or barrier semaphores. Data moves between devices by JAX's collectives and lax.ppermute only.
A program may use at most 192 MiB of HBM per device.

v0:
```python
import jax
import jax.numpy as jnp
from jax import lax
from jax.sharding import PartitionSpec as P

HEADS = 16
KV_HEADS = 8
DH = 128


score_scale = 1.0 / 12.0
softcap_limit = 50.0


def recompute(query_heads, key_heads, value_heads, segment_row):
    length = segment_row.shape[0]
    scores = (
        jnp.einsum("igrd,jgd->grij", query_heads, key_heads, preferred_element_type=jnp.float32)
        * score_scale
    )
    capped = softcap_limit * jnp.tanh(scores / softcap_limit)
    position = jnp.arange(length)
    allowed = (position[None, :] <= position[:, None]) & (
        segment_row[:, None] == segment_row[None, :]
    )
    weights = jnp.where(allowed, jnp.exp(capped), jnp.zeros_like(capped))
    probs = weights / jnp.sum(weights, axis=-1, keepdims=True)
    probs_low = probs.astype(jnp.bfloat16)
    context = jnp.einsum(
        "grij,jgd->igrd", probs_low, value_heads, preferred_element_type=jnp.float32
    ).astype(jnp.bfloat16)
    return (probs, capped, probs_low, context.reshape(length, -1))


def per_device(queries, keys, values, segments, out_weight, upstream, first_moment, second_moment):
    length = queries.shape[0]
    repeat = HEADS // KV_HEADS
    query_heads = queries.reshape(length, KV_HEADS, repeat, DH)
    key_heads = keys.reshape(length, KV_HEADS, DH)
    value_heads = values.reshape(length, KV_HEADS, DH)
    segment_row = segments[0]
    partial_rows = lax.dot_general(
        upstream,
        lax.all_gather(out_weight, "shard", axis=0, tiled=True),
        (((1,), (1,)), ((), ())),
        preferred_element_type=jnp.float32,
    )
    grad_context = partial_rows.astype(jnp.bfloat16)
    probs, capped, probs_low, context = recompute(query_heads, key_heads, value_heads, segment_row)
    grad_heads = grad_context.reshape(length, KV_HEADS, repeat, DH)
    grad_probs = jnp.einsum(
        "igrd,jgd->grij", grad_heads, value_heads, preferred_element_type=jnp.float32
    )
    grad_vals = jnp.einsum(
        "grij,igrd->jgd", probs_low, grad_heads, preferred_element_type=jnp.float32
    ).astype(jnp.bfloat16)
    delta = jnp.sum(probs * grad_probs, axis=-1, keepdims=True)
    grad_scores = (
        probs * (grad_probs - delta) * (1.0 - jnp.square(capped / softcap_limit)) * score_scale
    ).astype(jnp.bfloat16)
    grad_query = jnp.einsum(
        "grij,jgd->igrd", grad_scores, key_heads, preferred_element_type=jnp.float32
    ).astype(jnp.bfloat16)
    grad_key = jnp.einsum(
        "grij,igrd->jgd", grad_scores, query_heads, preferred_element_type=jnp.float32
    ).astype(jnp.bfloat16)
    replicas = lax.axis_size("replica")
    shards = lax.axis_size("shard")
    product = lax.dot_general(
        context, upstream, (((0,), (0,)), ((), ())), preferred_element_type=jnp.float32
    )
    group_total = lax.psum_scatter(
        lax.optimization_barrier(product.astype(jnp.bfloat16))
        .astype(jnp.float32)
        .astype(jnp.bfloat16),
        "shard",
        scatter_dimension=0,
        tiled=True,
    )
    total = lax.psum(group_total, "replica").astype(jnp.float32)
    gradient = total / (length * replicas * shards)
    moment_one = 0.9 * first_moment + 0.1 * gradient
    moment_two = 0.95 * second_moment + 0.05 * gradient * gradient
    adam_step = moment_one / (jnp.sqrt(moment_two) + 1e-08)
    return (
        grad_query.reshape(length, -1),
        grad_key.reshape(length, -1),
        grad_vals.reshape(length, -1),
        adam_step,
    )


def solution(mesh):
    return jax.shard_map(
        per_device,
        mesh=mesh,
        in_specs=(
            P(("replica", "shard"), None),
            P(("replica", "shard"), None),
            P(("replica", "shard"), None),
            P(("replica", "shard"), None),
            P("shard", None),
            P(("replica", "shard"), None),
            P("shard", None),
            P("shard", None),
        ),
        out_specs=(
            P(("replica", "shard"), None),
            P(("replica", "shard"), None),
            P(("replica", "shard"), None),
            P("shard", None),
        ),
        check_vma=False,
    )
```

profile of v0, /device:TPU:0, one launch (start us, length us, event | category | flops | bytes accessed | tf_op | source)
XLA Modules:
  0.0 458.7 jit_solution(12408215699053160514)
XLA Ops:
  7.2 0.0 all-gather.2.cloned.1.call-start
  7.2 0.7 all-gather.2.cloned.1.call-update
  7.9 0.0 reduce-scatter.2.cloned.1.call-start
  7.9 1.5 copy.47
  9.4 0.7 copy.30
  10.1 0.0 copy-start.1
  10.1 1.9 copy.48
  12.0 1.5 copy.36
  13.5 2.9 copy.45
  16.4 1.0 fusion.24
  17.4 0.0 copy-start.3
  17.4 0.0 slice-start
  17.4 10.5 %fusion.5 = (f32[8,2,512]{2,1,0:T(2,128)S(1)}, f32[8,512,512,2]{2,1,3,0:T(8,128)}) fusion(pred[512,512]{0,1:T(8,128)(4,1)S(1)} %fusion.24, bf16[512,8,128,1]{0,2,3,1:T(8,128)(2,1)S(1)} %copy.30, bf16[512,8,2,128]{0,3,2,1:T(8,128)(2,1)S(1)} %bitcast.107), kind=kOutput, calls=%fused_computation.11 | convolution fusion | flops 1090510848 | bytes 20217856 | tf_op jit(solution)/shard_map/igrd,jgd->grij/dot_general | solution.py:18
  27.9 0.0 copy-done.1
  27.9 0.0 copy-done.3
  27.9 0.0 slice-start.1
  27.9 8.9 %fusion.19 = bf16[8,2,512,128]{2,3,1,0:T(8,128)(2,1)S(1)} fusion(bf16[512,8,128,1]{0,2,3,1:T(8,128)(2,1)S(1)} %copy-done.3, f32[8,512,512,2]{2,1,3,0:T(8,128)} %get-tuple-element.9, f32[8,2,512]{2,1,0:T(2,128)S(1)} %get-tuple-element.8, pred[512,512]{0,1:T(8,128)(4,1)S(1)} %fusion.24), kind=kOutput, calls=%fused_computation.30 | convolution fusion | flops 1095761920 | bytes 20217856 | tf_op jit(solution)/shard_map/grij,jgd->igrd/dot_general | solution.py:29
  36.8 0.0 slice-done
  36.8 0.0 slice-done.1
  36.9 13.1 %convolution_convert_fusion = bf16[2048,4608]{1,0:T(8,128)(2,1)} fusion(bf16[512,2048]{0,1:T(8,128)(2,1)S(1)} %bitcast.120, bf16[512,4608]{1,0:T(8,128)(2,1)S(1)} %bitcast.119), kind=kOutput, calls=%fused_computation.1 | convolution fusion | flops 9673113600 | bytes 25690112 | tf_op jit(solution)/shard_map/dot_general | solution.py:69
  50.0 0.0 reduce-scatter.2.cloned.1.call-update
  50.0 0.0 copy-start.4
  50.0 0.2 all-reduce.2.cloned.1.call-start
  50.2 130.4 %all-gather.2.cloned.1.call-done = bf16[2048,4608]{1,0:T(8,128)(2,1)} async-done(((bf16[256,4608]{1,0:T(8,128)(2,1)}), bf16[2048,4608]{1,0:T(8,128)(2,1)}) %all-gather.2.cloned.1.call-update) | async-done | bytes 18874384 | tf_op jit(solution)/shard_map/all_gather | solution.py:44
  180.7 16.1 %convolution_convert_fusion.1 = bf16[512,2048]{1,0:T(8,128)(2,1)} fusion(bf16[512,4608]{1,0:T(8,128)(2,1)} %param.13, bf16[2048,4608]{1,0:T(8,128)(2,1)} %all-gather.2.cloned.1.call-done), kind=kOutput, calls=%fused_computation.26 | convolution fusion | flops 9664724992 | bytes 25690112 | tf_op jit(solution)/shard_map/dot_general | solution.py:42
  196.8 3.9 copy.46
  200.7 0.0 copy-done.4
  200.7 23.1 %bitcast_convert_fusion.1 = bf16[8,512,128]{1,2,0:T(8,128)(2,1)} fusion(bf16[512,8,2,128]{0,3,2,1:T(8,128)(2,1)S(1)} %bitcast.108, f32[8,512,512,2]{2,1,3,0:T(8,128)} %get-tuple-element.9, bf16[512,8,2,128]{0,3,2,1:T(8,128)(2,1)} %bitcast.109, bf16[512,8,128,1]{0,2,3,1:T(8,128)(2,1)S(1)} %copy-done.4, f32[8,2,512]{2,1,0:T(2,128)S(1)} %get-tuple-element.8, ...), kind=kOutput, calls=%fused_computation.29 | convolution fusion | flops 3288867328 | bytes 23363584 | tf_op jit(solution)/shard_map/grij,igrd->jgd/dot_general | solution.py:64
  223.9 2.3 copy.25
  226.1 143.1 %reduce-scatter.2.cloned.1.call-done = bf16[256,4608]{1,0:T(8,128)(2,1)} async-done(((bf16[2048,4608]{1,0:T(8,128)(2,1)}), bf16[256,4608]{1,0:T(8,128)(2,1)}) %reduce-scatter.2.cloned.1.call-update) | async-done | bytes 2359312 | tf_op jit(solution)/shard_map/reduce_scatter | solution.py:72
  369.2 0.0 all-reduce.2.cloned.1.call-update
  369.2 0.0 copy-start
  369.3 0.0 copy-start.2
  369.3 10.2 %bitcast_convert_fusion = bf16[8,128,512]{2,1,0:T(8,128)(2,1)} fusion(bf16[512,8,2,128]{0,3,2,1:T(8,128)(2,1)} %bitcast.110, f32[8,512,512,2]{2,1,3,0:T(8,128)} %get-tuple-element.9, f32[8,2,512]{2,1,0:T(2,128)S(1)} %get-tuple-element.8, pred[512,512]{0,1:T(8,128)(4,1)S(1)} %fusion.24), kind=kOutput, calls=%fused_computation.28 | convolution fusion | flops 1095237632 | bytes 20217856 | tf_op jit(solution)/shard_map/grij,igrd->jgd/dot_general | solution.py:54
  379.5 2.3 copy.26
  381.7 0.0 copy-done
  381.7 0.0 copy-done.2
  381.7 27.7 %convolution_convert_fusion.2 = bf16[8,2,512,128]{2,3,1,0:T(8,128)(2,1)} fusion(bf16[512,8,128,1]{0,2,3,1:T(8,128)(2,1)S(1)} %copy-done.2, f32[8,512,512,2]{2,1,3,0:T(8,128)} %get-tuple-element.9, bf16[512,8,2,128]{0,3,2,1:T(8,128)(2,1)S(1)} %bitcast.111, bf16[512,8,128,1]{0,2,3,1:T(8,128)(2,1)} %copy.36, f32[8,2,512]{2,1,0:T(2,128)S(1)} %get-tuple-element.8, ...), kind=kOutput, calls=%fused_computation.31 | convolution fusion | flops 3289391616 | bytes 23363584 | tf_op jit(solution)/shard_map/grij,jgd->igrd/dot_general | solution.py:61
  409.4 3.9 copy.24
  413.4 31.5 %all-reduce.2.cloned.1.call-done = bf16[256,4608]{1,0:T(8,128)(2,1)} async-done(((bf16[256,4608]{1,0:T(8,128)(2,1)}), bf16[256,4608]{1,0:T(8,128)(2,1)}) %all-reduce.2.cloned.1.call-update) | async-done | bytes 2359312 | tf_op jit(solution)/shard_map/psum | solution.py:80
  444.8 7.3 %fusion.8 = f32[256,4608]{1,0:T(8,128)} fusion(bf16[256,4608]{1,0:T(8,128)(2,1)} %all-reduce.2.cloned.1.call-done, f32[256,4608]{1,0:T(8,128)} %param.15, f32[256,4608]{1,0:T(8,128)} %param.14), kind=kLoop, calls=%fused_computation.17 | loop fusion | flops 12976128 | bytes 16515072 | tf_op jit(solution)/shard_map/div | solution.py:84
  (1 shorter events, 0.0 us)
Async XLA Ops:
  7.2 173.5 %all-gather.2.cloned.1.call-start = ((), (), s32[]{:S(2)}) async-start(), calls=%async_computation.1 | async-start | bytes 21233664 | tf_op jit(solution)/shard_map/all_gather | solution.py:44
  7.9 361.3 %reduce-scatter.2.cloned.1.call-start = ((), (), s32[]{:S(2)}) async-start(), calls=%async_computation.2 | async-start | bytes 21233664 | tf_op jit(solution)/shard_map/reduce_scatter | solution.py:72
  10.1 17.7 %copy-start.1 = (bf16[512,8,128,1]{0,2,3,1:T(8,128)(2,1)}, bf16[512,8,128,1]{0,2,3,1:T(8,128)(2,1)S(1)}, u32[]{:S(2)}) copy-start(bf16[512,8,128,1]{0,2,3,1:T(8,128)(2,1)S(1)} %copy.30) | copy-start | bytes 3145732
  17.4 10.5 %copy-start.3 = (bf16[512,8,128,1]{0,2,3,1:T(8,128)(2,1)S(1)}, bf16[512,8,128,1]{0,2,3,1:T(8,128)(2,1)}, u32[]{:S(2)}) copy-start(bf16[512,8,128,1]{0,2,3,1:T(8,128)(2,1)} %copy.36) | copy-start | bytes 3145732
  17.4 19.5 %slice-start = ((s8[4718592]{0:T(1024)(128)(4,1)}), s8[4194304]{0:T(1024)(128)(4,1)S(1)}, s32[]{:S(2)}) async-start(s8[4718592]{0:T(1024)(128)(4,1)} %bitcast.118), calls=%async_computation.4 | async-start | bytes 8388608
  27.9 9.0 %slice-start.1 = ((s8[4718592]{0:T(1024)(128)(4,1)}), s8[524288]{0:T(1024)(128)(4,1)S(1)}, s32[]{:S(2)}) async-start(s8[4718592]{0:T(1024)(128)(4,1)} %bitcast.118), calls=%async_computation.5 | async-start | bytes 1048576
  50.0 150.7 %copy-start.4 = (bf16[512,8,128,1]{0,2,3,1:T(8,128)(2,1)S(1)}, bf16[512,8,128,1]{0,2,3,1:T(8,128)(2,1)}, u32[]{:S(2)}) copy-start(bf16[512,8,128,1]{0,2,3,1:T(8,128)(2,1)} %copy.36) | copy-start | bytes 3145732
  50.0 394.8 %all-reduce.2.cloned.1.call-start = ((), (), s32[]{:S(2)}) async-start(), calls=%async_computation.3 | async-start | bytes 4718592 | tf_op jit(solution)/shard_map/psum | solution.py:80
  369.2 12.5 %copy-start = (bf16[512,2048]{0,1:T(8,128)(2,1)S(1)}, bf16[512,2048]{0,1:T(8,128)(2,1)}, u32[]{:S(2)}) copy-start(bf16[512,2048]{0,1:T(8,128)(2,1)} %copy.46) | copy-start | bytes 6291460
  369.3 12.5 %copy-start.2 = (bf16[512,8,128,1]{0,2,3,1:T(8,128)(2,1)S(1)}, bf16[512,8,128,1]{0,2,3,1:T(8,128)(2,1)}, u32[]{:S(2)}) copy-start(bf16[512,8,128,1]{0,2,3,1:T(8,128)(2,1)} %copy-done.1) | copy-start | bytes 3145732
Sparse Core Ops, SparseCore 0:
  9.6 170.9 all-gather.1
  183.0 186.1 reduce-scatter.1
  372.4 72.4 all-reduce.1
where the time goes:
time: 459 us
  waiting for transfers between devices  306 us (67%)
  matrix products  110 us (24%)
  local copies, waits for them, and re-layouts  20.8 us (5%)
  between operations  13.9 us (3%)
  other arithmetic  8.26 us (2%)
    reduce_scatter x1, waiting for transfers between devices, per_device(): lax.psum_scatter(lax.optimization_barrier(product.astype(jnp.bfloat16)).a...  143 us
    all_gather x1, waiting for transfers between devices, per_device(): lax.all_gather(out_weight, 'shard', axis=0, tiled=True)  130 us
    psum x1, waiting for transfers between devices, per_device(): total = lax.psum(group_total, 'replica').astype(jnp.float32)  31.5 us
    dot_general x1, matrix products, per_device(): jnp.einsum('grij,jgd->igrd', grad_scores, key_heads, preferred_element_ty...  27.7 us
    dot_general x1, matrix products, per_device(): jnp.einsum('grij,igrd->jgd', grad_scores, query_heads, preferred_element_...  23.1 us
    dot_general x1, matrix products, per_device(): lax.dot_general(upstream, lax.all_gather(out_weight, 'shard', axis=0, til...  16.1 us
    dot_general x1, matrix products, per_device(): lax.dot_general(context, upstream, (((0,), (0,)), ((), ())), preferred_el...  13.1 us
    unnamed x19, local copies, waits for them, and re-layouts  11.8 us
  transfers between devices with their start and end apart: 3, of which 3 were waited for; matrix products, arithmetic and copies ran while one was open for 29% of the time, Pallas kernels for 0%

commit v1 on v0

v1 whole, which is shorter than its diff:
```python
import functools

import jax
import jax.numpy as jnp
import numpy as np
from jax import lax
from jax.experimental import pallas as pl
from jax.experimental.pallas import tpu as pltpu
from jax.sharding import PartitionSpec as P

HEADS = 16
KV_HEADS = 8
DH = 128
REPEAT = HEADS // KV_HEADS

SCALE = 1.0 / 12.0
CAP = 50.0
VMEM = 40 * 1024 * 1024
F32 = jnp.float32
BF16 = jnp.bfloat16

NT = (((1,), (1,)), ((), ()))
NN = (((1,), (0,)), ((), ()))


def dot(a, b, dims):
    return lax.dot_general(a, b, dims, preferred_element_type=F32)


def call(body, grid, in_specs, out_specs, out_shape, scratch=(), aliases=None, cost=None):
    return pl.pallas_call(
        body,
        grid_spec=pltpu.PrefetchScalarGridSpec(
            num_scalar_prefetch=1,
            grid=grid,
            in_specs=in_specs,
            out_specs=out_specs,
            scratch_shapes=list(scratch),
        ),
        out_shape=out_shape,
        input_output_aliases=aliases or {},
        cost_estimate=cost,
        compiler_params=pltpu.CompilerParams(vmem_limit_bytes=VMEM),
    )


def fill_mask(mask_ref, seg_row_ref, seg_col_ref):
    length = mask_ref.shape[0]
    j = lax.broadcasted_iota(jnp.int32, (length, length), 0)
    i = lax.broadcasted_iota(jnp.int32, (length, length), 1)
    allowed = (j <= i) & (seg_col_ref[...] == seg_row_ref[...])
    mask_ref[...] = jnp.where(allowed, 1.0, 0.0).astype(F32)


def tiles_of(length):
    tile = 256
    return [(t * tile, tile, (t + 1) * tile) for t in range(length // tile)]


def softmax_tile(key, query, mask):
    cap_tanh = jnp.tanh(dot(key, query, NT) * (SCALE / CAP))
    weights = jnp.exp(cap_tanh * CAP) * mask
    inverse = 1.0 / jnp.sum(weights, axis=0, keepdims=True)
    return weights * inverse, cap_tanh


def forward_body(heads, sc_ref, q_ref, k_ref, v_ref, seg_row_ref, seg_col_ref, out_ref, mask_ref):
    @pl.when(pl.program_id(0) == 0)
    def _():
        fill_mask(mask_ref, seg_row_ref, seg_col_ref)

    value_t = v_ref[...].T
    for h in range(heads):
        for start, tile, upto in tiles_of(q_ref.shape[0]):
            probs, _ = softmax_tile(
                k_ref[:upto, :],
                q_ref[start : start + tile, h * DH : (h + 1) * DH],
                mask_ref[:upto, start : start + tile],
            )
            context = dot(value_t[:, :upto], probs.astype(BF16), NN)
            out_ref[h * DH : (h + 1) * DH, start : start + tile] = context.astype(BF16)


def forward(sc, flip, queries, keys, values, seg_row, seg_col, lay):
    length = queries.shape[0]
    per = lay.heads_shard

    def shard_of(i, sc):
        return 2 * i + (1 - sc[0] if flip else sc[0])

    def kv_of(i, sc):
        return (shard_of(i, sc) * per) // REPEAT

    pairs = lay.z * per * length * length
    return call(
        functools.partial(forward_body, per),
        (lay.z,),
        [
            pl.BlockSpec((length, per * DH), lambda i, sc: (0, shard_of(i, sc))),
            pl.BlockSpec((length, DH), lambda i, sc: (0, kv_of(i, sc))),
            pl.BlockSpec((length, DH), lambda i, sc: (0, kv_of(i, sc))),
            pl.BlockSpec((1, length), lambda i, sc: (0, 0)),
            pl.BlockSpec((length, 1), lambda i, sc: (0, 0)),
        ],
        pl.BlockSpec((per * DH, length), lambda i, sc: (i, 0)),
        jax.ShapeDtypeStruct((lay.z * per * DH, length), BF16),
        scratch=[pltpu.VMEM((length, length), F32)],
        cost=pl.CostEstimate(
            flops=4 * pairs * DH, transcendentals=2 * pairs, bytes_accessed=4 * length * HEADS * DH
        ),
    )(sc, queries, keys, values, seg_row, seg_col)


def product_body(
    half_tiles, first, last, sc_ref, c0_ref, c1_ref, u0_ref, u1_ref, sa_ref, ka_ref, sb_ref, kb_ref, acc_ref
):
    n = pl.program_id(0)
    half = acc_ref.shape[0] // 2
    acc = dot(c0_ref[...], u0_ref[...], NN) + dot(c1_ref[...], u1_ref[...], NN)
    acc_ref[...] = acc.astype(BF16)

    def split(bit, send_ref, keep_ref):
        keep_ref[...] = acc_ref[pl.ds(pl.multiple_of(bit * half, half), half), :]
        send_ref[...] = acc_ref[pl.ds(pl.multiple_of((1 - bit) * half, half), half), :]

    @pl.when(n < half_tiles)
    def _():
        split(sc_ref[first], sa_ref, ka_ref)

    @pl.when(n >= half_tiles)
    def _():
        split(sc_ref[last], sb_ref, kb_ref)


def product(sc, k, context0, context1, up0, up1, lay):
    length, width = up0.shape
    rows = lay.rows
    tile = width // 4
    at = lay.at_z + k
    left = lambda n, sc: (0, jnp.minimum(n, 1))
    right = lambda n, sc: (0, jnp.maximum(n - 2, 0))
    part = jax.ShapeDtypeStruct((rows // 2, width // 2), BF16)
    return call(
        functools.partial(product_body, 2, lay.at_bit(0), lay.at_bit(lay.bits - 1)),
        (4,),
        [
            pl.BlockSpec((rows, length), lambda n, sc: (sc[at], 0)),
            pl.BlockSpec((rows, length), lambda n, sc: (sc[at], 0)),
            pl.BlockSpec((length, tile), lambda n, sc: (0, n)),
            pl.BlockSpec((length, tile), lambda n, sc: (0, n)),
        ],
        [
            pl.BlockSpec((rows // 2, tile), left),
            pl.BlockSpec((rows // 2, tile), left),
            pl.BlockSpec((rows // 2, tile), right),
            pl.BlockSpec((rows // 2, tile), right),
        ],
        [part] * 4,
        scratch=[pltpu.VMEM((rows, tile), BF16)],
        cost=pl.CostEstimate(
            flops=4 * rows * length * width,
            transcendentals=0,
            bytes_accessed=4 * length * width + 2 * rows * width,
        ),
    )(sc, context0, context1, up0, up1)


def grad_context_body(parts, sc_ref, u0_ref, u1_ref, *refs):
    weights, (g0_ref, g1_ref, a0_ref, a1_ref) = refs[:-4], refs[-4:]
    n = pl.program_id(0)

    def add(weight_ref):
        d0 = dot(u0_ref[...], weight_ref[...], NT)
        d1 = dot(u1_ref[...], weight_ref[...], NT)

        @pl.when(n == 0)
        def _():
            a0_ref[...] = d0
            a1_ref[...] = d1

        @pl.when(n > 0)
        def _():
            a0_ref[...] += d0
            a1_ref[...] += d1

    if len(weights) == 1:
        add(weights[0])
    else:
        for p in range(parts):
            pl.when(n == p)(functools.partial(add, weights[p]))

    @pl.when(n == parts - 1)
    def _():
        g0_ref[...] = a0_ref[...].astype(BF16)
        g1_ref[...] = a1_ref[...].astype(BF16)


def grad_context(sc, up0, up1, weights, lay):
    length, width = up0.shape
    rows = lay.rows
    tile = width // 4
    at = lay.at_piece
    if len(weights) == 1:
        weight_specs = [pl.BlockSpec((rows, tile), lambda n, sc: (0, sc[at + n]))]
    else:
        weight_specs = [pl.BlockSpec((rows, tile), lambda n, sc: (0, 0))] * 4
    return call(
        functools.partial(grad_context_body, 4),
        (4,),
        [pl.BlockSpec((length, tile), lambda n, sc: (0, sc[at + n]))] * 2 + weight_specs,
        [pl.BlockSpec((length, rows), lambda n, sc: (0, 0))] * 2,
        [jax.ShapeDtypeStruct((length, rows), BF16)] * 2,
        scratch=[pltpu.VMEM((length, rows), F32)] * 2,
        cost=pl.CostEstimate(
            flops=4 * rows * length * width,
            transcendentals=0,
            bytes_accessed=4 * length * width + 2 * rows * width,
        ),
    )(sc, up0, up1, *weights)


def backward_body(
    per, sc_ref, q_ref, k_ref, v_ref, seg_row_ref, seg_col_ref, own_ref, other_ref, *refs
):
    gq_ref, gk_ref, gv_ref, mask_ref, ak_ref, av_ref = refs[-6:]
    group = pl.program_id(0)
    parity = sc_ref[0]

    @pl.when(group == 0)
    def _():
        fill_mask(mask_ref, seg_row_ref, seg_col_ref)

    key_t = k_ref[...].T
    ak_ref[...] = jnp.zeros_like(ak_ref)
    av_ref[...] = jnp.zeros_like(av_ref)
    for h in range(REPEAT):
        side = group if per == REPEAT else h
        column = h if per == REPEAT else 0
        cols = slice(column * DH, (column + 1) * DH)
        grad = jnp.where(side == parity, own_ref[:, cols], other_ref[:, cols])
        for start, tile, upto in tiles_of(q_ref.shape[0]):
            query = q_ref[start : start + tile, h * DH : (h + 1) * DH]
            probs, cap_tanh = softmax_tile(
                k_ref[:upto, :], query, mask_ref[:upto, start : start + tile]
            )
            grad_rows = grad[start : start + tile, :]
            grad_probs = dot(v_ref[:upto, :], grad_rows, NT)
            delta = jnp.sum(probs * grad_probs, axis=0, keepdims=True)
            scores = probs * (grad_probs - delta) * (SCALE - SCALE * (cap_tanh * cap_tanh))
            scores = scores.astype(BF16)
            av_ref[:upto, :] += dot(probs.astype(BF16), grad_rows, NN)
            ak_ref[:upto, :] += dot(scores, query, NN)
            grad_query = dot(key_t[:, :upto], scores, NN).T
            gq_ref[start : start + tile, h * DH : (h + 1) * DH] = grad_query.astype(BF16)
    gk_ref[...] = ak_ref[...].astype(BF16)
    gv_ref[...] = av_ref[...].astype(BF16)


def backward(sc, k, queries, keys, values, seg_row, seg_col, own, other, before, lay):
    length = queries.shape[0]
    per = lay.heads_shard
    groups = 2 * per // REPEAT
    at = lay.at_z + k

    def whole(i, sc):
        return (0, sc[at] * groups + i)

    if per == REPEAT:
        gc_spec = pl.BlockSpec((length, lay.rows), lambda i, sc: (0, 0))
    else:
        gc_spec = pl.BlockSpec((length, DH), lambda i, sc: (0, 0))
    in_specs = [
        pl.BlockSpec((length, REPEAT * DH), whole),
        pl.BlockSpec((length, DH), whole),
        pl.BlockSpec((length, DH), whole),
        pl.BlockSpec((1, length), lambda i, sc: (0, 0)),
        pl.BlockSpec((length, 1), lambda i, sc: (0, 0)),
        gc_spec,
        gc_spec,
    ]
    args = [sc, queries, keys, values, seg_row, seg_col, own, other]
    aliases = {}
    if before is not None:
        aliases = {len(args) + n: n for n in range(3)}
        in_specs += [pl.BlockSpec(memory_space=pl.ANY)] * 3
        args += list(before)
    pairs = 2 * per * length * length
    return call(
        functools.partial(backward_body, per),
        (groups,),
        in_specs,
        [
            pl.BlockSpec((length, REPEAT * DH), whole),
            pl.BlockSpec((length, DH), whole),
            pl.BlockSpec((length, DH), whole),
        ],
        [
            jax.ShapeDtypeStruct(queries.shape, BF16),
            jax.ShapeDtypeStruct(keys.shape, BF16),
            jax.ShapeDtypeStruct(values.shape, BF16),
        ],
        scratch=[
            pltpu.VMEM((length, length), F32),
            pltpu.VMEM((length, DH), F32),
            pltpu.VMEM((length, DH), F32),
        ],
        aliases=aliases,
        cost=pl.CostEstimate(
            flops=10 * pairs * DH, transcendentals=2 * pairs, bytes_accessed=20 * length * per * DH
        ),
    )(*args)


def adam_body(pieces, tokens, sc_ref, m1_ref, m2_ref, *refs):
    out_ref = refs[-1]
    n = pl.program_id(0)

    def step(piece_ref):
        gradient = piece_ref[...].astype(F32) * (1.0 / tokens)
        moment_one = 0.9 * m1_ref[...] + 0.1 * gradient
        moment_two = 0.95 * m2_ref[...] + 0.05 * gradient * gradient
        out_ref[...] = moment_one / (jnp.sqrt(moment_two) + 1e-08)

    for p in range(pieces):
        pl.when(n == p)(functools.partial(step, refs[p]))


def adam(places, pieces, first_moment, second_moment, tokens):
    rows, width = pieces[0].shape
    count = len(pieces)
    spec = pl.BlockSpec((rows, width), lambda n, at: (at[2 * n], at[2 * n + 1]))
    return call(
        functools.partial(adam_body, count, tokens),
        (count,),
        [spec, spec] + [pl.BlockSpec((rows, width), lambda n, at: (0, 0))] * count,
        spec,
        jax.ShapeDtypeStruct(first_moment.shape, F32),
        cost=pl.CostEstimate(
            flops=10 * first_moment.size,
            transcendentals=first_moment.size,
            bytes_accessed=14 * first_moment.size,
        ),
    )(places, first_moment, second_moment, *pieces)


class Layout:
    def __init__(self, replicas, shards, rows):
        self.replicas, self.shards, self.rows = replicas, shards, rows
        self.z = shards // 2
        self.bits = replicas.bit_length() - 1
        self.heads_shard = HEADS // shards
        self.order = [0] + list(range(1, self.z, 2)) + list(range(self.z - 2, 0, -2))
        self.place = [self.order.index(z) for z in range(self.z)]
        self.at_z = 1
        self.at_piece = self.at_z + self.z
        table = []
        for r in range(replicas):
            bits = [(r >> b) & 1 for b in range(self.bits)]
            x, y = bits[0], bits[-1]
            for s in range(shards):
                z, core = s // 2, s % 2
                zs = [self.order[(self.place[z] - k) % self.z] for k in range(self.z)]
                table.append([core] + zs + [x, 1 - x, 2 + y, 3 - y] + bits)
        self.table = np.array(table, np.int32)

    def at_bit(self, b):
        return self.at_piece + 4 + b

    def sibling(self, x):
        return lax.ppermute(x, "shard", [(s, s ^ 1) for s in range(self.shards)])

    def onward(self, x):
        perm = []
        for p in range(self.z):
            a, b = self.order[p], self.order[(p + 1) % self.z]
            perm += [(2 * a + core, 2 * b + core) for core in range(2)]
        return lax.ppermute(x, "shard", perm)

    def across(self, x, b):
        return lax.ppermute(x, "replica", [(r, r ^ (1 << b)) for r in range(self.replicas)])


def per_device(queries, keys, values, segments, out_weight, upstream, first_moment, second_moment):
    length, width = upstream.shape
    rows = out_weight.shape[0]
    lay = Layout(lax.axis_size("replica"), lax.axis_size("shard"), rows)
    device = lax.axis_index("replica") * lay.shards + lax.axis_index("shard")
    sc = lax.dynamic_index_in_dim(jnp.asarray(lay.table), device, 0, keepdims=False)
    bit = [sc[lay.at_bit(b)] for b in range(lay.bits)]
    left_bits = list(range(lay.bits))
    right_bits = left_bits[::-1]
    quarter = width // 4

    upstream_other = lay.sibling(upstream)

    ring_x = lax.dynamic_slice_in_dim(out_weight, bit[left_bits[0]] * quarter, quarter, 1)
    ring_y = lax.dynamic_slice_in_dim(
        out_weight, 2 * quarter + bit[right_bits[0]] * quarter, quarter, 1
    )
    weights = [(out_weight,)]
    for k in range(1, lay.z):
        ring_x, ring_y = lay.onward(ring_x), lay.onward(ring_y)
        weights.append(
            (
                ring_x,
                lay.across(ring_x, left_bits[0]),
                ring_y,
                lay.across(ring_y, right_bits[0]),
            )
        )

    seg_row = segments
    seg_col = segments.reshape(length, 1)
    context_send = forward(sc, True, queries, keys, values, seg_row, seg_col, lay)
    context_other = lay.sibling(context_send)
    context_own = forward(sc, False, queries, keys, values, seg_row, seg_col, lay)

    def halved(send, keep, received_before, order):
        total = keep.astype(F32) + lay.across(send, order[0]).astype(F32)
        for b in order[1:]:
            size = total.shape[0] // 2
            away = lax.dynamic_slice_in_dim(total, (1 - bit[b]) * size, size, 0).astype(BF16)
            stay = lax.dynamic_slice_in_dim(total, bit[b] * size, size, 0)
            total = stay + lay.across(away, b).astype(F32)
        if received_before is not None:
            total = total + received_before.astype(F32)
        return total.astype(BF16)

    passed = [None, None]
    for k in list(range(1, lay.z)) + [0]:
        send_l, keep_l, send_r, keep_r = product(
            sc, k, context_own, context_other, upstream, upstream_other, lay
        )
        sums = [
            halved(send_l, keep_l, passed[0], left_bits),
            halved(send_r, keep_r, passed[1], right_bits),
        ]
        if k:
            passed = [lay.onward(x) for x in sums]

    pieces, places = [], []
    for half, order in enumerate([left_bits, right_bits]):
        index = sum(bit[b] << (lay.bits - 1 - n) for n, b in enumerate(order))
        have = [(sums[half], index)]
        for n, b in reversed(list(enumerate(order))):
            weight = 1 << (lay.bits - 1 - n)
            flip = (1 - 2 * bit[b]) * weight
            have += [(lay.across(x, b), at + flip) for x, at in have]
        pieces += [x for x, _ in have]
        for _, at in have:
            places += [at, jnp.int32(half)]
    tokens = length * lay.replicas * lay.shards
    adam_step = adam(
        jnp.stack(places).astype(jnp.int32), pieces, first_moment, second_moment, tokens
    )

    grads = None
    for k in range(lay.z):
        own, send = grad_context(sc, upstream, upstream_other, weights[k], lay)
        grads = backward(
            sc, k, queries, keys, values, seg_row, seg_col, own, lay.sibling(send), grads, lay
        )
    return (*grads, adam_step)


def solution(mesh):
    both = P(("replica", "shard"), None)
    shard = P("shard", None)
    return jax.shard_map(
        per_device,
        mesh=mesh,
        in_specs=(both, both, both, both, shard, both, shard, shard),
        out_specs=(both, both, both, shard),
        check_vma=False,
    )
```

time: 459 us -> 276 us (0.60)
  waiting for transfers between devices: 306 us -> 106 us
  matrix products: 110 us -> 0 us
  Pallas kernels: 0 us -> 98.3 us
  starting transfers between devices: 0.3 us -> 45.6 us
  local copies, waits for them, and re-layouts: 20.8 us -> 14.2 us
  other arithmetic: 8.26 us -> 2.77 us
  between operations: 13.9 us -> 8.85 us
    reduce_scatter x1 -> x0, waiting for transfers between devices: 143 us -> none  [per_device(): lax.psum_scatter(lax.optimization_barrier(product.astype(jnp.bfloat16)).a...]
    all_gather x1 -> x0, waiting for transfers between devices: 130 us -> none  [per_device(): lax.all_gather(out_weight, 'shard', axis=0, tiled=True)]
    dot_general x7 -> x0, matrix products: 110 us -> none  [the longest x1 27.7 us: per_device(): jnp.einsum('grij,jgd->igrd', grad_scores, key_heads, preferred_element_ty...]
    ppermute x0 -> x46, waiting for transfers between devices: none -> 106 us  [the longest x12 53.1 us: onward(): return lax.ppermute(x, 'shard', perm)]
    pallas_call x0 -> x15, Pallas kernels: none -> 98.3 us  [the longest x4 26.4 us: grad_context(): call(functools.partial(grad_context_body, 4), (4,), [pl.BlockSpec((length...]
    ppermute x0 -> x46, starting transfers between devices: none -> 45.6 us  [the longest x28 33 us: across(): lax.ppermute(x, 'replica', [(r, r ^ 1 << b) for r in range(self.replicas)])]
    psum x1 -> x0, waiting for transfers between devices: 31.5 us -> none  [per_device(): total = lax.psum(group_total, 'replica').astype(jnp.float32)]
    reshape x4 -> x1, local copies, waits for them, and re-layouts: 8.97 us -> 0.14 us  [per_device(): seg_col = segments.reshape(length, 1)]
  transfers between devices with their start and end apart: 3 -> 46, of which waited for: 3 -> 19; matrix products, arithmetic and copies ran while one was open for 29% -> 3% of each run, Pallas kernels for 0% -> 33%
where the time goes in v1:
time: 276 us; the launch traced here: 275 us
  waiting for transfers between devices  106 us (38%)
  Pallas kernels  98.3 us (36%)
  starting transfers between devices  45.6 us (17%)
  local copies, waits for them, and re-layouts  14.2 us (5%)
  between operations  8.85 us (3%)
  other arithmetic  2.77 us (1%)
    ppermute x12, waiting for transfers between devices, onward(): return lax.ppermute(x, 'shard', perm)  53.1 us
    ppermute x28, waiting for transfers between devices, across(): lax.ppermute(x, 'replica', [(r, r ^ 1 << b) for r in range(self.replicas)])  52.4 us
    ppermute x28, starting transfers between devices, across(): lax.ppermute(x, 'replica', [(r, r ^ 1 << b) for r in range(self.replicas)])  33 us
    pallas_call x4, Pallas kernels, grad_context(): call(functools.partial(grad_context_body, 4), (4,), [pl.BlockSpec((length...  26.4 us
    pallas_call x4, Pallas kernels, product(): call(functools.partial(product_body, 2, lay.at_bit(0), lay.at_bit(lay.bit...  26.3 us
    pallas_call x4, Pallas kernels, backward(): call(functools.partial(backward_body, per), (groups,), in_specs, [pl.Bloc...  25.4 us
    pallas_call x2, Pallas kernels, forward(): call(functools.partial(forward_body, per), (lay.z,), [pl.BlockSpec((lengt...  13.8 us
    ppermute x12, starting transfers between devices, onward(): return lax.ppermute(x, 'shard', perm)  11.7 us
  transfers between devices with their start and end apart: 46, of which 19 were waited for; matrix products, arithmetic and copies ran while one was open for 3% of the time, Pallas kernels for 33%

profile of v1, /device:TPU:0, one launch (start us, length us, event | category | flops | bytes accessed | tf_op | source)
XLA Modules:
  0.0 275.3 jit_solution(6369158502694557530)
XLA Ops:
  3.7 2.5 constant_dynamic-slice_fusion
  6.2 2.6 collective-permute-start.5
  8.8 2.6 collective-permute-start.1
  11.6 1.2 copy-done.2
  12.8 1.2 copy-done.5
  14.0 7.2 %shard_map.129 = bf16[1024,512]{1,0:T(8,128)(2,1)} custom-call(s32[11]{0:T(128)S(1)} %get-tuple-element.79.sc_ref, bf16[512,2048]{1,0:T(8,128)(2,1)S(1)} %copy-done.1, bf16[512,1024]{1,0:T(8,128)(2,1)S(1)} %copy-done.2, bf16[512,1024]{1,0:T(8,128)(2,1)S(1)} %copy-done.5, s32[1,512]{1,0:T(1,128)S(1)} %copy-done.13, s32[512,1]{1,0:T(8,128)S(1)} %copy.25.seg_col_ref), custom_call_target="tpu_custom_call" | custom-call | flops 1073741824 | bytes 4194304 | tf_op jit(solution)/shard_map/pallas_call | solution.py:95
  21.3 3.1 %collective-permute-done.5.refs_2_ = bf16[256,1152]{1,0:T(8,128)(2,1)} collective-permute-done((bf16[256,1152]{1,0:T(8,128)(2,1)}, bf16[256,1152]{1,0:T(8,128)(2,1)}, u32[]{:S(2)}, u32[]{:S(2)}) %collective-permute-start.5) | collective-permute-done | bytes 589856 | tf_op jit(solution)/shard_map/ppermute | solution.py:377
  24.3 1.0 collective-permute-start.6
  25.4 11.6 %collective-permute-done.1.refs_0_ = bf16[256,1152]{1,0:T(8,128)(2,1)} collective-permute-done((bf16[256,1152]{1,0:T(8,128)(2,1)}, bf16[256,1152]{1,0:T(8,128)(2,1)}, u32[]{:S(2)}, u32[]{:S(2)}) %collective-permute-start.1) | collective-permute-done | bytes 589856 | tf_op jit(solution)/shard_map/ppermute | solution.py:377
  37.0 1.0 collective-permute-start.2
  44.5 1.2 copy-done.3
  45.7 1.2 copy-done.6
  46.9 6.5 %shard_map.128.c0_ref = bf16[1024,512]{1,0:T(8,128)(2,1)S(1)} custom-call(s32[11]{0:T(128)S(1)} %get-tuple-element.79.sc_ref, bf16[512,2048]{1,0:T(8,128)(2,1)S(1)} %copy-done.1, bf16[512,1024]{1,0:T(8,128)(2,1)S(1)} %copy-done.3, bf16[512,1024]{1,0:T(8,128)(2,1)S(1)} %copy-done.6, s32[1,512]{1,0:T(1,128)S(1)} %copy-done.13, s32[512,1]{1,0:T(8,128)S(1)} %copy.25.seg_col_ref), custom_call_target="tpu_custom_call" | custom-call | flops 1073741824 | bytes 4194304 | tf_op jit(solution)/shard_map/pallas_call | solution.py:95
  53.5 1.6 collective-permute-start.14
  55.0 1.5 collective-permute-start.13
  57.1 2.3 copy-done
  59.4 6.5 %shard_map.123 = (bf16[512,256]{1,0:T(8,128)(2,1)S(1)}, bf16[512,256]{1,0:T(8,128)(2,1)S(1)}) custom-call(s32[11]{0:T(128)S(1)} %get-tuple-element.79.sc_ref, bf16[512,4608]{1,0:T(8,128)(2,1)S(1)} %copy-done, bf16[512,4608]{1,0:T(8,128)(2,1)} %collective-permute-done.u1_ref, bf16[256,4608]{1,0:T(8,128)(2,1)S(1)} %copy-done.8), custom_call_target="tpu_custom_call" | custom-call | flops 2415919104 | bytes 11796480 | tf_op jit(solution)/shard_map/pallas_call | solution.py:207
  65.9 3.4 %collective-permute-start.7 = (bf16[256,1152]{1,0:T(8,128)(2,1)}, bf16[256,1152]{1,0:T(8,128)(2,1)S(1)}, u32[]{:S(2)}, u32[]{:S(2)}) collective-permute-start(bf16[256,1152]{1,0:T(8,128)(2,1)} %collective-permute-done.6.refs_2_), channel_id=1, source_target_pairs={{0,2},{1,3},{2,6},{3,7},{6,4},{7,5},{4,0},{5,1},{8,10},{9,11},{10,... | collective-permute-start | bytes 1769480 | tf_op jit(solution)/shard_map/ppermute | solution.py:377
  69.6 7.0 %shard_map.133 = (bf16[128,2304]{1,0:T(8,128)(2,1)}, bf16[128,2304]{1,0:T(8,128)(2,1)S(1)}, bf16[128,2304]{1,0:T(8,128)(2,1)S(1)}, bf16[128,2304]{1,0:T(8,128)(2,1)S(1)}) custom-call(s32[11]{0:T(128)S(1)} %get-tuple-element.79.sc_ref, bf16[1024,512]{1,0:T(8,128)(2,1)S(1)} %shard_map.128.c0_ref, bf16[1024,512]{1,0:T(8,128)(2,1)S(1)} %collective-permute-done.17.c1_ref, ...), custom_call_target="tpu_custom_call" | custom-call | flops 2415919104 | bytes 11796480 | tf_op jit(solution)/shard_map/pallas_call | solution.py:143
  76.6 6.4 %shard_map.132 = (bf16[128,2304]{1,0:T(8,128)(2,1)S(1)}, bf16[128,2304]{1,0:T(8,128)(2,1)S(1)}, bf16[128,2304]{1,0:T(8,128)(2,1)S(1)}, bf16[128,2304]{1,0:T(8,128)(2,1)S(1)}) custom-call(s32[11]{0:T(128)S(1)} %get-tuple-element.79.sc_ref, bf16[1024,512]{1,0:T(8,128)(2,1)S(1)} %shard_map.128.c0_ref, bf16[1024,512]{1,0:T(8,128)(2,1)S(1)} %collective-permute-done.17.c1_ref, ...), custom_call_target="tpu_custom_call" | custom-call | flops 2415919104 | bytes 11796480 | tf_op jit(solution)/shard_map/pallas_call | solution.py:143
  83.7 6.4 %shard_map.131 = (bf16[128,2304]{1,0:T(8,128)(2,1)S(1)}, bf16[128,2304]{1,0:T(8,128)(2,1)S(1)}, bf16[128,2304]{1,0:T(8,128)(2,1)S(1)}, bf16[128,2304]{1,0:T(8,128)(2,1)S(1)}) custom-call(s32[11]{0:T(128)S(1)} %get-tuple-element.79.sc_ref, bf16[1024,512]{1,0:T(8,128)(2,1)S(1)} %shard_map.128.c0_ref, bf16[1024,512]{1,0:T(8,128)(2,1)S(1)} %collective-permute-done.17.c1_ref, ...), custom_call_target="tpu_custom_call" | custom-call | flops 2415919104 | bytes 11796480 | tf_op jit(solution)/shard_map/pallas_call | solution.py:143
  90.2 0.8 copy-done.16
  91.0 0.8 copy-done.18
  91.8 1.5 collective-permute-start.24
  93.3 6.4 %shard_map.130 = (bf16[128,2304]{1,0:T(8,128)(2,1)S(1)}, bf16[128,2304]{1,0:T(8,128)(2,1)S(1)}, bf16[128,2304]{1,0:T(8,128)(2,1)S(1)}, bf16[128,2304]{1,0:T(8,128)(2,1)S(1)}) custom-call(s32[11]{0:T(128)S(1)} %get-tuple-element.79.sc_ref, bf16[1024,512]{1,0:T(8,128)(2,1)S(1)} %shard_map.128.c0_ref, bf16[1024,512]{1,0:T(8,128)(2,1)S(1)} %collective-permute-done.17.c1_ref, ...), custom_call_target="tpu_custom_call" | custom-call | flops 2415919104 | bytes 11796480 | tf_op jit(solution)/shard_map/pallas_call | solution.py:143
  99.8 0.8 copy-done.14
  100.6 1.5 collective-permute-start.8
  102.7 6.7 %shard_map.122 = (bf16[512,256]{1,0:T(8,128)(2,1)S(1)}, bf16[512,256]{1,0:T(8,128)(2,1)S(1)}) custom-call(s32[11]{0:T(128)S(1)} %get-tuple-element.79.sc_ref, bf16[512,4608]{1,0:T(8,128)(2,1)S(1)} %copy-done, bf16[512,4608]{1,0:T(8,128)(2,1)} %collective-permute-done.u1_ref, bf16[256,1152]{1,0:T(8,128)(2,1)} %collective-permute-done.1.refs_0_, ...), custom_call_target="tpu_custom_call" | custom-call | flops 2415919104 | bytes 11796480 | tf_op jit(solution)/shard_map/pallas_call | solution.py:207
  110.1 6.7 %shard_map.121 = (bf16[512,256]{1,0:T(8,128)(2,1)S(1)}, bf16[512,256]{1,0:T(8,128)(2,1)S(1)}) custom-call(s32[11]{0:T(128)S(1)} %get-tuple-element.79.sc_ref, bf16[512,4608]{1,0:T(8,128)(2,1)S(1)} %copy-done, bf16[512,4608]{1,0:T(8,128)(2,1)} %collective-permute-done.u1_ref, bf16[256,1152]{1,0:T(8,128)(2,1)} %collective-permute-done.2.refs_0_, ...), custom_call_target="tpu_custom_call" | custom-call | flops 2415919104 | bytes 11796480 | tf_op jit(solution)/shard_map/pallas_call | solution.py:207
  116.9 1.5 collective-permute-start.22
  118.5 1.3 convert_add_fusion.4
  119.8 6.0 %collective-permute-done.38 = bf16[128,2304]{1,0:T(8,128)(2,1)S(1)} collective-permute-done((bf16[128,2304]{1,0:T(8,128)(2,1)S(1)}, bf16[128,2304]{1,0:T(8,128)(2,1)S(1)}, u32[]{:S(2)}, u32[]{:S(2)}) %collective-permute-start.38) | collective-permute-done | bytes 589856 | tf_op jit(solution)/shard_map/ppermute | solution.py:380
  125.8 1.5 collective-permute-start.36
  127.4 7.0 %collective-permute-done.22 = bf16[128,2304]{1,0:T(8,128)(2,1)S(1)} collective-permute-done((bf16[128,2304]{1,0:T(8,128)(2,1)S(1)}, bf16[128,2304]{1,0:T(8,128)(2,1)S(1)}, u32[]{:S(2)}, u32[]{:S(2)}) %collective-permute-start.22) | collective-permute-done | bytes 589856 | tf_op jit(solution)/shard_map/ppermute | solution.py:380
  135.2 5.5 %collective-permute-done.36 = bf16[128,2304]{1,0:T(8,128)(2,1)S(1)} collective-permute-done((bf16[128,2304]{1,0:T(8,128)(2,1)S(1)}, bf16[128,2304]{1,0:T(8,128)(2,1)S(1)}, u32[]{:S(2)}, u32[]{:S(2)}) %collective-permute-start.36) | collective-permute-done | bytes 589856 | tf_op jit(solution)/shard_map/ppermute | solution.py:380
  141.3 6.4 %collective-permute-done.20 = bf16[128,2304]{1,0:T(8,128)(2,1)S(1)} collective-permute-done((bf16[128,2304]{1,0:T(8,128)(2,1)S(1)}, bf16[128,2304]{1,0:T(8,128)(2,1)S(1)}, u32[]{:S(2)}, u32[]{:S(2)}) %collective-permute-start.20) | collective-permute-done | bytes 589856 | tf_op jit(solution)/shard_map/ppermute | solution.py:380
  147.8 1.5 collective-permute-start.18
  149.5 5.2 %collective-permute-done.34 = bf16[128,2304]{1,0:T(8,128)(2,1)S(1)} collective-permute-done((bf16[128,2304]{1,0:T(8,128)(2,1)S(1)}, bf16[128,2304]{1,0:T(8,128)(2,1)S(1)}, u32[]{:S(2)}, u32[]{:S(2)}) %collective-permute-start.34) | collective-permute-done | bytes 589856 | tf_op jit(solution)/shard_map/ppermute | solution.py:380
  155.1 5.8 %collective-permute-done.18 = bf16[128,2304]{1,0:T(8,128)(2,1)S(1)} collective-permute-done((bf16[128,2304]{1,0:T(8,128)(2,1)S(1)}, bf16[128,2304]{1,0:T(8,128)(2,1)S(1)}, u32[]{:S(2)}, u32[]{:S(2)}) %collective-permute-start.18) | collective-permute-done | bytes 589856 | tf_op jit(solution)/shard_map/ppermute | solution.py:380
  160.9 1.5 collective-permute-start.25
  162.7 8.3 %collective-permute-done.32 = bf16[128,2304]{1,0:T(8,128)(2,1)S(1)} collective-permute-done((bf16[128,2304]{1,0:T(8,128)(2,1)S(1)}, bf16[128,2304]{1,0:T(8,128)(2,1)S(1)}, u32[]{:S(2)}, u32[]{:S(2)}) %collective-permute-start.32) | collective-permute-done | bytes 589856 | tf_op jit(solution)/shard_map/ppermute | solution.py:380
  170.9 0.9 collective-permute-start.39
  172.0 2.5 collective-permute-done.25
  174.8 2.8 %collective-permute-done.39 = bf16[64,2304]{1,0:T(8,128)(2,1)S(1)} collective-permute-done((bf16[64,2304]{1,0:T(8,128)(2,1)S(1)}, bf16[64,2304]{1,0:T(8,128)(2,1)S(1)}, u32[]{:S(2)}, u32[]{:S(2)}) %collective-permute-start.39) | collective-permute-done | bytes 294944 | tf_op jit(solution)/shard_map/ppermute | solution.py:380
  178.4 2.8 %collective-permute-done.23 = bf16[64,2304]{1,0:T(8,128)(2,1)S(1)} collective-permute-done((bf16[64,2304]{1,0:T(8,128)(2,1)S(1)}, bf16[64,2304]{1,0:T(8,128)(2,1)S(1)}, u32[]{:S(2)}, u32[]{:S(2)}) %collective-permute-start.23) | collective-permute-done | bytes 294944 | tf_op jit(solution)/shard_map/ppermute | solution.py:380
  181.2 1.0 collective-permute-start.37
  182.2 5.7 %collective-permute-done.26 = bf16[64,2304]{1,0:T(8,128)(2,1)S(1)} collective-permute-done((bf16[64,2304]{1,0:T(8,128)(2,1)S(1)}, bf16[64,2304]{1,0:T(8,128)(2,1)S(1)}, u32[]{:S(2)}, u32[]{:S(2)}) %collective-permute-start.26) | collective-permute-done | bytes 294944 | tf_op jit(solution)/shard_map/ppermute | solution.py:377
  188.3 9.0 %collective-permute-done.40 = bf16[64,2304]{1,0:T(8,128)(2,1)S(1)} collective-permute-done((bf16[64,2304]{1,0:T(8,128)(2,1)S(1)}, bf16[64,2304]{1,0:T(8,128)(2,1)S(1)}, u32[]{:S(2)}, u32[]{:S(2)}) %collective-permute-start.40) | collective-permute-done | bytes 294944 | tf_op jit(solution)/shard_map/ppermute | solution.py:377
  197.4 1.7 collective-permute-start.35
  199.2 6.7 %collective-permute-done.27 = bf16[64,2304]{1,0:T(8,128)(2,1)S(1)} collective-permute-done((bf16[64,2304]{1,0:T(8,128)(2,1)S(1)}, bf16[64,2304]{1,0:T(8,128)(2,1)S(1)}, u32[]{:S(2)}, u32[]{:S(2)}) %collective-permute-start.27) | collective-permute-done | bytes 294944 | tf_op jit(solution)/shard_map/ppermute | solution.py:377
  206.0 2.2 collective-permute-start.19
  208.2 5.3 %collective-permute-done.41 = bf16[64,2304]{1,0:T(8,128)(2,1)S(1)} collective-permute-done((bf16[64,2304]{1,0:T(8,128)(2,1)S(1)}, bf16[64,2304]{1,0:T(8,128)(2,1)S(1)}, u32[]{:S(2)}, u32[]{:S(2)}) %collective-permute-start.41) | collective-permute-done | bytes 294944 | tf_op jit(solution)/shard_map/ppermute | solution.py:377
  213.6 3.1 %collective-permute-start.33 = (bf16[64,2304]{1,0:T(8,128)(2,1)S(1)}, bf16[64,2304]{1,0:T(8,128)(2,1)S(1)}, u32[]{:S(2)}, u32[]{:S(2)}) collective-permute-start(bf16[64,2304]{1,0:T(8,128)(2,1)S(1)} %dynamic-slice_convert_fusion.3), channel_id=1, source_target_pairs={{0,8},{8,0},{16,24},{24,16},{1,9},{9,1},{17,25},{25,17},{2,10},{10... | collective-permute-start | bytes 884744 | tf_op jit(solution)/shard_map/ppermute | solution.py:380
  216.7 4.4 %collective-permute-done.28 = bf16[64,2304]{1,0:T(8,128)(2,1)S(1)} collective-permute-done((bf16[64,2304]{1,0:T(8,128)(2,1)S(1)}, bf16[64,2304]{1,0:T(8,128)(2,1)S(1)}, u32[]{:S(2)}, u32[]{:S(2)}) %collective-permute-start.28) | collective-permute-done | bytes 294944 | tf_op jit(solution)/shard_map/ppermute | solution.py:377
  221.5 7.3 %collective-permute-done.42 = bf16[64,2304]{1,0:T(8,128)(2,1)S(1)} collective-permute-done((bf16[64,2304]{1,0:T(8,128)(2,1)S(1)}, bf16[64,2304]{1,0:T(8,128)(2,1)S(1)}, u32[]{:S(2)}, u32[]{:S(2)}) %collective-permute-start.42) | collective-permute-done | bytes 294944 | tf_op jit(solution)/shard_map/ppermute | solution.py:377
  228.9 3.7 %collective-permute-start.29 = (bf16[64,2304]{1,0:T(8,128)(2,1)S(1)}, bf16[64,2304]{1,0:T(8,128)(2,1)S(1)}, u32[]{:S(2)}, u32[]{:S(2)}) collective-permute-start(bf16[64,2304]{1,0:T(8,128)(2,1)S(1)} %add_convert_fusion.4.refs_0_), channel_id=1, source_target_pairs={{0,16},{8,24},{16,0},{24,8},{1,17},{9,25},{17,1},{25,9},{2,18},{10... | collective-permute-start | bytes 884744 | tf_op jit(solution)/shard_map/ppermute | solution.py:380
  232.6 6.4 %shard_map.120 = (bf16[512,256]{1,0:T(8,128)(2,1)S(1)}, bf16[512,256]{1,0:T(8,128)(2,1)S(1)}) custom-call(s32[11]{0:T(128)S(1)} %get-tuple-element.79.sc_ref, bf16[512,4608]{1,0:T(8,128)(2,1)S(1)} %copy-done, bf16[512,4608]{1,0:T(8,128)(2,1)} %collective-permute-done.u1_ref, bf16[256,1152]{1,0:T(8,128)(2,1)S(1)} %collective-permute-done.3.refs_0_, ...), custom_call_target="tpu_custom_call" | custom-call | flops 2415919104 | bytes 11796480 | tf_op jit(solution)/shard_map/pallas_call | solution.py:207
  239.3 6.3 %shard_map.124 = (bf16[512,2048]{1,0:T(8,128)(2,1)}, bf16[512,1024]{1,0:T(8,128)(2,1)}, bf16[512,1024]{1,0:T(8,128)(2,1)}) custom-call(s32[11]{0:T(128)S(1)} %get-tuple-element.79.sc_ref, bf16[512,2048]{1,0:T(8,128)(2,1)S(1)} %copy-done.1, bf16[512,1024]{1,0:T(8,128)(2,1)S(1)} %copy-done.4, bf16[512,1024]{1,0:T(8,128)(2,1)S(1)} %copy-done.7, ...), custom_call_target="tpu_custom_call" | custom-call | flops 1342177280 | bytes 2621440 | tf_op jit(solution)/shard_map/pallas_call | solution.py:288
  245.6 1.8 collective-permute-start.30
  247.7 1.2 collective-permute-start.31
  249.7 6.3 %shard_map.125 = (bf16[512,2048]{1,0:T(8,128)(2,1)}, bf16[512,1024]{1,0:T(8,128)(2,1)}, bf16[512,1024]{1,0:T(8,128)(2,1)}) custom-call(s32[11]{0:T(128)S(1)} %get-tuple-element.79.sc_ref, bf16[512,2048]{1,0:T(8,128)(2,1)S(1)} %copy-done.1, bf16[512,1024]{1,0:T(8,128)(2,1)S(1)} %copy-done.4, ...), custom_call_target="tpu_custom_call", output_to_operand_aliasing={{0}: (8, {}), {1}: (9, {}), {2}: (10, {})} | custom-call | flops 1342177280 | bytes 2621440 | tf_op jit(solution)/shard_map/pallas_call | solution.py:288
  255.9 6.3 %shard_map.126 = (bf16[512,2048]{1,0:T(8,128)(2,1)}, bf16[512,1024]{1,0:T(8,128)(2,1)}, bf16[512,1024]{1,0:T(8,128)(2,1)}) custom-call(s32[11]{0:T(128)S(1)} %get-tuple-element.79.sc_ref, bf16[512,2048]{1,0:T(8,128)(2,1)S(1)} %copy-done.1, bf16[512,1024]{1,0:T(8,128)(2,1)S(1)} %copy-done.4, ...), custom_call_target="tpu_custom_call", output_to_operand_aliasing={{0}: (8, {}), {1}: (9, {}), {2}: (10, {})} | custom-call | flops 1342177280 | bytes 2621440 | tf_op jit(solution)/shard_map/pallas_call | solution.py:288
  262.2 6.5 %shard_map.127 = (bf16[512,2048]{1,0:T(8,128)(2,1)}, bf16[512,1024]{1,0:T(8,128)(2,1)}, bf16[512,1024]{1,0:T(8,128)(2,1)}) custom-call(s32[11]{0:T(128)S(1)} %get-tuple-element.79.sc_ref, bf16[512,2048]{1,0:T(8,128)(2,1)S(1)} %copy-done.1, bf16[512,1024]{1,0:T(8,128)(2,1)S(1)} %copy-done.4, ...), custom_call_target="tpu_custom_call", output_to_operand_aliasing={{0}: (8, {}), {1}: (9, {}), {2}: (10, {})} | custom-call | flops 1342177280 | bytes 2621440 | tf_op jit(solution)/shard_map/pallas_call | solution.py:288
  268.9 6.4 %shard_map.134 = f32[256,4608]{1,0:T(8,128)} custom-call(s32[16]{0:T(128)S(1)} %stack.35.sc_ref, f32[256,4608]{1,0:T(8,128)S(1)} %bitcast.23, f32[256,4608]{1,0:T(8,128)S(1)} %bitcast.25, bf16[64,2304]{1,0:T(8,128)(2,1)S(1)} %add_convert_fusion.4.refs_0_, bf16[64,2304]{1,0:T(8,128)(2,1)S(1)} %collective-permute-done.29.refs_1_, ...), custom_call_target="tpu_custom_call" | custom-call | flops 11796480 | bytes 16515072 | tf_op jit(solution)/shard_map/pallas_call | solution.py:332
  (134 shorter events, 10.9 us)
Async XLA Ops:
  0.6 55.9 %collective-permute-start = (bf16[512,4608]{1,0:T(8,128)(2,1)}, bf16[512,4608]{1,0:T(8,128)(2,1)}, u32[]{:S(2)}, u32[]{:S(2)}) collective-permute-start(bf16[512,4608]{1,0:T(8,128)(2,1)} %u0_ref.15), channel_id=1, source_target_pairs={{0,1},{1,0},{2,3},{3,2},{4,5},{5,4},{6,7},{7,6},{8,9},{9,8},{10,11... | collective-permute-start | bytes 14155784 | tf_op jit(solution)/shard_map/ppermute | solution.py:370
  3.7 7.7 %copy-start.13 = (s32[1,512]{1,0:T(1,128)S(1)}, s32[1,512]{1,0:T(1,128)}, u32[]{:S(2)}) copy-start(s32[1,512]{1,0:T(1,128)} %seg_row_ref.11) | copy-start | bytes 6148
  3.7 7.9 %copy-start.1 = (bf16[512,2048]{1,0:T(8,128)(2,1)S(1)}, bf16[512,2048]{1,0:T(8,128)(2,1)}, u32[]{:S(2)}) copy-start(bf16[512,2048]{1,0:T(8,128)(2,1)} %q_ref.11) | copy-start | bytes 6291460
  6.2 18.1 %collective-permute-start.5 = (bf16[256,1152]{1,0:T(8,128)(2,1)}, bf16[256,1152]{1,0:T(8,128)(2,1)}, u32[]{:S(2)}, u32[]{:S(2)}) collective-permute-start(bf16[256,1152]{1,0:T(8,128)(2,1)} %get-tuple-element.76), channel_id=1, source_target_pairs={{0,2},{1,3},{2,6},{3,7},{6,4},{7,5},{4,0},{5,1},{8,10},{9,11},{10,... | collective-permute-start | bytes 1769480 | tf_op jit(solution)/shard_map/ppermute | solution.py:377
  8.8 28.1 %collective-permute-start.1 = (bf16[256,1152]{1,0:T(8,128)(2,1)}, bf16[256,1152]{1,0:T(8,128)(2,1)}, u32[]{:S(2)}, u32[]{:S(2)}) collective-permute-start(bf16[256,1152]{1,0:T(8,128)(2,1)} %get-tuple-element.77), channel_id=1, source_target_pairs={{0,2},{1,3},{2,6},{3,7},{6,4},{7,5},{4,0},{5,1},{8,10},{9,11},{10,... | collective-permute-start | bytes 1769480 | tf_op jit(solution)/shard_map/ppermute | solution.py:377
  21.3 44.6 %collective-permute-start.17 = (bf16[1024,512]{1,0:T(8,128)(2,1)}, bf16[1024,512]{1,0:T(8,128)(2,1)S(1)}, u32[]{:S(2)}, u32[]{:S(2)}) collective-permute-start(bf16[1024,512]{1,0:T(8,128)(2,1)} %shard_map.129), channel_id=1, source_target_pairs={{0,1},{1,0},{2,3},{3,2},{4,5},{5,4},{6,7},{7,6},{8,9},{9,8},{10,11... | collective-permute-start | bytes 3145736 | tf_op jit(solution)/shard_map/ppermute | solution.py:370
  24.3 30.7 %collective-permute-start.6 = (bf16[256,1152]{1,0:T(8,128)(2,1)}, bf16[256,1152]{1,0:T(8,128)(2,1)}, u32[]{:S(2)}, u32[]{:S(2)}) collective-permute-start(bf16[256,1152]{1,0:T(8,128)(2,1)} %collective-permute-done.5.refs_2_), channel_id=1, source_target_pairs={{0,2},{1,3},{2,6},{3,7},{6,4},{7,5},{4,0},{5,1},{8,10},{9,11},{10,... | collective-permute-start | bytes 1769480 | tf_op jit(solution)/shard_map/ppermute | solution.py:377
  37.0 32.4 %collective-permute-start.2 = (bf16[256,1152]{1,0:T(8,128)(2,1)}, bf16[256,1152]{1,0:T(8,128)(2,1)}, u32[]{:S(2)}, u32[]{:S(2)}) collective-permute-start(bf16[256,1152]{1,0:T(8,128)(2,1)} %collective-permute-done.1.refs_0_), channel_id=1, source_target_pairs={{0,2},{1,3},{2,6},{3,7},{6,4},{7,5},{4,0},{5,1},{8,10},{9,11},{10,... | collective-permute-start | bytes 1769480 | tf_op jit(solution)/shard_map/ppermute | solution.py:377
  46.9 10.1 %copy-start.8 = (bf16[256,4608]{1,0:T(8,128)(2,1)S(1)}, bf16[256,4608]{1,0:T(8,128)(2,1)}, u32[]{:S(2)}) copy-start(bf16[256,4608]{1,0:T(8,128)(2,1)} %refs_0_.1) | copy-start | bytes 7077892
  53.5 29.6 %collective-permute-start.14 = (bf16[256,1152]{1,0:T(8,128)(2,1)}, bf16[256,1152]{1,0:T(8,128)(2,1)S(1)}, u32[]{:S(2)}, u32[]{:S(2)}) collective-permute-start(bf16[256,1152]{1,0:T(8,128)(2,1)} %collective-permute-done.5.refs_2_), channel_id=1, source_target_pairs={{0,16},{8,24},{16,0},{24,8},{1,17},{9,25},{17,1},{25,9},{2,18},{10... | collective-permute-start | bytes 1769480 | tf_op jit(solution)/shard_map/ppermute | solution.py:380
  55.0 36.8 %collective-permute-start.13 = (bf16[256,1152]{1,0:T(8,128)(2,1)}, bf16[256,1152]{1,0:T(8,128)(2,1)S(1)}, u32[]{:S(2)}, u32[]{:S(2)}) collective-permute-start(bf16[256,1152]{1,0:T(8,128)(2,1)} %collective-permute-done.1.refs_0_), channel_id=1, source_target_pairs={{0,8},{8,0},{16,24},{24,16},{1,9},{9,1},{17,25},{25,17},{2,10},{10... | collective-permute-start | bytes 1769480 | tf_op jit(solution)/shard_map/ppermute | solution.py:380
  56.5 52.9 %collective-permute-start.11 = (bf16[256,1152]{1,0:T(8,128)(2,1)}, bf16[256,1152]{1,0:T(8,128)(2,1)S(1)}, u32[]{:S(2)}, u32[]{:S(2)}) collective-permute-start(bf16[256,1152]{1,0:T(8,128)(2,1)} %collective-permute-done.6.refs_2_), channel_id=1, source_target_pairs={{0,16},{8,24},{16,0},{24,8},{1,17},{9,25},{17,1},{25,9},{2,18},{10... | collective-permute-start | bytes 1769480 | tf_op jit(solution)/shard_map/ppermute | solution.py:380
  65.9 10.7 %copy-start.24 = (bf16[512,256]{1,0:T(8,128)(2,1)}, bf16[512,256]{1,0:T(8,128)(2,1)S(1)}, u32[]{:S(2)}) copy-start(bf16[512,256]{1,0:T(8,128)(2,1)S(1)} %get-tuple-element.47) | copy-start | bytes 786436
  65.9 34.7 %collective-permute-start.7 = (bf16[256,1152]{1,0:T(8,128)(2,1)}, bf16[256,1152]{1,0:T(8,128)(2,1)S(1)}, u32[]{:S(2)}, u32[]{:S(2)}) collective-permute-start(bf16[256,1152]{1,0:T(8,128)(2,1)} %collective-permute-done.6.refs_2_), channel_id=1, source_target_pairs={{0,2},{1,3},{2,6},{3,7},{6,4},{7,5},{4,0},{5,1},{8,10},{9,11},{10,... | collective-permute-start | bytes 1769480 | tf_op jit(solution)/shard_map/ppermute | solution.py:377
  69.3 32.8 %collective-permute-start.3 = (bf16[256,1152]{1,0:T(8,128)(2,1)}, bf16[256,1152]{1,0:T(8,128)(2,1)S(1)}, u32[]{:S(2)}, u32[]{:S(2)}) collective-permute-start(bf16[256,1152]{1,0:T(8,128)(2,1)} %collective-permute-done.2.refs_0_), channel_id=1, source_target_pairs={{0,2},{1,3},{2,6},{3,7},{6,4},{7,5},{4,0},{5,1},{8,10},{9,11},{10,... | collective-permute-start | bytes 1769480 | tf_op jit(solution)/shard_map/ppermute | solution.py:377
  83.1 7.1 %copy-start.20 = (bf16[128,2304]{1,0:T(8,128)(2,1)}, bf16[128,2304]{1,0:T(8,128)(2,1)S(1)}, u32[]{:S(2)}) copy-start(bf16[128,2304]{1,0:T(8,128)(2,1)S(1)} %get-tuple-element.73) | copy-start | bytes 1769476
  83.1 7.1 %copy-start.22 = (bf16[128,2304]{1,0:T(8,128)(2,1)}, bf16[128,2304]{1,0:T(8,128)(2,1)S(1)}, u32[]{:S(2)}) copy-start(bf16[128,2304]{1,0:T(8,128)(2,1)S(1)} %get-tuple-element.65) | copy-start | bytes 1769476
  83.1 26.4 %collective-permute-start.10 = (bf16[256,1152]{1,0:T(8,128)(2,1)}, bf16[256,1152]{1,0:T(8,128)(2,1)S(1)}, u32[]{:S(2)}, u32[]{:S(2)}) collective-permute-start(bf16[256,1152]{1,0:T(8,128)(2,1)} %collective-permute-done.2.refs_0_), channel_id=1, source_target_pairs={{0,8},{8,0},{16,24},{24,16},{1,9},{9,1},{17,25},{25,17},{2,10},{10... | collective-permute-start | bytes 1769480 | tf_op jit(solution)/shard_map/ppermute | solution.py:380
  91.8 25.0 %collective-permute-start.24 = (bf16[128,2304]{1,0:T(8,128)(2,1)}, bf16[128,2304]{1,0:T(8,128)(2,1)}, u32[]{:S(2)}, u32[]{:S(2)}) collective-permute-start(bf16[128,2304]{1,0:T(8,128)(2,1)} %get-tuple-element.67), channel_id=1, source_target_pairs={{0,8},{8,0},{16,24},{24,16},{1,9},{9,1},{17,25},{25,17},{2,10},{10... | collective-permute-start | bytes 1769480 | tf_op jit(solution)/shard_map/ppermute | solution.py:380
  100.6 128.3 %collective-permute-start.8 = (bf16[256,1152]{1,0:T(8,128)(2,1)S(1)}, bf16[256,1152]{1,0:T(8,128)(2,1)S(1)}, u32[]{:S(2)}, u32[]{:S(2)}) collective-permute-start(bf16[256,1152]{1,0:T(8,128)(2,1)S(1)} %collective-permute-done.7.refs_2_), channel_id=1, source_target_pairs={{0,16},{8,24},{16,0},{24,8},{1,17},{9,25},{17,1},{25,9},{2,18},{10... | collective-permute-start | bytes 1769480 | tf_op jit(solution)/shard_map/ppermute | solution.py:380
  102.1 130.4 %collective-permute-start.4 = (bf16[256,1152]{1,0:T(8,128)(2,1)S(1)}, bf16[256,1152]{1,0:T(8,128)(2,1)S(1)}, u32[]{:S(2)}, u32[]{:S(2)}) collective-permute-start(bf16[256,1152]{1,0:T(8,128)(2,1)S(1)} %collective-permute-done.3.refs_0_), channel_id=1, source_target_pairs={{0,8},{8,0},{16,24},{24,16},{1,9},{9,1},{17,25},{25,17},{2,10},{10... | collective-permute-start | bytes 1769480 | tf_op jit(solution)/shard_map/ppermute | solution.py:380
  109.4 136.1 %collective-permute-start.15 = (bf16[512,256]{1,0:T(8,128)(2,1)S(1)}, bf16[512,256]{1,0:T(8,128)(2,1)S(1)}, u32[]{:S(2)}, u32[]{:S(2)}) collective-permute-start(bf16[512,256]{1,0:T(8,128)(2,1)S(1)} %get-tuple-element.45), channel_id=1, source_target_pairs={{0,1},{1,0},{2,3},{3,2},{4,5},{5,4},{6,7},{7,6},{8,9},{9,8},{10,11... | collective-permute-start | bytes 786440 | tf_op jit(solution)/shard_map/ppermute | solution.py:370
  109.5 7.4 %copy-start.23 = (bf16[128,2304]{1,0:T(8,128)(2,1)S(1)}, bf16[128,2304]{1,0:T(8,128)(2,1)}, u32[]{:S(2)}) copy-start(bf16[128,2304]{1,0:T(8,128)(2,1)} %copy-done.22) | copy-start | bytes 1769476
  109.5 8.9 %copy-start.12 = (bf16[128,2304]{1,0:T(8,128)(2,1)S(1)}, bf16[128,2304]{1,0:T(8,128)(2,1)}, u32[]{:S(2)}) copy-start(bf16[128,2304]{1,0:T(8,128)(2,1)} %copy-done.11) | copy-start | bytes 1769476
  109.5 16.3 %collective-permute-start.38 = (bf16[128,2304]{1,0:T(8,128)(2,1)S(1)}, bf16[128,2304]{1,0:T(8,128)(2,1)S(1)}, u32[]{:S(2)}, u32[]{:S(2)}) collective-permute-start(bf16[128,2304]{1,0:T(8,128)(2,1)S(1)} %get-tuple-element.75), channel_id=1, source_target_pairs={{0,16},{8,24},{16,0},{24,8},{1,17},{9,25},{17,1},{25,9},{2,18},{10... | collective-permute-start | bytes 1769480 | tf_op jit(solution)/shard_map/ppermute | solution.py:380
  116.9 17.5 %collective-permute-start.22 = (bf16[128,2304]{1,0:T(8,128)(2,1)S(1)}, bf16[128,2304]{1,0:T(8,128)(2,1)S(1)}, u32[]{:S(2)}, u32[]{:S(2)}) collective-permute-start(bf16[128,2304]{1,0:T(8,128)(2,1)S(1)} %copy-done.23), channel_id=1, source_target_pairs={{0,8},{8,0},{16,24},{24,16},{1,9},{9,1},{17,25},{25,17},{2,10},{10... | collective-permute-start | bytes 1769480 | tf_op jit(solution)/shard_map/ppermute | solution.py:380
  118.5 7.3 %copy-start.21 = (bf16[128,2304]{1,0:T(8,128)(2,1)S(1)}, bf16[128,2304]{1,0:T(8,128)(2,1)}, u32[]{:S(2)}) copy-start(bf16[128,2304]{1,0:T(8,128)(2,1)} %copy-done.20) | copy-start | bytes 1769476
  118.5 8.9 %copy-start.10 = (bf16[128,2304]{1,0:T(8,128)(2,1)S(1)}, bf16[128,2304]{1,0:T(8,128)(2,1)}, u32[]{:S(2)}) copy-start(bf16[128,2304]{1,0:T(8,128)(2,1)} %copy-done.9) | copy-start | bytes 1769476
  125.8 14.9 %collective-permute-start.36 = (bf16[128,2304]{1,0:T(8,128)(2,1)S(1)}, bf16[128,2304]{1,0:T(8,128)(2,1)S(1)}, u32[]{:S(2)}, u32[]{:S(2)}) collective-permute-start(bf16[128,2304]{1,0:T(8,128)(2,1)S(1)} %copy-done.21), channel_id=1, source_target_pairs={{0,16},{8,24},{16,0},{24,8},{1,17},{9,25},{17,1},{25,9},{2,18},{10... | collective-permute-start | bytes 1769480 | tf_op jit(solution)/shard_map/ppermute | solution.py:380
  127.3 7.1 %copy-start.19 = (bf16[128,2304]{1,0:T(8,128)(2,1)S(1)}, bf16[128,2304]{1,0:T(8,128)(2,1)}, u32[]{:S(2)}) copy-start(bf16[128,2304]{1,0:T(8,128)(2,1)} %copy-done.18) | copy-start | bytes 1769476
  134.4 13.3 %collective-permute-start.20 = (bf16[128,2304]{1,0:T(8,128)(2,1)S(1)}, bf16[128,2304]{1,0:T(8,128)(2,1)S(1)}, u32[]{:S(2)}, u32[]{:S(2)}) collective-permute-start(bf16[128,2304]{1,0:T(8,128)(2,1)S(1)} %copy-done.19), channel_id=1, source_target_pairs={{0,8},{8,0},{16,24},{24,16},{1,9},{9,1},{17,25},{25,17},{2,10},{10... | collective-permute-start | bytes 1769480 | tf_op jit(solution)/shard_map/ppermute | solution.py:380
  140.7 14.0 %collective-permute-start.34 = (bf16[128,2304]{1,0:T(8,128)(2,1)S(1)}, bf16[128,2304]{1,0:T(8,128)(2,1)S(1)}, u32[]{:S(2)}, u32[]{:S(2)}) collective-permute-start(bf16[128,2304]{1,0:T(8,128)(2,1)S(1)} %copy-done.17), channel_id=1, source_target_pairs={{0,16},{8,24},{16,0},{24,8},{1,17},{9,25},{17,1},{25,9},{2,18},{10... | collective-permute-start | bytes 1769480 | tf_op jit(solution)/shard_map/ppermute | solution.py:380
  147.8 13.1 %collective-permute-start.18 = (bf16[128,2304]{1,0:T(8,128)(2,1)S(1)}, bf16[128,2304]{1,0:T(8,128)(2,1)S(1)}, u32[]{:S(2)}, u32[]{:S(2)}) collective-permute-start(bf16[128,2304]{1,0:T(8,128)(2,1)S(1)} %copy-done.15), channel_id=1, source_target_pairs={{0,8},{8,0},{16,24},{24,16},{1,9},{9,1},{17,25},{25,17},{2,10},{10... | collective-permute-start | bytes 1769480 | tf_op jit(solution)/shard_map/ppermute | solution.py:380
  154.7 16.2 %collective-permute-start.32 = (bf16[128,2304]{1,0:T(8,128)(2,1)S(1)}, bf16[128,2304]{1,0:T(8,128)(2,1)S(1)}, u32[]{:S(2)}, u32[]{:S(2)}) collective-permute-start(bf16[128,2304]{1,0:T(8,128)(2,1)S(1)} %get-tuple-element.69), channel_id=1, source_target_pairs={{0,16},{8,24},{16,0},{24,8},{1,17},{9,25},{17,1},{25,9},{2,18},{10... | collective-permute-start | bytes 1769480 | tf_op jit(solution)/shard_map/ppermute | solution.py:380
  160.9 13.6 %collective-permute-start.25 = (bf16[64,2304]{1,0:T(8,128)(2,1)S(1)}, bf16[64,2304]{1,0:T(8,128)(2,1)S(1)}, u32[]{:S(2)}, u32[]{:S(2)}) collective-permute-start(bf16[64,2304]{1,0:T(8,128)(2,1)S(1)} %dynamic-slice_convert_fusion.4), channel_id=1, source_target_pairs={{0,16},{8,24},{16,0},{24,8},{1,17},{9,25},{17,1},{25,9},{2,18},{10... | collective-permute-start | bytes 884744 | tf_op jit(solution)/shard_map/ppermute | solution.py:380
  170.9 6.7 %collective-permute-start.39 = (bf16[64,2304]{1,0:T(8,128)(2,1)S(1)}, bf16[64,2304]{1,0:T(8,128)(2,1)S(1)}, u32[]{:S(2)}, u32[]{:S(2)}) collective-permute-start(bf16[64,2304]{1,0:T(8,128)(2,1)S(1)} %dynamic-slice_convert_fusion), channel_id=1, source_target_pairs={{0,8},{8,0},{16,24},{24,16},{1,9},{9,1},{17,25},{25,17},{2,10},{10... | collective-permute-start | bytes 884744 | tf_op jit(solution)/shard_map/ppermute | solution.py:380
  174.5 6.7 %collective-permute-start.23 = (bf16[64,2304]{1,0:T(8,128)(2,1)S(1)}, bf16[64,2304]{1,0:T(8,128)(2,1)S(1)}, u32[]{:S(2)}, u32[]{:S(2)}) collective-permute-start(bf16[64,2304]{1,0:T(8,128)(2,1)S(1)} %dynamic-slice_convert_fusion.5), channel_id=1, source_target_pairs={{0,16},{8,24},{16,0},{24,8},{1,17},{9,25},{17,1},{25,9},{2,18},{10... | collective-permute-start | bytes 884744 | tf_op jit(solution)/shard_map/ppermute | solution.py:380
  177.6 10.2 %collective-permute-start.26 = (bf16[64,2304]{1,0:T(8,128)(2,1)S(1)}, bf16[64,2304]{1,0:T(8,128)(2,1)S(1)}, u32[]{:S(2)}, u32[]{:S(2)}) collective-permute-start(bf16[64,2304]{1,0:T(8,128)(2,1)S(1)} %add_convert_fusion.7), channel_id=1, source_target_pairs={{0,2},{1,3},{2,6},{3,7},{6,4},{7,5},{4,0},{5,1},{8,10},{9,11},{10,... | collective-permute-start | bytes 884744 | tf_op jit(solution)/shard_map/ppermute | solution.py:377
  181.2 6.8 %collective-permute-start.37 = (bf16[64,2304]{1,0:T(8,128)(2,1)S(1)}, bf16[64,2304]{1,0:T(8,128)(2,1)S(1)}, u32[]{:S(2)}, u32[]{:S(2)}) collective-permute-start(bf16[64,2304]{1,0:T(8,128)(2,1)S(1)} %dynamic-slice_convert_fusion.1), channel_id=1, source_target_pairs={{0,8},{8,0},{16,24},{24,16},{1,9},{9,1},{17,25},{25,17},{2,10},{10... | collective-permute-start | bytes 884744 | tf_op jit(solution)/shard_map/ppermute | solution.py:380
  187.9 9.5 %collective-permute-start.40 = (bf16[64,2304]{1,0:T(8,128)(2,1)S(1)}, bf16[64,2304]{1,0:T(8,128)(2,1)S(1)}, u32[]{:S(2)}, u32[]{:S(2)}) collective-permute-start(bf16[64,2304]{1,0:T(8,128)(2,1)S(1)} %add_convert_fusion.3), channel_id=1, source_target_pairs={{0,2},{1,3},{2,6},{3,7},{6,4},{7,5},{4,0},{5,1},{8,10},{9,11},{10,... | collective-permute-start | bytes 884744 | tf_op jit(solution)/shard_map/ppermute | solution.py:377
  188.0 9.4 %collective-permute-start.21 = (bf16[64,2304]{1,0:T(8,128)(2,1)S(1)}, bf16[64,2304]{1,0:T(8,128)(2,1)S(1)}, u32[]{:S(2)}, u32[]{:S(2)}) collective-permute-start(bf16[64,2304]{1,0:T(8,128)(2,1)S(1)} %dynamic-slice_convert_fusion.6), channel_id=1, source_target_pairs={{0,16},{8,24},{16,0},{24,8},{1,17},{9,25},{17,1},{25,9},{2,18},{10... | collective-permute-start | bytes 884744 | tf_op jit(solution)/shard_map/ppermute | solution.py:380
  197.3 8.6 %collective-permute-start.27 = (bf16[64,2304]{1,0:T(8,128)(2,1)S(1)}, bf16[64,2304]{1,0:T(8,128)(2,1)S(1)}, u32[]{:S(2)}, u32[]{:S(2)}) collective-permute-start(bf16[64,2304]{1,0:T(8,128)(2,1)S(1)} %add_convert_fusion.6), channel_id=1, source_target_pairs={{0,2},{1,3},{2,6},{3,7},{6,4},{7,5},{4,0},{5,1},{8,10},{9,11},{10,... | collective-permute-start | bytes 884744 | tf_op jit(solution)/shard_map/ppermute | solution.py:377
  197.4 8.6 %collective-permute-start.35 = (bf16[64,2304]{1,0:T(8,128)(2,1)S(1)}, bf16[64,2304]{1,0:T(8,128)(2,1)S(1)}, u32[]{:S(2)}, u32[]{:S(2)}) collective-permute-start(bf16[64,2304]{1,0:T(8,128)(2,1)S(1)} %dynamic-slice_convert_fusion.2), channel_id=1, source_target_pairs={{0,8},{8,0},{16,24},{24,16},{1,9},{9,1},{17,25},{25,17},{2,10},{10... | collective-permute-start | bytes 884744 | tf_op jit(solution)/shard_map/ppermute | solution.py:380
  205.9 7.6 %collective-permute-start.41 = (bf16[64,2304]{1,0:T(8,128)(2,1)S(1)}, bf16[64,2304]{1,0:T(8,128)(2,1)S(1)}, u32[]{:S(2)}, u32[]{:S(2)}) collective-permute-start(bf16[64,2304]{1,0:T(8,128)(2,1)S(1)} %add_convert_fusion.2), channel_id=1, source_target_pairs={{0,2},{1,3},{2,6},{3,7},{6,4},{7,5},{4,0},{5,1},{8,10},{9,11},{10,... | collective-permute-start | bytes 884744 | tf_op jit(solution)/shard_map/ppermute | solution.py:377
  206.0 22.8 %copy-start.25 = (bf16[512,256]{1,0:T(8,128)(2,1)S(1)}, bf16[512,256]{1,0:T(8,128)(2,1)}, u32[]{:S(2)}) copy-start(bf16[512,256]{1,0:T(8,128)(2,1)} %copy-done.24) | copy-start | bytes 786436
  206.0 7.6 %collective-permute-start.19 = (bf16[64,2304]{1,0:T(8,128)(2,1)S(1)}, bf16[64,2304]{1,0:T(8,128)(2,1)S(1)}, u32[]{:S(2)}, u32[]{:S(2)}) collective-permute-start(bf16[64,2304]{1,0:T(8,128)(2,1)S(1)} %dynamic-slice_convert_fusion.7), channel_id=1, source_target_pairs={{0,16},{8,24},{16,0},{24,8},{1,17},{9,25},{17,1},{25,9},{2,18},{10... | collective-permute-start | bytes 884744 | tf_op jit(solution)/shard_map/ppermute | solution.py:380
  213.5 7.6 %collective-permute-start.28 = (bf16[64,2304]{1,0:T(8,128)(2,1)S(1)}, bf16[64,2304]{1,0:T(8,128)(2,1)S(1)}, u32[]{:S(2)}, u32[]{:S(2)}) collective-permute-start(bf16[64,2304]{1,0:T(8,128)(2,1)S(1)} %add_convert_fusion.5), channel_id=1, source_target_pairs={{0,2},{1,3},{2,6},{3,7},{6,4},{7,5},{4,0},{5,1},{8,10},{9,11},{10,... | collective-permute-start | bytes 884744 | tf_op jit(solution)/shard_map/ppermute | solution.py:377
  213.6 7.8 %collective-permute-start.33 = (bf16[64,2304]{1,0:T(8,128)(2,1)S(1)}, bf16[64,2304]{1,0:T(8,128)(2,1)S(1)}, u32[]{:S(2)}, u32[]{:S(2)}) collective-permute-start(bf16[64,2304]{1,0:T(8,128)(2,1)S(1)} %dynamic-slice_convert_fusion.3), channel_id=1, source_target_pairs={{0,8},{8,0},{16,24},{24,16},{1,9},{9,1},{17,25},{25,17},{2,10},{10... | collective-permute-start | bytes 884744 | tf_op jit(solution)/shard_map/ppermute | solution.py:380
  221.2 7.6 %collective-permute-start.42 = (bf16[64,2304]{1,0:T(8,128)(2,1)S(1)}, bf16[64,2304]{1,0:T(8,128)(2,1)S(1)}, u32[]{:S(2)}, u32[]{:S(2)}) collective-permute-start(bf16[64,2304]{1,0:T(8,128)(2,1)S(1)} %add_convert_fusion.1), channel_id=1, source_target_pairs={{0,2},{1,3},{2,6},{3,7},{6,4},{7,5},{4,0},{5,1},{8,10},{9,11},{10,... | collective-permute-start | bytes 884744 | tf_op jit(solution)/shard_map/ppermute | solution.py:377
  221.4 26.0 %collective-permute-start.12 = (bf16[512,256]{1,0:T(8,128)(2,1)S(1)}, bf16[512,256]{1,0:T(8,128)(2,1)S(1)}, u32[]{:S(2)}, u32[]{:S(2)}) collective-permute-start(bf16[512,256]{1,0:T(8,128)(2,1)S(1)} %get-tuple-element.43), channel_id=1, source_target_pairs={{0,1},{1,0},{2,3},{3,2},{4,5},{5,4},{6,7},{7,6},{8,9},{9,8},{10,11... | collective-permute-start | bytes 786440 | tf_op jit(solution)/shard_map/ppermute | solution.py:370
  228.8 10.2 %collective-permute-start.16 = (bf16[512,256]{1,0:T(8,128)(2,1)S(1)}, bf16[512,256]{1,0:T(8,128)(2,1)S(1)}, u32[]{:S(2)}, u32[]{:S(2)}) collective-permute-start(bf16[512,256]{1,0:T(8,128)(2,1)S(1)} %copy-done.25), channel_id=1, source_target_pairs={{0,1},{1,0},{2,3},{3,2},{4,5},{5,4},{6,7},{7,6},{8,9},{9,8},{10,11... | collective-permute-start | bytes 786440 | tf_op jit(solution)/shard_map/ppermute | solution.py:370
  228.9 10.4 %copy-start.4 = (bf16[512,1024]{1,0:T(8,128)(2,1)S(1)}, bf16[512,1024]{1,0:T(8,128)(2,1)}, u32[]{:S(2)}) copy-start(bf16[512,1024]{1,0:T(8,128)(2,1)} %k_ref.11) | copy-start | bytes 3145732
  228.9 10.4 %copy-start.7 = (bf16[512,1024]{1,0:T(8,128)(2,1)S(1)}, bf16[512,1024]{1,0:T(8,128)(2,1)}, u32[]{:S(2)}) copy-start(bf16[512,1024]{1,0:T(8,128)(2,1)} %v_ref.11) | copy-start | bytes 3145732
  228.9 18.8 %collective-permute-start.29 = (bf16[64,2304]{1,0:T(8,128)(2,1)S(1)}, bf16[64,2304]{1,0:T(8,128)(2,1)S(1)}, u32[]{:S(2)}, u32[]{:S(2)}) collective-permute-start(bf16[64,2304]{1,0:T(8,128)(2,1)S(1)} %add_convert_fusion.4.refs_0_), channel_id=1, source_target_pairs={{0,16},{8,24},{16,0},{24,8},{1,17},{9,25},{17,1},{25,9},{2,18},{10... | collective-permute-start | bytes 884744 | tf_op jit(solution)/shard_map/ppermute | solution.py:380
  232.6 16.3 %collective-permute-start.43 = (bf16[64,2304]{1,0:T(8,128)(2,1)S(1)}, bf16[64,2304]{1,0:T(8,128)(2,1)S(1)}, u32[]{:S(2)}, u32[]{:S(2)}) collective-permute-start(bf16[64,2304]{1,0:T(8,128)(2,1)S(1)} %add_convert_fusion.refs_4_), channel_id=1, source_target_pairs={{0,8},{8,0},{16,24},{24,16},{1,9},{9,1},{17,25},{25,17},{2,10},{10... | collective-permute-start | bytes 884744 | tf_op jit(solution)/shard_map/ppermute | solution.py:380
  239.0 23.2 %collective-permute-start.9 = (bf16[512,256]{1,0:T(8,128)(2,1)S(1)}, bf16[512,256]{1,0:T(8,128)(2,1)S(1)}, u32[]{:S(2)}, u32[]{:S(2)}) collective-permute-start(bf16[512,256]{1,0:T(8,128)(2,1)S(1)} %get-tuple-element.41), channel_id=1, source_target_pairs={{0,1},{1,0},{2,3},{3,2},{4,5},{5,4},{6,7},{7,6},{8,9},{9,8},{10,11... | collective-permute-start | bytes 786440 | tf_op jit(solution)/shard_map/ppermute | solution.py:370
  245.6 23.2 %collective-permute-start.30 = (bf16[64,2304]{1,0:T(8,128)(2,1)S(1)}, bf16[64,2304]{1,0:T(8,128)(2,1)S(1)}, u32[]{:S(2)}, u32[]{:S(2)}) collective-permute-start(bf16[64,2304]{1,0:T(8,128)(2,1)S(1)} %add_convert_fusion.4.refs_0_), channel_id=1, source_target_pairs={{0,8},{8,0},{16,24},{24,16},{1,9},{9,1},{17,25},{25,17},{2,10},{10... | collective-permute-start | bytes 884744 | tf_op jit(solution)/shard_map/ppermute | solution.py:380
  247.4 21.4 %collective-permute-start.44 = (bf16[64,2304]{1,0:T(8,128)(2,1)S(1)}, bf16[64,2304]{1,0:T(8,128)(2,1)S(1)}, u32[]{:S(2)}, u32[]{:S(2)}) collective-permute-start(bf16[64,2304]{1,0:T(8,128)(2,1)S(1)} %add_convert_fusion.refs_4_), channel_id=1, source_target_pairs={{0,16},{8,24},{16,0},{24,8},{1,17},{9,25},{17,1},{25,9},{2,18},{10... | collective-permute-start | bytes 884744 | tf_op jit(solution)/shard_map/ppermute | solution.py:380
  247.7 21.1 %collective-permute-start.31 = (bf16[64,2304]{1,0:T(8,128)(2,1)S(1)}, bf16[64,2304]{1,0:T(8,128)(2,1)S(1)}, u32[]{:S(2)}, u32[]{:S(2)}) collective-permute-start(bf16[64,2304]{1,0:T(8,128)(2,1)S(1)} %collective-permute-done.29.refs_1_), channel_id=1, source_target_pairs={{0,8},{8,0},{16,24},{24,16},{1,9},{9,1},{17,25},{25,17},{2,10},{10... | collective-permute-start | bytes 884744 | tf_op jit(solution)/shard_map/ppermute | solution.py:380
  248.9 19.9 %collective-permute-start.45 = (bf16[64,2304]{1,0:T(8,128)(2,1)S(1)}, bf16[64,2304]{1,0:T(8,128)(2,1)S(1)}, u32[]{:S(2)}, u32[]{:S(2)}) collective-permute-start(bf16[64,2304]{1,0:T(8,128)(2,1)S(1)} %collective-permute-done.43.refs_5_), channel_id=1, source_target_pairs={{0,16},{8,24},{16,0},{24,8},{1,17},{9,25},{17,1},{25,9},{2,18},{10... | collective-permute-start | bytes 884744 | tf_op jit(solution)/shard_map/ppermute | solution.py:380
  249.7 19.2 %slice-start.2 = ((s8[4718592]{0:T(1024)(128)(4,1)}), s8[4194304]{0:T(1024)(128)(4,1)S(1)}, s32[]{:S(2)}) async-start(s8[4718592]{0:T(1024)(128)(4,1)} %bitcast.24), calls=%async_computation.2 | async-start | bytes 8388608
  255.9 12.9 %slice-start.3 = ((s8[4718592]{0:T(1024)(128)(4,1)}), s8[524288]{0:T(1024)(128)(4,1)S(1)}, s32[]{:S(2)}) async-start(s8[4718592]{0:T(1024)(128)(4,1)} %bitcast.24), calls=%async_computation.3 | async-start | bytes 1048576
  262.2 6.6 %slice-start = ((s8[4718592]{0:T(1024)(128)(4,1)}), s8[4194304]{0:T(1024)(128)(4,1)S(1)}, s32[]{:S(2)}) async-start(s8[4718592]{0:T(1024)(128)(4,1)} %bitcast.22), calls=%async_computation | async-start | bytes 8388608
  262.2 6.6 %slice-start.1 = ((s8[4718592]{0:T(1024)(128)(4,1)}), s8[524288]{0:T(1024)(128)(4,1)S(1)}, s32[]{:S(2)}) async-start(s8[4718592]{0:T(1024)(128)(4,1)} %bitcast.22), calls=%async_computation.1 | async-start | bytes 1048576
  (12 other events, 34.8 us)

commit v2 on v1

v2 whole, which is shorter than its diff:
```python
import functools

import jax
import jax.numpy as jnp
import numpy as np
from jax import lax
from jax.experimental import pallas as pl
from jax.experimental.pallas import tpu as pltpu
from jax.sharding import PartitionSpec as P

HEADS = 16
KV_HEADS = 8
DH = 128
REPEAT = HEADS // KV_HEADS

SCALE = 1.0 / 12.0
CAP = 50.0
VMEM = 40 * 1024 * 1024
F32 = jnp.float32
BF16 = jnp.bfloat16

NT = (((1,), (1,)), ((), ()))
NN = (((1,), (0,)), ((), ()))


def dot(a, b, dims):
    return lax.dot_general(a, b, dims, preferred_element_type=F32)


def call(body, sc, grid, ins, outs, scratch=(), through=(), before=()):
    n_in, n_out, n_before, n_through = len(ins), len(outs), len(before), len(through)

    def kernel(sc_ref, *refs):
        at = n_in + n_before + n_through
        body(sc_ref, *refs[:n_in], *refs[at : at + n_out], *refs[at + n_out + n_through :])

    anywhere = pl.BlockSpec(memory_space=pl.ANY)
    aliases = {1 + n_in + n: n for n in range(n_before)}
    aliases.update({1 + n_in + n_before + n: n_out + n for n in range(n_through)})
    results = pl.pallas_call(
        kernel,
        grid_spec=pltpu.PrefetchScalarGridSpec(
            num_scalar_prefetch=1,
            grid=grid,
            in_specs=[pl.BlockSpec(block, index) for _, block, index in ins]
            + [anywhere] * (n_before + n_through),
            out_specs=[pl.BlockSpec(block, index) for _, _, block, index in outs]
            + [anywhere] * n_through,
            scratch_shapes=list(scratch),
        ),
        out_shape=[jax.ShapeDtypeStruct(shape, dtype) for shape, dtype, _, _ in outs]
        + [jax.ShapeDtypeStruct(x.shape, x.dtype) for x in through],
        input_output_aliases=aliases,
        cost_estimate=pl.CostEstimate(flops=1, transcendentals=0, bytes_accessed=1),
        compiler_params=pltpu.CompilerParams(vmem_limit_bytes=VMEM),
    )(sc, *[array for array, _, _ in ins], *before, *through)
    return results[:n_out], results[n_out:]


def first(*_):
    return (0, 0)


def fill_mask(mask_ref, seg_row_ref, seg_col_ref):
    length = mask_ref.shape[0]
    j = lax.broadcasted_iota(jnp.int32, (length, length), 0)
    i = lax.broadcasted_iota(jnp.int32, (length, length), 1)
    allowed = (j <= i) & (seg_col_ref[...] == seg_row_ref[...])
    mask_ref[...] = jnp.where(allowed, 1.0, 0.0).astype(F32)


def tiles_of(length):
    tile = 256
    return [(t * tile, tile, (t + 1) * tile) for t in range(length // tile)]


def softmax_tile(key, query, mask):
    cap_tanh = jnp.tanh(dot(key, query, NT) * (SCALE / CAP))
    weights = jnp.exp(cap_tanh * CAP) * mask
    inverse = 1.0 / jnp.sum(weights, axis=0, keepdims=True)
    return weights * inverse, cap_tanh


def cut_body(sc_ref, a_ref, b_ref, x_ref, y_ref):
    x_ref[...] = a_ref[...]
    y_ref[...] = b_ref[...]


def cut(sc, weight, lay, through):
    rows, width = weight.shape
    block = (rows, width // 4)
    at = lay.at_piece
    return call(
        cut_body,
        sc,
        (1,),
        [
            (weight, block, lambda n, sc: (0, sc[at])),
            (weight, block, lambda n, sc: (0, sc[at + 2])),
        ],
        [(block, BF16, block, first)] * 2,
        through=through,
    )


def forward_body(
    heads, sc_ref, q_ref, k_ref, v_ref, seg_row_ref, seg_col_ref, send_ref, own_ref, mask_ref
):
    @pl.when(pl.program_id(0) == 0)
    def _():
        fill_mask(mask_ref, seg_row_ref, seg_col_ref)

    def run(out_ref):
        value_t = v_ref[...].T
        for h in range(heads):
            for start, tile, upto in tiles_of(q_ref.shape[0]):
                probs, _ = softmax_tile(
                    k_ref[:upto, :],
                    q_ref[start : start + tile, h * DH : (h + 1) * DH],
                    mask_ref[:upto, start : start + tile],
                )
                context = dot(value_t[:, :upto], probs.astype(BF16), NN)
                out_ref[h * DH : (h + 1) * DH, start : start + tile] = context.astype(BF16)

    pl.when(pl.program_id(0) == 0)(functools.partial(run, send_ref))
    pl.when(pl.program_id(0) == 1)(functools.partial(run, own_ref))


def forward(sc, k, block, lay, through):
    queries, keys, values, seg_row, seg_col = block
    length = queries.shape[0]
    per = lay.heads_shard
    at = lay.at_z + k

    def shard_of(i, sc):
        return 2 * sc[at] + jnp.where(i == 0, 1 - sc[0], sc[0])

    def kv_of(i, sc):
        return (0, (shard_of(i, sc) * per) // REPEAT)

    out = ((per * DH, length), BF16, (per * DH, length), first)
    return call(
        functools.partial(forward_body, per),
        sc,
        (2,),
        [
            (queries, (length, per * DH), lambda i, sc: (0, shard_of(i, sc))),
            (keys, (length, DH), kv_of),
            (values, (length, DH), kv_of),
            (seg_row, (1, length), first),
            (seg_col, (length, 1), first),
        ],
        [out, out],
        scratch=[pltpu.VMEM((length, length), F32)],
        through=through,
    )


def product_body(count, at_x, at_y, sc_ref, *refs):
    own, other = refs[:count], refs[count : 2 * count]
    u0_ref, u1_ref = refs[2 * count : 2 * count + 2]
    outs, acc_ref = refs[2 * count + 2 : -1], refs[-1]
    n = pl.program_id(0)
    rows = acc_ref.shape[0] // count
    half = rows // 2

    def stack(parts):
        return parts[0][...] if count == 1 else jnp.concatenate([p[...] for p in parts], axis=0)

    acc = dot(stack(own), u0_ref[...], NN) + dot(stack(other), u1_ref[...], NN)
    acc_ref[...] = acc.astype(BF16)

    def split(bit, side):
        for c in range(count):
            send_ref, keep_ref = outs[4 * c + side], outs[4 * c + side + 1]
            stay = pl.multiple_of(c * rows + bit * half, half)
            away = pl.multiple_of(c * rows + (1 - bit) * half, half)
            keep_ref[...] = acc_ref[pl.ds(stay, half), :]
            send_ref[...] = acc_ref[pl.ds(away, half), :]

    @pl.when(n < 2)
    def _():
        split(sc_ref[at_x], 0)

    @pl.when(n >= 2)
    def _():
        split(sc_ref[at_y], 2)


def product(sc, own, other, up0, up1, lay, through):
    length, width = up0.shape
    rows = lay.rows
    tile = width // 4
    count = len(own)
    half, block = (rows // 2, width // 2), (rows // 2, tile)
    left = (half, BF16, block, lambda n, sc: (0, jnp.minimum(n, 1)))
    right = (half, BF16, block, lambda n, sc: (0, jnp.maximum(n - 2, 0)))
    return call(
        functools.partial(product_body, count, lay.at_bit(0), lay.at_bit(lay.bits - 1)),
        sc,
        (4,),
        [(x, (rows, length), first) for x in (*own, *other)]
        + [(u, (length, tile), lambda n, sc: (0, n)) for u in (up0, up1)],
        [left, left, right, right] * count,
        scratch=[pltpu.VMEM((count * rows, tile), BF16)],
        through=through,
    )


def combine_body(counts, merged, sc_ref, *refs):
    outs = refs[sum(counts) :]
    at = 0
    for side, count in enumerate(counts):
        total = refs[at][...].astype(F32)
        for ref in refs[at + 1 : at + count]:
            total = total + ref[...].astype(F32)
        at += count
        if merged:
            width = total.shape[1]
            outs[0][:, side * width : (side + 1) * width] = total.astype(BF16)
        else:
            outs[side][...] = total.astype(BF16)


def combine(sc, terms, ring, away, merged, lay, through):
    count = len(terms[0])
    deep = count if away else lay.bits
    width = terms[0][0].shape[1]
    size = lay.rows >> deep
    ins, counts = [], []
    for side in range(2):
        order = list(range(lay.bits))
        order = order[::-1] if side else order

        def place(level, order=order):
            def index(n, sc):
                at = 0
                for m in range(level, deep):
                    bit = sc[lay.at_bit(order[m])]
                    bit = 1 - bit if away and m == deep - 1 else bit
                    at = 2 * at + bit
                return (at, 0)

            return index

        for m, x in enumerate(terms[side]):
            ins.append((x, (size, width), place(max(m, 1))))
        if ring is not None:
            ins.append((ring, (size, width), lambda n, sc, side=side: (0, side)))
        counts.append(count + (ring is not None))
    if merged:
        outs = [((size, 2 * width), BF16, (size, 2 * width), first)]
    else:
        outs = [((size, width), BF16, (size, width), first)] * 2
    return call(
        functools.partial(combine_body, counts, merged), sc, (1,), ins, outs, through=through
    )


def grad_context_body(parts, sc_ref, u0_ref, u1_ref, *refs):
    weights, (g0_ref, g1_ref, a0_ref, a1_ref) = refs[:-4], refs[-4:]
    n = pl.program_id(0)

    def add(weight_ref):
        d0 = dot(u0_ref[...], weight_ref[...], NT)
        d1 = dot(u1_ref[...], weight_ref[...], NT)

        @pl.when(n == 0)
        def _():
            a0_ref[...] = d0
            a1_ref[...] = d1

        @pl.when(n > 0)
        def _():
            a0_ref[...] += d0
            a1_ref[...] += d1

    if len(weights) == 1:
        add(weights[0])
    else:
        for p in range(parts):
            pl.when(n == p)(functools.partial(add, weights[p]))

    @pl.when(n == parts - 1)
    def _():
        g0_ref[...] = a0_ref[...].astype(BF16)
        g1_ref[...] = a1_ref[...].astype(BF16)


def grad_context(sc, up0, up1, weights, lay, through):
    length, width = up0.shape
    rows = lay.rows
    tile = width // 4
    at = lay.at_piece
    if len(weights) == 1:
        weight_ins = [(weights[0], (rows, tile), lambda n, sc: (0, sc[at + n]))]
    else:
        weight_ins = [(w, (rows, tile), first) for w in weights]
    return call(
        functools.partial(grad_context_body, 4),
        sc,
        (4,),
        [(u, (length, tile), lambda n, sc: (0, sc[at + n])) for u in (up0, up1)] + weight_ins,
        [((length, rows), BF16, (length, rows), first)] * 2,
        scratch=[pltpu.VMEM((length, rows), F32)] * 2,
        through=through,
    )


def backward_body(
    per, sc_ref, q_ref, k_ref, v_ref, seg_row_ref, seg_col_ref, own_ref, other_ref, *refs
):
    gq_ref, gk_ref, gv_ref, mask_ref, ak_ref, av_ref = refs[-6:]
    group = pl.program_id(0)
    parity = sc_ref[0]

    @pl.when(group == 0)
    def _():
        fill_mask(mask_ref, seg_row_ref, seg_col_ref)

    key_t = k_ref[...].T
    ak_ref[...] = jnp.zeros_like(ak_ref)
    av_ref[...] = jnp.zeros_like(av_ref)
    for h in range(REPEAT):
        side = group if per == REPEAT else h
        column = h if per == REPEAT else 0
        cols = slice(column * DH, (column + 1) * DH)
        grad = jnp.where(side == parity, own_ref[:, cols], other_ref[:, cols])
        for start, tile, upto in tiles_of(q_ref.shape[0]):
            query = q_ref[start : start + tile, h * DH : (h + 1) * DH]
            probs, cap_tanh = softmax_tile(
                k_ref[:upto, :], query, mask_ref[:upto, start : start + tile]
            )
            grad_rows = grad[start : start + tile, :]
            grad_probs = dot(v_ref[:upto, :], grad_rows, NT)
            delta = jnp.sum(probs * grad_probs, axis=0, keepdims=True)
            scores = probs * (grad_probs - delta) * (SCALE - SCALE * (cap_tanh * cap_tanh))
            scores = scores.astype(BF16)
            av_ref[:upto, :] += dot(probs.astype(BF16), grad_rows, NN)
            ak_ref[:upto, :] += dot(scores, query, NN)
            grad_query = dot(key_t[:, :upto], scores, NN).T
            gq_ref[start : start + tile, h * DH : (h + 1) * DH] = grad_query.astype(BF16)
    gk_ref[...] = ak_ref[...].astype(BF16)
    gv_ref[...] = av_ref[...].astype(BF16)


def backward(sc, k, block, own, other, before, lay, through):
    queries, keys, values, seg_row, seg_col = block
    length = queries.shape[0]
    per = lay.heads_shard
    groups = 2 * per // REPEAT
    at = lay.at_z + k

    def whole(i, sc):
        return (0, sc[at] * groups + i)

    heads = (length, REPEAT * DH), whole
    one = (length, DH), whole
    return call(
        functools.partial(backward_body, per),
        sc,
        (groups,),
        [
            (queries, *heads),
            (keys, *one),
            (values, *one),
            (seg_row, (1, length), first),
            (seg_col, (length, 1), first),
            (own, (length, lay.rows), first),
            (other, (length, lay.rows), first),
        ],
        [(queries.shape, BF16, *heads), (keys.shape, BF16, *one), (values.shape, BF16, *one)],
        scratch=[
            pltpu.VMEM((length, length), F32),
            pltpu.VMEM((length, DH), F32),
            pltpu.VMEM((length, DH), F32),
        ],
        before=before,
        through=through,
    )


def adam_body(pieces, tokens, sc_ref, m1_ref, m2_ref, *refs):
    out_ref = refs[-1]
    n = pl.program_id(0)

    def step(piece_ref):
        gradient = piece_ref[...].astype(F32) * (1.0 / tokens)
        moment_one = 0.9 * m1_ref[...] + 0.1 * gradient
        moment_two = 0.95 * m2_ref[...] + 0.05 * gradient * gradient
        out_ref[...] = moment_one / (jnp.sqrt(moment_two) + 1e-08)

    for p in range(pieces):
        pl.when(n == p)(functools.partial(step, refs[p]))


def adam(sc, pieces, first_moment, second_moment, tokens, lay, before, through):
    rows, width = pieces[0][0].shape
    count = len(pieces)
    places = []
    for _, side, flips in pieces:
        order = list(range(lay.bits))
        order = order[::-1] if side else order
        row = 0
        for b, flip in zip(order, flips):
            bit = sc[lay.at_bit(b)]
            row = 2 * row + (1 - bit if flip else bit)
        places += [row, jnp.int32(side)]
    at = lambda n, at: (at[2 * n], at[2 * n + 1])
    block = (rows, width)
    return call(
        functools.partial(adam_body, count, tokens),
        jnp.stack(places).astype(jnp.int32),
        (count,),
        [(first_moment, block, at), (second_moment, block, at)]
        + [(x, block, first) for x, _, _ in pieces],
        [(first_moment.shape, F32, block, at)],
        before=before,
        through=through,
    )


class Layout:
    def __init__(self, replicas, shards, rows):
        self.replicas, self.shards, self.rows = replicas, shards, rows
        self.z = shards // 2
        self.bits = replicas.bit_length() - 1
        self.heads_shard = HEADS // shards
        self.order = [0] + list(range(1, self.z, 2)) + list(range(self.z - 2, 0, -2))
        self.place = [self.order.index(z) for z in range(self.z)]
        self.at_z = 1
        self.at_piece = self.at_z + self.z
        table = []
        for r in range(replicas):
            bits = [(r >> b) & 1 for b in range(self.bits)]
            x, y = bits[0], bits[-1]
            for s in range(shards):
                z, core = s // 2, s % 2
                zs = [self.order[(self.place[z] - k) % self.z] for k in range(self.z)]
                table.append([core] + zs + [x, 1 - x, 2 + y, 3 - y] + bits)
        self.table = np.array(table, np.int32)

    def at_bit(self, b):
        return self.at_piece + 4 + b

    def sibling(self, x):
        return lax.ppermute(x, "shard", [(s, s ^ 1) for s in range(self.shards)])

    def onward(self, x):
        perm = []
        for p in range(self.z):
            a, b = self.order[p], self.order[(p + 1) % self.z]
            perm += [(2 * a + core, 2 * b + core) for core in range(2)]
        return lax.ppermute(x, "shard", perm)

    def across(self, x, b):
        return lax.ppermute(x, "replica", [(r, r ^ (1 << b)) for r in range(self.replicas)])


def per_device(queries, keys, values, segments, out_weight, upstream, first_moment, second_moment):
    length, width = upstream.shape
    lay = Layout(lax.axis_size("replica"), lax.axis_size("shard"), out_weight.shape[0])
    tokens = length * lay.replicas * lay.shards
    device = lax.axis_index("replica") * lay.shards + lax.axis_index("shard")
    sc = lax.dynamic_index_in_dim(jnp.asarray(lay.table), device, 0, keepdims=False)
    orders = [list(range(lay.bits)), list(range(lay.bits))[::-1]]
    block = (queries, keys, values, segments, segments.reshape(length, 1))

    token = jnp.zeros((8, 128), F32)
    arrived = [{}, {}]
    crossed = [{}, {}]
    context_own, context_other = {}, {}
    terms = {}
    ring = {}
    final = []
    grads = ()
    gc_own, gc_other = {}, {}

    def run(function, *args, relays=(), **more):
        nonlocal token
        held = [arrived[side][k] for side, k in relays]
        outs, handed = function(*args, through=[token, *held], **more)
        token = handed[0]
        for (side, k), x in zip(relays, handed[1:]):
            arrived[side][k] = x
            if k + 1 < lay.z:
                arrived[side][k + 1] = lay.onward(x)
            crossed[side][k] = lay.across(x, orders[side][0])
        return outs

    def do_forward(k, relays=()):
        send, context_own[k] = run(forward, sc, k, block, lay, relays=relays)
        context_other[k] = lay.sibling(send)

    def do_product(ks, relays=()):
        outs = run(
            product,
            sc,
            [context_own[k] for k in ks],
            [context_other[k] for k in ks],
            upstream,
            upstream_other,
            lay,
            relays=relays,
        )
        for n, k in enumerate(ks):
            send_l, keep_l, send_r, keep_r = outs[4 * n : 4 * n + 4]
            terms[k] = [
                [keep_l, lay.across(send_l, orders[0][0])],
                [keep_r, lay.across(send_r, orders[1][0])],
            ]

    def do_halve(k, relays=()):
        sends = run(combine, sc, terms[k], None, True, False, lay, relays=relays)
        stage = len(terms[k][0]) - 1
        for side in range(2):
            terms[k][side].append(lay.across(sends[side], orders[side][stage]))

    def do_sum(k, relays=()):
        outs = run(combine, sc, terms[k], ring.get(k), False, k > 0, lay, relays=relays)
        if k:
            ring[(k + 1) % lay.z] = lay.onward(outs[0])
        else:
            final.extend(outs)

    def do_grad_context(k, relays=()):
        weights = [out_weight]
        if k:
            weights = [arrived[0][k], crossed[0][k], arrived[1][k], crossed[1][k]]
        gc_own[k], send = run(
            grad_context, sc, upstream, upstream_other, weights, lay, relays=relays
        )
        gc_other[k] = lay.sibling(send)

    def do_backward(k, relays=()):
        nonlocal grads
        grads = run(
            backward, sc, k, block, gc_own[k], gc_other[k], grads, lay, relays=relays
        )

    upstream_other = lay.sibling(upstream)
    for side, x in enumerate(run(cut, sc, out_weight, lay)):
        arrived[side][1] = lay.onward(x)

    early, rest = list(range(1, lay.z)), list(range(3, lay.z))
    halvings = range(lay.bits - 1)
    do_forward(1)
    do_forward(2)
    do_product([1])
    for k in rest:
        do_forward(k)
    do_forward(0, relays=[(0, 1)])
    do_product(early[1:])
    do_halve(1)
    do_product([0], relays=[(1, 1)])
    do_grad_context(0)
    do_backward(0, relays=[(0, 2)])
    do_halve(2)
    for k in rest:
        do_halve(k, relays=[(1, 2)] if k == 3 else [(0, k - 1), (1, k - 1)])
    do_grad_context(1)
    do_backward(1)
    for n in list(halvings)[1:]:
        do_halve(1)
    do_sum(1)
    do_halve(0)
    for n in list(halvings)[1:]:
        do_halve(2)
    last = lay.z - 1
    do_sum(2, relays=[(0, last), (1, last)])
    do_grad_context(2)
    do_backward(2)
    for n in list(halvings)[1:]:
        for k in [*rest, 0]:
            do_halve(k)
    for k in rest:
        do_sum(k)
    do_sum(0)
    have = [[(final[side], side, (False,) * lay.bits)] for side in range(2)]
    for n in range(lay.bits - 1, -1, -1):
        for side in range(2):
            have[side] += [
                (lay.across(x, orders[side][n]), side, flips[:n] + (True,) + flips[n + 1 :])
                for x, _, flips in have[side]
            ]
    for k in rest:
        do_grad_context(k)
        do_backward(k)
    near = [p for side in range(2) for p in have[side][:-1]]
    far = [have[side][-1] for side in range(2)]
    adam_step = run(adam, sc, near, first_moment, second_moment, tokens, lay, before=())
    adam_step = run(adam, sc, far, first_moment, second_moment, tokens, lay, before=adam_step)
    return (*grads, *adam_step)


def solution(mesh):
    both = P(("replica", "shard"), None)
    shard = P("shard", None)
    return jax.shard_map(
        per_device,
        mesh=mesh,
        in_specs=(both, both, both, both, shard, both, shard, shard),
        out_specs=(both, both, both, shard),
        check_vma=False,
    )
```

time: 276 us -> 263 us (0.953)
  waiting for transfers between devices: 106 us -> 71.2 us
  Pallas kernels: 98.3 us -> 111 us
  starting transfers between devices: 45.6 us -> 52.4 us
  local copies, waits for them, and re-layouts: 14.2 us -> 19.6 us
    ppermute x12 -> x9, waiting for transfers between devices: 53.1 us -> 25.2 us  [onward(): return lax.ppermute(x, 'shard', perm)]
    pallas_call x15 -> x26, Pallas kernels: 98.3 us -> 111 us  [call(): pl.pallas_call(kernel, grid_spec=pltpu.PrefetchScalarGridSpec(num_scalar_...]
    ppermute x12 -> x9, starting transfers between devices: 11.7 us -> 20.9 us  [onward(): return lax.ppermute(x, 'shard', perm)]
    unnamed x60 -> x108, local copies, waits for them, and re-layouts: 9.79 us -> 17.9 us
    ppermute x28, waiting for transfers between devices: 52.4 us -> 44.5 us  [across(): lax.ppermute(x, 'replica', [(r, r ^ 1 << b) for r in range(self.replicas)])]
    ppermute x28, starting transfers between devices: 33 us -> 29.5 us  [across(): lax.ppermute(x, 'replica', [(r, r ^ 1 << b) for r in range(self.replicas)])]
  transfers between devices with their start and end apart: 46 -> 46, of which waited for: 19 -> 13; matrix products, arithmetic and copies ran while one was open for 3% -> 1% of each run, Pallas kernels for 33% -> 41%
where the time goes in v2:
time: 263 us; the launch traced here: 260 us
  Pallas kernels  111 us (42%)
  waiting for transfers between devices  71.2 us (27%)
  starting transfers between devices  52.4 us (20%)
  local copies, waits for them, and re-layouts  19.6 us (7%)
  between operations  6.16 us (2%)
    pallas_call x26, Pallas kernels, call(): pl.pallas_call(kernel, grid_spec=pltpu.PrefetchScalarGridSpec(num_scalar_...  111 us
    ppermute x28, waiting for transfers between devices, across(): lax.ppermute(x, 'replica', [(r, r ^ 1 << b) for r in range(self.replicas)])  44.5 us
    ppermute x28, starting transfers between devices, across(): lax.ppermute(x, 'replica', [(r, r ^ 1 << b) for r in range(self.replicas)])  29.5 us
    ppermute x9, waiting for transfers between devices, onward(): return lax.ppermute(x, 'shard', perm)  25.2 us
    ppermute x9, starting transfers between devices, onward(): return lax.ppermute(x, 'shard', perm)  20.9 us
    unnamed x108, local copies, waits for them, and re-layouts  17.9 us
  transfers between devices with their start and end apart: 46, of which 13 were waited for; matrix products, arithmetic and copies ran while one was open for 1% of the time, Pallas kernels for 41%

profile of v2, /device:TPU:0, one launch (start us, length us, event | category | flops | bytes accessed | tf_op | source)
XLA Modules:
  0.0 260.0 jit_solution(11117528774193072502)
XLA Ops:
  2.0 1.7 copy-done.7
  3.6 1.5 shard_map.120
  5.3 1.2 copy-done.1
  6.6 1.2 copy-done.4
  7.8 3.5 %shard_map.121 = (bf16[256,512]{1,0:T(8,128)(2,1)S(1)}, bf16[256,512]{1,0:T(8,128)(2,1)S(1)}, f32[8,128]{1,0:T(8,128)S(1)}) custom-call(s32[11]{0:T(128)S(1)} %get-tuple-element.189.sc_ref, bf16[512,2048]{1,0:T(8,128)(2,1)S(1)} %copy-done, bf16[512,1024]{1,0:T(8,128)(2,1)S(1)} %copy-done.1, ...), custom_call_target="tpu_custom_call", output_to_operand_aliasing={{2}: (6, {})} | custom-call | flops 1 | bytes 1 | tf_op jit(solution)/shard_map/pallas_call | solution.py:40
  11.5 2.9 %collective-permute-start.4 = (bf16[256,1152]{1,0:T(8,128)(2,1)S(1)}, bf16[256,1152]{1,0:T(8,128)(2,1)}, u32[]{:S(2)}, u32[]{:S(2)}) collective-permute-start(bf16[256,1152]{1,0:T(8,128)(2,1)S(1)} %get-tuple-element.107), channel_id=1, source_target_pairs={{0,2},{1,3},{2,6},{3,7},{6,4},{7,5},{4,0},{5,1},{8,10},{9,11},{10,... | collective-permute-start | bytes 1769480 | tf_op jit(solution)/shard_map/ppermute | solution.py:454
  14.4 3.5 %shard_map.122 = (bf16[256,512]{1,0:T(8,128)(2,1)S(1)}, bf16[256,512]{1,0:T(8,128)(2,1)S(1)}, f32[8,128]{1,0:T(8,128)S(1)}) custom-call(s32[11]{0:T(128)S(1)} %get-tuple-element.189.sc_ref, bf16[512,2048]{1,0:T(8,128)(2,1)S(1)} %copy-done, bf16[512,1024]{1,0:T(8,128)(2,1)S(1)} %copy-done.1, ...), custom_call_target="tpu_custom_call", output_to_operand_aliasing={{2}: (6, {})} | custom-call | flops 1 | bytes 1 | tf_op jit(solution)/shard_map/pallas_call | solution.py:40
  18.0 6.4 %shard_map.123 = (bf16[128,2304]{1,0:T(8,128)(2,1)S(1)}, bf16[128,2304]{1,0:T(8,128)(2,1)S(1)}, bf16[128,2304]{1,0:T(8,128)(2,1)S(1)}, bf16[128,2304]{1,0:T(8,128)(2,1)S(1)}, f32[8,128]{1,0:T(8,128)S(1)}) custom-call(s32[11]{0:T(128)S(1)} %get-tuple-element.189.sc_ref, ...), custom_call_target="tpu_custom_call", output_to_operand_aliasing={{4}: (5, {})} | custom-call | flops 1 | bytes 1 | tf_op jit(solution)/shard_map/pallas_call | solution.py:40
  24.4 1.6 collective-permute-start.8
  26.0 1.5 collective-permute-start.9
  27.5 3.5 %shard_map.124 = (bf16[256,512]{1,0:T(8,128)(2,1)S(1)}, bf16[256,512]{1,0:T(8,128)(2,1)S(1)}, f32[8,128]{1,0:T(8,128)S(1)}) custom-call(s32[11]{0:T(128)S(1)} %get-tuple-element.189.sc_ref, bf16[512,2048]{1,0:T(8,128)(2,1)S(1)} %copy-done, bf16[512,1024]{1,0:T(8,128)(2,1)S(1)} %copy-done.2, ...), custom_call_target="tpu_custom_call", output_to_operand_aliasing={{2}: (6, {})} | custom-call | flops 1 | bytes 1 | tf_op jit(solution)/shard_map/pallas_call | solution.py:40
  31.6 2.6 collective-permute-start.10
  34.2 3.5 %shard_map.125 = (bf16[256,512]{1,0:T(8,128)(2,1)S(1)}, bf16[256,512]{1,0:T(8,128)(2,1)S(1)}, f32[8,128]{1,0:T(8,128)S(1)}, bf16[256,1152]{1,0:T(8,128)(2,1)}) custom-call(s32[11]{0:T(128)S(1)} %get-tuple-element.189.sc_ref, bf16[512,2048]{1,0:T(8,128)(2,1)S(1)} %copy-done, ...), custom_call_target="tpu_custom_call", output_to_operand_aliasing={{2}: (6, {}), {3}: (7, {})} | custom-call | flops 1 | bytes 1 | tf_op jit(solution)/shard_map/pallas_call | solution.py:40
  38.5 9.7 %shard_map.126 = (bf16[128,2304]{1,0:T(8,128)(2,1)}, bf16[128,2304]{1,0:T(8,128)(2,1)S(1)}, bf16[128,2304]{1,0:T(8,128)(2,1)S(1)}, bf16[128,2304]{1,0:T(8,128)(2...) custom-call(s32[11]{0:T(128)S(1)} %get-tuple-element.189.sc_ref, ...), custom_call_target="tpu_custom_call", output_to_operand_aliasing={{8}: (7, {})} | custom-call | flops 1 | bytes 1 | tf_op jit(solution)/shard_map/pallas_call | solution.py:40
  48.9 1.2 collective-permute-start.6
  50.1 1.3 shard_map.127
  52.2 7.2 %shard_map.128 = (bf16[128,2304]{1,0:T(8,128)(2,1)}, bf16[128,2304]{1,0:T(8,128)(2,1)S(1)}, bf16[128,2304]{1,0:T(8,128)(2,1)}, bf16[128,2304]{1,0:T(8,128)(2,1)S...) custom-call(s32[11]{0:T(128)S(1)} %get-tuple-element.189.sc_ref, ...), custom_call_target="tpu_custom_call", output_to_operand_aliasing={{4}: (5, {}), {5}: (6, {})} | custom-call | flops 1 | bytes 1 | tf_op jit(solution)/shard_map/pallas_call | solution.py:40
  59.5 0.9 copy-done.18
  61.2 6.5 %shard_map.129 = (bf16[512,256]{1,0:T(8,128)(2,1)S(1)}, bf16[512,256]{1,0:T(8,128)(2,1)S(1)}, f32[8,128]{1,0:T(8,128)S(1)}) custom-call(s32[11]{0:T(128)S(1)} %get-tuple-element.189.sc_ref, bf16[512,4608]{1,0:T(8,128)(2,1)S(1)} %bitcast.14, bf16[512,4608]{1,0:T(8,128)(2,1)} %collective-permute-done.refs_3_.refs_5_.refs_1_, ...), custom_call_target="tpu_custom_call", output_to_operand_aliasing={{2}: (4, {})} | custom-call | flops 1 | bytes 1 | tf_op jit(solution)/shard_map/pallas_call | solution.py:40
  69.1 1.5 collective-permute-start.19
  71.6 0.9 collective-permute-start.17
  72.4 12.0 %collective-permute-done.18.refs_1_ = bf16[128,2304]{1,0:T(8,128)(2,1)S(1)} collective-permute-done((bf16[128,2304]{1,0:T(8,128)(2,1)S(1)}, bf16[128,2304]{1,0:T(8,128)(2,1)S(1)}, u32[]{:S(2)}, u32[]{:S(2)}) %collective-permute-start.18) | collective-permute-done | bytes 589856 | tf_op jit(solution)/shard_map/ppermute | solution.py:457
  85.3 6.3 %shard_map.130 = (bf16[512,2048]{1,0:T(8,128)(2,1)}, bf16[512,1024]{1,0:T(8,128)(2,1)}, bf16[512,1024]{1,0:T(8,128)(2,1)}, f32[8,128]{1,0:T(8,128)S(1)}, bf16[256,1152]{1,0:T(8,128)(2,1)S(1)}) custom-call(s32[11]{0:T(128)S(1)} %get-tuple-element.189.sc_ref, bf16[512,2048]{1,0:T(8,128)(2,1)S(1)} %copy-done, ...), custom_call_target="tpu_custom_call", output_to_operand_aliasing={{3}: (8, {}), {4}: (9, {})} | custom-call | flops 1 | bytes 1 | tf_op jit(solution)/shard_map/pallas_call | solution.py:40
  91.6 2.4 shard_map.131
  94.1 1.4 shard_map.132
  96.3 1.7 collective-permute-done.17.refs_5_
  98.0 6.6 %shard_map.133 = (bf16[512,256]{1,0:T(8,128)(2,1)S(1)}, bf16[512,256]{1,0:T(8,128)(2,1)S(1)}, f32[8,128]{1,0:T(8,128)S(1)}) custom-call(s32[11]{0:T(128)S(1)} %get-tuple-element.189.sc_ref, bf16[512,4608]{1,0:T(8,128)(2,1)S(1)} %bitcast.14, bf16[512,4608]{1,0:T(8,128)(2,1)} %collective-permute-done.refs_3_.refs_5_.refs_1_, ...), custom_call_target="tpu_custom_call", output_to_operand_aliasing={{2}: (7, {})} | custom-call | flops 1 | bytes 1 | tf_op jit(solution)/shard_map/pallas_call | solution.py:40
  104.7 1.3 collective-permute-start.15
  106.8 1.5 collective-permute-start.23
  108.9 1.2 collective-permute-start.25
  110.0 6.3 %shard_map.134 = (bf16[512,2048]{1,0:T(8,128)(2,1)}, bf16[512,1024]{1,0:T(8,128)(2,1)}, bf16[512,1024]{1,0:T(8,128)(2,1)}, f32[8,128]{1,0:T(8,128)S(1)}) custom-call(s32[11]{0:T(128)S(1)} %get-tuple-element.189.sc_ref, bf16[512,2048]{1,0:T(8,128)(2,1)S(1)} %copy-done, ...), custom_call_target="tpu_custom_call", output_to_operand_aliasing={{0}: (8, {}), {1}: (9, {}), {2}: (10, {}), {3}: (11, {})} | custom-call | flops 1 | bytes 1 | tf_op jit(solution)/shard_map/pallas_call | solution.py:40
  117.2 1.3 collective-permute-start.27
  118.5 2.4 collective-permute-done.23.refs_6_
  121.3 11.8 %collective-permute-done.24.refs_1_ = bf16[128,2304]{1,0:T(8,128)(2,1)S(1)} collective-permute-done((bf16[128,2304]{1,0:T(8,128)(2,1)}, bf16[128,2304]{1,0:T(8,128)(2,1)S(1)}, u32[]{:S(2)}, u32[]{:S(2)}) %collective-permute-start.24) | collective-permute-done | bytes 589856 | tf_op jit(solution)/shard_map/ppermute | solution.py:457
  133.1 1.2 collective-permute-start.34
  135.9 10.3 %collective-permute-done.27.refs_10_ = bf16[256,1152]{1,0:T(8,128)(2,1)S(1)} collective-permute-done((bf16[256,1152]{1,0:T(8,128)(2,1)S(1)}, bf16[256,1152]{1,0:T(8,128)(2,1)S(1)}, u32[]{:S(2)}, u32[]{:S(2)}) %collective-permute-start.27) | collective-permute-done | bytes 589856 | tf_op jit(solution)/shard_map/ppermute | solution.py:454
  146.2 10.6 %collective-permute-done.22.refs_3_.refs_7_ = bf16[64,4608]{1,0:T(8,128)(2,1)S(1)} collective-permute-done((bf16[64,4608]{1,0:T(8,128)(2,1)S(1)}, bf16[64,4608]{1,0:T(8,128)(2,1)S(1)}, u32[]{:S(2)}, u32[]{:S(2)}) %collective-permute-start.22) | collective-permute-done | bytes 589856 | tf_op jit(solution)/shard_map/ppermute | solution.py:454
  156.9 1.9 shard_map.137
  158.8 10.8 %collective-permute-start.32 = (bf16[64,4608]{1,0:T(8,128)(2,1)S(1)}, bf16[64,4608]{1,0:T(8,128)(2,1)S(1)}, u32[]{:S(2)}, u32[]{:S(2)}) collective-permute-start(bf16[64,4608]{1,0:T(8,128)(2,1)S(1)} %get-tuple-element.159), channel_id=1, source_target_pairs={{0,2},{1,3},{2,6},{3,7},{6,4},{7,5},{4,0},{5,1},{8,10},{9,11},{10,... | collective-permute-start | bytes 1769480 | tf_op jit(solution)/shard_map/ppermute | solution.py:454
  169.5 0.9 collective-permute-start.31
  170.5 1.5 collective-permute-start.33
  172.0 6.4 %shard_map.138 = (bf16[512,256]{1,0:T(8,128)(2,1)S(1)}, bf16[512,256]{1,0:T(8,128)(2,1)S(1)}, f32[8,128]{1,0:T(8,128)S(1)}) custom-call(s32[11]{0:T(128)S(1)} %get-tuple-element.189.sc_ref, bf16[512,4608]{1,0:T(8,128)(2,1)S(1)} %bitcast.14, bf16[512,4608]{1,0:T(8,128)(2,1)} %collective-permute-done.refs_3_.refs_5_.refs_1_, ...), custom_call_target="tpu_custom_call", output_to_operand_aliasing={{2}: (7, {})} | custom-call | flops 1 | bytes 1 | tf_op jit(solution)/shard_map/pallas_call | solution.py:40
  178.5 1.5 collective-permute-done.36.refs_6_
  180.0 6.3 %shard_map.139 = (bf16[512,2048]{1,0:T(8,128)(2,1)}, bf16[512,1024]{1,0:T(8,128)(2,1)}, bf16[512,1024]{1,0:T(8,128)(2,1)}, f32[8,128]{1,0:T(8,128)S(1)}) custom-call(s32[11]{0:T(128)S(1)} %get-tuple-element.189.sc_ref, bf16[512,2048]{1,0:T(8,128)(2,1)S(1)} %copy-done, ...), custom_call_target="tpu_custom_call", output_to_operand_aliasing={{0}: (8, {}), {1}: (9, {}), {2}: (10, {}), {3}: (11, {})} | custom-call | flops 1 | bytes 1 | tf_op jit(solution)/shard_map/pallas_call | solution.py:40
  187.3 1.9 collective-permute-start.37
  190.2 1.5 collective-permute-start.28
  191.7 1.5 collective-permute-start.29
  193.2 5.8 %collective-permute-done.30.refs_2_ = bf16[64,2304]{1,0:T(8,128)(2,1)S(1)} collective-permute-done((bf16[64,2304]{1,0:T(8,128)(2,1)S(1)}, bf16[64,2304]{1,0:T(8,128)(2,1)S(1)}, u32[]{:S(2)}, u32[]{:S(2)}) %collective-permute-start.30) | collective-permute-done | bytes 294944 | tf_op jit(solution)/shard_map/ppermute | solution.py:457
  199.6 4.2 %collective-permute-done.37.refs_3_.refs_7_ = bf16[64,4608]{1,0:T(8,128)(2,1)S(1)} collective-permute-done((bf16[64,4608]{1,0:T(8,128)(2,1)S(1)}, bf16[64,4608]{1,0:T(8,128)(2,1)S(1)}, u32[]{:S(2)}, u32[]{:S(2)}) %collective-permute-start.37) | collective-permute-done | bytes 589856 | tf_op jit(solution)/shard_map/ppermute | solution.py:454
  205.2 1.2 collective-permute-start.42
  207.3 5.0 %collective-permute-done.28.refs_3_ = bf16[256,1152]{1,0:T(8,128)(2,1)S(1)} collective-permute-done((bf16[256,1152]{1,0:T(8,128)(2,1)S(1)}, bf16[256,1152]{1,0:T(8,128)(2,1)S(1)}, u32[]{:S(2)}, u32[]{:S(2)}) %collective-permute-start.28) | collective-permute-done | bytes 589856 | tf_op jit(solution)/shard_map/ppermute | solution.py:457
  212.2 1.5 collective-permute-start.45
  213.7 4.4 %collective-permute-done.40.refs_3_ = bf16[64,2304]{1,0:T(8,128)(2,1)} collective-permute-done((bf16[64,2304]{1,0:T(8,128)(2,1)S(1)}, bf16[64,2304]{1,0:T(8,128)(2,1)}, u32[]{:S(2)}, u32[]{:S(2)}) %collective-permute-start.40) | collective-permute-done | bytes 294944 | tf_op jit(solution)/shard_map/ppermute | solution.py:457
  218.7 1.5 collective-permute-start.43
  220.2 7.1 %shard_map.142 = (bf16[512,256]{1,0:T(8,128)(2,1)S(1)}, bf16[512,256]{1,0:T(8,128)(2,1)}, f32[8,128]{1,0:T(8,128)S(1)}) custom-call(s32[11]{0:T(128)S(1)} %get-tuple-element.189.sc_ref, bf16[512,4608]{1,0:T(8,128)(2,1)S(1)} %bitcast.14, bf16[512,4608]{1,0:T(8,128)(2,1)} %collective-permute-done.refs_3_.refs_5_.refs_1_, ...), custom_call_target="tpu_custom_call", output_to_operand_aliasing={{2}: (7, {})} | custom-call | flops 1 | bytes 1 | tf_op jit(solution)/shard_map/pallas_call | solution.py:40
  233.6 1.2 copy-done.3
  234.8 1.2 copy-done.6
  236.0 0.9 copy-done.42
  237.0 6.3 %shard_map.143 = (bf16[512,2048]{1,0:T(8,128)(2,1)}, bf16[512,1024]{1,0:T(8,128)(2,1)}, bf16[512,1024]{1,0:T(8,128)(2,1)}, f32[8,128]{1,0:T(8,128)S(1)}) custom-call(s32[11]{0:T(128)S(1)} %get-tuple-element.189.sc_ref, bf16[512,2048]{1,0:T(8,128)(2,1)S(1)} %copy-done, ...), custom_call_target="tpu_custom_call", output_to_operand_aliasing={{0}: (8, {}), {1}: (9, {}), {2}: (10, {}), {3}: (11, {})} | custom-call | flops 1 | bytes 1 | tf_op jit(solution)/shard_map/pallas_call | solution.py:40
  243.3 2.3 copy-done.9
  245.6 2.3 copy-done.10
  247.9 6.2 %shard_map.144 = (f32[256,4608]{1,0:T(8,128)}, f32[8,128]{1,0:T(8,128)S(1)}) custom-call(s32[12]{0:T(128)S(1)} %stack.39.sc_ref, f32[256,4608]{1,0:T(8,128)S(1)} %copy-done.9, f32[256,4608]{1,0:T(8,128)S(1)} %copy-done.10, bf16[64,2304]{1,0:T(8,128)(2,1)S(1)} %get-tuple-element.182.refs_2_, ...), custom_call_target="tpu_custom_call", output_to_operand_aliasing={{1}: (9, {})} | custom-call | flops 1 | bytes 1 | tf_op jit(solution)/shard_map/pallas_call | solution.py:40
  254.2 2.3 copy-done.11
  256.5 3.3 %shard_map.145 = (f32[256,4608]{1,0:T(8,128)}, f32[8,128]{1,0:T(8,128)S(1)}) custom-call(s32[4]{0:T(128)S(1)} %pad_add_fusion.sc_ref, f32[256,4608]{1,0:T(8,128)S(1)} %bitcast.16, f32[256,4608]{1,0:T(8,128)S(1)} %copy-done.11, bf16[64,2304]{1,0:T(8,128)(2,1)} %collective-permute-done.41.refs_2_, ...), custom_call_target="tpu_custom_call", output_to_operand_aliasing={{0}: (5, {}), {1}: (6, {})} | custom-call | flops 1 | bytes 1 | tf_op jit(solution)/shard_map/pallas_call | solution.py:40
  (170 shorter events, 20.4 us)
Async XLA Ops:
  0.6 17.3 %collective-permute-start = (bf16[512,4608]{1,0:T(8,128)(2,1)}, bf16[512,4608]{1,0:T(8,128)(2,1)}, u32[]{:S(2)}, u32[]{:S(2)}) collective-permute-start(bf16[512,4608]{1,0:T(8,128)(2,1)} %refs_0_.26), channel_id=1, source_target_pairs={{0,1},{1,0},{2,3},{3,2},{4,5},{5,4},{6,7},{7,6},{8,9},{9,8},{10,11... | collective-permute-start | bytes 14155784 | tf_op jit(solution)/shard_map/ppermute | solution.py:447
  11.3 6.6 %collective-permute-start.1 = (bf16[256,512]{1,0:T(8,128)(2,1)S(1)}, bf16[256,512]{1,0:T(8,128)(2,1)S(1)}, u32[]{:S(2)}, u32[]{:S(2)}) collective-permute-start(bf16[256,512]{1,0:T(8,128)(2,1)S(1)} %get-tuple-element.100), channel_id=1, source_target_pairs={{0,1},{1,0},{2,3},{3,2},{4,5},{5,4},{6,7},{7,6},{8,9},{9,8},{10,11... | collective-permute-start | bytes 786440 | tf_op jit(solution)/shard_map/ppermute | solution.py:447
  11.5 20.2 %collective-permute-start.4 = (bf16[256,1152]{1,0:T(8,128)(2,1)S(1)}, bf16[256,1152]{1,0:T(8,128)(2,1)}, u32[]{:S(2)}, u32[]{:S(2)}) collective-permute-start(bf16[256,1152]{1,0:T(8,128)(2,1)S(1)} %get-tuple-element.107), channel_id=1, source_target_pairs={{0,2},{1,3},{2,6},{3,7},{6,4},{7,5},{4,0},{5,1},{8,10},{9,11},{10,... | collective-permute-start | bytes 1769480 | tf_op jit(solution)/shard_map/ppermute | solution.py:454
  24.4 25.7 %copy-start.33 = (bf16[128,2304]{1,0:T(8,128)(2,1)}, bf16[128,2304]{1,0:T(8,128)(2,1)S(1)}, u32[]{:S(2)}) copy-start(bf16[128,2304]{1,0:T(8,128)(2,1)S(1)} %get-tuple-element.115.refs_0_) | copy-start | bytes 1769476
  24.4 25.6 %copy-start.35 = (bf16[128,2304]{1,0:T(8,128)(2,1)}, bf16[128,2304]{1,0:T(8,128)(2,1)S(1)}, u32[]{:S(2)}) copy-start(bf16[128,2304]{1,0:T(8,128)(2,1)S(1)} %get-tuple-element.117.refs_2_.refs_3_) | copy-start | bytes 1769476
  24.4 24.4 %collective-permute-start.8 = (bf16[128,2304]{1,0:T(8,128)(2,1)S(1)}, bf16[128,2304]{1,0:T(8,128)(2,1)S(1)}, u32[]{:S(2)}, u32[]{:S(2)}) collective-permute-start(bf16[128,2304]{1,0:T(8,128)(2,1)S(1)} %get-tuple-element.116), channel_id=1, source_target_pairs={{0,8},{8,0},{16,24},{24,16},{1,9},{9,1},{17,25},{25,17},{2,10},{10... | collective-permute-start | bytes 1769480 | tf_op jit(solution)/shard_map/ppermute | solution.py:457
  26.0 24.1 %collective-permute-start.9 = (bf16[128,2304]{1,0:T(8,128)(2,1)S(1)}, bf16[128,2304]{1,0:T(8,128)(2,1)S(1)}, u32[]{:S(2)}, u32[]{:S(2)}) collective-permute-start(bf16[128,2304]{1,0:T(8,128)(2,1)S(1)} %get-tuple-element.118), channel_id=1, source_target_pairs={{0,16},{8,24},{16,0},{24,8},{1,17},{9,25},{17,1},{25,9},{2,18},{10... | collective-permute-start | bytes 1769480 | tf_op jit(solution)/shard_map/ppermute | solution.py:457
  27.5 10.3 %collective-permute-start.2 = (bf16[256,512]{1,0:T(8,128)(2,1)S(1)}, bf16[256,512]{1,0:T(8,128)(2,1)S(1)}, u32[]{:S(2)}, u32[]{:S(2)}) collective-permute-start(bf16[256,512]{1,0:T(8,128)(2,1)S(1)} %get-tuple-element.104), channel_id=1, source_target_pairs={{0,1},{1,0},{2,3},{3,2},{4,5},{5,4},{6,7},{7,6},{8,9},{9,8},{10,11... | collective-permute-start | bytes 786440 | tf_op jit(solution)/shard_map/ppermute | solution.py:447
  31.1 7.5 %collective-permute-start.3 = (bf16[256,512]{1,0:T(8,128)(2,1)S(1)}, bf16[256,512]{1,0:T(8,128)(2,1)S(1)}, u32[]{:S(2)}, u32[]{:S(2)}) collective-permute-start(bf16[256,512]{1,0:T(8,128)(2,1)S(1)} %get-tuple-element.105), channel_id=1, source_target_pairs={{0,1},{1,0},{2,3},{3,2},{4,5},{5,4},{6,7},{7,6},{8,9},{9,8},{10,11... | collective-permute-start | bytes 786440 | tf_op jit(solution)/shard_map/ppermute | solution.py:447
  31.6 20.6 %collective-permute-start.10 = (bf16[256,1152]{1,0:T(8,128)(2,1)}, bf16[256,1152]{1,0:T(8,128)(2,1)S(1)}, u32[]{:S(2)}, u32[]{:S(2)}) collective-permute-start(bf16[256,1152]{1,0:T(8,128)(2,1)} %get-tuple-element.121), channel_id=1, source_target_pairs={{0,2},{1,3},{2,6},{3,7},{6,4},{7,5},{4,0},{5,1},{8,10},{9,11},{10,... | collective-permute-start | bytes 1769480 | tf_op jit(solution)/shard_map/ppermute | solution.py:454
  37.8 31.4 %collective-permute-start.12 = (bf16[256,1152]{1,0:T(8,128)(2,1)}, bf16[256,1152]{1,0:T(8,128)(2,1)S(1)}, u32[]{:S(2)}, u32[]{:S(2)}) collective-permute-start(bf16[256,1152]{1,0:T(8,128)(2,1)} %get-tuple-element.126.refs_2_), channel_id=1, source_target_pairs={{0,2},{1,3},{2,6},{3,7},{6,4},{7,5},{4,0},{5,1},{8,10},{9,11},{10,... | collective-permute-start | bytes 1769480 | tf_op jit(solution)/shard_map/ppermute | solution.py:454
  48.3 43.4 %copy-start.24 = (bf16[128,2304]{1,0:T(8,128)(2,1)}, bf16[128,2304]{1,0:T(8,128)(2,1)S(1)}, u32[]{:S(2)}) copy-start(bf16[128,2304]{1,0:T(8,128)(2,1)S(1)} %get-tuple-element.109.refs_0_) | copy-start | bytes 1769476
  48.3 45.8 %copy-start.12 = (bf16[128,2304]{1,0:T(8,128)(2,1)}, bf16[128,2304]{1,0:T(8,128)(2,1)S(1)}, u32[]{:S(2)}) copy-start(bf16[128,2304]{1,0:T(8,128)(2,1)S(1)} %get-tuple-element.134.refs_2_.refs_4_) | copy-start | bytes 1769476
  48.3 22.4 %collective-permute-start.5 = (bf16[128,2304]{1,0:T(8,128)(2,1)}, bf16[128,2304]{1,0:T(8,128)(2,1)}, u32[]{:S(2)}, u32[]{:S(2)}) collective-permute-start(bf16[128,2304]{1,0:T(8,128)(2,1)} %get-tuple-element.110), channel_id=1, source_target_pairs={{0,8},{8,0},{16,24},{24,16},{1,9},{9,1},{17,25},{25,17},{2,10},{10... | collective-permute-start | bytes 1769480 | tf_op jit(solution)/shard_map/ppermute | solution.py:457
  48.9 22.2 %collective-permute-start.6 = (bf16[128,2304]{1,0:T(8,128)(2,1)S(1)}, bf16[128,2304]{1,0:T(8,128)(2,1)}, u32[]{:S(2)}, u32[]{:S(2)}) collective-permute-start(bf16[128,2304]{1,0:T(8,128)(2,1)S(1)} %get-tuple-element.112), channel_id=1, source_target_pairs={{0,16},{8,24},{16,0},{24,8},{1,17},{9,25},{17,1},{25,9},{2,18},{10... | collective-permute-start | bytes 1769480 | tf_op jit(solution)/shard_map/ppermute | solution.py:457
  50.0 2.2 collective-permute-start.7
  61.2 24.1 %copy-start.5 = (bf16[512,1024]{1,0:T(8,128)(2,1)S(1)}, bf16[512,1024]{1,0:T(8,128)(2,1)}, u32[]{:S(2)}) copy-start(bf16[512,1024]{1,0:T(8,128)(2,1)} %refs_2_.21) | copy-start | bytes 3145732
  67.7 23.9 %copy-start.27 = (bf16[128,2304]{1,0:T(8,128)(2,1)S(1)}, bf16[128,2304]{1,0:T(8,128)(2,1)}, u32[]{:S(2)}) copy-start(bf16[128,2304]{1,0:T(8,128)(2,1)} %copy-done.26) | copy-start | bytes 1769476
  67.7 3.8 %collective-permute-start.11 = (bf16[512,256]{1,0:T(8,128)(2,1)S(1)}, bf16[512,256]{1,0:T(8,128)(2,1)S(1)}, u32[]{:S(2)}, u32[]{:S(2)}) collective-permute-start(bf16[512,256]{1,0:T(8,128)(2,1)S(1)} %get-tuple-element.124), channel_id=1, source_target_pairs={{0,1},{1,0},{2,3},{3,2},{4,5},{5,4},{6,7},{7,6},{8,9},{9,8},{10,11... | collective-permute-start | bytes 786440 | tf_op jit(solution)/shard_map/ppermute | solution.py:447
  68.3 16.2 %collective-permute-start.18 = (bf16[128,2304]{1,0:T(8,128)(2,1)S(1)}, bf16[128,2304]{1,0:T(8,128)(2,1)S(1)}, u32[]{:S(2)}, u32[]{:S(2)}) collective-permute-start(bf16[128,2304]{1,0:T(8,128)(2,1)S(1)} %get-tuple-element.133), channel_id=1, source_target_pairs={{0,8},{8,0},{16,24},{24,16},{1,9},{9,1},{17,25},{25,17},{2,10},{10... | collective-permute-start | bytes 1769480 | tf_op jit(solution)/shard_map/ppermute | solution.py:457
  69.1 24.9 %collective-permute-start.19 = (bf16[128,2304]{1,0:T(8,128)(2,1)S(1)}, bf16[128,2304]{1,0:T(8,128)(2,1)S(1)}, u32[]{:S(2)}, u32[]{:S(2)}) collective-permute-start(bf16[128,2304]{1,0:T(8,128)(2,1)S(1)} %get-tuple-element.135), channel_id=1, source_target_pairs={{0,16},{8,24},{16,0},{24,8},{1,17},{9,25},{17,1},{25,9},{2,18},{10... | collective-permute-start | bytes 1769480 | tf_op jit(solution)/shard_map/ppermute | solution.py:457
  70.7 23.4 %collective-permute-start.20 = (bf16[256,1152]{1,0:T(8,128)(2,1)S(1)}, bf16[256,1152]{1,0:T(8,128)(2,1)S(1)}, u32[]{:S(2)}, u32[]{:S(2)}) collective-permute-start(bf16[256,1152]{1,0:T(8,128)(2,1)S(1)} %get-tuple-element.131.refs_4_), channel_id=1, source_target_pairs={{0,2},{1,3},{2,6},{3,7},{6,4},{7,5},{4,0},{5,1},{8,10},{9,11},{10,... | collective-permute-start | bytes 1769480 | tf_op jit(solution)/shard_map/ppermute | solution.py:454
  71.0 25.2 %collective-permute-start.16 = (bf16[256,1152]{1,0:T(8,128)(2,1)}, bf16[256,1152]{1,0:T(8,128)(2,1)S(1)}, u32[]{:S(2)}, u32[]{:S(2)}) collective-permute-start(bf16[256,1152]{1,0:T(8,128)(2,1)} %get-tuple-element.126.refs_2_), channel_id=1, source_target_pairs={{0,8},{8,0},{16,24},{24,16},{1,9},{9,1},{17,25},{25,17},{2,10},{10... | collective-permute-start | bytes 1769480 | tf_op jit(solution)/shard_map/ppermute | solution.py:457
  71.6 26.4 %collective-permute-start.17 = (bf16[256,1152]{1,0:T(8,128)(2,1)S(1)}, bf16[256,1152]{1,0:T(8,128)(2,1)S(1)}, u32[]{:S(2)}, u32[]{:S(2)}) collective-permute-start(bf16[256,1152]{1,0:T(8,128)(2,1)S(1)} %get-tuple-element.131.refs_4_), channel_id=1, source_target_pairs={{0,16},{8,24},{16,0},{24,8},{1,17},{9,25},{17,1},{25,9},{2,18},{10... | collective-permute-start | bytes 1769480 | tf_op jit(solution)/shard_map/ppermute | solution.py:457
  84.5 23.8 %collective-permute-start.14 = (bf16[64,2304]{1,0:T(8,128)(2,1)}, bf16[64,2304]{1,0:T(8,128)(2,1)S(1)}, u32[]{:S(2)}, u32[]{:S(2)}) collective-permute-start(bf16[64,2304]{1,0:T(8,128)(2,1)} %get-tuple-element.129), channel_id=1, source_target_pairs={{0,16},{8,24},{16,0},{24,8},{1,17},{9,25},{17,1},{25,9},{2,18},{10... | collective-permute-start | bytes 884744 | tf_op jit(solution)/shard_map/ppermute | solution.py:457
  104.6 4.2 %collective-permute-start.21 = (bf16[512,256]{1,0:T(8,128)(2,1)S(1)}, bf16[512,256]{1,0:T(8,128)(2,1)S(1)}, u32[]{:S(2)}, u32[]{:S(2)}) collective-permute-start(bf16[512,256]{1,0:T(8,128)(2,1)S(1)} %get-tuple-element.139), channel_id=1, source_target_pairs={{0,1},{1,0},{2,3},{3,2},{4,5},{5,4},{6,7},{7,6},{8,9},{9,8},{10,11... | collective-permute-start | bytes 786440 | tf_op jit(solution)/shard_map/ppermute | solution.py:447
  104.7 11.6 %collective-permute-start.15 = (bf16[64,2304]{1,0:T(8,128)(2,1)S(1)}, bf16[64,2304]{1,0:T(8,128)(2,1)S(1)}, u32[]{:S(2)}, u32[]{:S(2)}) collective-permute-start(bf16[64,2304]{1,0:T(8,128)(2,1)S(1)} %copy-done.45), channel_id=1, source_target_pairs={{0,8},{8,0},{16,24},{24,16},{1,9},{9,1},{17,25},{25,17},{2,10},{10... | collective-permute-start | bytes 884744 | tf_op jit(solution)/shard_map/ppermute | solution.py:457
  106.0 11.2 %collective-permute-start.13 = (bf16[64,2304]{1,0:T(8,128)(2,1)}, bf16[64,2304]{1,0:T(8,128)(2,1)S(1)}, u32[]{:S(2)}, u32[]{:S(2)}) collective-permute-start(bf16[64,2304]{1,0:T(8,128)(2,1)} %get-tuple-element.128), channel_id=1, source_target_pairs={{0,16},{8,24},{16,0},{24,8},{1,17},{9,25},{17,1},{25,9},{2,18},{10... | collective-permute-start | bytes 884744 | tf_op jit(solution)/shard_map/ppermute | solution.py:457
  106.8 14.1 %collective-permute-start.23 = (bf16[64,2304]{1,0:T(8,128)(2,1)S(1)}, bf16[64,2304]{1,0:T(8,128)(2,1)S(1)}, u32[]{:S(2)}, u32[]{:S(2)}) collective-permute-start(bf16[64,2304]{1,0:T(8,128)(2,1)S(1)} %get-tuple-element.146), channel_id=1, source_target_pairs={{0,8},{8,0},{16,24},{24,16},{1,9},{9,1},{17,25},{25,17},{2,10},{10... | collective-permute-start | bytes 884744 | tf_op jit(solution)/shard_map/ppermute | solution.py:457
  108.3 24.8 %collective-permute-start.24 = (bf16[128,2304]{1,0:T(8,128)(2,1)}, bf16[128,2304]{1,0:T(8,128)(2,1)S(1)}, u32[]{:S(2)}, u32[]{:S(2)}) collective-permute-start(bf16[128,2304]{1,0:T(8,128)(2,1)} %get-tuple-element.148), channel_id=1, source_target_pairs={{0,8},{8,0},{16,24},{24,16},{1,9},{9,1},{17,25},{25,17},{2,10},{10... | collective-permute-start | bytes 1769480 | tf_op jit(solution)/shard_map/ppermute | solution.py:457
  108.9 25.4 %collective-permute-start.25 = (bf16[128,2304]{1,0:T(8,128)(2,1)}, bf16[128,2304]{1,0:T(8,128)(2,1)S(1)}, u32[]{:S(2)}, u32[]{:S(2)}) collective-permute-start(bf16[128,2304]{1,0:T(8,128)(2,1)} %get-tuple-element.150), channel_id=1, source_target_pairs={{0,16},{8,24},{16,0},{24,8},{1,17},{9,25},{17,1},{25,9},{2,18},{10... | collective-permute-start | bytes 1769480 | tf_op jit(solution)/shard_map/ppermute | solution.py:457
  110.0 25.1 %copy-start.19 = (bf16[128,2304]{1,0:T(8,128)(2,1)S(1)}, bf16[128,2304]{1,0:T(8,128)(2,1)}, u32[]{:S(2)}) copy-start(bf16[128,2304]{1,0:T(8,128)(2,1)} %copy-done.18) | copy-start | bytes 1769476
  110.0 25.1 %copy-start.22 = (bf16[128,2304]{1,0:T(8,128)(2,1)S(1)}, bf16[128,2304]{1,0:T(8,128)(2,1)}, u32[]{:S(2)}) copy-start(bf16[128,2304]{1,0:T(8,128)(2,1)} %copy-done.21) | copy-start | bytes 1769476
  116.3 40.5 %copy-start.25 = (bf16[128,2304]{1,0:T(8,128)(2,1)S(1)}, bf16[128,2304]{1,0:T(8,128)(2,1)}, u32[]{:S(2)}) copy-start(bf16[128,2304]{1,0:T(8,128)(2,1)} %copy-done.24) | copy-start | bytes 1769476
  116.3 40.5 %copy-start.28 = (bf16[128,2304]{1,0:T(8,128)(2,1)S(1)}, bf16[128,2304]{1,0:T(8,128)(2,1)}, u32[]{:S(2)}) copy-start(bf16[128,2304]{1,0:T(8,128)(2,1)} %copy-done.26) | copy-start | bytes 1769476
  116.3 19.5 %collective-permute-start.26 = (bf16[256,1152]{1,0:T(8,128)(2,1)S(1)}, bf16[256,1152]{1,0:T(8,128)(2,1)S(1)}, u32[]{:S(2)}, u32[]{:S(2)}) collective-permute-start(bf16[256,1152]{1,0:T(8,128)(2,1)S(1)} %get-tuple-element.153.refs_2_), channel_id=1, source_target_pairs={{0,2},{1,3},{2,6},{3,7},{6,4},{7,5},{4,0},{5,1},{8,10},{9,11},{10,... | collective-permute-start | bytes 1769480 | tf_op jit(solution)/shard_map/ppermute | solution.py:454
  117.2 29.0 %collective-permute-start.27 = (bf16[256,1152]{1,0:T(8,128)(2,1)S(1)}, bf16[256,1152]{1,0:T(8,128)(2,1)S(1)}, u32[]{:S(2)}, u32[]{:S(2)}) collective-permute-start(bf16[256,1152]{1,0:T(8,128)(2,1)S(1)} %get-tuple-element.154.refs_4_), channel_id=1, source_target_pairs={{0,2},{1,3},{2,6},{3,7},{6,4},{7,5},{4,0},{5,1},{8,10},{9,11},{10,... | collective-permute-start | bytes 1769480 | tf_op jit(solution)/shard_map/ppermute | solution.py:454
  120.9 35.9 %collective-permute-start.22 = (bf16[64,4608]{1,0:T(8,128)(2,1)S(1)}, bf16[64,4608]{1,0:T(8,128)(2,1)S(1)}, u32[]{:S(2)}, u32[]{:S(2)}) collective-permute-start(bf16[64,4608]{1,0:T(8,128)(2,1)S(1)} %get-tuple-element.145), channel_id=1, source_target_pairs={{0,2},{1,3},{2,6},{3,7},{6,4},{7,5},{4,0},{5,1},{8,10},{9,11},{10,... | collective-permute-start | bytes 1769480 | tf_op jit(solution)/shard_map/ppermute | solution.py:454
  133.1 23.8 %copy-start.29 = (bf16[128,2304]{1,0:T(8,128)(2,1)}, bf16[128,2304]{1,0:T(8,128)(2,1)S(1)}, u32[]{:S(2)}) copy-start(bf16[128,2304]{1,0:T(8,128)(2,1)S(1)} %collective-permute-done.24.refs_1_) | copy-start | bytes 1769476
  133.1 38.9 %collective-permute-start.34 = (bf16[256,1152]{1,0:T(8,128)(2,1)S(1)}, bf16[256,1152]{1,0:T(8,128)(2,1)S(1)}, u32[]{:S(2)}, u32[]{:S(2)}) collective-permute-start(bf16[256,1152]{1,0:T(8,128)(2,1)S(1)} %get-tuple-element.153.refs_2_), channel_id=1, source_target_pairs={{0,8},{8,0},{16,24},{24,16},{1,9},{9,1},{17,25},{25,17},{2,10},{10... | collective-permute-start | bytes 1769480 | tf_op jit(solution)/shard_map/ppermute | solution.py:457
  134.3 37.7 %copy-start.31 = (bf16[128,2304]{1,0:T(8,128)(2,1)}, bf16[128,2304]{1,0:T(8,128)(2,1)S(1)}, u32[]{:S(2)}) copy-start(bf16[128,2304]{1,0:T(8,128)(2,1)S(1)} %collective-permute-done.25.refs_3_.refs_5_) | copy-start | bytes 1769476
  134.3 37.7 %collective-permute-start.35 = (bf16[256,1152]{1,0:T(8,128)(2,1)S(1)}, bf16[256,1152]{1,0:T(8,128)(2,1)S(1)}, u32[]{:S(2)}, u32[]{:S(2)}) collective-permute-start(bf16[256,1152]{1,0:T(8,128)(2,1)S(1)} %get-tuple-element.154.refs_4_), channel_id=1, source_target_pairs={{0,16},{8,24},{16,0},{24,8},{1,17},{9,25},{17,1},{25,9},{2,18},{10... | collective-permute-start | bytes 1769480 | tf_op jit(solution)/shard_map/ppermute | solution.py:457
  135.9 33.7 %copy-start.48 = (bf16[64,2304]{1,0:T(8,128)(2,1)}, bf16[64,2304]{1,0:T(8,128)(2,1)S(1)}, u32[]{:S(2)}) copy-start(bf16[64,2304]{1,0:T(8,128)(2,1)S(1)} %get-tuple-element.157) | copy-start | bytes 884740
  135.9 36.1 %copy-start.46 = (bf16[64,2304]{1,0:T(8,128)(2,1)}, bf16[64,2304]{1,0:T(8,128)(2,1)S(1)}, u32[]{:S(2)}) copy-start(bf16[64,2304]{1,0:T(8,128)(2,1)S(1)} %get-tuple-element.170) | copy-start | bytes 884740
  158.8 27.6 %collective-permute-start.32 = (bf16[64,4608]{1,0:T(8,128)(2,1)S(1)}, bf16[64,4608]{1,0:T(8,128)(2,1)S(1)}, u32[]{:S(2)}, u32[]{:S(2)}) collective-permute-start(bf16[64,4608]{1,0:T(8,128)(2,1)S(1)} %get-tuple-element.159), channel_id=1, source_target_pairs={{0,2},{1,3},{2,6},{3,7},{6,4},{7,5},{4,0},{5,1},{8,10},{9,11},{10,... | collective-permute-start | bytes 1769480 | tf_op jit(solution)/shard_map/ppermute | solution.py:454
  169.5 16.8 %collective-permute-start.31 = (bf16[64,2304]{1,0:T(8,128)(2,1)}, bf16[64,2304]{1,0:T(8,128)(2,1)S(1)}, u32[]{:S(2)}, u32[]{:S(2)}) collective-permute-start(bf16[64,2304]{1,0:T(8,128)(2,1)} %get-tuple-element.158), channel_id=1, source_target_pairs={{0,16},{8,24},{16,0},{24,8},{1,17},{9,25},{17,1},{25,9},{2,18},{10... | collective-permute-start | bytes 884744 | tf_op jit(solution)/shard_map/ppermute | solution.py:457
  170.5 15.9 %collective-permute-start.33 = (bf16[64,2304]{1,0:T(8,128)(2,1)}, bf16[64,2304]{1,0:T(8,128)(2,1)S(1)}, u32[]{:S(2)}, u32[]{:S(2)}) collective-permute-start(bf16[64,2304]{1,0:T(8,128)(2,1)} %get-tuple-element.160), channel_id=1, source_target_pairs={{0,8},{8,0},{16,24},{24,16},{1,9},{9,1},{17,25},{25,17},{2,10},{10... | collective-permute-start | bytes 884744 | tf_op jit(solution)/shard_map/ppermute | solution.py:457
  178.4 1.6 collective-permute-start.36
  180.0 23.7 %copy-start.20 = (bf16[128,2304]{1,0:T(8,128)(2,1)S(1)}, bf16[128,2304]{1,0:T(8,128)(2,1)}, u32[]{:S(2)}) copy-start(bf16[128,2304]{1,0:T(8,128)(2,1)} %copy-done.18) | copy-start | bytes 1769476
  180.0 23.7 %copy-start.23 = (bf16[128,2304]{1,0:T(8,128)(2,1)S(1)}, bf16[128,2304]{1,0:T(8,128)(2,1)}, u32[]{:S(2)}) copy-start(bf16[128,2304]{1,0:T(8,128)(2,1)} %copy-done.21) | copy-start | bytes 1769476
  180.0 23.7 %copy-start.30 = (bf16[128,2304]{1,0:T(8,128)(2,1)S(1)}, bf16[128,2304]{1,0:T(8,128)(2,1)}, u32[]{:S(2)}) copy-start(bf16[128,2304]{1,0:T(8,128)(2,1)} %copy-done.29) | copy-start | bytes 1769476
  180.0 23.7 %copy-start.32 = (bf16[128,2304]{1,0:T(8,128)(2,1)S(1)}, bf16[128,2304]{1,0:T(8,128)(2,1)}, u32[]{:S(2)}) copy-start(bf16[128,2304]{1,0:T(8,128)(2,1)} %copy-done.31) | copy-start | bytes 1769476
  187.3 16.5 %collective-permute-start.37 = (bf16[64,4608]{1,0:T(8,128)(2,1)S(1)}, bf16[64,4608]{1,0:T(8,128)(2,1)S(1)}, u32[]{:S(2)}, u32[]{:S(2)}) collective-permute-start(bf16[64,4608]{1,0:T(8,128)(2,1)S(1)} %get-tuple-element.169), channel_id=1, source_target_pairs={{0,2},{1,3},{2,6},{3,7},{6,4},{7,5},{4,0},{5,1},{8,10},{9,11},{10,... | collective-permute-start | bytes 1769480 | tf_op jit(solution)/shard_map/ppermute | solution.py:454
  189.1 9.9 %collective-permute-start.30 = (bf16[64,2304]{1,0:T(8,128)(2,1)S(1)}, bf16[64,2304]{1,0:T(8,128)(2,1)S(1)}, u32[]{:S(2)}, u32[]{:S(2)}) collective-permute-start(bf16[64,2304]{1,0:T(8,128)(2,1)S(1)} %copy-done.49), channel_id=1, source_target_pairs={{0,16},{8,24},{16,0},{24,8},{1,17},{9,25},{17,1},{25,9},{2,18},{10... | collective-permute-start | bytes 884744 | tf_op jit(solution)/shard_map/ppermute | solution.py:457
  189.6 9.9 %collective-permute-start.38 = (bf16[64,2304]{1,0:T(8,128)(2,1)S(1)}, bf16[64,2304]{1,0:T(8,128)(2,1)S(1)}, u32[]{:S(2)}, u32[]{:S(2)}) collective-permute-start(bf16[64,2304]{1,0:T(8,128)(2,1)S(1)} %copy-done.47), channel_id=1, source_target_pairs={{0,8},{8,0},{16,24},{24,16},{1,9},{9,1},{17,25},{25,17},{2,10},{10... | collective-permute-start | bytes 884744 | tf_op jit(solution)/shard_map/ppermute | solution.py:457
  190.2 22.0 %collective-permute-start.28 = (bf16[256,1152]{1,0:T(8,128)(2,1)S(1)}, bf16[256,1152]{1,0:T(8,128)(2,1)S(1)}, u32[]{:S(2)}, u32[]{:S(2)}) collective-permute-start(bf16[256,1152]{1,0:T(8,128)(2,1)S(1)} %get-tuple-element.155.refs_2_), channel_id=1, source_target_pairs={{0,8},{8,0},{16,24},{24,16},{1,9},{9,1},{17,25},{25,17},{2,10},{10... | collective-permute-start | bytes 1769480 | tf_op jit(solution)/shard_map/ppermute | solution.py:457
  191.7 28.5 %collective-permute-start.29 = (bf16[256,1152]{1,0:T(8,128)(2,1)S(1)}, bf16[256,1152]{1,0:T(8,128)(2,1)S(1)}, u32[]{:S(2)}, u32[]{:S(2)}) collective-permute-start(bf16[256,1152]{1,0:T(8,128)(2,1)S(1)} %get-tuple-element.156.refs_4_), channel_id=1, source_target_pairs={{0,16},{8,24},{16,0},{24,8},{1,17},{9,25},{17,1},{25,9},{2,18},{10... | collective-permute-start | bytes 1769480 | tf_op jit(solution)/shard_map/ppermute | solution.py:457
  204.6 13.5 %collective-permute-start.40 = (bf16[64,2304]{1,0:T(8,128)(2,1)S(1)}, bf16[64,2304]{1,0:T(8,128)(2,1)}, u32[]{:S(2)}, u32[]{:S(2)}) collective-permute-start(bf16[64,2304]{1,0:T(8,128)(2,1)S(1)} %get-tuple-element.182.refs_2_), channel_id=1, source_target_pairs={{0,16},{8,24},{16,0},{24,8},{1,17},{9,25},{17,1},{25,9},{2,18},{10... | collective-permute-start | bytes 884744 | tf_op jit(solution)/shard_map/ppermute | solution.py:457
  205.2 13.4 %collective-permute-start.42 = (bf16[64,2304]{1,0:T(8,128)(2,1)S(1)}, bf16[64,2304]{1,0:T(8,128)(2,1)}, u32[]{:S(2)}, u32[]{:S(2)}) collective-permute-start(bf16[64,2304]{1,0:T(8,128)(2,1)S(1)} %get-tuple-element.183.refs_5_), channel_id=1, source_target_pairs={{0,8},{8,0},{16,24},{24,16},{1,9},{9,1},{17,25},{25,17},{2,10},{10... | collective-permute-start | bytes 884744 | tf_op jit(solution)/shard_map/ppermute | solution.py:457
  206.4 36.8 %collective-permute-start.44 = (bf16[64,2304]{1,0:T(8,128)(2,1)S(1)}, bf16[64,2304]{1,0:T(8,128)(2,1)}, u32[]{:S(2)}, u32[]{:S(2)}) collective-permute-start(bf16[64,2304]{1,0:T(8,128)(2,1)S(1)} %get-tuple-element.182.refs_2_), channel_id=1, source_target_pairs={{0,8},{8,0},{16,24},{24,16},{1,9},{9,1},{17,25},{25,17},{2,10},{10... | collective-permute-start | bytes 884744 | tf_op jit(solution)/shard_map/ppermute | solution.py:457
  212.2 31.0 %collective-permute-start.45 = (bf16[64,2304]{1,0:T(8,128)(2,1)S(1)}, bf16[64,2304]{1,0:T(8,128)(2,1)}, u32[]{:S(2)}, u32[]{:S(2)}) collective-permute-start(bf16[64,2304]{1,0:T(8,128)(2,1)S(1)} %get-tuple-element.183.refs_5_), channel_id=1, source_target_pairs={{0,16},{8,24},{16,0},{24,8},{1,17},{9,25},{17,1},{25,9},{2,18},{10... | collective-permute-start | bytes 884744 | tf_op jit(solution)/shard_map/ppermute | solution.py:457
  218.1 36.0 %collective-permute-start.41 = (bf16[64,2304]{1,0:T(8,128)(2,1)}, bf16[64,2304]{1,0:T(8,128)(2,1)}, u32[]{:S(2)}, u32[]{:S(2)}) collective-permute-start(bf16[64,2304]{1,0:T(8,128)(2,1)} %collective-permute-done.40.refs_3_), channel_id=1, source_target_pairs={{0,8},{8,0},{16,24},{24,16},{1,9},{9,1},{17,25},{25,17},{2,10},{10... | collective-permute-start | bytes 884744 | tf_op jit(solution)/shard_map/ppermute | solution.py:457
  218.7 35.5 %collective-permute-start.43 = (bf16[64,2304]{1,0:T(8,128)(2,1)}, bf16[64,2304]{1,0:T(8,128)(2,1)}, u32[]{:S(2)}, u32[]{:S(2)}) collective-permute-start(bf16[64,2304]{1,0:T(8,128)(2,1)} %collective-permute-done.42.refs_6_), channel_id=1, source_target_pairs={{0,16},{8,24},{16,0},{24,8},{1,17},{9,25},{17,1},{25,9},{2,18},{10... | collective-permute-start | bytes 884744 | tf_op jit(solution)/shard_map/ppermute | solution.py:457
  228.0 5.6 %collective-permute-start.39 = (bf16[512,256]{1,0:T(8,128)(2,1)}, bf16[512,256]{1,0:T(8,128)(2,1)S(1)}, u32[]{:S(2)}, u32[]{:S(2)}) collective-permute-start(bf16[512,256]{1,0:T(8,128)(2,1)} %get-tuple-element.174), channel_id=1, source_target_pairs={{0,1},{1,0},{2,3},{3,2},{4,5},{5,4},{6,7},{7,6},{8,9},{9,8},{10,11... | collective-permute-start | bytes 786440 | tf_op jit(solution)/shard_map/ppermute | solution.py:447
  (36 other events, 215.3 us)

commit v3 on v2

--- a/solution.py
+++ b/solution.py
@@ -15,7 +15,7 @@
 
 SCALE = 1.0 / 12.0
 CAP = 50.0
-VMEM = 40 * 1024 * 1024
+VMEM = 60 * 1024 * 1024
 F32 = jnp.float32
 BF16 = jnp.bfloat16
 
@@ -103,54 +103,71 @@
     )
 
 
-def forward_body(
-    heads, sc_ref, q_ref, k_ref, v_ref, seg_row_ref, seg_col_ref, send_ref, own_ref, mask_ref
-):
+def pick(sc, whole, lay, through):
+    rows, width = lay.rows, whole.shape[1]
+    block = (rows, width)
+    return call(
+        pick_body,
+        sc,
+        (lay.z - 1,),
+        [(whole, block, lambda n, sc: (sc[lay.at_z + 1 + n], 0))],
+        [(((lay.z - 1) * rows, width), BF16, block, lambda n, sc: (n, 0))],
+        through=through,
+    )
+
+
+def pick_body(sc_ref, in_ref, out_ref):
+    out_ref[...] = in_ref[...]
+
+
+def forward_body(heads, sc_ref, q_ref, k_ref, v_ref, seg_row_ref, seg_col_ref, out_ref, mask_ref):
     @pl.when(pl.program_id(0) == 0)
     def _():
         fill_mask(mask_ref, seg_row_ref, seg_col_ref)
 
-    def run(out_ref):
-        value_t = v_ref[...].T
-        for h in range(heads):
-            for start, tile, upto in tiles_of(q_ref.shape[0]):
-                probs, _ = softmax_tile(
-                    k_ref[:upto, :],
-                    q_ref[start : start + tile, h * DH : (h + 1) * DH],
-                    mask_ref[:upto, start : start + tile],
-                )
-                context = dot(value_t[:, :upto], probs.astype(BF16), NN)
-                out_ref[h * DH : (h + 1) * DH, start : start + tile] = context.astype(BF16)
-
-    pl.when(pl.program_id(0) == 0)(functools.partial(run, send_ref))
-    pl.when(pl.program_id(0) == 1)(functools.partial(run, own_ref))
-
-
-def forward(sc, k, block, lay, through):
+    value_t = v_ref[...].T
+    for h in range(heads):
+        for start, tile, upto in tiles_of(q_ref.shape[0]):
+            probs, _ = softmax_tile(
+                k_ref[:upto, :],
+                q_ref[start : start + tile, h * DH : (h + 1) * DH],
+                mask_ref[:upto, start : start + tile],
+            )
+            context = dot(value_t[:, :upto], probs.astype(BF16), NN)
+            out_ref[h * DH : (h + 1) * DH, start : start + tile] = context.astype(BF16)
+
+
+def forward(sc, ks, sides, block, lay, through):
     queries, keys, values, seg_row, seg_col = block
     length = queries.shape[0]
     per = lay.heads_shard
-    at = lay.at_z + k
+    count = len(ks)
 
     def shard_of(i, sc):
-        return 2 * sc[at] + jnp.where(i == 0, 1 - sc[0], sc[0])
+        k = lax.rem(ks[0] + lax.rem(i, count), lay.z)
+        if len(sides) == 2:
+            own = i >= count
+        else:
+            own = sides[0] == 1
+        return 2 * sc[lay.at_z + k] + jnp.where(own, sc[0], 1 - sc[0])
 
     def kv_of(i, sc):
         return (0, (shard_of(i, sc) * per) // REPEAT)
 
-    out = ((per * DH, length), BF16, (per * DH, length), first)
+    rows = per * DH
+    steps = count * len(sides)
     return call(
         functools.partial(forward_body, per),
         sc,
-        (2,),
+        (steps,),
         [
-            (queries, (length, per * DH), lambda i, sc: (0, shard_of(i, sc))),
+            (queries, (length, rows), lambda i, sc: (0, shard_of(i, sc))),
             (keys, (length, DH), kv_of),
             (values, (length, DH), kv_of),
             (seg_row, (1, length), first),
             (seg_col, (length, 1), first),
         ],
-        [out, out],
+        [((steps * rows, length), BF16, (rows, length), lambda i, sc: (i, 0))],
         scratch=[pltpu.VMEM((length, length), F32)],
         through=through,
     )
@@ -199,7 +216,7 @@
         functools.partial(product_body, count, lay.at_bit(0), lay.at_bit(lay.bits - 1)),
         sc,
         (4,),
-        [(x, (rows, length), first) for x in (*own, *other)]
+        [(x, (rows, length), lambda n, sc, at=at: (at, 0)) for x, at in (*own, *other)]
         + [(u, (length, tile), lambda n, sc: (0, n)) for u in (up0, up1)],
         [left, left, right, right] * count,
         scratch=[pltpu.VMEM((count * rows, tile), BF16)],
@@ -289,7 +306,7 @@
 
 def grad_context(sc, up0, up1, weights, lay, through):
     length, width = up0.shape
-    rows = lay.rows
+    rows = weights[0].shape[0]
     tile = width // 4
     at = lay.at_piece
     if len(weights) == 1:
@@ -344,7 +361,7 @@
     gv_ref[...] = av_ref[...].astype(BF16)
 
 
-def backward(sc, k, block, own, other, before, lay, through):
+def backward(sc, k, block, own, other, column, before, lay, through):
     queries, keys, values, seg_row, seg_col = block
     length = queries.shape[0]
     per = lay.heads_shard
@@ -366,8 +383,8 @@
             (values, *one),
             (seg_row, (1, length), first),
             (seg_col, (length, 1), first),
-            (own, (length, lay.rows), first),
-            (other, (length, lay.rows), first),
+            (own, (length, lay.rows), lambda i, sc: (0, column)),
+            (other, (length, lay.rows), lambda i, sc: (0, column)),
         ],
         [(queries.shape, BF16, *heads), (keys.shape, BF16, *one), (values.shape, BF16, *one)],
         scratch=[
@@ -446,6 +463,10 @@
     def sibling(self, x):
         return lax.ppermute(x, "shard", [(s, s ^ 1) for s in range(self.shards)])
 
+    def gather_z(self, x):
+        groups = [list(range(core, self.shards, 2)) for core in range(2)]
+        return lax.all_gather(x, "shard", axis_index_groups=groups, axis=0, tiled=True)
+
     def onward(self, x):
         perm = []
         for p in range(self.z):
@@ -466,131 +487,140 @@
     orders = [list(range(lay.bits)), list(range(lay.bits))[::-1]]
     block = (queries, keys, values, segments, segments.reshape(length, 1))
 
-    token = jnp.zeros((8, 128), F32)
-    arrived = [{}, {}]
-    crossed = [{}, {}]
-    context_own, context_other = {}, {}
+    box = {"token": jnp.zeros((8, 128), F32)}
     terms = {}
     ring = {}
     final = []
     grads = ()
-    gc_own, gc_other = {}, {}
-
-    def run(function, *args, relays=(), **more):
-        nonlocal token
-        held = [arrived[side][k] for side, k in relays]
-        outs, handed = function(*args, through=[token, *held], **more)
-        token = handed[0]
-        for (side, k), x in zip(relays, handed[1:]):
-            arrived[side][k] = x
-            if k + 1 < lay.z:
-                arrived[side][k + 1] = lay.onward(x)
-            crossed[side][k] = lay.across(x, orders[side][0])
+
+    def run(function, *args, held=(), **more):
+        names = ["token", *held]
+        outs, handed = function(*args, through=[box[n] for n in names], **more)
+        box.update(zip(names, handed))
         return outs
 
-    def do_forward(k, relays=()):
-        send, context_own[k] = run(forward, sc, k, block, lay, relays=relays)
-        context_other[k] = lay.sibling(send)
-
-    def do_product(ks, relays=()):
-        outs = run(
-            product,
-            sc,
-            [context_own[k] for k in ks],
-            [context_other[k] for k in ks],
-            upstream,
-            upstream_other,
-            lay,
-            relays=relays,
-        )
-        for n, k in enumerate(ks):
-            send_l, keep_l, send_r, keep_r = outs[4 * n : 4 * n + 4]
-            terms[k] = [
-                [keep_l, lay.across(send_l, orders[0][0])],
-                [keep_r, lay.across(send_r, orders[1][0])],
-            ]
-
-    def do_halve(k, relays=()):
-        sends = run(combine, sc, terms[k], None, True, False, lay, relays=relays)
-        stage = len(terms[k][0]) - 1
+    def do_product(k, held=()):
+        own, other = contexts[k]
+        outs = run(product, sc, [own], [other], upstream, upstream_other, lay, held=held)
+        box["send", k, 0], keep_l, box["send", k, 1], keep_r = outs
+        terms[k] = [[keep_l], [keep_r]]
+
+    def send(k):
         for side in range(2):
-            terms[k][side].append(lay.across(sends[side], orders[side][stage]))
-
-    def do_sum(k, relays=()):
-        outs = run(combine, sc, terms[k], ring.get(k), False, k > 0, lay, relays=relays)
+            stage = len(terms[k][side]) - 1
+            got = lay.across(box["send", k, side], orders[side][stage])
+            terms[k][side].append(got)
+
+    def do_halve(k, held=()):
+        for stage in range(1, lay.bits):
+            outs = run(combine, sc, terms[k], None, True, False, lay, held=held)
+            box["send", k, 0], box["send", k, 1] = outs
+            held = ()
+            if stage < lay.bits - 1:
+                send(k)
+
+    def do_sum(k, held=()):
+        outs = run(combine, sc, terms[k], ring.get(k), False, k > 0, lay, held=held)
         if k:
             ring[(k + 1) % lay.z] = lay.onward(outs[0])
         else:
             final.extend(outs)
 
-    def do_grad_context(k, relays=()):
-        weights = [out_weight]
-        if k:
-            weights = [arrived[0][k], crossed[0][k], arrived[1][k], crossed[1][k]]
-        gc_own[k], send = run(
-            grad_context, sc, upstream, upstream_other, weights, lay, relays=relays
-        )
-        gc_other[k] = lay.sibling(send)
-
-    def do_backward(k, relays=()):
+    def sends(k):
+        return [("send", k, 0), ("send", k, 1)]
+
+    def do_backward(k, gc, column, held=()):
         nonlocal grads
-        grads = run(
-            backward, sc, k, block, gc_own[k], gc_other[k], grads, lay, relays=relays
-        )
+        grads = run(backward, sc, k, block, *gc, column, grads, lay, held=held)
 
     upstream_other = lay.sibling(upstream)
-    for side, x in enumerate(run(cut, sc, out_weight, lay)):
-        arrived[side][1] = lay.onward(x)
-
-    early, rest = list(range(1, lay.z)), list(range(3, lay.z))
-    halvings = range(lay.bits - 1)
-    do_forward(1)
-    do_forward(2)
-    do_product([1])
-    for k in rest:
-        do_forward(k)
-    do_forward(0, relays=[(0, 1)])
-    do_product(early[1:])
+    gathered = [lay.gather_z(x) for x in run(cut, sc, out_weight, lay)]
+
+    late = [*range(2, lay.z), 0]
+    contexts = {}
+    (both_sides,) = run(forward, sc, [1], [0, 1], block, lay)
+    rows = lay.rows
+    contexts[1] = (both_sides, 1), (lay.sibling(both_sides[:rows]), 0)
+    (away,) = run(forward, sc, late, [0], block, lay)
+    away = lay.sibling(away)
+    do_product(1)
+    send(1)
+    (stay,) = run(forward, sc, late, [1], block, lay)
+    for n, k in enumerate(late):
+        contexts[k] = (stay, n), (away, n)
+    do_product(2)
+    send(2)
     do_halve(1)
-    do_product([0], relays=[(1, 1)])
-    do_grad_context(0)
-    do_backward(0, relays=[(0, 2)])
-    do_halve(2)
-    for k in rest:
-        do_halve(k, relays=[(1, 2)] if k == 3 else [(0, k - 1), (1, k - 1)])
-    do_grad_context(1)
-    do_backward(1)
-    for n in list(halvings)[1:]:
-        do_halve(1)
-    do_sum(1)
+    send(1)
+    own, away = run(grad_context, sc, upstream, upstream_other, [out_weight], lay)
+    gc = own, lay.sibling(away)
+    do_product(3)
+    do_halve(2, held=sends(3))
+    send(3)
+    do_backward(0, gc, 0)
+    do_sum(1, held=sends(2))
+    send(2)
+    do_product(0)
+    for k in range(4, lay.z):
+        do_product(k)
+        send(k)
+    for k in range(3, lay.z):
+        do_halve(k)
+        send(k)
+    do_sum(2)
+    mine = [run(pick, sc, whole, lay)[0] for whole in gathered]
+    weights = [mine[0], lay.across(mine[0], orders[0][0]), mine[1], lay.across(mine[1], orders[1][0])]
+    for k in range(3, lay.z):
+        do_sum(k, held=sends(0) if k == lay.z - 1 else ())
+    send(0)
+    own, away = run(grad_context, sc, upstream, upstream_other, weights, lay)
+    gc = own, lay.sibling(away)
     do_halve(0)
-    for n in list(halvings)[1:]:
-        do_halve(2)
-    last = lay.z - 1
-    do_sum(2, relays=[(0, last), (1, last)])
-    do_grad_context(2)
-    do_backward(2)
-    for n in list(halvings)[1:]:
-        for k in [*rest, 0]:
-            do_halve(k)
-    for k in rest:
-        do_sum(k)
+    send(0)
+    for k in range(1, lay.z - 2):
+        do_backward(k, gc, k - 1)
     do_sum(0)
+
     have = [[(final[side], side, (False,) * lay.bits)] for side in range(2)]
+
+    def spread(n, side, piece):
+        x, _, flips = piece
+        flips = flips[:n] + (True,) + flips[n + 1 :]
+        return lay.across(x, orders[side][n]), side, flips
+
+    moments = first_moment, second_moment, tokens, lay
+    near, far = [], []
     for n in range(lay.bits - 1, -1, -1):
         for side in range(2):
-            have[side] += [
-                (lay.across(x, orders[side][n]), side, flips[:n] + (True,) + flips[n + 1 :])
-                for x, _, flips in have[side]
-            ]
-    for k in rest:
-        do_grad_context(k)
-        do_backward(k)
-    near = [p for side in range(2) for p in have[side][:-1]]
-    far = [have[side][-1] for side in range(2)]
-    adam_step = run(adam, sc, near, first_moment, second_moment, tokens, lay, before=())
-    adam_step = run(adam, sc, far, first_moment, second_moment, tokens, lay, before=adam_step)
-    return (*grads, *adam_step)
+            have[side].append(spread(n, side, have[side][0]))
+    do_backward(lay.z - 2, gc, lay.z - 3)
+    for side in range(2):
+        box["got", side] = have[side][1][0]
+    step = run(
+        adam,
+        sc,
+        [have[0][0], have[1][0]],
+        *moments,
+        before=(),
+        held=[("got", 0), ("got", 1)],
+    )
+    for side in range(2):
+        have[side][1] = (box["got", side], *have[side][1][1:])
+        pieces = [have[side][1]]
+        done = {p[2] for p in have[side]}
+        near += have[side][1:]
+        for n in range(lay.bits - 2, -1, -1):
+            base = [have[side][m] for m in range(1, lay.bits) if m <= lay.bits - 1 - n]
+            base += [p for s, p in far if s == side]
+            for p in base:
+                flips = p[2][:n] + (True,) + p[2][n + 1 :]
+                if flips not in done:
+                    done.add(flips)
+                    far.append((side, spread(n, side, p)))
+    do_backward(lay.z - 1, gc, lay.z - 2)
+    step = run(adam, sc, near, *moments, before=step)
+    step = run(adam, sc, [p for _, p in far], *moments, before=step)
+    return (*grads, *step)
 
 
 def solution(mesh):

time: 263 us -> 286 us (1.087)
  Pallas kernels: 111 us -> 156 us
  starting transfers between devices: 52.4 us -> 29.9 us
  between operations: 6.16 us -> 19.6 us
  waiting for transfers between devices: 71.2 us -> 61 us
    pallas_call x26 -> x27, Pallas kernels: 111 us -> 156 us  [call(): pl.pallas_call(kernel, grid_spec=pltpu.PrefetchScalarGridSpec(num_scalar_...]
    ppermute x9 -> x3, starting transfers between devices: 20.9 us -> 2.25 us  [onward(): return lax.ppermute(x, 'shard', perm)]
    ppermute x9 -> x3, waiting for transfers between devices: 25.2 us -> 14.5 us  [onward(): return lax.ppermute(x, 'shard', perm)]
    unnamed x108 -> x70, local copies, waits for them, and re-layouts: 17.9 us -> 13.2 us
    ppermute x28 -> x24, starting transfers between devices: 29.5 us -> 26.4 us  [across(): lax.ppermute(x, 'replica', [(r, r ^ 1 << b) for r in range(self.replicas)])]
    ppermute x28 -> x24, waiting for transfers between devices: 44.5 us -> 44.1 us  [across(): lax.ppermute(x, 'replica', [(r, r ^ 1 << b) for r in range(self.replicas)])]
  transfers between devices with their start and end apart: 46 -> 34, of which waited for: 13 -> 5; matrix products, arithmetic and copies ran while one was open for 1% -> 1% of each run, Pallas kernels for 41% -> 50%
where the time goes in v3:
time: 286 us; the launch traced here: 285 us
  Pallas kernels  156 us (55%)
  waiting for transfers between devices  61 us (21%)
  starting transfers between devices  29.9 us (10%)
  between operations  19.6 us (7%)
  local copies, waits for them, and re-layouts  17.1 us (6%)
    pallas_call x27, Pallas kernels, call(): pl.pallas_call(kernel, grid_spec=pltpu.PrefetchScalarGridSpec(num_scalar_...  156 us
    ppermute x24, waiting for transfers between devices, across(): lax.ppermute(x, 'replica', [(r, r ^ 1 << b) for r in range(self.replicas)])  44.1 us
    ppermute x24, starting transfers between devices, across(): lax.ppermute(x, 'replica', [(r, r ^ 1 << b) for r in range(self.replicas)])  26.4 us
    ppermute x3, waiting for transfers between devices, onward(): return lax.ppermute(x, 'shard', perm)  14.5 us
    unnamed x70, local copies, waits for them, and re-layouts  13.2 us
  transfers between devices with their start and end apart: 34, of which 5 were waited for; matrix products, arithmetic and copies ran while one was open for 1% of the time, Pallas kernels for 50%

profile of v3, /device:TPU:0, one launch (start us, length us, event | category | flops | bytes accessed | tf_op | source)
XLA Modules:
  0.0 284.6 jit_solution(4966374584790058504)
XLA Ops:
  7.2 1.2 constant_dynamic-slice_fusion
  9.0 3.1 %shard_map.120 = (bf16[256,1152]{1,0:T(8,128)(2,1)}, bf16[256,1152]{1,0:T(8,128)(2,1)}, f32[8,128]{1,0:T(8,128)}) custom-call(s32[11]{0:T(128)} %get-tuple-element.183.sc_ref, bf16[256,4608]{1,0:T(8,128)(2,1)} %refs_2_.17, bf16[256,4608]{1,0:T(8,128)(2,1)} %refs_2_.17, f32[8,128]{1,0:T(8,128)} %broadcast_in_dim.3.refs_2_), custom_call_target="tpu_custom_call", output_to_operand_aliasing={{2}: (3, {})} | custom-call | flops 1 | bytes 1 | tf_op jit(solution)/shard_map/pallas_call | solution.py:40
  12.9 0.8 copy.65.refs_4_
  13.8 5.4 %shard_map.121 = (bf16[512,512]{1,0:T(8,128)(2,1)}, f32[8,128]{1,0:T(8,128)}) custom-call(s32[11]{0:T(128)} %get-tuple-element.183.sc_ref, bf16[512,2048]{1,0:T(8,128)(2,1)} %refs_0_.23, bf16[512,1024]{1,0:T(8,128)(2,1)} %refs_1_.19, bf16[512,1024]{1,0:T(8,128)(2,1)} %refs_2_.23, s32[1,512]{1,0:T(1,128)} %refs_3_.13, ...), custom_call_target="tpu_custom_call", output_to_operand_aliasing={{1}: (6, {})} | custom-call | flops 1 | bytes 1 | tf_op jit(solution)/shard_map/pallas_call | solution.py:40
  19.2 7.0 %shard_map.122 = (bf16[768,512]{1,0:T(8,128)(2,1)}, f32[8,128]{1,0:T(8,128)}) custom-call(s32[11]{0:T(128)} %get-tuple-element.183.sc_ref, bf16[512,2048]{1,0:T(8,128)(2,1)} %refs_0_.23, bf16[512,1024]{1,0:T(8,128)(2,1)} %refs_1_.19, bf16[512,1024]{1,0:T(8,128)(2,1)} %refs_2_.23, s32[1,512]{1,0:T(1,128)} %refs_3_.13, ...), custom_call_target="tpu_custom_call", output_to_operand_aliasing={{1}: (6, {})} | custom-call | flops 1 | bytes 1 | tf_op jit(solution)/shard_map/pallas_call | solution.py:40
  26.8 2.2 collective-permute-done.1.refs_1_
  29.0 0.7 copy-done.29
  29.7 8.1 %shard_map.123 = (bf16[128,2304]{1,0:T(8,128)(2,1)}, bf16[128,2304]{1,0:T(8,128)(2,1)}, bf16[128,2304]{1,0:T(8,128)(2,1)}, bf16[128,2304]{1,0:T(8,128)(2,1)}, f32[8,128]{1,0:T(8,128)}) custom-call(s32[11]{0:T(128)} %get-tuple-element.183.sc_ref, bf16[512,512]{1,0:T(8,128)(2,1)} %get-tuple-element.95.refs_0_, ...), custom_call_target="tpu_custom_call", output_to_operand_aliasing={{4}: (5, {})} | custom-call | flops 1 | bytes 1 | tf_op jit(solution)/shard_map/pallas_call | solution.py:40
  37.8 2.9 %collective-permute-start.4 = (bf16[128,2304]{1,0:T(8,128)(2,1)}, bf16[128,2304]{1,0:T(8,128)(2,1)S(1)}, u32[]{:S(2)}, u32[]{:S(2)}) collective-permute-start(bf16[128,2304]{1,0:T(8,128)(2,1)} %get-tuple-element.105), channel_id=1, source_target_pairs={{0,8},{8,0},{16,24},{24,16},{1,9},{9,1},{17,25},{25,17},{2,10},{10... | collective-permute-start | bytes 1769480 | tf_op jit(solution)/shard_map/ppermute | solution.py:478
  40.7 1.5 collective-permute-start.5
  42.2 6.9 %shard_map.124 = (bf16[768,512]{1,0:T(8,128)(2,1)}, f32[8,128]{1,0:T(8,128)}) custom-call(s32[11]{0:T(128)} %get-tuple-element.183.sc_ref, bf16[512,2048]{1,0:T(8,128)(2,1)} %refs_0_.23, bf16[512,1024]{1,0:T(8,128)(2,1)} %refs_1_.19, bf16[512,1024]{1,0:T(8,128)(2,1)} %refs_2_.23, s32[1,512]{1,0:T(1,128)} %refs_3_.13, ...), custom_call_target="tpu_custom_call", output_to_operand_aliasing={{1}: (6, {})} | custom-call | flops 1 | bytes 1 | tf_op jit(solution)/shard_map/pallas_call | solution.py:40
  49.2 0.9 copy-done
  50.0 8.1 %shard_map.125 = (bf16[128,2304]{1,0:T(8,128)(2,1)}, bf16[128,2304]{1,0:T(8,128)(2,1)}, bf16[128,2304]{1,0:T(8,128)(2,1)}, bf16[128,2304]{1,0:T(8,128)(2,1)}, f32[8,128]{1,0:T(8,128)}) custom-call(s32[11]{0:T(128)} %get-tuple-element.183.sc_ref, bf16[768,512]{1,0:T(8,128)(2,1)} %get-tuple-element.99.refs_0_, ...), custom_call_target="tpu_custom_call", output_to_operand_aliasing={{4}: (5, {})} | custom-call | flops 1 | bytes 1 | tf_op jit(solution)/shard_map/pallas_call | solution.py:40
  58.8 0.8 copy-done.11
  59.8 2.8 shard_map.126
  62.6 2.0 collective-permute-start.6
  64.6 1.5 collective-permute-start.7
  66.1 8.3 %shard_map.127 = (bf16[512,256]{1,0:T(8,128)(2,1)}, bf16[512,256]{1,0:T(8,128)(2,1)}, f32[8,128]{1,0:T(8,128)}) custom-call(s32[11]{0:T(128)} %get-tuple-element.183.sc_ref, bf16[512,4608]{1,0:T(8,128)(2,1)} %refs_0_.19, bf16[512,4608]{1,0:T(8,128)(2,1)} %collective-permute-done.refs_3_.refs_1_, ...), custom_call_target="tpu_custom_call", output_to_operand_aliasing={{2}: (4, {})} | custom-call | flops 1 | bytes 1 | tf_op jit(solution)/shard_map/pallas_call | solution.py:40
  74.3 8.1 %shard_map.128 = (bf16[128,2304]{1,0:T(8,128)(2,1)}, bf16[128,2304]{1,0:T(8,128)(2,1)}, bf16[128,2304]{1,0:T(8,128)(2,1)}, bf16[128,2304]{1,0:T(8,128)(2,1)}, f32[8,128]{1,0:T(8,128)}) custom-call(s32[11]{0:T(128)} %get-tuple-element.183.sc_ref, bf16[768,512]{1,0:T(8,128)(2,1)} %get-tuple-element.99.refs_0_, ...), custom_call_target="tpu_custom_call", output_to_operand_aliasing={{4}: (5, {})} | custom-call | flops 1 | bytes 1 | tf_op jit(solution)/shard_map/pallas_call | solution.py:40
  82.5 0.8 copy-done.6
  83.5 2.8 shard_map.129
  86.3 0.8 collective-permute-start.13
  87.2 0.7 copy-done.28
  87.9 7.5 %shard_map.130 = (bf16[512,2048]{1,0:T(8,128)(2,1)}, bf16[512,1024]{1,0:T(8,128)(2,1)}, bf16[512,1024]{1,0:T(8,128)(2,1)}, f32[8,128]{1,0:T(8,128)}) custom-call(s32[11]{0:T(128)} %get-tuple-element.183.sc_ref, bf16[512,2048]{1,0:T(8,128)(2,1)} %refs_0_.23, bf16[512,1024]{1,0:T(8,128)(2,1)} %refs_1_.19, ...), custom_call_target="tpu_custom_call", output_to_operand_aliasing={{3}: (8, {})} | custom-call | flops 1 | bytes 1 | tf_op jit(solution)/shard_map/pallas_call | solution.py:40
  95.4 0.7 copy-done.16
  96.2 3.1 %shard_map.131 = (bf16[64,4608]{1,0:T(8,128)(2,1)}, f32[8,128]{1,0:T(8,128)}, bf16[64,2304]{1,0:T(8,128)(2,1)}, bf16[64,2304]{1,0:T(8,128)(2,1)}) custom-call(s32[11]{0:T(128)} %get-tuple-element.183.sc_ref, bf16[128,2304]{1,0:T(8,128)(2,1)} %get-tuple-element.104.refs_0_, ...), custom_call_target="tpu_custom_call", output_to_operand_aliasing={{1}: (7, {}), {2}: (8, {}), {3}: (9, {})} | custom-call | flops 1 | bytes 1 | tf_op jit(solution)/shard_map/pallas_call | solution.py:40
  99.3 2.0 collective-permute-start.11
  101.3 1.6 collective-permute-start.10
  102.9 1.2 collective-permute-start.12
  104.1 8.2 %shard_map.132 = (bf16[128,2304]{1,0:T(8,128)(2,1)}, bf16[128,2304]{1,0:T(8,128)(2,1)}, bf16[128,2304]{1,0:T(8,128)(2,1)}, bf16[128,2304]{1,0:T(8,128)(2,1)}, f32[8,128]{1,0:T(8,128)}) custom-call(s32[11]{0:T(128)} %get-tuple-element.183.sc_ref, bf16[768,512]{1,0:T(8,128)(2,1)} %get-tuple-element.99.refs_0_, ...), custom_call_target="tpu_custom_call", output_to_operand_aliasing={{4}: (5, {})} | custom-call | flops 1 | bytes 1 | tf_op jit(solution)/shard_map/pallas_call | solution.py:40
  112.3 0.8 copy-done.5
  113.3 2.8 shard_map.133
  116.1 12.5 %collective-permute-done.11.refs_3_.refs_7_ = bf16[64,4608]{1,0:T(8,128)(2,1)S(1)} collective-permute-done((bf16[64,4608]{1,0:T(8,128)(2,1)}, bf16[64,4608]{1,0:T(8,128)(2,1)S(1)}, u32[]{:S(2)}, u32[]{:S(2)}) %collective-permute-start.11) | collective-permute-done | bytes 589856 | tf_op jit(solution)/shard_map/ppermute | solution.py:475
  128.6 0.8 copy-done.3
  129.4 3.3 %shard_map.134 = (bf16[64,4608]{1,0:T(8,128)(2,1)}, f32[8,128]{1,0:T(8,128)}) custom-call(s32[11]{0:T(128)} %get-tuple-element.183.sc_ref, bf16[128,2304]{1,0:T(8,128)(2,1)} %get-tuple-element.102.refs_0_, bf16[128,2304]{1,0:T(8,128)(2,1)} %copy-done.6, bf16[64,2304]{1,0:T(8,128)(2,1)} %copy-done.18, ...), custom_call_target="tpu_custom_call", output_to_operand_aliasing={{1}: (9, {})} | custom-call | flops 1 | bytes 1 | tf_op jit(solution)/shard_map/pallas_call | solution.py:40
  132.8 4.3 %shard_map.135 = (bf16[768,1152]{1,0:T(8,128)(2,1)}, f32[8,128]{1,0:T(8,128)}) custom-call(s32[11]{0:T(128)} %get-tuple-element.183.sc_ref, bf16[1024,1152]{1,0:T(8,128)(2,1)} %all-gather.3.cloned.1.call-done.refs_0_, f32[8,128]{1,0:T(8,128)} %get-tuple-element.134.refs_1_), custom_call_target="tpu_custom_call", output_to_operand_aliasing={{1}: (2, {})} | custom-call | flops 1 | bytes 1 | tf_op jit(solution)/shard_map/pallas_call | solution.py:40
  137.1 4.2 %shard_map.136 = (bf16[768,1152]{1,0:T(8,128)(2,1)}, f32[8,128]{1,0:T(8,128)}) custom-call(s32[11]{0:T(128)} %get-tuple-element.183.sc_ref, bf16[1024,1152]{1,0:T(8,128)(2,1)} %all-gather.5.cloned.1.call-done.refs_0_, f32[8,128]{1,0:T(8,128)} %get-tuple-element.137.refs_1_), custom_call_target="tpu_custom_call", output_to_operand_aliasing={{1}: (2, {})} | custom-call | flops 1 | bytes 1 | tf_op jit(solution)/shard_map/pallas_call | solution.py:40
  141.3 1.5 collective-permute-start.16
  142.7 1.5 collective-permute-start.15
  145.4 42.9 %collective-permute-done.17.refs_2_ = bf16[64,2304]{1,0:T(8,128)(2,1)S(1)} collective-permute-done((bf16[64,2304]{1,0:T(8,128)(2,1)S(1)}, bf16[64,2304]{1,0:T(8,128)(2,1)S(1)}, u32[]{:S(2)}, u32[]{:S(2)}) %collective-permute-start.17) | collective-permute-done | bytes 294944 | tf_op jit(solution)/shard_map/ppermute | solution.py:478
  188.3 1.2 collective-permute-done.19.refs_6_
  189.5 0.7 copy-done.23
  190.4 3.4 %shard_map.137 = (bf16[64,4608]{1,0:T(8,128)(2,1)}, f32[8,128]{1,0:T(8,128)}, bf16[128,2304]{1,0:T(8,128)(2,1)}, bf16[128,2304]{1,0:T(8,128)(2,1)}) custom-call(s32[11]{0:T(128)} %get-tuple-element.183.sc_ref, bf16[128,2304]{1,0:T(8,128)(2,1)} %get-tuple-element.127.refs_0_, ...), custom_call_target="tpu_custom_call", output_to_operand_aliasing={{1}: (9, {}), {2}: (10, {}), {3}: (11, {})} | custom-call | flops 1 | bytes 1 | tf_op jit(solution)/shard_map/pallas_call | solution.py:40
  193.8 1.4 collective-permute-start.21
  195.8 16.0 %shard_map.138 = (bf16[512,768]{1,0:T(8,128)(2,1)}, bf16[512,768]{1,0:T(8,128)(2,1)}, f32[8,128]{1,0:T(8,128)}) custom-call(s32[11]{0:T(128)} %get-tuple-element.183.sc_ref, bf16[512,4608]{1,0:T(8,128)(2,1)} %refs_0_.19, bf16[512,4608]{1,0:T(8,128)(2,1)} %collective-permute-done.refs_3_.refs_1_, ...), custom_call_target="tpu_custom_call", output_to_operand_aliasing={{2}: (7, {})} | custom-call | flops 1 | bytes 1 | tf_op jit(solution)/shard_map/pallas_call | solution.py:40
  212.1 0.8 copy-done.9
  213.1 2.8 shard_map.139
  215.9 1.5 collective-permute-start.23
  217.9 0.9 copy-done.1
  218.8 7.5 %shard_map.140 = (bf16[512,2048]{1,0:T(8,128)(2,1)}, bf16[512,1024]{1,0:T(8,128)(2,1)}, bf16[512,1024]{1,0:T(8,128)(2,1)}, f32[8,128]{1,0:T(8,128)}) custom-call(s32[11]{0:T(128)} %get-tuple-element.183.sc_ref, bf16[512,2048]{1,0:T(8,128)(2,1)} %refs_0_.23, ...), custom_call_target="tpu_custom_call", output_to_operand_aliasing={{0}: (8, {}), {1}: (9, {}), {2}: (10, {}), {3}: (11, {})} | custom-call | flops 1 | bytes 1 | tf_op jit(solution)/shard_map/pallas_call | solution.py:40
  226.4 2.1 collective-permute-done.24.refs_3_.refs_7_
  228.4 0.8 copy-done.2
  229.4 3.2 %shard_map.141 = (bf16[64,2304]{1,0:T(8,128)(2,1)}, bf16[64,2304]{1,0:T(8,128)(2,1)}, f32[8,128]{1,0:T(8,128)}) custom-call(s32[11]{0:T(128)} %get-tuple-element.183.sc_ref, bf16[128,2304]{1,0:T(8,128)(2,1)} %get-tuple-element.151.refs_0_, bf16[128,2304]{1,0:T(8,128)(2,1)} %copy-done.9, ...), custom_call_target="tpu_custom_call", output_to_operand_aliasing={{2}: (9, {})} | custom-call | flops 1 | bytes 1 | tf_op jit(solution)/shard_map/pallas_call | solution.py:40
  232.7 1.5 collective-permute-start.26
  238.6 1.4 collective-permute-start.30
  240.6 7.5 %shard_map.142 = (bf16[512,2048]{1,0:T(8,128)(2,1)}, bf16[512,1024]{1,0:T(8,128)(2,1)}, bf16[512,1024]{1,0:T(8,128)(2,1)}, f32[8,128]{1,0:T(8,128)}) custom-call(s32[11]{0:T(128)} %get-tuple-element.183.sc_ref, bf16[512,2048]{1,0:T(8,128)(2,1)} %refs_0_.23, ...), custom_call_target="tpu_custom_call", output_to_operand_aliasing={{0}: (8, {}), {1}: (9, {}), {2}: (10, {}), {3}: (11, {})} | custom-call | flops 1 | bytes 1 | tf_op jit(solution)/shard_map/pallas_call | solution.py:40
  248.2 0.7 copy-done.14
  249.0 3.8 %shard_map.143 = (f32[256,4608]{1,0:T(8,128)}, f32[8,128]{1,0:T(8,128)}, bf16[64,2304]{1,0:T(8,128)(2,1)}, bf16[64,2304]{1,0:T(8,128)(2,1)}) custom-call(s32[4]{0:T(128)} %pad_add_fusion.1.sc_ref, f32[256,4608]{1,0:T(8,128)} %refs_0_.25, f32[256,4608]{1,0:T(8,128)} %refs_1_.21, ...), custom_call_target="tpu_custom_call", output_to_operand_aliasing={{1}: (5, {}), {2}: (6, {}), {3}: (7, {})} | custom-call | flops 1 | bytes 1 | tf_op jit(solution)/shard_map/pallas_call | solution.py:40
  253.4 1.5 collective-permute-start.29
  257.4 0.7 stack.43.sc_ref
  258.8 7.5 %shard_map.144 = (bf16[512,2048]{1,0:T(8,128)(2,1)}, bf16[512,1024]{1,0:T(8,128)(2,1)}, bf16[512,1024]{1,0:T(8,128)(2,1)}, f32[8,128]{1,0:T(8,128)}) custom-call(s32[11]{0:T(128)} %get-tuple-element.183.sc_ref, bf16[512,2048]{1,0:T(8,128)(2,1)} %refs_0_.23, ...), custom_call_target="tpu_custom_call", output_to_operand_aliasing={{0}: (8, {}), {1}: (9, {}), {2}: (10, {}), {3}: (11, {})} | custom-call | flops 1 | bytes 1 | tf_op jit(solution)/shard_map/pallas_call | solution.py:40
  267.1 6.0 %shard_map.145 = (f32[256,4608]{1,0:T(8,128)}, f32[8,128]{1,0:T(8,128)}) custom-call(s32[8]{0:T(128)} %stack.43.sc_ref, f32[256,4608]{1,0:T(8,128)} %refs_0_.25, f32[256,4608]{1,0:T(8,128)} %refs_1_.21, bf16[64,2304]{1,0:T(8,128)(2,1)} %get-tuple-element.175.refs_2_, bf16[64,2304]{1,0:T(8,128)(2,1)} %copy-done.24, ...), custom_call_target="tpu_custom_call", output_to_operand_aliasing={{0}: (7, {}), {1}: (8, {})} | custom-call | flops 1 | bytes 1 | tf_op jit(solution)/shard_map/pallas_call | solution.py:40
  273.2 0.7 copy-done.26
  274.0 3.8 %shard_map.146 = (f32[256,4608]{1,0:T(8,128)}, f32[8,128]{1,0:T(8,128)}) custom-call(s32[4]{0:T(128)} %pad_add_fusion.sc_ref, f32[256,4608]{1,0:T(8,128)} %refs_0_.25, f32[256,4608]{1,0:T(8,128)} %refs_1_.21, bf16[64,2304]{1,0:T(8,128)(2,1)} %copy-done.26, bf16[64,2304]{1,0:T(8,128)(2,1)} %copy-done.27, ...), custom_call_target="tpu_custom_call", output_to_operand_aliasing={{0}: (5, {}), {1}: (6, {})} | custom-call | flops 1 | bytes 1 | tf_op jit(solution)/shard_map/pallas_call | solution.py:40
  (111 shorter events, 11.4 us)
Async XLA Ops:
  7.2 125.6 %all-gather.3.cloned.1.call-start = ((), (), s32[]{:S(2)}) async-start(), calls=%async_computation | async-start | bytes 2949120 | tf_op jit(solution)/shard_map/all_gather | solution.py:468
  9.0 3.9 %copy-start.30 = (s32[1,512]{1,0:T(1,128)S(1)}, s32[1,512]{1,0:T(1,128)}, u32[]{:S(2)}) copy-start(s32[1,512]{1,0:T(1,128)} %refs_3_.13) | copy-start | bytes 6148
  12.2 124.9 %all-gather.5.cloned.1.call-start = ((), (), s32[]{:S(2)}) async-start(), calls=%async_computation.1 | async-start | bytes 2949120 | tf_op jit(solution)/shard_map/all_gather | solution.py:468
  12.2 16.8 %collective-permute-start = (bf16[512,4608]{1,0:T(8,128)(2,1)}, bf16[512,4608]{1,0:T(8,128)(2,1)}, u32[]{:S(2)}, u32[]{:S(2)}) collective-permute-start(bf16[512,4608]{1,0:T(8,128)(2,1)} %refs_0_.19), channel_id=1, source_target_pairs={{0,1},{1,0},{2,3},{3,2},{4,5},{5,4},{6,7},{7,6},{8,9},{9,8},{10,11... | collective-permute-start | bytes 14155784 | tf_op jit(solution)/shard_map/ppermute | solution.py:464
  19.2 7.5 %copy-start.13 = (bf16[512,512]{1,0:T(8,128)(2,1)S(1)}, bf16[512,512]{1,0:T(8,128)(2,1)}, u32[]{:S(2)}) copy-start(bf16[512,512]{1,0:T(8,128)(2,1)} %get-tuple-element.95.refs_0_) | copy-start | bytes 1572868
  26.2 22.9 %collective-permute-start.2 = (bf16[768,512]{1,0:T(8,128)(2,1)}, bf16[768,512]{1,0:T(8,128)(2,1)S(1)}, u32[]{:S(2)}, u32[]{:S(2)}) collective-permute-start(bf16[768,512]{1,0:T(8,128)(2,1)} %get-tuple-element.100), channel_id=1, source_target_pairs={{0,1},{1,0},{2,3},{3,2},{4,5},{5,4},{6,7},{7,6},{8,9},{9,8},{10,11... | collective-permute-start | bytes 2359304 | tf_op jit(solution)/shard_map/ppermute | solution.py:464
  26.7 2.3 collective-permute-start.1
  37.8 21.0 %collective-permute-start.4 = (bf16[128,2304]{1,0:T(8,128)(2,1)}, bf16[128,2304]{1,0:T(8,128)(2,1)S(1)}, u32[]{:S(2)}, u32[]{:S(2)}) collective-permute-start(bf16[128,2304]{1,0:T(8,128)(2,1)} %get-tuple-element.105), channel_id=1, source_target_pairs={{0,8},{8,0},{16,24},{24,16},{1,9},{9,1},{17,25},{25,17},{2,10},{10... | collective-permute-start | bytes 1769480 | tf_op jit(solution)/shard_map/ppermute | solution.py:478
  40.7 18.1 %collective-permute-start.5 = (bf16[128,2304]{1,0:T(8,128)(2,1)}, bf16[128,2304]{1,0:T(8,128)(2,1)S(1)}, u32[]{:S(2)}, u32[]{:S(2)}) collective-permute-start(bf16[128,2304]{1,0:T(8,128)(2,1)} %get-tuple-element.107), channel_id=1, source_target_pairs={{0,16},{8,24},{16,0},{24,8},{1,17},{9,25},{17,1},{25,9},{2,18},{10... | collective-permute-start | bytes 1769480 | tf_op jit(solution)/shard_map/ppermute | solution.py:478
  49.2 0.9 copy-start
  58.2 24.3 %collective-permute-start.3 = (bf16[128,2304]{1,0:T(8,128)(2,1)}, bf16[128,2304]{1,0:T(8,128)(2,1)S(1)}, u32[]{:S(2)}, u32[]{:S(2)}) collective-permute-start(bf16[128,2304]{1,0:T(8,128)(2,1)} %get-tuple-element.103), channel_id=1, source_target_pairs={{0,8},{8,0},{16,24},{24,16},{1,9},{9,1},{17,25},{25,17},{2,10},{10... | collective-permute-start | bytes 1769480 | tf_op jit(solution)/shard_map/ppermute | solution.py:478
  58.7 23.8 %collective-permute-start.9 = (bf16[128,2304]{1,0:T(8,128)(2,1)}, bf16[128,2304]{1,0:T(8,128)(2,1)S(1)}, u32[]{:S(2)}, u32[]{:S(2)}) collective-permute-start(bf16[128,2304]{1,0:T(8,128)(2,1)} %get-tuple-element.115), channel_id=1, source_target_pairs={{0,16},{8,24},{16,0},{24,8},{1,17},{9,25},{17,1},{25,9},{2,18},{10... | collective-permute-start | bytes 1769480 | tf_op jit(solution)/shard_map/ppermute | solution.py:478
  58.8 0.8 copy-start.11
  58.8 1.1 copy-start.12
  62.6 32.8 %collective-permute-start.6 = (bf16[64,2304]{1,0:T(8,128)(2,1)}, bf16[64,2304]{1,0:T(8,128)(2,1)S(1)}, u32[]{:S(2)}, u32[]{:S(2)}) collective-permute-start(bf16[64,2304]{1,0:T(8,128)(2,1)} %get-tuple-element.109), channel_id=1, source_target_pairs={{0,16},{8,24},{16,0},{24,8},{1,17},{9,25},{17,1},{25,9},{2,18},{10... | collective-permute-start | bytes 884744 | tf_op jit(solution)/shard_map/ppermute | solution.py:478
  64.6 30.8 %collective-permute-start.7 = (bf16[64,2304]{1,0:T(8,128)(2,1)}, bf16[64,2304]{1,0:T(8,128)(2,1)S(1)}, u32[]{:S(2)}, u32[]{:S(2)}) collective-permute-start(bf16[64,2304]{1,0:T(8,128)(2,1)} %get-tuple-element.110), channel_id=1, source_target_pairs={{0,8},{8,0},{16,24},{24,16},{1,9},{9,1},{17,25},{25,17},{2,10},{10... | collective-permute-start | bytes 884744 | tf_op jit(solution)/shard_map/ppermute | solution.py:478
  74.3 12.8 %collective-permute-start.8 = (bf16[512,256]{1,0:T(8,128)(2,1)}, bf16[512,256]{1,0:T(8,128)(2,1)S(1)}, u32[]{:S(2)}, u32[]{:S(2)}) collective-permute-start(bf16[512,256]{1,0:T(8,128)(2,1)} %get-tuple-element.113), channel_id=1, source_target_pairs={{0,1},{1,0},{2,3},{3,2},{4,5},{5,4},{6,7},{7,6},{8,9},{9,8},{10,11... | collective-permute-start | bytes 786440 | tf_op jit(solution)/shard_map/ppermute | solution.py:464
  82.5 0.8 copy-start.6
  82.5 1.0 copy-start.8
  86.3 26.0 %collective-permute-start.13 = (bf16[128,2304]{1,0:T(8,128)(2,1)}, bf16[128,2304]{1,0:T(8,128)(2,1)S(1)}, u32[]{:S(2)}, u32[]{:S(2)}) collective-permute-start(bf16[128,2304]{1,0:T(8,128)(2,1)} %get-tuple-element.128), channel_id=1, source_target_pairs={{0,8},{8,0},{16,24},{24,16},{1,9},{9,1},{17,25},{25,17},{2,10},{10... | collective-permute-start | bytes 1769480 | tf_op jit(solution)/shard_map/ppermute | solution.py:478
  87.1 25.2 %collective-permute-start.14 = (bf16[128,2304]{1,0:T(8,128)(2,1)}, bf16[128,2304]{1,0:T(8,128)(2,1)S(1)}, u32[]{:S(2)}, u32[]{:S(2)}) collective-permute-start(bf16[128,2304]{1,0:T(8,128)(2,1)} %get-tuple-element.130), channel_id=1, source_target_pairs={{0,16},{8,24},{16,0},{24,8},{1,17},{9,25},{17,1},{25,9},{2,18},{10... | collective-permute-start | bytes 1769480 | tf_op jit(solution)/shard_map/ppermute | solution.py:478
  95.4 0.8 copy-start.17
  99.3 29.3 %collective-permute-start.11 = (bf16[64,4608]{1,0:T(8,128)(2,1)}, bf16[64,4608]{1,0:T(8,128)(2,1)S(1)}, u32[]{:S(2)}, u32[]{:S(2)}) collective-permute-start(bf16[64,4608]{1,0:T(8,128)(2,1)} %get-tuple-element.125), channel_id=1, source_target_pairs={{0,2},{1,3},{2,6},{3,7},{6,4},{7,5},{4,0},{5,1},{8,10},{9,11},{10,... | collective-permute-start | bytes 1769480 | tf_op jit(solution)/shard_map/ppermute | solution.py:475
  101.3 14.8 %collective-permute-start.10 = (bf16[64,2304]{1,0:T(8,128)(2,1)}, bf16[64,2304]{1,0:T(8,128)(2,1)S(1)}, u32[]{:S(2)}, u32[]{:S(2)}) collective-permute-start(bf16[64,2304]{1,0:T(8,128)(2,1)} %get-tuple-element.124), channel_id=1, source_target_pairs={{0,16},{8,24},{16,0},{24,8},{1,17},{9,25},{17,1},{25,9},{2,18},{10... | collective-permute-start | bytes 884744 | tf_op jit(solution)/shard_map/ppermute | solution.py:478
  102.9 13.2 %collective-permute-start.12 = (bf16[64,2304]{1,0:T(8,128)(2,1)}, bf16[64,2304]{1,0:T(8,128)(2,1)S(1)}, u32[]{:S(2)}, u32[]{:S(2)}) collective-permute-start(bf16[64,2304]{1,0:T(8,128)(2,1)} %get-tuple-element.126), channel_id=1, source_target_pairs={{0,8},{8,0},{16,24},{24,16},{1,9},{9,1},{17,25},{25,17},{2,10},{10... | collective-permute-start | bytes 884744 | tf_op jit(solution)/shard_map/ppermute | solution.py:478
  112.3 0.8 copy-start.5
  112.3 1.0 copy-start.7
  116.1 12.5 %copy-start.18 = (bf16[64,2304]{1,0:T(8,128)(2,1)}, bf16[64,2304]{1,0:T(8,128)(2,1)S(1)}, u32[]{:S(2)}) copy-start(bf16[64,2304]{1,0:T(8,128)(2,1)S(1)} %collective-permute-done.10.refs_2_) | copy-start | bytes 884740
  116.1 12.5 %copy-start.19 = (bf16[64,2304]{1,0:T(8,128)(2,1)}, bf16[64,2304]{1,0:T(8,128)(2,1)S(1)}, u32[]{:S(2)}) copy-start(bf16[64,2304]{1,0:T(8,128)(2,1)S(1)} %collective-permute-done.12.refs_6_) | copy-start | bytes 884740
  128.6 0.8 copy-start.3
  132.8 11.5 %copy-start.32 = (bf16[64,4608]{1,0:T(8,128)(2,1)S(1)}, bf16[64,4608]{1,0:T(8,128)(2,1)}, u32[]{:S(2)}) copy-start(bf16[64,4608]{1,0:T(8,128)(2,1)} %get-tuple-element.140) | copy-start | bytes 1769476
  132.8 11.5 %copy-start.34 = (bf16[64,2304]{1,0:T(8,128)(2,1)S(1)}, bf16[64,2304]{1,0:T(8,128)(2,1)}, u32[]{:S(2)}) copy-start(bf16[64,2304]{1,0:T(8,128)(2,1)} %get-tuple-element.139) | copy-start | bytes 884740
  132.8 12.1 %copy-start.33 = (bf16[64,2304]{1,0:T(8,128)(2,1)S(1)}, bf16[64,2304]{1,0:T(8,128)(2,1)}, u32[]{:S(2)}) copy-start(bf16[64,2304]{1,0:T(8,128)(2,1)} %get-tuple-element.141) | copy-start | bytes 884740
  141.3 54.5 %collective-permute-start.16 = (bf16[768,1152]{1,0:T(8,128)(2,1)}, bf16[768,1152]{1,0:T(8,128)(2,1)}, u32[]{:S(2)}, u32[]{:S(2)}) collective-permute-start(bf16[768,1152]{1,0:T(8,128)(2,1)} %get-tuple-element.138.refs_4_), channel_id=1, source_target_pairs={{0,16},{8,24},{16,0},{24,8},{1,17},{9,25},{17,1},{25,9},{2,18},{10... | collective-permute-start | bytes 5308424 | tf_op jit(solution)/shard_map/ppermute | solution.py:478
  142.7 53.1 %collective-permute-start.15 = (bf16[768,1152]{1,0:T(8,128)(2,1)}, bf16[768,1152]{1,0:T(8,128)(2,1)}, u32[]{:S(2)}, u32[]{:S(2)}) collective-permute-start(bf16[768,1152]{1,0:T(8,128)(2,1)} %get-tuple-element.135.refs_2_), channel_id=1, source_target_pairs={{0,8},{8,0},{16,24},{24,16},{1,9},{9,1},{17,25},{25,17},{2,10},{10... | collective-permute-start | bytes 5308424 | tf_op jit(solution)/shard_map/ppermute | solution.py:478
  144.2 45.2 %collective-permute-start.18 = (bf16[64,4608]{1,0:T(8,128)(2,1)S(1)}, bf16[64,4608]{1,0:T(8,128)(2,1)S(1)}, u32[]{:S(2)}, u32[]{:S(2)}) collective-permute-start(bf16[64,4608]{1,0:T(8,128)(2,1)S(1)} %copy-done.32), channel_id=1, source_target_pairs={{0,2},{1,3},{2,6},{3,7},{6,4},{7,5},{4,0},{5,1},{8,10},{9,11},{10,... | collective-permute-start | bytes 1769480 | tf_op jit(solution)/shard_map/ppermute | solution.py:475
  144.2 44.0 %collective-permute-start.17 = (bf16[64,2304]{1,0:T(8,128)(2,1)S(1)}, bf16[64,2304]{1,0:T(8,128)(2,1)S(1)}, u32[]{:S(2)}, u32[]{:S(2)}) collective-permute-start(bf16[64,2304]{1,0:T(8,128)(2,1)S(1)} %copy-done.34), channel_id=1, source_target_pairs={{0,16},{8,24},{16,0},{24,8},{1,17},{9,25},{17,1},{25,9},{2,18},{10... | collective-permute-start | bytes 884744 | tf_op jit(solution)/shard_map/ppermute | solution.py:478
  144.8 44.6 %collective-permute-start.19 = (bf16[64,2304]{1,0:T(8,128)(2,1)S(1)}, bf16[64,2304]{1,0:T(8,128)(2,1)S(1)}, u32[]{:S(2)}, u32[]{:S(2)}) collective-permute-start(bf16[64,2304]{1,0:T(8,128)(2,1)S(1)} %copy-done.33), channel_id=1, source_target_pairs={{0,8},{8,0},{16,24},{24,16},{1,9},{9,1},{17,25},{25,17},{2,10},{10... | collective-permute-start | bytes 884744 | tf_op jit(solution)/shard_map/ppermute | solution.py:478
  188.3 1.2 copy-start.22
  189.4 0.7 copy-start.23
  189.4 0.9 copy-start.4
  193.8 18.3 %collective-permute-start.21 = (bf16[128,2304]{1,0:T(8,128)(2,1)}, bf16[128,2304]{1,0:T(8,128)(2,1)S(1)}, u32[]{:S(2)}, u32[]{:S(2)}) collective-permute-start(bf16[128,2304]{1,0:T(8,128)(2,1)} %get-tuple-element.152), channel_id=1, source_target_pairs={{0,8},{8,0},{16,24},{24,16},{1,9},{9,1},{17,25},{25,17},{2,10},{10... | collective-permute-start | bytes 1769480 | tf_op jit(solution)/shard_map/ppermute | solution.py:478
  195.2 16.9 %collective-permute-start.22 = (bf16[128,2304]{1,0:T(8,128)(2,1)}, bf16[128,2304]{1,0:T(8,128)(2,1)S(1)}, u32[]{:S(2)}, u32[]{:S(2)}) collective-permute-start(bf16[128,2304]{1,0:T(8,128)(2,1)} %get-tuple-element.154), channel_id=1, source_target_pairs={{0,16},{8,24},{16,0},{24,8},{1,17},{9,25},{17,1},{25,9},{2,18},{10... | collective-permute-start | bytes 1769480 | tf_op jit(solution)/shard_map/ppermute | solution.py:478
  195.8 16.0 %copy-start.31 = (bf16[64,4608]{1,0:T(8,128)(2,1)S(1)}, bf16[64,4608]{1,0:T(8,128)(2,1)}, u32[]{:S(2)}) copy-start(bf16[64,4608]{1,0:T(8,128)(2,1)} %get-tuple-element.161) | copy-start | bytes 1769476
  211.8 6.2 %collective-permute-start.20 = (bf16[512,768]{1,0:T(8,128)(2,1)}, bf16[512,768]{1,0:T(8,128)(2,1)S(1)}, u32[]{:S(2)}, u32[]{:S(2)}) collective-permute-start(bf16[512,768]{1,0:T(8,128)(2,1)} %get-tuple-element.147), channel_id=1, source_target_pairs={{0,1},{1,0},{2,3},{3,2},{4,5},{5,4},{6,7},{7,6},{8,9},{9,8},{10,11... | collective-permute-start | bytes 2359304 | tf_op jit(solution)/shard_map/ppermute | solution.py:464
  211.8 16.6 %collective-permute-start.24 = (bf16[64,4608]{1,0:T(8,128)(2,1)S(1)}, bf16[64,4608]{1,0:T(8,128)(2,1)S(1)}, u32[]{:S(2)}, u32[]{:S(2)}) collective-permute-start(bf16[64,4608]{1,0:T(8,128)(2,1)S(1)} %copy-done.31), channel_id=1, source_target_pairs={{0,2},{1,3},{2,6},{3,7},{6,4},{7,5},{4,0},{5,1},{8,10},{9,11},{10,... | collective-permute-start | bytes 1769480 | tf_op jit(solution)/shard_map/ppermute | solution.py:475
  212.1 0.8 copy-start.9
  212.1 1.0 copy-start.10
  215.9 12.6 %collective-permute-start.23 = (bf16[64,2304]{1,0:T(8,128)(2,1)}, bf16[64,2304]{1,0:T(8,128)(2,1)S(1)}, u32[]{:S(2)}, u32[]{:S(2)}) collective-permute-start(bf16[64,2304]{1,0:T(8,128)(2,1)} %get-tuple-element.160), channel_id=1, source_target_pairs={{0,16},{8,24},{16,0},{24,8},{1,17},{9,25},{17,1},{25,9},{2,18},{10... | collective-permute-start | bytes 884744 | tf_op jit(solution)/shard_map/ppermute | solution.py:478
  217.3 11.1 %collective-permute-start.25 = (bf16[64,2304]{1,0:T(8,128)(2,1)}, bf16[64,2304]{1,0:T(8,128)(2,1)S(1)}, u32[]{:S(2)}, u32[]{:S(2)}) collective-permute-start(bf16[64,2304]{1,0:T(8,128)(2,1)} %get-tuple-element.162), channel_id=1, source_target_pairs={{0,8},{8,0},{16,24},{24,16},{1,9},{9,1},{17,25},{25,17},{2,10},{10... | collective-permute-start | bytes 884744 | tf_op jit(solution)/shard_map/ppermute | solution.py:478
  217.9 0.9 copy-start.1
  228.4 0.9 copy-start.2
  228.4 1.0 copy-start.20
  228.4 1.0 copy-start.21
  232.7 15.5 %collective-permute-start.26 = (bf16[64,2304]{1,0:T(8,128)(2,1)}, bf16[64,2304]{1,0:T(8,128)(2,1)S(1)}, u32[]{:S(2)}, u32[]{:S(2)}) collective-permute-start(bf16[64,2304]{1,0:T(8,128)(2,1)} %get-tuple-element.168.refs_2_), channel_id=1, source_target_pairs={{0,16},{8,24},{16,0},{24,8},{1,17},{9,25},{17,1},{25,9},{2,18},{10... | collective-permute-start | bytes 884744 | tf_op jit(solution)/shard_map/ppermute | solution.py:478
  234.1 14.0 %collective-permute-start.27 = (bf16[64,2304]{1,0:T(8,128)(2,1)}, bf16[64,2304]{1,0:T(8,128)(2,1)S(1)}, u32[]{:S(2)}, u32[]{:S(2)}) collective-permute-start(bf16[64,2304]{1,0:T(8,128)(2,1)} %get-tuple-element.169.refs_3_), channel_id=1, source_target_pairs={{0,8},{8,0},{16,24},{24,16},{1,9},{9,1},{17,25},{25,17},{2,10},{10... | collective-permute-start | bytes 884744 | tf_op jit(solution)/shard_map/ppermute | solution.py:478
  238.6 27.7 %collective-permute-start.30 = (bf16[64,2304]{1,0:T(8,128)(2,1)}, bf16[64,2304]{1,0:T(8,128)(2,1)S(1)}, u32[]{:S(2)}, u32[]{:S(2)}) collective-permute-start(bf16[64,2304]{1,0:T(8,128)(2,1)} %get-tuple-element.168.refs_2_), channel_id=1, source_target_pairs={{0,8},{8,0},{16,24},{24,16},{1,9},{9,1},{17,25},{25,17},{2,10},{10... | collective-permute-start | bytes 884744 | tf_op jit(solution)/shard_map/ppermute | solution.py:478
  240.0 26.3 %collective-permute-start.31 = (bf16[64,2304]{1,0:T(8,128)(2,1)}, bf16[64,2304]{1,0:T(8,128)(2,1)S(1)}, u32[]{:S(2)}, u32[]{:S(2)}) collective-permute-start(bf16[64,2304]{1,0:T(8,128)(2,1)} %get-tuple-element.169.refs_3_), channel_id=1, source_target_pairs={{0,16},{8,24},{16,0},{24,8},{1,17},{9,25},{17,1},{25,9},{2,18},{10... | collective-permute-start | bytes 884744 | tf_op jit(solution)/shard_map/ppermute | solution.py:478
  248.1 0.7 copy-start.14
  248.2 0.8 copy-start.15
  252.8 20.4 %collective-permute-start.28 = (bf16[64,2304]{1,0:T(8,128)(2,1)}, bf16[64,2304]{1,0:T(8,128)(2,1)S(1)}, u32[]{:S(2)}, u32[]{:S(2)}) collective-permute-start(bf16[64,2304]{1,0:T(8,128)(2,1)} %get-tuple-element.175.refs_2_), channel_id=1, source_target_pairs={{0,8},{8,0},{16,24},{24,16},{1,9},{9,1},{17,25},{25,17},{2,10},{10... | collective-permute-start | bytes 884744 | tf_op jit(solution)/shard_map/ppermute | solution.py:478
  253.4 19.8 %collective-permute-start.29 = (bf16[64,2304]{1,0:T(8,128)(2,1)}, bf16[64,2304]{1,0:T(8,128)(2,1)S(1)}, u32[]{:S(2)}, u32[]{:S(2)}) collective-permute-start(bf16[64,2304]{1,0:T(8,128)(2,1)} %get-tuple-element.176.refs_4_), channel_id=1, source_target_pairs={{0,16},{8,24},{16,0},{24,8},{1,17},{9,25},{17,1},{25,9},{2,18},{10... | collective-permute-start | bytes 884744 | tf_op jit(solution)/shard_map/ppermute | solution.py:478
  266.3 0.8 copy-start.25
  273.2 0.8 copy-start.27
  (5 other events, 3.5 us)
Sparse Core Ops, SparseCore 0:
  12.3 53.1 all-gather.2
  67.1 56.1 all-gather.4

commit v4 on v3

--- a/solution.py
+++ b/solution.py
@@ -15,7 +15,7 @@
 
 SCALE = 1.0 / 12.0
 CAP = 50.0
-VMEM = 60 * 1024 * 1024
+MIB = 1024 * 1024
 F32 = jnp.float32
 BF16 = jnp.bfloat16
 
@@ -27,7 +27,7 @@
     return lax.dot_general(a, b, dims, preferred_element_type=F32)
 
 
-def call(body, sc, grid, ins, outs, scratch=(), through=(), before=()):
+def call(body, sc, grid, ins, outs, scratch=(), through=(), before=(), mib=20):
     n_in, n_out, n_before, n_through = len(ins), len(outs), len(before), len(through)
 
     def kernel(sc_ref, *refs):
@@ -35,6 +35,7 @@
         body(sc_ref, *refs[:n_in], *refs[at : at + n_out], *refs[at + n_out + n_through :])
 
     anywhere = pl.BlockSpec(memory_space=pl.ANY)
+    stay = pl.BlockSpec(memory_space=pltpu.HBM)
     aliases = {1 + n_in + n: n for n in range(n_before)}
     aliases.update({1 + n_in + n_before + n: n_out + n for n in range(n_through)})
     results = pl.pallas_call(
@@ -43,16 +44,17 @@
             num_scalar_prefetch=1,
             grid=grid,
             in_specs=[pl.BlockSpec(block, index) for _, block, index in ins]
-            + [anywhere] * (n_before + n_through),
+            + [anywhere] * n_before
+            + [stay] * n_through,
             out_specs=[pl.BlockSpec(block, index) for _, _, block, index in outs]
-            + [anywhere] * n_through,
+            + [stay] * n_through,
             scratch_shapes=list(scratch),
         ),
         out_shape=[jax.ShapeDtypeStruct(shape, dtype) for shape, dtype, _, _ in outs]
         + [jax.ShapeDtypeStruct(x.shape, x.dtype) for x in through],
         input_output_aliases=aliases,
         cost_estimate=pl.CostEstimate(flops=1, transcendentals=0, bytes_accessed=1),
-        compiler_params=pltpu.CompilerParams(vmem_limit_bytes=VMEM),
+        compiler_params=pltpu.CompilerParams(vmem_limit_bytes=mib * MIB),
     )(sc, *[array for array, _, _ in ins], *before, *through)
     return results[:n_out], results[n_out:]
 
@@ -81,12 +83,13 @@
     return weights * inverse, cap_tanh
 
 
-def cut_body(sc_ref, a_ref, b_ref, x_ref, y_ref):
+def cut_body(sc_ref, a_ref, b_ref, x_ref, y_ref, token_ref):
     x_ref[...] = a_ref[...]
     y_ref[...] = b_ref[...]
-
-
-def cut(sc, weight, lay, through):
+    token_ref[...] = jnp.zeros_like(token_ref)
+
+
+def cut(sc, weight, lay):
     rows, width = weight.shape
     block = (rows, width // 4)
     at = lay.at_piece
@@ -98,9 +101,29 @@
             (weight, block, lambda n, sc: (0, sc[at])),
             (weight, block, lambda n, sc: (0, sc[at + 2])),
         ],
-        [(block, BF16, block, first)] * 2,
+        [(block, BF16, block, first)] * 2 + [((8, 128), F32, (8, 128), first)],
+    )
+
+
+def pack(sc, parts, lay, through):
+    rows, width = parts[0].shape
+    block = (rows, width)
+    return call(
+        functools.partial(pack_body, len(parts)),
+        sc,
+        (len(parts),),
+        [(x, block, first) for x in parts],
+        [((len(parts) * rows, width), BF16, block, lambda n, sc: (n, 0))],
         through=through,
     )
+
+
+def pack_body(count, sc_ref, *refs):
+    def copy(p):
+        refs[-1][...] = refs[p][...]
+
+    for p in range(count):
+        pl.when(pl.program_id(0) == p)(functools.partial(copy, p))
 
 
 def pick(sc, whole, lay, through):
@@ -321,6 +344,7 @@
         [((length, rows), BF16, (length, rows), first)] * 2,
         scratch=[pltpu.VMEM((length, rows), F32)] * 2,
         through=through,
+        mib=20 if len(weights) == 1 else 36,
     )
 
 
@@ -414,26 +438,26 @@
 def adam(sc, pieces, first_moment, second_moment, tokens, lay, before, through):
     rows, width = pieces[0][0].shape
     count = len(pieces)
-    places = []
-    for _, side, flips in pieces:
-        order = list(range(lay.bits))
-        order = order[::-1] if side else order
-        row = 0
-        for b, flip in zip(order, flips):
-            bit = sc[lay.at_bit(b)]
-            row = 2 * row + (1 - bit if flip else bit)
-        places += [row, jnp.int32(side)]
-    at = lambda n, at: (at[2 * n], at[2 * n + 1])
+    columns = [lay.at_place(side, flips) for _, side, flips in pieces]
+
+    def at(n, sc):
+        row, side = sc[columns[0]], pieces[0][1]
+        for p in range(1, count):
+            row = jnp.where(n == p, sc[columns[p]], row)
+            side = jnp.where(n == p, pieces[p][1], side)
+        return (row, side)
+
     block = (rows, width)
     return call(
         functools.partial(adam_body, count, tokens),
-        jnp.stack(places).astype(jnp.int32),
+        sc,
         (count,),
         [(first_moment, block, at), (second_moment, block, at)]
         + [(x, block, first) for x, _, _ in pieces],
         [(first_moment.shape, F32, block, at)],
         before=before,
         through=through,
+        mib=60,
     )
 
 
@@ -454,7 +478,11 @@
             for s in range(shards):
                 z, core = s // 2, s % 2
                 zs = [self.order[(self.place[z] - k) % self.z] for k in range(self.z)]
-                table.append([core] + zs + [x, 1 - x, 2 + y, 3 - y] + bits)
+                row = [core] + zs + [x, 1 - x, 2 + y, 3 - y] + bits
+                for order in (bits, bits[::-1]):
+                    here = sum(b << n for n, b in enumerate(order[::-1]))
+                    row += [here ^ flips for flips in range(replicas)]
+                table.append(row)
         self.table = np.array(table, np.int32)
 
     def at_bit(self, b):
@@ -462,6 +490,10 @@
 
     def sibling(self, x):
         return lax.ppermute(x, "shard", [(s, s ^ 1) for s in range(self.shards)])
+
+    def at_place(self, side, flips):
+        code = sum(int(f) << n for n, f in enumerate(flips[::-1]))
+        return self.at_piece + 4 + self.bits + side * self.replicas + code
 
     def gather_z(self, x):
         groups = [list(range(core, self.shards, 2)) for core in range(2)]
@@ -487,7 +519,7 @@
     orders = [list(range(lay.bits)), list(range(lay.bits))[::-1]]
     block = (queries, keys, values, segments, segments.reshape(length, 1))
 
-    box = {"token": jnp.zeros((8, 128), F32)}
+    box = {}
     terms = {}
     ring = {}
     final = []
@@ -534,7 +566,13 @@
         grads = run(backward, sc, k, block, *gc, column, grads, lay, held=held)
 
     upstream_other = lay.sibling(upstream)
-    gathered = [lay.gather_z(x) for x in run(cut, sc, out_weight, lay)]
+    part_x, part_y, box["token"] = cut(sc, out_weight, lay)[0]
+    gathered = lay.gather_z(part_x)
+    box["ring", 1] = lay.onward(part_y)
+
+    def relay(k):
+        if k + 1 < lay.z:
+            box["ring", k + 1] = lay.onward(box["ring", k])
 
     late = [*range(2, lay.z), 0]
     contexts = {}
@@ -545,31 +583,43 @@
     away = lay.sibling(away)
     do_product(1)
     send(1)
-    (stay,) = run(forward, sc, late, [1], block, lay)
+    (stay,) = run(forward, sc, late, [1], block, lay, held=[("ring", 1)])
+    relay(1)
     for n, k in enumerate(late):
         contexts[k] = (stay, n), (away, n)
     do_product(2)
     send(2)
-    do_halve(1)
+    do_halve(1, held=[("ring", 2)])
+    relay(2)
     send(1)
-    own, away = run(grad_context, sc, upstream, upstream_other, [out_weight], lay)
-    gc = own, lay.sibling(away)
     do_product(3)
     do_halve(2, held=sends(3))
     send(3)
-    do_backward(0, gc, 0)
-    do_sum(1, held=sends(2))
+    own, away = run(
+        grad_context, sc, upstream, upstream_other, [out_weight], lay, held=[("ring", 3)]
+    )
+    relay(3)
+    box["gc"] = lay.sibling(away)
+    do_sum(1, held=[*sends(2), "gc"])
     send(2)
+    do_backward(0, (own, box["gc"]), 0)
     do_product(0)
     for k in range(4, lay.z):
-        do_product(k)
+        do_product(k, held=[("ring", k)])
+        relay(k)
         send(k)
     for k in range(3, lay.z):
         do_halve(k)
         send(k)
+    (mine_y,) = run(pack, sc, [box["ring", k] for k in range(1, lay.z)], lay)
     do_sum(2)
-    mine = [run(pick, sc, whole, lay)[0] for whole in gathered]
-    weights = [mine[0], lay.across(mine[0], orders[0][0]), mine[1], lay.across(mine[1], orders[1][0])]
+    (mine_x,) = run(pick, sc, gathered, lay)
+    weights = [
+        mine_x,
+        lay.across(mine_x, orders[0][0]),
+        mine_y,
+        lay.across(mine_y, orders[1][0]),
+    ]
     for k in range(3, lay.z):
         do_sum(k, held=sends(0) if k == lay.z - 1 else ())
     send(0)
@@ -606,7 +656,6 @@
     )
     for side in range(2):
         have[side][1] = (box["got", side], *have[side][1][1:])
-        pieces = [have[side][1]]
         done = {p[2] for p in have[side]}
         near += have[side][1:]
         for n in range(lay.bits - 2, -1, -1):

time: 286 us -> 259 us (0.906)
  Pallas kernels: 156 us -> 110 us
  starting transfers between devices: 29.9 us -> 46.7 us
  waiting for transfers between devices: 61 us -> 71.8 us
  between operations: 19.6 us -> 14.6 us
    pallas_call x27, Pallas kernels: 156 us -> 110 us  [call(): pl.pallas_call(kernel, grid_spec=pltpu.PrefetchScalarGridSpec(num_scalar_...]
    ppermute x3 -> x6, starting transfers between devices: 2.25 us -> 20.9 us  [onward(): return lax.ppermute(x, 'shard', perm)]
    ppermute x3 -> x6, waiting for transfers between devices: 14.5 us -> 31.8 us  [onward(): return lax.ppermute(x, 'shard', perm)]
    ppermute x24, waiting for transfers between devices: 44.1 us -> 39.8 us  [across(): lax.ppermute(x, 'replica', [(r, r ^ 1 << b) for r in range(self.replicas)])]
    unnamed x70 -> x90, local copies, waits for them, and re-layouts: 13.2 us -> 14.7 us
  transfers between devices with their start and end apart: 34 -> 36, of which waited for: 5 -> 8; matrix products, arithmetic and copies ran while one was open for 1% -> 0% of each run, Pallas kernels for 50% -> 41%
where the time goes in v4:
time: 259 us; the launch traced here: 258 us
  Pallas kernels  110 us (42%)
  waiting for transfers between devices  71.8 us (28%)
  starting transfers between devices  46.7 us (18%)
  local copies, waits for them, and re-layouts  15.5 us (6%)
  between operations  14.6 us (6%)
    pallas_call x27, Pallas kernels, call(): pl.pallas_call(kernel, grid_spec=pltpu.PrefetchScalarGridSpec(num_scalar_...  110 us
    ppermute x24, waiting for transfers between devices, across(): lax.ppermute(x, 'replica', [(r, r ^ 1 << b) for r in range(self.replicas)])  39.8 us
    ppermute x6, waiting for transfers between devices, onward(): return lax.ppermute(x, 'shard', perm)  31.8 us
    ppermute x24, starting transfers between devices, across(): lax.ppermute(x, 'replica', [(r, r ^ 1 << b) for r in range(self.replicas)])  24.5 us
    ppermute x6, starting transfers between devices, onward(): return lax.ppermute(x, 'shard', perm)  20.9 us
    unnamed x90, local copies, waits for them, and re-layouts  14.7 us
  transfers between devices with their start and end apart: 36, of which 8 were waited for; matrix products, arithmetic and copies ran while one was open for 0% of the time, Pallas kernels for 41%

profile of v4, /device:TPU:0, one launch (start us, length us, event | category | flops | bytes accessed | tf_op | source)
XLA Modules:
  0.0 258.3 jit_solution(8779312810106301305)
XLA Ops:
  7.7 0.7 dynamic-slice_bitcast_fusion.sc_ref
  8.4 1.7 copy-done.8
  10.1 1.5 shard_map.120
  11.6 0.8 copy-done.35
  12.4 2.7 %collective-permute-start.2 = (bf16[256,1152]{1,0:T(8,128)(2,1)}, bf16[256,1152]{1,0:T(8,128)(2,1)S(1)}, u32[]{:S(2)}, u32[]{:S(2)}) collective-permute-start(bf16[256,1152]{1,0:T(8,128)(2,1)} %copy-done.35), channel_id=1, source_target_pairs={{0,2},{1,3},{2,6},{3,7},{6,4},{7,5},{4,0},{5,1},{8,10},{9,11},{10,... | collective-permute-start | bytes 1769480 | tf_op jit(solution)/shard_map/ppermute | solution.py:507
  15.2 1.2 copy-done.1
  16.5 1.2 copy-done.4
  17.7 3.7 %shard_map.121 = (bf16[512,512]{1,0:T(8,128)(2,1)S(1)}, f32[8,128]{1,0:T(8,128)S(1)}) custom-call(s32[19]{0:T(128)S(1)} %dynamic-slice_bitcast_fusion.sc_ref, bf16[512,2048]{1,0:T(8,128)(2,1)S(1)} %copy-done, bf16[512,1024]{1,0:T(8,128)(2,1)S(1)} %copy-done.1, bf16[512,1024]{1,0:T(8,128)(2,1)S(1)} %copy-done.4, ...), custom_call_target="tpu_custom_call", output_to_operand_aliasing={{1}: (6, {})} | custom-call | flops 1 | bytes 1 | tf_op jit(solution)/shard_map/pallas_call | solution.py:41
  21.6 5.2 %shard_map.122 = (bf16[768,512]{1,0:T(8,128)(2,1)S(1)}, f32[8,128]{1,0:T(8,128)S(1)}) custom-call(s32[19]{0:T(128)S(1)} %dynamic-slice_bitcast_fusion.sc_ref, bf16[512,2048]{1,0:T(8,128)(2,1)S(1)} %copy-done, bf16[512,1024]{1,0:T(8,128)(2,1)S(1)} %copy-done.1, bf16[512,1024]{1,0:T(8,128)(2,1)S(1)} %copy-done.4, ...), custom_call_target="tpu_custom_call", output_to_operand_aliasing={{1}: (6, {})} | custom-call | flops 1 | bytes 1 | tf_op jit(solution)/shard_map/pallas_call | solution.py:41
  27.3 6.4 %shard_map.123 = (bf16[128,2304]{1,0:T(8,128)(2,1)S(1)}, bf16[128,2304]{1,0:T(8,128)(2,1)S(1)}, bf16[128,2304]{1,0:T(8,128)(2,1)S(1)}, bf16[128,2304]{1,0:T(8,128)(2,1)S(1)}, f32[8,128]{1,0:T(8,128)S(1)}) custom-call(s32[19]{0:T(128)S(1)} %dynamic-slice_bitcast_fusion.sc_ref, ...), custom_call_target="tpu_custom_call", output_to_operand_aliasing={{4}: (5, {})} | custom-call | flops 1 | bytes 1 | tf_op jit(solution)/shard_map/pallas_call | solution.py:41
  33.8 3.4 %collective-permute-done.2.refs_6_ = bf16[256,1152]{1,0:T(8,128)(2,1)S(1)} collective-permute-done((bf16[256,1152]{1,0:T(8,128)(2,1)}, bf16[256,1152]{1,0:T(8,128)(2,1)S(1)}, u32[]{:S(2)}, u32[]{:S(2)}) %collective-permute-start.2) | collective-permute-done | bytes 589856 | tf_op jit(solution)/shard_map/ppermute | solution.py:507
  37.1 5.2 %shard_map.124 = (bf16[768,512]{1,0:T(8,128)(2,1)S(1)}, f32[8,128]{1,0:T(8,128)S(1)}, bf16[256,1152]{1,0:T(8,128)(2,1)S(1)}) custom-call(s32[19]{0:T(128)S(1)} %dynamic-slice_bitcast_fusion.sc_ref, bf16[512,2048]{1,0:T(8,128)(2,1)S(1)} %copy-done, bf16[512,1024]{1,0:T(8,128)(2,1)S(1)} %copy-done.2, ...), custom_call_target="tpu_custom_call", output_to_operand_aliasing={{1}: (6, {}), {2}: (7, {})} | custom-call | flops 1 | bytes 1 | tf_op jit(solution)/shard_map/pallas_call | solution.py:41
  42.4 8.4 %collective-permute-start.7 = (bf16[256,1152]{1,0:T(8,128)(2,1)S(1)}, bf16[256,1152]{1,0:T(8,128)(2,1)S(1)}, u32[]{:S(2)}, u32[]{:S(2)}) collective-permute-start(bf16[256,1152]{1,0:T(8,128)(2,1)S(1)} %get-tuple-element.114.refs_0_), channel_id=1, source_target_pairs={{0,2},{1,3},{2,6},{3,7},{6,4},{7,5},{4,0},{5,1},{8,10},{9,11},{10,... | collective-permute-start | bytes 1769480 | tf_op jit(solution)/shard_map/ppermute | solution.py:507
  50.8 1.0 collective-permute-start.5
  51.8 1.6 collective-permute-start.6
  53.4 6.4 %shard_map.125 = (bf16[128,2304]{1,0:T(8,128)(2,1)S(1)}, bf16[128,2304]{1,0:T(8,128)(2,1)S(1)}, bf16[128,2304]{1,0:T(8,128)(2,1)S(1)}, bf16[128,2304]{1,0:T(8,128)(2,1)S(1)}, f32[8,128]{1,0:T(8,128)S(1)}) custom-call(s32[19]{0:T(128)S(1)} %dynamic-slice_bitcast_fusion.sc_ref, ...), custom_call_target="tpu_custom_call", output_to_operand_aliasing={{4}: (5, {})} | custom-call | flops 1 | bytes 1 | tf_op jit(solution)/shard_map/pallas_call | solution.py:41
  60.3 1.0 collective-permute-start.4
  61.4 19.7 %collective-permute-done.7.refs_5_ = bf16[256,1152]{1,0:T(8,128)(2,1)S(1)} collective-permute-done((bf16[256,1152]{1,0:T(8,128)(2,1)S(1)}, bf16[256,1152]{1,0:T(8,128)(2,1)S(1)}, u32[]{:S(2)}, u32[]{:S(2)}) %collective-permute-start.7) | collective-permute-done | bytes 589856 | tf_op jit(solution)/shard_map/ppermute | solution.py:507
  81.8 0.8 collective-permute-start.11
  82.6 1.5 collective-permute-start.8
  84.1 1.5 collective-permute-start.9
  85.6 6.4 %shard_map.127 = (bf16[128,2304]{1,0:T(8,128)(2,1)S(1)}, bf16[128,2304]{1,0:T(8,128)(2,1)S(1)}, bf16[128,2304]{1,0:T(8,128)(2,1)S(1)}, bf16[128,2304]{1,0:T(8,128)(2,1)S(1)}, f32[8,128]{1,0:T(8,128)S(1)}) custom-call(s32[19]{0:T(128)S(1)} %dynamic-slice_bitcast_fusion.sc_ref, ...), custom_call_target="tpu_custom_call", output_to_operand_aliasing={{4}: (5, {})} | custom-call | flops 1 | bytes 1 | tf_op jit(solution)/shard_map/pallas_call | solution.py:41
  92.1 0.7 shard_map.128
  92.8 4.9 %collective-permute-done.11.refs_4_ = bf16[256,1152]{1,0:T(8,128)(2,1)S(1)} collective-permute-done((bf16[256,1152]{1,0:T(8,128)(2,1)S(1)}, bf16[256,1152]{1,0:T(8,128)(2,1)S(1)}, u32[]{:S(2)}, u32[]{:S(2)}) %collective-permute-start.11) | collective-permute-done | bytes 589856 | tf_op jit(solution)/shard_map/ppermute | solution.py:507
  97.7 6.5 %shard_map.129 = (bf16[512,256]{1,0:T(8,128)(2,1)S(1)}, bf16[512,256]{1,0:T(8,128)(2,1)S(1)}, f32[8,128]{1,0:T(8,128)S(1)}, bf16[256,1152]{1,0:T(8,128)(2,1)S(1)}) custom-call(s32[19]{0:T(128)S(1)} %dynamic-slice_bitcast_fusion.sc_ref, bf16[512,4608]{1,0:T(8,128)(2,1)S(1)} %bitcast.4, ...), custom_call_target="tpu_custom_call", output_to_operand_aliasing={{2}: (4, {}), {3}: (5, {})} | custom-call | flops 1 | bytes 1 | tf_op jit(solution)/shard_map/pallas_call | solution.py:41
  104.4 1.4 collective-permute-start.17
  105.8 0.8 shard_map.130
  106.6 1.9 collective-permute-start.14
  109.0 1.0 collective-permute-start.15
  110.0 6.3 %shard_map.131 = (bf16[512,2048]{1,0:T(8,128)(2,1)}, bf16[512,1024]{1,0:T(8,128)(2,1)}, bf16[512,1024]{1,0:T(8,128)(2,1)}, f32[8,128]{1,0:T(8,128)S(1)}) custom-call(s32[19]{0:T(128)S(1)} %dynamic-slice_bitcast_fusion.sc_ref, bf16[512,2048]{1,0:T(8,128)(2,1)S(1)} %copy-done, bf16[512,1024]{1,0:T(8,128)(2,1)S(1)} %copy-done.2, ...), custom_call_target="tpu_custom_call", output_to_operand_aliasing={{3}: (8, {})} | custom-call | flops 1 | bytes 1 | tf_op jit(solution)/shard_map/pallas_call | solution.py:41
  116.3 7.1 %shard_map.132 = (bf16[128,2304]{1,0:T(8,128)(2,1)}, bf16[128,2304]{1,0:T(8,128)(2,1)S(1)}, bf16[128,2304]{1,0:T(8,128)(2,1)}, bf16[128,2304]{1,0:T(8,128)(2,1)S(1)}, f32[8,128]{1,0:T(8,128)S(1)}) custom-call(s32[19]{0:T(128)S(1)} %dynamic-slice_bitcast_fusion.sc_ref, ...), custom_call_target="tpu_custom_call", output_to_operand_aliasing={{4}: (5, {})} | custom-call | flops 1 | bytes 1 | tf_op jit(solution)/shard_map/pallas_call | solution.py:41
  124.2 0.7 copy-done.29
  124.9 2.3 shard_map.134
  127.2 1.1 collective-permute-start.19
  128.3 0.8 shard_map.135
  129.2 0.8 copy-done.36
  130.1 1.8 copy-done.27
  131.8 0.7 shard_map.136
  132.6 1.6 collective-permute-start.18
  134.2 3.4 %collective-permute-start.21 = (bf16[64,4608]{1,0:T(8,128)(2,1)}, bf16[64,4608]{1,0:T(8,128)(2,1)S(1)}, u32[]{:S(2)}, u32[]{:S(2)}) collective-permute-start(bf16[64,4608]{1,0:T(8,128)(2,1)} %copy-done.36), channel_id=1, source_target_pairs={{0,2},{1,3},{2,6},{3,7},{6,4},{7,5},{4,0},{5,1},{8,10},{9,11},{10,... | collective-permute-start | bytes 1769480 | tf_op jit(solution)/shard_map/ppermute | solution.py:507
  138.0 0.9 collective-permute-start.22
  139.0 34.5 %collective-permute-done.20.refs_2_ = bf16[64,2304]{1,0:T(8,128)(2,1)S(1)} collective-permute-done((bf16[64,2304]{1,0:T(8,128)(2,1)}, bf16[64,2304]{1,0:T(8,128)(2,1)S(1)}, u32[]{:S(2)}, u32[]{:S(2)}) %collective-permute-start.20) | collective-permute-done | bytes 294944 | tf_op jit(solution)/shard_map/ppermute | solution.py:510
  173.5 4.8 %collective-permute-done.22.refs_6_ = bf16[64,2304]{1,0:T(8,128)(2,1)S(1)} collective-permute-done((bf16[64,2304]{1,0:T(8,128)(2,1)}, bf16[64,2304]{1,0:T(8,128)(2,1)S(1)}, u32[]{:S(2)}, u32[]{:S(2)}) %collective-permute-start.22) | collective-permute-done | bytes 294944 | tf_op jit(solution)/shard_map/ppermute | solution.py:510
  178.3 0.8 shard_map.137
  179.1 1.6 collective-permute-start.24
  181.2 13.4 %shard_map.138 = (bf16[512,768]{1,0:T(8,128)(2,1)S(1)}, bf16[512,768]{1,0:T(8,128)(2,1)S(1)}, f32[8,128]{1,0:T(8,128)S(1)}) custom-call(s32[19]{0:T(128)S(1)} %dynamic-slice_bitcast_fusion.sc_ref, bf16[512,4608]{1,0:T(8,128)(2,1)S(1)} %bitcast.6, bf16[512,4608]{1,0:T(8,128)(2,1)} %collective-permute-done.refs_3_.refs_1_, ...), custom_call_target="tpu_custom_call", output_to_operand_aliasing={{2}: (7, {})} | custom-call | flops 1 | bytes 1 | tf_op jit(solution)/shard_map/pallas_call | solution.py:41
  194.7 3.6 %collective-permute-start.27 = (bf16[64,4608]{1,0:T(8,128)(2,1)S(1)}, bf16[64,4608]{1,0:T(8,128)(2,1)S(1)}, u32[]{:S(2)}, u32[]{:S(2)}) collective-permute-start(bf16[64,4608]{1,0:T(8,128)(2,1)S(1)} %get-tuple-element.169), channel_id=1, source_target_pairs={{0,2},{1,3},{2,6},{3,7},{6,4},{7,5},{4,0},{5,1},{8,10},{9,11},{10,... | collective-permute-start | bytes 1769480 | tf_op jit(solution)/shard_map/ppermute | solution.py:507
  199.1 1.6 collective-permute-start.26
  201.2 6.3 %shard_map.140 = (bf16[512,2048]{1,0:T(8,128)(2,1)}, bf16[512,1024]{1,0:T(8,128)(2,1)}, bf16[512,1024]{1,0:T(8,128)(2,1)}, f32[8,128]{1,0:T(8,128)S(1)}) custom-call(s32[19]{0:T(128)S(1)} %dynamic-slice_bitcast_fusion.sc_ref, bf16[512,2048]{1,0:T(8,128)(2,1)S(1)} %copy-done, ...), custom_call_target="tpu_custom_call", output_to_operand_aliasing={{0}: (8, {}), {1}: (9, {}), {2}: (10, {}), {3}: (11, {})} | custom-call | flops 1 | bytes 1 | tf_op jit(solution)/shard_map/pallas_call | solution.py:41
  207.5 3.8 %collective-permute-done.27.refs_3_.refs_7_ = bf16[64,4608]{1,0:T(8,128)(2,1)S(1)} collective-permute-done((bf16[64,4608]{1,0:T(8,128)(2,1)S(1)}, bf16[64,4608]{1,0:T(8,128)(2,1)S(1)}, u32[]{:S(2)}, u32[]{:S(2)}) %collective-permute-start.27) | collective-permute-done | bytes 589856 | tf_op jit(solution)/shard_map/ppermute | solution.py:507
  211.3 0.8 shard_map.141
  212.2 1.6 collective-permute-start.29
  214.3 1.5 collective-permute-start.33
  216.3 6.3 %shard_map.142 = (bf16[512,2048]{1,0:T(8,128)(2,1)}, bf16[512,1024]{1,0:T(8,128)(2,1)}, bf16[512,1024]{1,0:T(8,128)(2,1)}, f32[8,128]{1,0:T(8,128)S(1)}) custom-call(s32[19]{0:T(128)S(1)} %dynamic-slice_bitcast_fusion.sc_ref, bf16[512,2048]{1,0:T(8,128)(2,1)S(1)} %copy-done, ...), custom_call_target="tpu_custom_call", output_to_operand_aliasing={{0}: (8, {}), {1}: (9, {}), {2}: (10, {}), {3}: (11, {})} | custom-call | flops 1 | bytes 1 | tf_op jit(solution)/shard_map/pallas_call | solution.py:41
  224.0 0.7 copy-done.40
  224.7 3.8 %shard_map.143 = (f32[256,4608]{1,0:T(8,128)}, f32[8,128]{1,0:T(8,128)}, bf16[64,2304]{1,0:T(8,128)(2,1)}, bf16[64,2304]{1,0:T(8,128)(2,1)}) custom-call(s32[19]{0:T(128)} %copy-done.30, f32[256,4608]{1,0:T(8,128)} %refs_0_.25, f32[256,4608]{1,0:T(8,128)} %refs_1_.21, ...), custom_call_target="tpu_custom_call", output_to_operand_aliasing={{1}: (5, {}), {2}: (6, {}), {3}: (7, {})} | custom-call | flops 1 | bytes 1 | tf_op jit(solution)/shard_map/pallas_call | solution.py:41
  228.5 1.2 collective-permute-start.31
  229.7 0.9 collective-permute-start.32
  230.6 1.2 copy-done.7
  231.8 1.1 copy-done.11
  233.0 1.1 copy-done.13
  234.8 6.3 %shard_map.144 = (bf16[512,2048]{1,0:T(8,128)(2,1)}, bf16[512,1024]{1,0:T(8,128)(2,1)}, bf16[512,1024]{1,0:T(8,128)(2,1)}, f32[8,128]{1,0:T(8,128)S(1)}) custom-call(s32[19]{0:T(128)S(1)} %copy-done.31, bf16[512,2048]{1,0:T(8,128)(2,1)S(1)} %copy-done, ...), custom_call_target="tpu_custom_call", output_to_operand_aliasing={{0}: (8, {}), {1}: (9, {}), {2}: (10, {}), {3}: (11, {})} | custom-call | flops 1 | bytes 1 | tf_op jit(solution)/shard_map/pallas_call | solution.py:41
  241.7 6.0 %shard_map.145 = (f32[256,4608]{1,0:T(8,128)}, f32[8,128]{1,0:T(8,128)}) custom-call(s32[19]{0:T(128)} %copy-done.30, f32[256,4608]{1,0:T(8,128)} %refs_0_.25, f32[256,4608]{1,0:T(8,128)} %refs_1_.21, bf16[64,2304]{1,0:T(8,128)(2,1)} %get-tuple-element.183.refs_2_, ...), custom_call_target="tpu_custom_call", output_to_operand_aliasing={{0}: (7, {}), {1}: (8, {})} | custom-call | flops 1 | bytes 1 | tf_op jit(solution)/shard_map/pallas_call | solution.py:41
  247.7 3.7 %shard_map.146 = (f32[256,4608]{1,0:T(8,128)}, f32[8,128]{1,0:T(8,128)}) custom-call(s32[19]{0:T(128)} %copy-done.30, f32[256,4608]{1,0:T(8,128)} %refs_0_.25, f32[256,4608]{1,0:T(8,128)} %refs_1_.21, bf16[64,2304]{1,0:T(8,128)(2,1)} %collective-permute-done.31.refs_2_, ...), custom_call_target="tpu_custom_call", output_to_operand_aliasing={{0}: (5, {}), {1}: (6, {})} | custom-call | flops 1 | bytes 1 | tf_op jit(solution)/shard_map/pallas_call | solution.py:41
  (131 shorter events, 10.0 us)
Async XLA Ops:
  7.2 122.9 %all-gather.2.cloned.1.call-start = ((), (), s32[]{:S(2)}) async-start(), calls=%async_computation | async-start | bytes 2949120 | tf_op jit(solution)/shard_map/all_gather | solution.py:500
  7.2 20.0 %collective-permute-start = (bf16[512,4608]{1,0:T(8,128)(2,1)}, bf16[512,4608]{1,0:T(8,128)(2,1)}, u32[]{:S(2)}, u32[]{:S(2)}) collective-permute-start(bf16[512,4608]{1,0:T(8,128)(2,1)} %refs_0_.19), channel_id=1, source_target_pairs={{0,1},{1,0},{2,3},{3,2},{4,5},{5,4},{6,7},{7,6},{8,9},{9,8},{10,11... | collective-permute-start | bytes 14155784 | tf_op jit(solution)/shard_map/ppermute | solution.py:492
  10.1 206.2 %copy-start.30 = (s32[19]{0:T(128)}, s32[19]{0:T(128)S(1)}, u32[]{:S(2)}) copy-start(s32[19]{0:T(128)S(1)} %dynamic-slice_bitcast_fusion.sc_ref) | copy-start | bytes 232
  10.1 5.0 %copy-start.34 = (s32[1,512]{1,0:T(1,128)S(1)}, s32[1,512]{1,0:T(1,128)}, u32[]{:S(2)}) copy-start(s32[1,512]{1,0:T(1,128)} %refs_3_.13) | copy-start | bytes 6148
  10.1 5.1 %copy-start = (bf16[512,2048]{1,0:T(8,128)(2,1)S(1)}, bf16[512,2048]{1,0:T(8,128)(2,1)}, u32[]{:S(2)}) copy-start(bf16[512,2048]{1,0:T(8,128)(2,1)} %refs_0_.23) | copy-start | bytes 6291460
  12.4 14.9 %slice-start = ((s8[4718592]{0:T(1024)(128)(4,1)}), s8[524288]{0:T(1024)(128)(4,1)S(1)}, s32[]{:S(2)}) async-start(s8[4718592]{0:T(1024)(128)(4,1)} %bitcast.3), calls=%async_computation.1 | async-start | bytes 1048576
  12.4 24.7 %collective-permute-start.2 = (bf16[256,1152]{1,0:T(8,128)(2,1)}, bf16[256,1152]{1,0:T(8,128)(2,1)S(1)}, u32[]{:S(2)}, u32[]{:S(2)}) collective-permute-start(bf16[256,1152]{1,0:T(8,128)(2,1)} %copy-done.35), channel_id=1, source_target_pairs={{0,2},{1,3},{2,6},{3,7},{6,4},{7,5},{4,0},{5,1},{8,10},{9,11},{10,... | collective-permute-start | bytes 1769480 | tf_op jit(solution)/shard_map/ppermute | solution.py:507
  17.7 9.6 %slice-start.1 = ((s8[4718592]{0:T(1024)(128)(4,1)}), s8[4194304]{0:T(1024)(128)(4,1)S(1)}, s32[]{:S(2)}) async-start(s8[4718592]{0:T(1024)(128)(4,1)} %bitcast.3), calls=%async_computation.2 | async-start | bytes 8388608
  21.4 5.9 %collective-permute-start.1 = (bf16[256,512]{1,0:T(8,128)(2,1)S(1)}, bf16[256,512]{1,0:T(8,128)(2,1)S(1)}, u32[]{:S(2)}, u32[]{:S(2)}) collective-permute-start(bf16[256,512]{1,0:T(8,128)(2,1)S(1)} %slice.3), channel_id=1, source_target_pairs={{0,1},{1,0},{2,3},{3,2},{4,5},{5,4},{6,7},{7,6},{8,9},{9,8},{10,11... | collective-permute-start | bytes 786440 | tf_op jit(solution)/shard_map/ppermute | solution.py:492
  26.9 26.5 %collective-permute-start.3 = (bf16[768,512]{1,0:T(8,128)(2,1)S(1)}, bf16[768,512]{1,0:T(8,128)(2,1)S(1)}, u32[]{:S(2)}, u32[]{:S(2)}) collective-permute-start(bf16[768,512]{1,0:T(8,128)(2,1)S(1)} %get-tuple-element.105), channel_id=1, source_target_pairs={{0,1},{1,0},{2,3},{3,2},{4,5},{5,4},{6,7},{7,6},{8,9},{9,8},{10,11... | collective-permute-start | bytes 2359304 | tf_op jit(solution)/shard_map/ppermute | solution.py:492
  27.3 9.9 %copy-start.2 = (bf16[512,1024]{1,0:T(8,128)(2,1)S(1)}, bf16[512,1024]{1,0:T(8,128)(2,1)}, u32[]{:S(2)}) copy-start(bf16[512,1024]{1,0:T(8,128)(2,1)} %refs_1_.19) | copy-start | bytes 3145732
  27.3 9.9 %copy-start.5 = (bf16[512,1024]{1,0:T(8,128)(2,1)S(1)}, bf16[512,1024]{1,0:T(8,128)(2,1)}, u32[]{:S(2)}) copy-start(bf16[512,1024]{1,0:T(8,128)(2,1)} %refs_2_.23) | copy-start | bytes 3145732
  42.4 17.5 %copy-start.28 = (bf16[256,1152]{1,0:T(8,128)(2,1)}, bf16[256,1152]{1,0:T(8,128)(2,1)S(1)}, u32[]{:S(2)}) copy-start(bf16[256,1152]{1,0:T(8,128)(2,1)S(1)} %get-tuple-element.114.refs_0_) | copy-start | bytes 1769476
  42.4 38.7 %collective-permute-start.7 = (bf16[256,1152]{1,0:T(8,128)(2,1)S(1)}, bf16[256,1152]{1,0:T(8,128)(2,1)S(1)}, u32[]{:S(2)}, u32[]{:S(2)}) collective-permute-start(bf16[256,1152]{1,0:T(8,128)(2,1)S(1)} %get-tuple-element.114.refs_0_), channel_id=1, source_target_pairs={{0,2},{1,3},{2,6},{3,7},{6,4},{7,5},{4,0},{5,1},{8,10},{9,11},{10,... | collective-permute-start | bytes 1769480 | tf_op jit(solution)/shard_map/ppermute | solution.py:507
  50.8 30.3 %collective-permute-start.5 = (bf16[128,2304]{1,0:T(8,128)(2,1)S(1)}, bf16[128,2304]{1,0:T(8,128)(2,1)S(1)}, u32[]{:S(2)}, u32[]{:S(2)}) collective-permute-start(bf16[128,2304]{1,0:T(8,128)(2,1)S(1)} %get-tuple-element.110), channel_id=1, source_target_pairs={{0,8},{8,0},{16,24},{24,16},{1,9},{9,1},{17,25},{25,17},{2,10},{10... | collective-permute-start | bytes 1769480 | tf_op jit(solution)/shard_map/ppermute | solution.py:510
  51.8 29.3 %collective-permute-start.6 = (bf16[128,2304]{1,0:T(8,128)(2,1)S(1)}, bf16[128,2304]{1,0:T(8,128)(2,1)S(1)}, u32[]{:S(2)}, u32[]{:S(2)}) collective-permute-start(bf16[128,2304]{1,0:T(8,128)(2,1)S(1)} %get-tuple-element.112), channel_id=1, source_target_pairs={{0,16},{8,24},{16,0},{24,8},{1,17},{9,25},{17,1},{25,9},{2,18},{10... | collective-permute-start | bytes 1769480 | tf_op jit(solution)/shard_map/ppermute | solution.py:510
  59.8 32.3 %collective-permute-start.10 = (bf16[128,2304]{1,0:T(8,128)(2,1)S(1)}, bf16[128,2304]{1,0:T(8,128)(2,1)S(1)}, u32[]{:S(2)}, u32[]{:S(2)}) collective-permute-start(bf16[128,2304]{1,0:T(8,128)(2,1)S(1)} %get-tuple-element.118), channel_id=1, source_target_pairs={{0,16},{8,24},{16,0},{24,8},{1,17},{9,25},{17,1},{25,9},{2,18},{10... | collective-permute-start | bytes 1769480 | tf_op jit(solution)/shard_map/ppermute | solution.py:510
  60.3 31.8 %collective-permute-start.4 = (bf16[128,2304]{1,0:T(8,128)(2,1)S(1)}, bf16[128,2304]{1,0:T(8,128)(2,1)S(1)}, u32[]{:S(2)}, u32[]{:S(2)}) collective-permute-start(bf16[128,2304]{1,0:T(8,128)(2,1)S(1)} %get-tuple-element.108), channel_id=1, source_target_pairs={{0,8},{8,0},{16,24},{24,16},{1,9},{9,1},{17,25},{25,17},{2,10},{10... | collective-permute-start | bytes 1769480 | tf_op jit(solution)/shard_map/ppermute | solution.py:510
  81.8 16.0 %collective-permute-start.11 = (bf16[256,1152]{1,0:T(8,128)(2,1)S(1)}, bf16[256,1152]{1,0:T(8,128)(2,1)S(1)}, u32[]{:S(2)}, u32[]{:S(2)}) collective-permute-start(bf16[256,1152]{1,0:T(8,128)(2,1)S(1)} %get-tuple-element.124.refs_1_), channel_id=1, source_target_pairs={{0,2},{1,3},{2,6},{3,7},{6,4},{7,5},{4,0},{5,1},{8,10},{9,11},{10,... | collective-permute-start | bytes 1769480 | tf_op jit(solution)/shard_map/ppermute | solution.py:507
  82.6 23.1 %collective-permute-start.8 = (bf16[64,2304]{1,0:T(8,128)(2,1)S(1)}, bf16[64,2304]{1,0:T(8,128)(2,1)S(1)}, u32[]{:S(2)}, u32[]{:S(2)}) collective-permute-start(bf16[64,2304]{1,0:T(8,128)(2,1)S(1)} %get-tuple-element.115), channel_id=1, source_target_pairs={{0,16},{8,24},{16,0},{24,8},{1,17},{9,25},{17,1},{25,9},{2,18},{10... | collective-permute-start | bytes 884744 | tf_op jit(solution)/shard_map/ppermute | solution.py:510
  84.1 21.6 %collective-permute-start.9 = (bf16[64,2304]{1,0:T(8,128)(2,1)S(1)}, bf16[64,2304]{1,0:T(8,128)(2,1)S(1)}, u32[]{:S(2)}, u32[]{:S(2)}) collective-permute-start(bf16[64,2304]{1,0:T(8,128)(2,1)S(1)} %get-tuple-element.116), channel_id=1, source_target_pairs={{0,8},{8,0},{16,24},{24,16},{1,9},{9,1},{17,25},{25,17},{2,10},{10... | collective-permute-start | bytes 884744 | tf_op jit(solution)/shard_map/ppermute | solution.py:510
  92.1 31.4 %copy-start.17 = (bf16[128,2304]{1,0:T(8,128)(2,1)}, bf16[128,2304]{1,0:T(8,128)(2,1)S(1)}, u32[]{:S(2)}) copy-start(bf16[128,2304]{1,0:T(8,128)(2,1)S(1)} %get-tuple-element.135.refs_2_.refs_4_) | copy-start | bytes 1769476
  92.1 5.7 %copy-start.9 = (bf16[256,4608]{1,0:T(8,128)(2,1)S(1)}, bf16[256,4608]{1,0:T(8,128)(2,1)}, u32[]{:S(2)}) copy-start(bf16[256,4608]{1,0:T(8,128)(2,1)} %refs_2_.18) | copy-start | bytes 7077892
  104.2 1.6 collective-permute-start.12
  104.3 19.1 %collective-permute-start.16 = (bf16[128,2304]{1,0:T(8,128)(2,1)S(1)}, bf16[128,2304]{1,0:T(8,128)(2,1)S(1)}, u32[]{:S(2)}, u32[]{:S(2)}) collective-permute-start(bf16[128,2304]{1,0:T(8,128)(2,1)S(1)} %get-tuple-element.134), channel_id=1, source_target_pairs={{0,8},{8,0},{16,24},{24,16},{1,9},{9,1},{17,25},{25,17},{2,10},{10... | collective-permute-start | bytes 1769480 | tf_op jit(solution)/shard_map/ppermute | solution.py:510
  104.4 19.0 %collective-permute-start.17 = (bf16[128,2304]{1,0:T(8,128)(2,1)S(1)}, bf16[128,2304]{1,0:T(8,128)(2,1)S(1)}, u32[]{:S(2)}, u32[]{:S(2)}) collective-permute-start(bf16[128,2304]{1,0:T(8,128)(2,1)S(1)} %get-tuple-element.136), channel_id=1, source_target_pairs={{0,16},{8,24},{16,0},{24,8},{1,17},{9,25},{17,1},{25,9},{2,18},{10... | collective-permute-start | bytes 1769480 | tf_op jit(solution)/shard_map/ppermute | solution.py:510
  106.6 21.7 %collective-permute-start.14 = (bf16[64,4608]{1,0:T(8,128)(2,1)S(1)}, bf16[64,4608]{1,0:T(8,128)(2,1)S(1)}, u32[]{:S(2)}, u32[]{:S(2)}) collective-permute-start(bf16[64,4608]{1,0:T(8,128)(2,1)S(1)} %get-tuple-element.130), channel_id=1, source_target_pairs={{0,2},{1,3},{2,6},{3,7},{6,4},{7,5},{4,0},{5,1},{8,10},{9,11},{10,... | collective-permute-start | bytes 1769480 | tf_op jit(solution)/shard_map/ppermute | solution.py:507
  108.5 19.7 %collective-permute-start.13 = (bf16[64,2304]{1,0:T(8,128)(2,1)S(1)}, bf16[64,2304]{1,0:T(8,128)(2,1)S(1)}, u32[]{:S(2)}, u32[]{:S(2)}) collective-permute-start(bf16[64,2304]{1,0:T(8,128)(2,1)S(1)} %get-tuple-element.129), channel_id=1, source_target_pairs={{0,16},{8,24},{16,0},{24,8},{1,17},{9,25},{17,1},{25,9},{2,18},{10... | collective-permute-start | bytes 884744 | tf_op jit(solution)/shard_map/ppermute | solution.py:510
  109.0 19.2 %collective-permute-start.15 = (bf16[64,2304]{1,0:T(8,128)(2,1)S(1)}, bf16[64,2304]{1,0:T(8,128)(2,1)S(1)}, u32[]{:S(2)}, u32[]{:S(2)}) collective-permute-start(bf16[64,2304]{1,0:T(8,128)(2,1)S(1)} %get-tuple-element.131), channel_id=1, source_target_pairs={{0,8},{8,0},{16,24},{24,16},{1,9},{9,1},{17,25},{25,17},{2,10},{10... | collective-permute-start | bytes 884744 | tf_op jit(solution)/shard_map/ppermute | solution.py:510
  123.4 4.9 %copy-start.19 = (bf16[128,2304]{1,0:T(8,128)(2,1)}, bf16[128,2304]{1,0:T(8,128)(2,1)S(1)}, u32[]{:S(2)}) copy-start(bf16[128,2304]{1,0:T(8,128)(2,1)S(1)} %get-tuple-element.159.refs_0_) | copy-start | bytes 1769476
  123.4 4.9 %copy-start.21 = (bf16[128,2304]{1,0:T(8,128)(2,1)}, bf16[128,2304]{1,0:T(8,128)(2,1)S(1)}, u32[]{:S(2)}) copy-start(bf16[128,2304]{1,0:T(8,128)(2,1)S(1)} %get-tuple-element.161.refs_2_.refs_4_) | copy-start | bytes 1769476
  123.4 4.9 %copy-start.23 = (bf16[128,2304]{1,0:T(8,128)(2,1)}, bf16[128,2304]{1,0:T(8,128)(2,1)S(1)}, u32[]{:S(2)}) copy-start(bf16[128,2304]{1,0:T(8,128)(2,1)S(1)} %collective-permute-done.16.refs_1_) | copy-start | bytes 1769476
  123.4 4.9 %copy-start.25 = (bf16[128,2304]{1,0:T(8,128)(2,1)}, bf16[128,2304]{1,0:T(8,128)(2,1)S(1)}, u32[]{:S(2)}) copy-start(bf16[128,2304]{1,0:T(8,128)(2,1)S(1)} %collective-permute-done.17.refs_3_.refs_5_) | copy-start | bytes 1769476
  127.2 54.0 %collective-permute-start.19 = (bf16[768,1152]{1,0:T(8,128)(2,1)}, bf16[768,1152]{1,0:T(8,128)(2,1)}, u32[]{:S(2)}, u32[]{:S(2)}) collective-permute-start(bf16[768,1152]{1,0:T(8,128)(2,1)} %get-tuple-element.146.refs_4_), channel_id=1, source_target_pairs={{0,16},{8,24},{16,0},{24,8},{1,17},{9,25},{17,1},{25,9},{2,18},{10... | collective-permute-start | bytes 5308424 | tf_op jit(solution)/shard_map/ppermute | solution.py:510
  128.3 52.9 %slice-start.2 = ((s8[4718592]{0:T(1024)(128)(4,1)}), s8[524288]{0:T(1024)(128)(4,1)S(1)}, s32[]{:S(2)}) async-start(s8[4718592]{0:T(1024)(128)(4,1)} %bitcast.5), calls=%async_computation.3 | async-start | bytes 1048576
  130.0 48.2 %copy-start.18 = (bf16[128,2304]{1,0:T(8,128)(2,1)S(1)}, bf16[128,2304]{1,0:T(8,128)(2,1)}, u32[]{:S(2)}) copy-start(bf16[128,2304]{1,0:T(8,128)(2,1)} %copy-done.17) | copy-start | bytes 1769476
  130.0 48.2 %copy-start.24 = (bf16[128,2304]{1,0:T(8,128)(2,1)S(1)}, bf16[128,2304]{1,0:T(8,128)(2,1)}, u32[]{:S(2)}) copy-start(bf16[128,2304]{1,0:T(8,128)(2,1)} %copy-done.23) | copy-start | bytes 1769476
  130.0 48.2 %copy-start.26 = (bf16[128,2304]{1,0:T(8,128)(2,1)S(1)}, bf16[128,2304]{1,0:T(8,128)(2,1)}, u32[]{:S(2)}) copy-start(bf16[128,2304]{1,0:T(8,128)(2,1)} %copy-done.25) | copy-start | bytes 1769476
  131.8 49.3 %slice-start.3 = ((s8[4718592]{0:T(1024)(128)(4,1)}), s8[4194304]{0:T(1024)(128)(4,1)S(1)}, s32[]{:S(2)}) async-start(s8[4718592]{0:T(1024)(128)(4,1)} %bitcast.5), calls=%async_computation.4 | async-start | bytes 8388608
  132.6 48.6 %collective-permute-start.18 = (bf16[768,1152]{1,0:T(8,128)(2,1)S(1)}, bf16[768,1152]{1,0:T(8,128)(2,1)S(1)}, u32[]{:S(2)}, u32[]{:S(2)}) collective-permute-start(bf16[768,1152]{1,0:T(8,128)(2,1)S(1)} %get-tuple-element.145.refs_2_), channel_id=1, source_target_pairs={{0,8},{8,0},{16,24},{24,16},{1,9},{9,1},{17,25},{25,17},{2,10},{10... | collective-permute-start | bytes 5308424 | tf_op jit(solution)/shard_map/ppermute | solution.py:510
  134.2 44.1 %collective-permute-start.21 = (bf16[64,4608]{1,0:T(8,128)(2,1)}, bf16[64,4608]{1,0:T(8,128)(2,1)S(1)}, u32[]{:S(2)}, u32[]{:S(2)}) collective-permute-start(bf16[64,4608]{1,0:T(8,128)(2,1)} %copy-done.36), channel_id=1, source_target_pairs={{0,2},{1,3},{2,6},{3,7},{6,4},{7,5},{4,0},{5,1},{8,10},{9,11},{10,... | collective-permute-start | bytes 1769480 | tf_op jit(solution)/shard_map/ppermute | solution.py:507
  137.5 36.0 %collective-permute-start.20 = (bf16[64,2304]{1,0:T(8,128)(2,1)}, bf16[64,2304]{1,0:T(8,128)(2,1)S(1)}, u32[]{:S(2)}, u32[]{:S(2)}) collective-permute-start(bf16[64,2304]{1,0:T(8,128)(2,1)} %copy-done.38), channel_id=1, source_target_pairs={{0,16},{8,24},{16,0},{24,8},{1,17},{9,25},{17,1},{25,9},{2,18},{10... | collective-permute-start | bytes 884744 | tf_op jit(solution)/shard_map/ppermute | solution.py:510
  138.0 40.2 %collective-permute-start.22 = (bf16[64,2304]{1,0:T(8,128)(2,1)}, bf16[64,2304]{1,0:T(8,128)(2,1)S(1)}, u32[]{:S(2)}, u32[]{:S(2)}) collective-permute-start(bf16[64,2304]{1,0:T(8,128)(2,1)} %copy-done.37), channel_id=1, source_target_pairs={{0,8},{8,0},{16,24},{24,16},{1,9},{9,1},{17,25},{25,17},{2,10},{10... | collective-permute-start | bytes 884744 | tf_op jit(solution)/shard_map/ppermute | solution.py:510
  179.1 19.2 %collective-permute-start.24 = (bf16[128,2304]{1,0:T(8,128)(2,1)}, bf16[128,2304]{1,0:T(8,128)(2,1)S(1)}, u32[]{:S(2)}, u32[]{:S(2)}) collective-permute-start(bf16[128,2304]{1,0:T(8,128)(2,1)} %get-tuple-element.160), channel_id=1, source_target_pairs={{0,8},{8,0},{16,24},{24,16},{1,9},{9,1},{17,25},{25,17},{2,10},{10... | collective-permute-start | bytes 1769480 | tf_op jit(solution)/shard_map/ppermute | solution.py:510
  180.7 17.7 %collective-permute-start.25 = (bf16[128,2304]{1,0:T(8,128)(2,1)}, bf16[128,2304]{1,0:T(8,128)(2,1)S(1)}, u32[]{:S(2)}, u32[]{:S(2)}) collective-permute-start(bf16[128,2304]{1,0:T(8,128)(2,1)} %get-tuple-element.162), channel_id=1, source_target_pairs={{0,16},{8,24},{16,0},{24,8},{1,17},{9,25},{17,1},{25,9},{2,18},{10... | collective-permute-start | bytes 1769480 | tf_op jit(solution)/shard_map/ppermute | solution.py:510
  181.2 17.2 %copy-start.20 = (bf16[128,2304]{1,0:T(8,128)(2,1)S(1)}, bf16[128,2304]{1,0:T(8,128)(2,1)}, u32[]{:S(2)}) copy-start(bf16[128,2304]{1,0:T(8,128)(2,1)} %copy-done.19) | copy-start | bytes 1769476
  181.2 17.2 %copy-start.22 = (bf16[128,2304]{1,0:T(8,128)(2,1)S(1)}, bf16[128,2304]{1,0:T(8,128)(2,1)}, u32[]{:S(2)}) copy-start(bf16[128,2304]{1,0:T(8,128)(2,1)} %copy-done.21) | copy-start | bytes 1769476
  194.6 21.7 %copy-start.10 = (bf16[512,768]{1,0:T(8,128)(2,1)}, bf16[512,768]{1,0:T(8,128)(2,1)S(1)}, u32[]{:S(2)}) copy-start(bf16[512,768]{1,0:T(8,128)(2,1)S(1)} %get-tuple-element.154.refs_5_) | copy-start | bytes 2359300
  194.6 6.6 %copy-start.3 = (bf16[512,1024]{1,0:T(8,128)(2,1)S(1)}, bf16[512,1024]{1,0:T(8,128)(2,1)}, u32[]{:S(2)}) copy-start(bf16[512,1024]{1,0:T(8,128)(2,1)} %refs_1_.19) | copy-start | bytes 3145732
  194.6 6.6 %copy-start.6 = (bf16[512,1024]{1,0:T(8,128)(2,1)S(1)}, bf16[512,1024]{1,0:T(8,128)(2,1)}, u32[]{:S(2)}) copy-start(bf16[512,1024]{1,0:T(8,128)(2,1)} %refs_2_.23) | copy-start | bytes 3145732
  194.6 6.6 %collective-permute-start.23 = (bf16[512,768]{1,0:T(8,128)(2,1)S(1)}, bf16[512,768]{1,0:T(8,128)(2,1)S(1)}, u32[]{:S(2)}, u32[]{:S(2)}) collective-permute-start(bf16[512,768]{1,0:T(8,128)(2,1)S(1)} %get-tuple-element.155), channel_id=1, source_target_pairs={{0,1},{1,0},{2,3},{3,2},{4,5},{5,4},{6,7},{7,6},{8,9},{9,8},{10,11... | collective-permute-start | bytes 2359304 | tf_op jit(solution)/shard_map/ppermute | solution.py:492
  194.7 16.6 %collective-permute-start.27 = (bf16[64,4608]{1,0:T(8,128)(2,1)S(1)}, bf16[64,4608]{1,0:T(8,128)(2,1)S(1)}, u32[]{:S(2)}, u32[]{:S(2)}) collective-permute-start(bf16[64,4608]{1,0:T(8,128)(2,1)S(1)} %get-tuple-element.169), channel_id=1, source_target_pairs={{0,2},{1,3},{2,6},{3,7},{6,4},{7,5},{4,0},{5,1},{8,10},{9,11},{10,... | collective-permute-start | bytes 1769480 | tf_op jit(solution)/shard_map/ppermute | solution.py:507
  199.1 12.3 %collective-permute-start.26 = (bf16[64,2304]{1,0:T(8,128)(2,1)S(1)}, bf16[64,2304]{1,0:T(8,128)(2,1)S(1)}, u32[]{:S(2)}, u32[]{:S(2)}) collective-permute-start(bf16[64,2304]{1,0:T(8,128)(2,1)S(1)} %get-tuple-element.168), channel_id=1, source_target_pairs={{0,16},{8,24},{16,0},{24,8},{1,17},{9,25},{17,1},{25,9},{2,18},{10... | collective-permute-start | bytes 884744 | tf_op jit(solution)/shard_map/ppermute | solution.py:510
  200.7 10.7 %collective-permute-start.28 = (bf16[64,2304]{1,0:T(8,128)(2,1)S(1)}, bf16[64,2304]{1,0:T(8,128)(2,1)S(1)}, u32[]{:S(2)}, u32[]{:S(2)}) collective-permute-start(bf16[64,2304]{1,0:T(8,128)(2,1)S(1)} %get-tuple-element.170), channel_id=1, source_target_pairs={{0,8},{8,0},{16,24},{24,16},{1,9},{9,1},{17,25},{25,17},{2,10},{10... | collective-permute-start | bytes 884744 | tf_op jit(solution)/shard_map/ppermute | solution.py:510
  201.2 15.1 %copy-start.12 = (bf16[512,768]{1,0:T(8,128)(2,1)}, bf16[512,768]{1,0:T(8,128)(2,1)S(1)}, u32[]{:S(2)}) copy-start(bf16[512,768]{1,0:T(8,128)(2,1)S(1)} %collective-permute-done.23.refs_6_) | copy-start | bytes 2359300
  212.2 10.5 %copy-start.32 = (bf16[64,2304]{1,0:T(8,128)(2,1)}, bf16[64,2304]{1,0:T(8,128)(2,1)S(1)}, u32[]{:S(2)}) copy-start(bf16[64,2304]{1,0:T(8,128)(2,1)S(1)} %get-tuple-element.177.refs_3_) | copy-start | bytes 884740
  212.2 10.4 %copy-start.33 = (bf16[64,2304]{1,0:T(8,128)(2,1)}, bf16[64,2304]{1,0:T(8,128)(2,1)S(1)}, u32[]{:S(2)}) copy-start(bf16[64,2304]{1,0:T(8,128)(2,1)S(1)} %get-tuple-element.176.refs_2_) | copy-start | bytes 884740
  212.2 11.0 %collective-permute-start.29 = (bf16[64,2304]{1,0:T(8,128)(2,1)S(1)}, bf16[64,2304]{1,0:T(8,128)(2,1)S(1)}, u32[]{:S(2)}, u32[]{:S(2)}) collective-permute-start(bf16[64,2304]{1,0:T(8,128)(2,1)S(1)} %get-tuple-element.176.refs_2_), channel_id=1, source_target_pairs={{0,16},{8,24},{16,0},{24,8},{1,17},{9,25},{17,1},{25,9},{2,18},{10... | collective-permute-start | bytes 884744 | tf_op jit(solution)/shard_map/ppermute | solution.py:510
  213.8 9.9 %collective-permute-start.30 = (bf16[64,2304]{1,0:T(8,128)(2,1)S(1)}, bf16[64,2304]{1,0:T(8,128)(2,1)S(1)}, u32[]{:S(2)}, u32[]{:S(2)}) collective-permute-start(bf16[64,2304]{1,0:T(8,128)(2,1)S(1)} %get-tuple-element.177.refs_3_), channel_id=1, source_target_pairs={{0,8},{8,0},{16,24},{24,16},{1,9},{9,1},{17,25},{25,17},{2,10},{10... | collective-permute-start | bytes 884744 | tf_op jit(solution)/shard_map/ppermute | solution.py:510
  214.3 27.3 %collective-permute-start.33 = (bf16[64,2304]{1,0:T(8,128)(2,1)S(1)}, bf16[64,2304]{1,0:T(8,128)(2,1)}, u32[]{:S(2)}, u32[]{:S(2)}) collective-permute-start(bf16[64,2304]{1,0:T(8,128)(2,1)S(1)} %get-tuple-element.176.refs_2_), channel_id=1, source_target_pairs={{0,8},{8,0},{16,24},{24,16},{1,9},{9,1},{17,25},{25,17},{2,10},{10... | collective-permute-start | bytes 884744 | tf_op jit(solution)/shard_map/ppermute | solution.py:510
  215.8 25.8 %collective-permute-start.34 = (bf16[64,2304]{1,0:T(8,128)(2,1)S(1)}, bf16[64,2304]{1,0:T(8,128)(2,1)}, u32[]{:S(2)}, u32[]{:S(2)}) collective-permute-start(bf16[64,2304]{1,0:T(8,128)(2,1)S(1)} %get-tuple-element.177.refs_3_), channel_id=1, source_target_pairs={{0,16},{8,24},{16,0},{24,8},{1,17},{9,25},{17,1},{25,9},{2,18},{10... | collective-permute-start | bytes 884744 | tf_op jit(solution)/shard_map/ppermute | solution.py:510
  224.7 5.9 %copy-start.31 = (s32[19]{0:T(128)S(1)}, s32[19]{0:T(128)}, u32[]{:S(2)}) copy-start(s32[19]{0:T(128)} %copy-done.30) | copy-start | bytes 232
  228.5 19.2 %collective-permute-start.31 = (bf16[64,2304]{1,0:T(8,128)(2,1)}, bf16[64,2304]{1,0:T(8,128)(2,1)}, u32[]{:S(2)}, u32[]{:S(2)}) collective-permute-start(bf16[64,2304]{1,0:T(8,128)(2,1)} %get-tuple-element.183.refs_2_), channel_id=1, source_target_pairs={{0,8},{8,0},{16,24},{24,16},{1,9},{9,1},{17,25},{25,17},{2,10},{10... | collective-permute-start | bytes 884744 | tf_op jit(solution)/shard_map/ppermute | solution.py:510
  229.7 18.0 %collective-permute-start.32 = (bf16[64,2304]{1,0:T(8,128)(2,1)}, bf16[64,2304]{1,0:T(8,128)(2,1)}, u32[]{:S(2)}, u32[]{:S(2)}) collective-permute-start(bf16[64,2304]{1,0:T(8,128)(2,1)} %get-tuple-element.184.refs_4_), channel_id=1, source_target_pairs={{0,16},{8,24},{16,0},{24,8},{1,17},{9,25},{17,1},{25,9},{2,18},{10... | collective-permute-start | bytes 884744 | tf_op jit(solution)/shard_map/ppermute | solution.py:510
  (17 other events, 24.2 us)
Sparse Core Ops, SparseCore 0:
  12.5 68.2 all-gather.1

commit v5 on v3

v5 whole, which is shorter than its diff:
```python
import functools

import jax
import jax.numpy as jnp
import numpy as np
from jax import lax
from jax.experimental import pallas as pl
from jax.experimental.pallas import tpu as pltpu
from jax.sharding import PartitionSpec as P

HEADS = 16
KV_HEADS = 8
DH = 128
REPEAT = HEADS // KV_HEADS

SCALE = 1.0 / 12.0
CAP = 50.0
MIB = 1024 * 1024
F32 = jnp.float32
BF16 = jnp.bfloat16

NT = (((1,), (1,)), ((), ()))
NN = (((1,), (0,)), ((), ()))


def dot(a, b, dims):
    return lax.dot_general(a, b, dims, preferred_element_type=F32)


def call(body, sc, grid, ins, outs, scratch=(), through=(), before=(), mib=20):
    n_in, n_out, n_before, n_through = len(ins), len(outs), len(before), len(through)

    def kernel(sc_ref, *refs):
        at = n_in + n_before + n_through
        body(sc_ref, *refs[:n_in], *refs[at : at + n_out], *refs[at + n_out + n_through :])

    anywhere = pl.BlockSpec(memory_space=pl.ANY)
    stay = pl.BlockSpec(memory_space=pltpu.HBM)
    aliases = {1 + n_in + n: n for n in range(n_before)}
    aliases.update({1 + n_in + n_before + n: n_out + n for n in range(n_through)})
    results = pl.pallas_call(
        kernel,
        grid_spec=pltpu.PrefetchScalarGridSpec(
            num_scalar_prefetch=1,
            grid=grid,
            in_specs=[pl.BlockSpec(block, index) for _, block, index in ins]
            + [anywhere] * n_before
            + [stay] * n_through,
            out_specs=[pl.BlockSpec(block, index) for _, _, block, index in outs]
            + [stay] * n_through,
            scratch_shapes=list(scratch),
        ),
        out_shape=[jax.ShapeDtypeStruct(shape, dtype) for shape, dtype, _, _ in outs]
        + [jax.ShapeDtypeStruct(x.shape, x.dtype) for x in through],
        input_output_aliases=aliases,
        cost_estimate=pl.CostEstimate(flops=1, transcendentals=0, bytes_accessed=1),
        compiler_params=pltpu.CompilerParams(vmem_limit_bytes=mib * MIB),
    )(sc, *[array for array, _, _ in ins], *before, *through)
    return results[:n_out], results[n_out:]


def first(*_):
    return (0, 0)


def fill_mask(mask_ref, seg_row_ref, seg_col_ref):
    length = mask_ref.shape[0]
    j = lax.broadcasted_iota(jnp.int32, (length, length), 0)
    i = lax.broadcasted_iota(jnp.int32, (length, length), 1)
    allowed = (j <= i) & (seg_col_ref[...] == seg_row_ref[...])
    mask_ref[...] = jnp.where(allowed, 1.0, 0.0).astype(F32)


def tiles_of(length):
    tile = 256
    return [(t * tile, tile, (t + 1) * tile) for t in range(length // tile)]


def softmax_tile(key, query, mask):
    cap_tanh = jnp.tanh(dot(key, query, NT) * (SCALE / CAP))
    weights = jnp.exp(cap_tanh * CAP) * mask
    inverse = 1.0 / jnp.sum(weights, axis=0, keepdims=True)
    return weights * inverse, cap_tanh


def cut_body(sc_ref, in_ref, out_ref, token_ref):
    out_ref[...] = in_ref[...]
    token_ref[...] = jnp.zeros_like(token_ref)


def cut(sc, weight, lay):
    block = (weight.shape[0], weight.shape[1] // 2)
    return call(
        cut_body,
        sc,
        (1,),
        [(weight, block, lambda n, sc: (0, sc[lay.at_bit(0)]))],
        [(block, BF16, block, first), ((8, 128), F32, (8, 128), first)],
    )


def forward_body(heads, sc_ref, q_ref, k_ref, v_ref, seg_row_ref, seg_col_ref, out_ref, mask_ref):
    @pl.when(pl.program_id(0) == 0)
    def _():
        fill_mask(mask_ref, seg_row_ref, seg_col_ref)

    value_t = v_ref[...].T
    for h in range(heads):
        for start, tile, upto in tiles_of(q_ref.shape[0]):
            probs, _ = softmax_tile(
                k_ref[:upto, :],
                q_ref[start : start + tile, h * DH : (h + 1) * DH],
                mask_ref[:upto, start : start + tile],
            )
            context = dot(value_t[:, :upto], probs.astype(BF16), NN)
            out_ref[h * DH : (h + 1) * DH, start : start + tile] = context.astype(BF16)


def forward(sc, ks, sides, block, lay, through):
    queries, keys, values, seg_row, seg_col = block
    length = queries.shape[0]
    per = lay.heads_shard
    count = len(ks)

    def shard_of(i, sc):
        k = lax.rem(ks[0] + lax.rem(i, count), lay.z)
        if len(sides) == 2:
            own = i >= count
        else:
            own = sides[0] == 1
        return 2 * sc[lay.at_z + k] + jnp.where(own, sc[0], 1 - sc[0])

    def kv_of(i, sc):
        return (0, (shard_of(i, sc) * per) // REPEAT)

    rows = per * DH
    steps = count * len(sides)
    return call(
        functools.partial(forward_body, per),
        sc,
        (steps,),
        [
            (queries, (length, rows), lambda i, sc: (0, shard_of(i, sc))),
            (keys, (length, DH), kv_of),
            (values, (length, DH), kv_of),
            (seg_row, (1, length), first),
            (seg_col, (length, 1), first),
        ],
        [((steps * rows, length), BF16, (rows, length), lambda i, sc: (i, 0))],
        scratch=[pltpu.VMEM((length, length), F32)],
        through=through,
    )


def product_body(at_bit, sc_ref, c0_ref, c1_ref, u0_ref, u1_ref, send_ref, keep_ref, acc_ref):
    half = acc_ref.shape[0] // 2
    acc = dot(c0_ref[...], u0_ref[...], NN) + dot(c1_ref[...], u1_ref[...], NN)
    acc_ref[...] = acc.astype(BF16)
    bit = sc_ref[at_bit]
    keep_ref[...] = acc_ref[pl.ds(pl.multiple_of(bit * half, half), half), :]
    send_ref[...] = acc_ref[pl.ds(pl.multiple_of((1 - bit) * half, half), half), :]


def product(sc, own, other, up0, up1, lay, through):
    length, width = up0.shape
    rows = lay.rows
    tile = width // 4
    out = ((rows // 2, width), BF16, (rows // 2, tile), lambda n, sc: (0, n))
    return call(
        functools.partial(product_body, lay.at_bit(0)),
        sc,
        (4,),
        [(x, (rows, length), lambda n, sc, at=at: (at, 0)) for x, at in (own, other)]
        + [(u, (length, tile), lambda n, sc: (0, n)) for u in (up0, up1)],
        [out, out],
        scratch=[pltpu.VMEM((rows, tile), BF16)],
        through=through,
    )


def combine_body(sc_ref, *refs):
    total = refs[0][...].astype(F32)
    for ref in refs[1:-1]:
        total = total + ref[...].astype(F32)
    refs[-1][...] = total.astype(BF16)


def combine(sc, terms, ring, away, lay, through):
    deep = len(terms) if away else lay.bits
    width = terms[0].shape[1]
    size = lay.rows >> deep
    ins = []

    def place(level):
        def index(n, sc):
            at = 0
            for m in range(level, deep):
                bit = sc[lay.at_bit(m)]
                at = 2 * at + (1 - bit if away and m == deep - 1 else bit)
            return (at, 0)

        return index

    for m, x in enumerate(terms):
        ins.append((x, (size, width), place(max(m, 1))))
    if ring is not None:
        ins.append((ring, (size, width), first))
    out = ((size, width), BF16, (size, width), first)
    return call(combine_body, sc, (1,), ins, [out], through=through)


def grad_context_body(sets, sc_ref, u0_ref, u1_ref, *refs):
    weights, (g0_ref, g1_ref, a0_ref, a1_ref) = refs[:-4], refs[-4:]
    n = pl.program_id(0)
    rows = a0_ref.shape[1] // len(sets)

    def add(weight_ref, cols):
        d0 = dot(u0_ref[...], weight_ref[...], NT)
        d1 = dot(u1_ref[...], weight_ref[...], NT)

        @pl.when(n == 0)
        def _():
            a0_ref[:, cols] = d0
            a1_ref[:, cols] = d1

        @pl.when(n > 0)
        def _():
            a0_ref[:, cols] += d0
            a1_ref[:, cols] += d1

    at = 0
    for index, count in enumerate(sets):
        cols = slice(index * rows, (index + 1) * rows)
        if count == 1:
            add(weights[at], cols)
        else:
            pl.when(n < 2)(functools.partial(add, weights[at], cols))
            pl.when(n >= 2)(functools.partial(add, weights[at + 1], cols))
        at += count

    @pl.when(n == 3)
    def _():
        g0_ref[...] = a0_ref[...].astype(BF16)
        g1_ref[...] = a1_ref[...].astype(BF16)


def grad_context(sc, up0, up1, weight_sets, lay, through):
    length, width = up0.shape
    rows, tile = lay.rows, width // 4
    total = rows * len(weight_sets)
    at = lay.at_piece
    ins = [(u, (length, tile), lambda n, sc: (0, sc[at + n])) for u in (up0, up1)]
    for weights in weight_sets:
        if len(weights) == 1:
            ins.append((weights[0], (rows, tile), lambda n, sc: (0, sc[at + n])))
        else:
            ins.append((weights[0], (rows, tile), lambda n, sc: (0, jnp.minimum(n, 1))))
            ins.append((weights[1], (rows, tile), lambda n, sc: (0, jnp.maximum(n - 2, 0))))
    return call(
        functools.partial(grad_context_body, [len(w) for w in weight_sets]),
        sc,
        (4,),
        ins,
        [((length, total), BF16, (length, total), first)] * 2,
        scratch=[pltpu.VMEM((length, total), F32)] * 2,
        through=through,
        mib=28,
    )


def backward_body(
    per, sc_ref, q_ref, k_ref, v_ref, seg_row_ref, seg_col_ref, own_ref, other_ref, *refs
):
    gq_ref, gk_ref, gv_ref, mask_ref, ak_ref, av_ref = refs[-6:]
    group = pl.program_id(0)
    parity = sc_ref[0]

    @pl.when(group == 0)
    def _():
        fill_mask(mask_ref, seg_row_ref, seg_col_ref)

    key_t = k_ref[...].T
    ak_ref[...] = jnp.zeros_like(ak_ref)
    av_ref[...] = jnp.zeros_like(av_ref)
    for h in range(REPEAT):
        side = group if per == REPEAT else h
        column = h if per == REPEAT else 0
        cols = slice(column * DH, (column + 1) * DH)
        grad = jnp.where(side == parity, own_ref[:, cols], other_ref[:, cols])
        for start, tile, upto in tiles_of(q_ref.shape[0]):
            query = q_ref[start : start + tile, h * DH : (h + 1) * DH]
            probs, cap_tanh = softmax_tile(
                k_ref[:upto, :], query, mask_ref[:upto, start : start + tile]
            )
            grad_rows = grad[start : start + tile, :]
            grad_probs = dot(v_ref[:upto, :], grad_rows, NT)
            delta = jnp.sum(probs * grad_probs, axis=0, keepdims=True)
            scores = probs * (grad_probs - delta) * (SCALE - SCALE * (cap_tanh * cap_tanh))
            scores = scores.astype(BF16)
            av_ref[:upto, :] += dot(probs.astype(BF16), grad_rows, NN)
            ak_ref[:upto, :] += dot(scores, query, NN)
            grad_query = dot(key_t[:, :upto], scores, NN).T
            gq_ref[start : start + tile, h * DH : (h + 1) * DH] = grad_query.astype(BF16)
    gk_ref[...] = ak_ref[...].astype(BF16)
    gv_ref[...] = av_ref[...].astype(BF16)


def backward(sc, k, block, own, other, column, before, lay, through):
    queries, keys, values, seg_row, seg_col = block
    length = queries.shape[0]
    per = lay.heads_shard
    groups = 2 * per // REPEAT
    at = lay.at_z + k

    def whole(i, sc):
        return (0, sc[at] * groups + i)

    heads = (length, REPEAT * DH), whole
    one = (length, DH), whole
    return call(
        functools.partial(backward_body, per),
        sc,
        (groups,),
        [
            (queries, *heads),
            (keys, *one),
            (values, *one),
            (seg_row, (1, length), first),
            (seg_col, (length, 1), first),
            (own, (length, lay.rows), lambda i, sc: (0, column)),
            (other, (length, lay.rows), lambda i, sc: (0, column)),
        ],
        [(queries.shape, BF16, *heads), (keys.shape, BF16, *one), (values.shape, BF16, *one)],
        scratch=[
            pltpu.VMEM((length, length), F32),
            pltpu.VMEM((length, DH), F32),
            pltpu.VMEM((length, DH), F32),
        ],
        before=before,
        through=through,
    )


def adam_body(pieces, tokens, sc_ref, m1_ref, m2_ref, *refs):
    out_ref = refs[-1]
    n = pl.program_id(0)

    def step(piece_ref):
        gradient = piece_ref[...].astype(F32) * (1.0 / tokens)
        moment_one = 0.9 * m1_ref[...] + 0.1 * gradient
        moment_two = 0.95 * m2_ref[...] + 0.05 * gradient * gradient
        out_ref[...] = moment_one / (jnp.sqrt(moment_two) + 1e-08)

    for p in range(pieces):
        pl.when(n == p)(functools.partial(step, refs[p]))


def adam(sc, pieces, first_moment, second_moment, tokens, lay, before, through):
    rows, width = pieces[0][0].shape
    count = len(pieces)
    columns = [lay.at_place(flips) for _, flips in pieces]

    def at(n, sc):
        row = sc[columns[0]]
        for p in range(1, count):
            row = jnp.where(n == p, sc[columns[p]], row)
        return (row, 0)

    block = (rows, width)
    return call(
        functools.partial(adam_body, count, tokens),
        sc,
        (count,),
        [(first_moment, block, at), (second_moment, block, at)]
        + [(x, block, first) for x, _ in pieces],
        [(first_moment.shape, F32, block, at)],
        before=before,
        through=through,
        mib=60,
    )


class Layout:
    def __init__(self, replicas, shards, rows):
        self.replicas, self.shards, self.rows = replicas, shards, rows
        self.z = shards // 2
        self.bits = replicas.bit_length() - 1
        self.heads_shard = HEADS // shards
        self.order = [0] + list(range(1, self.z, 2)) + list(range(self.z - 2, 0, -2))
        self.place = [self.order.index(z) for z in range(self.z)]
        self.at_z = 1
        self.at_piece = self.at_z + self.z
        table = []
        for r in range(replicas):
            for s in range(shards):
                z, core = s // 2, s % 2
                zs = [self.order[(self.place[z] - k) % self.z] for k in range(self.z)]
                bits = [(r >> self.bit_of(core, n)) & 1 for n in range(self.bits)]
                b = 2 * bits[0]
                here = sum(bit << n for n, bit in enumerate(bits[::-1]))
                places = [here ^ flips for flips in range(replicas)]
                table.append([core] + zs + [b, b + 1, 2 - b, 3 - b] + bits + places)
        self.table = np.array(table, np.int32)

    def bit_of(self, core, n):
        return self.bits - 1 - n if core else n

    def at_bit(self, n):
        return self.at_piece + 4 + n

    def at_place(self, flips):
        code = sum(int(f) << n for n, f in enumerate(flips[::-1]))
        return self.at_piece + 4 + self.bits + code

    def sibling(self, x):
        return lax.ppermute(x, "shard", [(s, s ^ 1) for s in range(self.shards)])

    def onward(self, x):
        perm = []
        for p in range(self.z):
            a, b = self.order[p], self.order[(p + 1) % self.z]
            perm += [(2 * a + core, 2 * b + core) for core in range(2)]
        return lax.ppermute(x, "shard", perm)

    def across(self, x, n):
        perm = []
        for r in range(self.replicas):
            for s in range(self.shards):
                partner = r ^ (1 << self.bit_of(s % 2, n))
                perm.append((r * self.shards + s, partner * self.shards + s))
        return lax.ppermute(x, ("replica", "shard"), perm)


def per_device(queries, keys, values, segments, out_weight, upstream, first_moment, second_moment):
    length, width = upstream.shape
    lay = Layout(lax.axis_size("replica"), lax.axis_size("shard"), out_weight.shape[0])
    tokens = length * lay.replicas * lay.shards
    device = lax.axis_index("replica") * lay.shards + lax.axis_index("shard")
    sc = lax.dynamic_index_in_dim(jnp.asarray(lay.table), device, 0, keepdims=False)
    block = (queries, keys, values, segments, segments.reshape(length, 1))

    box = {}
    terms = {}
    gc = {}
    grads = ()

    def run(function, *args, held=(), **more):
        names = ["token", *held]
        outs, handed = function(*args, through=[box[n] for n in names], **more)
        box.update(zip(names, handed))
        return outs

    def do_product(k, held=()):
        own, other = contexts[k]
        box["send", k], keep = run(
            product, sc, own, other, upstream, upstream_other, lay, held=held
        )
        terms[k] = [keep]

    def send(k):
        terms[k].append(lay.across(box["send", k], len(terms[k]) - 1))

    def do_halve(k, held=()):
        for stage in range(1, lay.bits):
            (box["send", k],) = run(combine, sc, terms[k], None, True, lay, held=held)
            held = ()
            if stage < lay.bits - 1:
                send(k)

    def do_sum(k, held=()):
        (box["sum", k],) = run(combine, sc, terms[k], box.get(("part", k)), False, lay, held=held)

    def pass_sum(k):
        box["part", (k + 1) % lay.z] = lay.onward(box["sum", k])

    def pass_weights(k):
        if k + 1 < lay.z:
            box["ring", k + 1] = lay.onward(box["ring", k])

    def cross_weights(k):
        box["cross", k] = lay.across(box["ring", k], 0)

    def do_grad_context(ks, held=()):
        sets = [[box["ring", k], box["cross", k]] if k else [out_weight] for k in ks]
        own, box["away", ks[0]] = run(
            grad_context, sc, upstream, upstream_other, sets, lay, held=held
        )
        for n, k in enumerate(ks):
            gc[k] = own, ks[0], n

    def swap_grad_context(k):
        box["gc", k] = lay.sibling(box["away", k])

    def do_backward(k, held=()):
        nonlocal grads
        own, base, column = gc[k]
        grads = run(backward, sc, k, block, own, box["gc", base], column, grads, lay, held=held)

    upstream_other = lay.sibling(upstream)
    box["ring", 1], box["token"] = cut(sc, out_weight, lay)[0]
    box["ring", 1] = lay.onward(box["ring", 1])

    late = [*range(2, lay.z), 0]
    rows = lay.rows
    contexts = {}
    (both_sides,) = run(forward, sc, [1], [0, 1], block, lay)
    contexts[1] = (both_sides, 1), (lay.sibling(both_sides[:rows]), 0)
    (away,) = run(forward, sc, late, [0], block, lay)
    away = lay.sibling(away)
    do_product(1)
    send(1)
    (stay,) = run(forward, sc, late, [1], block, lay)
    for n, k in enumerate(late):
        contexts[k] = (stay, n), (away, n)
    do_product(2)
    send(2)
    do_halve(1, held=[("ring", 1)])
    pass_weights(1)
    cross_weights(1)
    send(1)
    do_product(3)
    send(3)
    do_halve(2)
    send(2)
    do_product(0)
    do_grad_context([0, 1])
    swap_grad_context(0)
    do_sum(1, held=[("ring", 2), ("gc", 0)])
    pass_sum(1)
    pass_weights(2)
    cross_weights(2)
    do_backward(0)
    do_halve(3)
    send(3)
    do_backward(1)
    do_sum(2, held=[("send", 0)])
    pass_sum(2)
    send(0)
    for k in range(4, lay.z):
        do_product(k, held=[("ring", k - 1)])
        pass_weights(k - 1)
        cross_weights(k - 1)
        send(k)
        do_halve(k)
        send(k)
    last = lay.z - 1
    for k in range(2, last):
        do_grad_context([k])
        swap_grad_context(k)
        do_backward(k)
    do_halve(0, held=[("ring", last)])
    send(0)
    cross_weights(last)
    for k in range(3, lay.z):
        do_sum(k)
        pass_sum(k)
    do_grad_context([last])
    swap_grad_context(last)
    do_sum(0)

    have = [(box["sum", 0], (False,) * lay.bits)]

    def spread(n, piece):
        x, flips = piece
        return lay.across(x, n), flips[:n] + (True,) + flips[n + 1 :]

    moments = first_moment, second_moment, tokens, lay
    direct = [spread(n, have[0]) for n in range(lay.bits - 1, -1, -1)]
    do_backward(last)
    near = [have[0], *direct]
    have = [have[0], direct[0]]
    done = {flips for _, flips in near}
    far = []
    for n in range(lay.bits - 2, -1, -1):
        more = []
        for x, flips in have:
            flips = flips[:n] + (True,) + flips[n + 1 :]
            if flips in done:
                more += [p for p in near if p[1] == flips]
            else:
                more.append((lay.across(x, n), flips))
                far.append(more[-1])
        have += more
    step = run(adam, sc, near, *moments, before=())
    step = run(adam, sc, far, *moments, before=step)
    return (*grads, *step)


def solution(mesh):
    both = P(("replica", "shard"), None)
    shard = P("shard", None)
    return jax.shard_map(
        per_device,
        mesh=mesh,
        in_specs=(both, both, both, both, shard, both, shard, shard),
        out_specs=(both, both, both, shard),
        check_vma=False,
    )
```

time: 286 us -> 200 us (0.70)
  Pallas kernels: 156 us -> 106 us
  between operations: 19.6 us -> 0.96 us
  waiting for transfers between devices: 61 us -> 50.3 us
  local copies, waits for them, and re-layouts: 17.1 us -> 8.95 us
    pallas_call x27 -> x25, Pallas kernels: 156 us -> 106 us  [call(): pl.pallas_call(kernel, grid_spec=pltpu.PrefetchScalarGridSpec(num_scalar_...]
    ppermute x24 -> x14, waiting for transfers between devices: 44.1 us -> 32.9 us  [across(): return lax.ppermute(x, ('replica', 'shard'), perm)]
    ppermute x3 -> x6, starting transfers between devices: 2.25 us -> 13.2 us  [onward(): return lax.ppermute(x, 'shard', perm)]
    ppermute x24 -> x14, starting transfers between devices: 26.4 us -> 17.5 us  [across(): return lax.ppermute(x, ('replica', 'shard'), perm)]
    unnamed x70 -> x32, local copies, waits for them, and re-layouts: 13.2 us -> 7.42 us
    ppermute x3 -> x6, waiting for transfers between devices: 14.5 us -> 15.6 us  [onward(): return lax.ppermute(x, 'shard', perm)]
  transfers between devices with their start and end apart: 34 -> 26, of which waited for: 5 -> 10; matrix products, arithmetic and copies ran while one was open for 1% -> 1% of each run, Pallas kernels for 50% -> 51%
where the time goes in v5:
time: 200 us; the launch traced here: 199 us
  Pallas kernels  106 us (53%)
  waiting for transfers between devices  50.3 us (25%)
  starting transfers between devices  32.1 us (16%)
  local copies, waits for them, and re-layouts  8.95 us (4%)
    pallas_call x25, Pallas kernels, call(): pl.pallas_call(kernel, grid_spec=pltpu.PrefetchScalarGridSpec(num_scalar_...  106 us
    ppermute x14, waiting for transfers between devices, across(): return lax.ppermute(x, ('replica', 'shard'), perm)  32.9 us
    ppermute x14, starting transfers between devices, across(): return lax.ppermute(x, ('replica', 'shard'), perm)  17.5 us
    ppermute x6, waiting for transfers between devices, onward(): return lax.ppermute(x, 'shard', perm)  15.6 us
    ppermute x6, starting transfers between devices, onward(): return lax.ppermute(x, 'shard', perm)  13.2 us
    unnamed x32, local copies, waits for them, and re-layouts  7.42 us
  transfers between devices with their start and end apart: 26, of which 10 were waited for; matrix products, arithmetic and copies ran while one was open for 1% of the time, Pallas kernels for 51%

profile of v5, /device:TPU:0, one launch (start us, length us, event | category | flops | bytes accessed | tf_op | source)
XLA Modules:
  0.0 198.8 jit_solution(14396121446323107956)
XLA Ops:
  0.6 0.5 collective-permute-start
  1.1 0.7 dynamic-slice_bitcast_fusion.sc_ref
  1.8 1.7 copy-done.5
  3.5 0.6 shard_map.120
  4.2 1.0 copy-done.11
  5.2 0.8 copy.58.refs_4_
  6.0 1.2 copy-done.1
  7.2 1.2 copy-done.3
  8.5 3.7 %shard_map.121 = (bf16[512,512]{1,0:T(8,128)(2,1)S(1)}, f32[8,128]{1,0:T(8,128)S(1)}) custom-call(s32[15]{0:T(128)S(1)} %dynamic-slice_bitcast_fusion.sc_ref, bf16[512,2048]{1,0:T(8,128)(2,1)S(1)} %copy-done, bf16[512,1024]{1,0:T(8,128)(2,1)S(1)} %copy-done.1, bf16[512,1024]{1,0:T(8,128)(2,1)S(1)} %copy-done.3, ...), custom_call_target="tpu_custom_call", output_to_operand_aliasing={{1}: (6, {})} | custom-call | flops 1 | bytes 1 | tf_op jit(solution)/shard_map/pallas_call | solution.py:41
  12.3 3.0 %collective-permute-start.5 = (bf16[256,2304]{1,0:T(8,128)(2,1)}, bf16[256,2304]{1,0:T(8,128)(2,1)S(1)}, u32[]{:S(2)}, u32[]{:S(2)}) collective-permute-start(bf16[256,2304]{1,0:T(8,128)(2,1)} %copy-done.11), channel_id=1, source_target_pairs={{0,2},{1,3},{2,6},{3,7},{6,4},{7,5},{4,0},{5,1},{8,10},{9,11},{10,... | collective-permute-start | bytes 3538952 | tf_op jit(solution)/shard_map/ppermute | solution.py:423
  15.3 5.2 %shard_map.122 = (bf16[768,512]{1,0:T(8,128)(2,1)S(1)}, f32[8,128]{1,0:T(8,128)S(1)}) custom-call(s32[15]{0:T(128)S(1)} %dynamic-slice_bitcast_fusion.sc_ref, bf16[512,2048]{1,0:T(8,128)(2,1)S(1)} %copy-done, bf16[512,1024]{1,0:T(8,128)(2,1)S(1)} %copy-done.1, bf16[512,1024]{1,0:T(8,128)(2,1)S(1)} %copy-done.3, ...), custom_call_target="tpu_custom_call", output_to_operand_aliasing={{1}: (6, {})} | custom-call | flops 1 | bytes 1 | tf_op jit(solution)/shard_map/pallas_call | solution.py:41
  20.6 6.3 %shard_map.123 = (bf16[128,4608]{1,0:T(8,128)(2,1)S(1)}, bf16[128,4608]{1,0:T(8,128)(2,1)S(1)}, f32[8,128]{1,0:T(8,128)S(1)}) custom-call(s32[15]{0:T(128)S(1)} %dynamic-slice_bitcast_fusion.sc_ref, bf16[512,512]{1,0:T(8,128)(2,1)S(1)} %get-tuple-element.74.refs_0_, ...), custom_call_target="tpu_custom_call", output_to_operand_aliasing={{2}: (5, {})} | custom-call | flops 1 | bytes 1 | tf_op jit(solution)/shard_map/pallas_call | solution.py:41
  26.9 1.6 collective-permute-start.4
  28.5 5.2 %shard_map.124 = (bf16[768,512]{1,0:T(8,128)(2,1)S(1)}, f32[8,128]{1,0:T(8,128)S(1)}) custom-call(s32[15]{0:T(128)S(1)} %dynamic-slice_bitcast_fusion.sc_ref, bf16[512,2048]{1,0:T(8,128)(2,1)S(1)} %copy-done, bf16[512,1024]{1,0:T(8,128)(2,1)S(1)} %copy-done.2, bf16[512,1024]{1,0:T(8,128)(2,1)S(1)} %copy-done.3, ...), custom_call_target="tpu_custom_call", output_to_operand_aliasing={{1}: (6, {})} | custom-call | flops 1 | bytes 1 | tf_op jit(solution)/shard_map/pallas_call | solution.py:41
  33.7 6.3 %shard_map.125 = (bf16[128,4608]{1,0:T(8,128)(2,1)S(1)}, bf16[128,4608]{1,0:T(8,128)(2,1)S(1)}, f32[8,128]{1,0:T(8,128)S(1)}) custom-call(s32[15]{0:T(128)S(1)} %dynamic-slice_bitcast_fusion.sc_ref, bf16[768,512]{1,0:T(8,128)(2,1)S(1)} %get-tuple-element.78.refs_0_, ...), custom_call_target="tpu_custom_call", output_to_operand_aliasing={{2}: (5, {})} | custom-call | flops 1 | bytes 1 | tf_op jit(solution)/shard_map/pallas_call | solution.py:41
  40.0 1.1 collective-permute-start.3
  41.1 1.7 collective-permute-done.5.refs_3_
  42.7 0.4 collective-permute-done.4.refs_1_
  43.2 0.7 shard_map.126
  43.9 1.6 collective-permute-start.8
  45.4 2.6 %collective-permute-start.9 = (bf16[256,2304]{1,0:T(8,128)(2,1)S(1)}, bf16[256,2304]{1,0:T(8,128)(2,1)S(1)}, u32[]{:S(2)}, u32[]{:S(2)}) collective-permute-start(bf16[256,2304]{1,0:T(8,128)(2,1)S(1)} %get-tuple-element.93.refs_3_), channel_id=1, source_target_pairs={{0,2},{1,3},{2,6},{3,7},{6,4},{7,5},{4,0},{5,1},{8,10},{9,11},{10,... | collective-permute-start | bytes 3538952 | tf_op jit(solution)/shard_map/ppermute | solution.py:423
  48.0 6.3 %shard_map.127 = (bf16[128,4608]{1,0:T(8,128)(2,1)S(1)}, bf16[128,4608]{1,0:T(8,128)(2,1)S(1)}, f32[8,128]{1,0:T(8,128)S(1)}) custom-call(s32[15]{0:T(128)S(1)} %dynamic-slice_bitcast_fusion.sc_ref, bf16[768,512]{1,0:T(8,128)(2,1)S(1)} %get-tuple-element.78.refs_0_, ...), custom_call_target="tpu_custom_call", output_to_operand_aliasing={{2}: (5, {})} | custom-call | flops 1 | bytes 1 | tf_op jit(solution)/shard_map/pallas_call | solution.py:41
  54.3 0.6 collective-permute-start.12
  54.9 1.5 collective-permute-start.7
  56.4 0.5 collective-permute-done.3.refs_1_
  56.9 0.7 shard_map.128
  57.6 6.3 %shard_map.129 = (bf16[128,4608]{1,0:T(8,128)(2,1)S(1)}, bf16[128,4608]{1,0:T(8,128)(2,1)S(1)}, f32[8,128]{1,0:T(8,128)S(1)}) custom-call(s32[15]{0:T(128)S(1)} %dynamic-slice_bitcast_fusion.sc_ref, bf16[768,512]{1,0:T(8,128)(2,1)S(1)} %get-tuple-element.78.refs_0_, ...), custom_call_target="tpu_custom_call", output_to_operand_aliasing={{2}: (5, {})} | custom-call | flops 1 | bytes 1 | tf_op jit(solution)/shard_map/pallas_call | solution.py:41
  63.9 11.3 %collective-permute-done.8.refs_4_ = bf16[256,2304]{1,0:T(8,128)(2,1)S(1)} collective-permute-done((bf16[256,2304]{1,0:T(8,128)(2,1)S(1)}, bf16[256,2304]{1,0:T(8,128)(2,1)S(1)}, u32[]{:S(2)}, u32[]{:S(2)}) %collective-permute-start.8) | collective-permute-done | bytes 1179680 | tf_op jit(solution)/shard_map/ppermute | solution.py:431
  75.2 10.4 %shard_map.130 = (bf16[512,512]{1,0:T(8,128)(2,1)S(1)}, bf16[512,512]{1,0:T(8,128)(2,1)S(1)}, f32[8,128]{1,0:T(8,128)S(1)}) custom-call(s32[15]{0:T(128)S(1)} %dynamic-slice_bitcast_fusion.sc_ref, bf16[512,4608]{1,0:T(8,128)(2,1)S(1)} %bitcast.4, bf16[512,4608]{1,0:T(8,128)(2,1)} %collective-permute-done.refs_3_.refs_1_, ...), custom_call_target="tpu_custom_call", output_to_operand_aliasing={{2}: (6, {})} | custom-call | flops 1 | bytes 1 | tf_op jit(solution)/shard_map/pallas_call | solution.py:41
  85.7 1.6 collective-permute-start.6
  87.6 0.8 shard_map.131
  88.4 2.6 %collective-permute-start.11 = (bf16[64,4608]{1,0:T(8,128)(2,1)S(1)}, bf16[64,4608]{1,0:T(8,128)(2,1)S(1)}, u32[]{:S(2)}, u32[]{:S(2)}) collective-permute-start(bf16[64,4608]{1,0:T(8,128)(2,1)S(1)} %get-tuple-element.97), channel_id=1, source_target_pairs={{0,2},{1,3},{2,6},{3,7},{6,4},{7,5},{4,0},{5,1},{8,10},{9,11},{10,... | collective-permute-start | bytes 1769480 | tf_op jit(solution)/shard_map/ppermute | solution.py:423
  91.0 1.1 collective-permute-start.14
  92.5 6.3 %shard_map.132 = (bf16[512,2048]{1,0:T(8,128)(2,1)}, bf16[512,1024]{1,0:T(8,128)(2,1)}, bf16[512,1024]{1,0:T(8,128)(2,1)}, f32[8,128]{1,0:T(8,128)S(1)}) custom-call(s32[15]{0:T(128)S(1)} %dynamic-slice_bitcast_fusion.sc_ref, bf16[512,2048]{1,0:T(8,128)(2,1)S(1)} %copy-done, bf16[512,1024]{1,0:T(8,128)(2,1)S(1)} %copy-done.2, ...), custom_call_target="tpu_custom_call", output_to_operand_aliasing={{3}: (8, {})} | custom-call | flops 1 | bytes 1 | tf_op jit(solution)/shard_map/pallas_call | solution.py:41
  98.8 0.7 shard_map.133
  99.5 6.3 %shard_map.134 = (bf16[512,2048]{1,0:T(8,128)(2,1)}, bf16[512,1024]{1,0:T(8,128)(2,1)}, bf16[512,1024]{1,0:T(8,128)(2,1)}, f32[8,128]{1,0:T(8,128)S(1)}) custom-call(s32[15]{0:T(128)S(1)} %dynamic-slice_bitcast_fusion.sc_ref, bf16[512,2048]{1,0:T(8,128)(2,1)S(1)} %copy-done, ...), custom_call_target="tpu_custom_call", output_to_operand_aliasing={{0}: (8, {}), {1}: (9, {}), {2}: (10, {}), {3}: (11, {})} | custom-call | flops 1 | bytes 1 | tf_op jit(solution)/shard_map/pallas_call | solution.py:41
  105.8 0.8 shard_map.135
  106.7 1.0 collective-permute-start.13
  107.8 6.5 %shard_map.136 = (bf16[512,256]{1,0:T(8,128)(2,1)S(1)}, bf16[512,256]{1,0:T(8,128)(2,1)S(1)}, f32[8,128]{1,0:T(8,128)S(1)}) custom-call(s32[15]{0:T(128)S(1)} %dynamic-slice_bitcast_fusion.sc_ref, bf16[512,4608]{1,0:T(8,128)(2,1)S(1)} %bitcast.4, bf16[512,4608]{1,0:T(8,128)(2,1)} %collective-permute-done.refs_3_.refs_1_, ...), custom_call_target="tpu_custom_call", output_to_operand_aliasing={{2}: (5, {})} | custom-call | flops 1 | bytes 1 | tf_op jit(solution)/shard_map/pallas_call | solution.py:41
  114.3 0.7 collective-permute-start.15
  115.0 1.5 collective-permute-start.18
  116.5 2.6 %collective-permute-start.19 = (bf16[64,4608]{1,0:T(8,128)(2,1)S(1)}, bf16[64,4608]{1,0:T(8,128)(2,1)S(1)}, u32[]{:S(2)}, u32[]{:S(2)}) collective-permute-start(bf16[64,4608]{1,0:T(8,128)(2,1)S(1)} %get-tuple-element.122), channel_id=1, source_target_pairs={{0,2},{1,3},{2,6},{3,7},{6,4},{7,5},{4,0},{5,1},{8,10},{9,11},{10,... | collective-permute-start | bytes 1769480 | tf_op jit(solution)/shard_map/ppermute | solution.py:423
  119.1 6.3 %shard_map.137 = (bf16[512,2048]{1,0:T(8,128)(2,1)}, bf16[512,1024]{1,0:T(8,128)(2,1)}, bf16[512,1024]{1,0:T(8,128)(2,1)}, f32[8,128]{1,0:T(8,128)S(1)}) custom-call(s32[15]{0:T(128)S(1)} %dynamic-slice_bitcast_fusion.sc_ref, bf16[512,2048]{1,0:T(8,128)(2,1)S(1)} %copy-done, ...), custom_call_target="tpu_custom_call", output_to_operand_aliasing={{0}: (8, {}), {1}: (9, {}), {2}: (10, {}), {3}: (11, {})} | custom-call | flops 1 | bytes 1 | tf_op jit(solution)/shard_map/pallas_call | solution.py:41
  125.4 5.4 %collective-permute-done.16.refs_3_ = bf16[256,2304]{1,0:T(8,128)(2,1)S(1)} collective-permute-done((bf16[256,2304]{1,0:T(8,128)(2,1)S(1)}, bf16[256,2304]{1,0:T(8,128)(2,1)S(1)}, u32[]{:S(2)}, u32[]{:S(2)}) %collective-permute-start.16) | collective-permute-done | bytes 1179680 | tf_op jit(solution)/shard_map/ppermute | solution.py:423
  130.8 0.7 shard_map.138
  131.5 1.1 collective-permute-start.17
  132.6 1.5 collective-permute-start.21
  134.1 8.5 %collective-permute-done.19.refs_3_ = bf16[64,4608]{1,0:T(8,128)(2,1)S(1)} collective-permute-done((bf16[64,4608]{1,0:T(8,128)(2,1)S(1)}, bf16[64,4608]{1,0:T(8,128)(2,1)S(1)}, u32[]{:S(2)}, u32[]{:S(2)}) %collective-permute-start.19) | collective-permute-done | bytes 589856 | tf_op jit(solution)/shard_map/ppermute | solution.py:423
  142.6 0.8 shard_map.139
  143.4 2.0 collective-permute-start.22
  145.4 7.4 %collective-permute-done.17.refs_3_ = bf16[256,2304]{1,0:T(8,128)(2,1)S(1)} collective-permute-done((bf16[256,2304]{1,0:T(8,128)(2,1)S(1)}, bf16[256,2304]{1,0:T(8,128)(2,1)S(1)}, u32[]{:S(2)}, u32[]{:S(2)}) %collective-permute-start.17) | collective-permute-done | bytes 1179680 | tf_op jit(solution)/shard_map/ppermute | solution.py:431
  152.8 6.5 %shard_map.140 = (bf16[512,256]{1,0:T(8,128)(2,1)S(1)}, bf16[512,256]{1,0:T(8,128)(2,1)S(1)}, f32[8,128]{1,0:T(8,128)S(1)}) custom-call(s32[15]{0:T(128)S(1)} %dynamic-slice_bitcast_fusion.sc_ref, bf16[512,4608]{1,0:T(8,128)(2,1)S(1)} %bitcast.4, bf16[512,4608]{1,0:T(8,128)(2,1)} %collective-permute-done.refs_3_.refs_1_, ...), custom_call_target="tpu_custom_call", output_to_operand_aliasing={{2}: (5, {})} | custom-call | flops 1 | bytes 1 | tf_op jit(solution)/shard_map/pallas_call | solution.py:41
  159.4 0.8 shard_map.141
  160.2 1.4 collective-permute-start.23
  161.6 1.1 collective-permute-start.25
  162.7 13.2 %collective-permute-done.23.refs_3_ = bf16[64,4608]{1,0:T(8,128)(2,1)} collective-permute-done((bf16[64,4608]{1,0:T(8,128)(2,1)S(1)}, bf16[64,4608]{1,0:T(8,128)(2,1)}, u32[]{:S(2)}, u32[]{:S(2)}) %collective-permute-start.23) | collective-permute-done | bytes 589856 | tf_op jit(solution)/shard_map/ppermute | solution.py:431
  175.9 0.9 collective-permute-start.24
  176.7 1.5 collective-permute-done.20.refs_6_
  178.3 6.3 %shard_map.142 = (bf16[512,2048]{1,0:T(8,128)(2,1)}, bf16[512,1024]{1,0:T(8,128)(2,1)}, bf16[512,1024]{1,0:T(8,128)(2,1)}, f32[8,128]{1,0:T(8,128)S(1)}) custom-call(s32[15]{0:T(128)S(1)} %dynamic-slice_bitcast_fusion.sc_ref, bf16[512,2048]{1,0:T(8,128)(2,1)S(1)} %copy-done, ...), custom_call_target="tpu_custom_call", output_to_operand_aliasing={{0}: (8, {}), {1}: (9, {}), {2}: (10, {}), {3}: (11, {})} | custom-call | flops 1 | bytes 1 | tf_op jit(solution)/shard_map/pallas_call | solution.py:41
  184.6 0.6 copy-done.7
  185.2 0.8 copy-done.13
  186.0 7.8 %shard_map.143 = (f32[256,4608]{1,0:T(8,128)}, f32[8,128]{1,0:T(8,128)}) custom-call(s32[15]{0:T(128)} %copy-done.9, f32[256,4608]{1,0:T(8,128)} %refs_0_.25, f32[256,4608]{1,0:T(8,128)} %refs_1_.17, bf16[64,4608]{1,0:T(8,128)(2,1)} %copy-done.8, bf16[64,4608]{1,0:T(8,128)(2,1)} %collective-permute-done.23.refs_3_, ...), custom_call_target="tpu_custom_call", output_to_operand_aliasing={{1}: (6, {})} | custom-call | flops 1 | bytes 1 | tf_op jit(solution)/shard_map/pallas_call | solution.py:41
  193.8 0.8 copy-done.12
  194.6 4.2 %shard_map.144 = (f32[256,4608]{1,0:T(8,128)}, f32[8,128]{1,0:T(8,128)}) custom-call(s32[15]{0:T(128)} %copy-done.9, f32[256,4608]{1,0:T(8,128)} %refs_0_.25, f32[256,4608]{1,0:T(8,128)} %refs_1_.17, bf16[64,4608]{1,0:T(8,128)(2,1)} %copy-done.12, f32[256,4608]{1,0:T(8,128)} %get-tuple-element.139.refs_3_, ...), custom_call_target="tpu_custom_call", output_to_operand_aliasing={{0}: (4, {}), {1}: (5, {})} | custom-call | flops 1 | bytes 1 | tf_op jit(solution)/shard_map/pallas_call | solution.py:41
  (49 shorter events, 1.1 us)
Async XLA Ops:
  0.6 19.9 %collective-permute-start = (bf16[512,4608]{1,0:T(8,128)(2,1)}, bf16[512,4608]{1,0:T(8,128)(2,1)}, u32[]{:S(2)}, u32[]{:S(2)}) collective-permute-start(bf16[512,4608]{1,0:T(8,128)(2,1)} %refs_0_.22), channel_id=1, source_target_pairs={{0,1},{1,0},{2,3},{3,2},{4,5},{5,4},{6,7},{7,6},{8,9},{9,8},{10,11... | collective-permute-start | bytes 14155784 | tf_op jit(solution)/shard_map/ppermute | solution.py:416
  1.8 1.7 copy-start.5
  3.5 174.8 %copy-start.9 = (s32[15]{0:T(128)}, s32[15]{0:T(128)S(1)}, u32[]{:S(2)}) copy-start(s32[15]{0:T(128)S(1)} %dynamic-slice_bitcast_fusion.sc_ref) | copy-start | bytes 184
  3.5 2.5 %copy-start = (bf16[512,2048]{1,0:T(8,128)(2,1)S(1)}, bf16[512,2048]{1,0:T(8,128)(2,1)}, u32[]{:S(2)}) copy-start(bf16[512,2048]{1,0:T(8,128)(2,1)} %refs_0_.23) | copy-start | bytes 6291460
  3.5 2.5 %copy-start.10 = (s32[1,512]{1,0:T(1,128)S(1)}, s32[1,512]{1,0:T(1,128)}, u32[]{:S(2)}) copy-start(s32[1,512]{1,0:T(1,128)} %refs_3_.13) | copy-start | bytes 6148
  3.5 17.0 %slice-start = ((s8[4718592]{0:T(1024)(128)(4,1)}), s8[524288]{0:T(1024)(128)(4,1)S(1)}, s32[]{:S(2)}) async-start(s8[4718592]{0:T(1024)(128)(4,1)} %bitcast.3), calls=%async_computation | async-start | bytes 1048576
  4.1 1.0 copy-start.11
  6.0 1.2 copy-start.1
  7.2 1.2 copy-start.3
  8.5 12.1 %slice-start.1 = ((s8[4718592]{0:T(1024)(128)(4,1)}), s8[4194304]{0:T(1024)(128)(4,1)S(1)}, s32[]{:S(2)}) async-start(s8[4718592]{0:T(1024)(128)(4,1)} %bitcast.3), calls=%async_computation.1 | async-start | bytes 8388608
  12.2 8.4 %collective-permute-start.1 = (bf16[256,512]{1,0:T(8,128)(2,1)S(1)}, bf16[256,512]{1,0:T(8,128)(2,1)S(1)}, u32[]{:S(2)}, u32[]{:S(2)}) collective-permute-start(bf16[256,512]{1,0:T(8,128)(2,1)S(1)} %slice.3), channel_id=1, source_target_pairs={{0,1},{1,0},{2,3},{3,2},{4,5},{5,4},{6,7},{7,6},{8,9},{9,8},{10,11... | collective-permute-start | bytes 786440 | tf_op jit(solution)/shard_map/ppermute | solution.py:416
  12.3 30.4 %collective-permute-start.5 = (bf16[256,2304]{1,0:T(8,128)(2,1)}, bf16[256,2304]{1,0:T(8,128)(2,1)S(1)}, u32[]{:S(2)}, u32[]{:S(2)}) collective-permute-start(bf16[256,2304]{1,0:T(8,128)(2,1)} %copy-done.11), channel_id=1, source_target_pairs={{0,2},{1,3},{2,6},{3,7},{6,4},{7,5},{4,0},{5,1},{8,10},{9,11},{10,... | collective-permute-start | bytes 3538952 | tf_op jit(solution)/shard_map/ppermute | solution.py:423
  20.6 7.9 %copy-start.2 = (bf16[512,1024]{1,0:T(8,128)(2,1)S(1)}, bf16[512,1024]{1,0:T(8,128)(2,1)}, u32[]{:S(2)}) copy-start(bf16[512,1024]{1,0:T(8,128)(2,1)} %refs_1_.15) | copy-start | bytes 3145732
  26.9 16.3 %collective-permute-start.4 = (bf16[128,4608]{1,0:T(8,128)(2,1)S(1)}, bf16[128,4608]{1,0:T(8,128)(2,1)S(1)}, u32[]{:S(2)}, u32[]{:S(2)}) collective-permute-start(bf16[128,4608]{1,0:T(8,128)(2,1)S(1)} %get-tuple-element.84), channel_id=1, source_target_pairs={{0,8},{1,17},{2,10},{3,19},{4,12},{5,21},{6,14},{7,23},{8,0},{9,25... | collective-permute-start | bytes 3538952 | tf_op jit(solution)/shard_map/ppermute | solution.py:431
  28.5 5.2 %collective-permute-start.2 = (bf16[768,512]{1,0:T(8,128)(2,1)S(1)}, bf16[768,512]{1,0:T(8,128)(2,1)S(1)}, u32[]{:S(2)}, u32[]{:S(2)}) collective-permute-start(bf16[768,512]{1,0:T(8,128)(2,1)S(1)} %get-tuple-element.79), channel_id=1, source_target_pairs={{0,1},{1,0},{2,3},{3,2},{4,5},{5,4},{6,7},{7,6},{8,9},{9,8},{10,11... | collective-permute-start | bytes 2359304 | tf_op jit(solution)/shard_map/ppermute | solution.py:416
  40.0 16.9 %collective-permute-start.3 = (bf16[128,4608]{1,0:T(8,128)(2,1)S(1)}, bf16[128,4608]{1,0:T(8,128)(2,1)S(1)}, u32[]{:S(2)}, u32[]{:S(2)}) collective-permute-start(bf16[128,4608]{1,0:T(8,128)(2,1)S(1)} %get-tuple-element.82), channel_id=1, source_target_pairs={{0,8},{1,17},{2,10},{3,19},{4,12},{5,21},{6,14},{7,23},{8,0},{9,25... | collective-permute-start | bytes 3538952 | tf_op jit(solution)/shard_map/ppermute | solution.py:431
  43.9 31.4 %collective-permute-start.8 = (bf16[256,2304]{1,0:T(8,128)(2,1)S(1)}, bf16[256,2304]{1,0:T(8,128)(2,1)S(1)}, u32[]{:S(2)}, u32[]{:S(2)}) collective-permute-start(bf16[256,2304]{1,0:T(8,128)(2,1)S(1)} %get-tuple-element.93.refs_3_), channel_id=1, source_target_pairs={{0,8},{1,17},{2,10},{3,19},{4,12},{5,21},{6,14},{7,23},{8,0},{9,25... | collective-permute-start | bytes 3538952 | tf_op jit(solution)/shard_map/ppermute | solution.py:431
  45.4 41.9 %collective-permute-start.9 = (bf16[256,2304]{1,0:T(8,128)(2,1)S(1)}, bf16[256,2304]{1,0:T(8,128)(2,1)S(1)}, u32[]{:S(2)}, u32[]{:S(2)}) collective-permute-start(bf16[256,2304]{1,0:T(8,128)(2,1)S(1)} %get-tuple-element.93.refs_3_), channel_id=1, source_target_pairs={{0,2},{1,3},{2,6},{3,7},{6,4},{7,5},{4,0},{5,1},{8,10},{9,11},{10,... | collective-permute-start | bytes 3538952 | tf_op jit(solution)/shard_map/ppermute | solution.py:423
  54.3 44.5 %collective-permute-start.12 = (bf16[128,4608]{1,0:T(8,128)(2,1)S(1)}, bf16[128,4608]{1,0:T(8,128)(2,1)S(1)}, u32[]{:S(2)}, u32[]{:S(2)}) collective-permute-start(bf16[128,4608]{1,0:T(8,128)(2,1)S(1)} %get-tuple-element.105), channel_id=1, source_target_pairs={{0,8},{1,17},{2,10},{3,19},{4,12},{5,21},{6,14},{7,23},{8,0},{9,25... | collective-permute-start | bytes 3538952 | tf_op jit(solution)/shard_map/ppermute | solution.py:431
  54.9 32.4 %collective-permute-start.7 = (bf16[64,4608]{1,0:T(8,128)(2,1)S(1)}, bf16[64,4608]{1,0:T(8,128)(2,1)S(1)}, u32[]{:S(2)}, u32[]{:S(2)}) collective-permute-start(bf16[64,4608]{1,0:T(8,128)(2,1)S(1)} %get-tuple-element.92), channel_id=1, source_target_pairs={{0,16},{1,9},{2,18},{3,11},{4,20},{5,13},{6,22},{7,15},{8,24},{9,1... | collective-permute-start | bytes 1769480 | tf_op jit(solution)/shard_map/ppermute | solution.py:431
  57.5 17.7 %copy-start.6 = (bf16[256,4608]{1,0:T(8,128)(2,1)S(1)}, bf16[256,4608]{1,0:T(8,128)(2,1)}, u32[]{:S(2)}) copy-start(bf16[256,4608]{1,0:T(8,128)(2,1)} %refs_2_.19) | copy-start | bytes 7077892
  85.6 2.0 collective-permute-start.10
  85.7 20.1 %collective-permute-start.6 = (bf16[64,4608]{1,0:T(8,128)(2,1)S(1)}, bf16[64,4608]{1,0:T(8,128)(2,1)S(1)}, u32[]{:S(2)}, u32[]{:S(2)}) collective-permute-start(bf16[64,4608]{1,0:T(8,128)(2,1)S(1)} %get-tuple-element.91), channel_id=1, source_target_pairs={{0,16},{1,9},{2,18},{3,11},{4,20},{5,13},{6,22},{7,15},{8,24},{9,1... | collective-permute-start | bytes 1769480 | tf_op jit(solution)/shard_map/ppermute | solution.py:431
  87.6 4.9 %copy-start.4 = (bf16[512,1024]{1,0:T(8,128)(2,1)S(1)}, bf16[512,1024]{1,0:T(8,128)(2,1)}, u32[]{:S(2)}) copy-start(bf16[512,1024]{1,0:T(8,128)(2,1)} %refs_2_.23) | copy-start | bytes 3145732
  88.4 17.5 %collective-permute-start.11 = (bf16[64,4608]{1,0:T(8,128)(2,1)S(1)}, bf16[64,4608]{1,0:T(8,128)(2,1)S(1)}, u32[]{:S(2)}, u32[]{:S(2)}) collective-permute-start(bf16[64,4608]{1,0:T(8,128)(2,1)S(1)} %get-tuple-element.97), channel_id=1, source_target_pairs={{0,2},{1,3},{2,6},{3,7},{6,4},{7,5},{4,0},{5,1},{8,10},{9,11},{10,... | collective-permute-start | bytes 1769480 | tf_op jit(solution)/shard_map/ppermute | solution.py:423
  91.0 16.7 %collective-permute-start.14 = (bf16[256,2304]{1,0:T(8,128)(2,1)S(1)}, bf16[256,2304]{1,0:T(8,128)(2,1)S(1)}, u32[]{:S(2)}, u32[]{:S(2)}) collective-permute-start(bf16[256,2304]{1,0:T(8,128)(2,1)S(1)} %get-tuple-element.111.refs_2_), channel_id=1, source_target_pairs={{0,8},{1,17},{2,10},{3,19},{4,12},{5,21},{6,14},{7,23},{8,0},{9,25... | collective-permute-start | bytes 3538952 | tf_op jit(solution)/shard_map/ppermute | solution.py:431
  92.1 38.7 %collective-permute-start.16 = (bf16[256,2304]{1,0:T(8,128)(2,1)S(1)}, bf16[256,2304]{1,0:T(8,128)(2,1)S(1)}, u32[]{:S(2)}, u32[]{:S(2)}) collective-permute-start(bf16[256,2304]{1,0:T(8,128)(2,1)S(1)} %get-tuple-element.111.refs_2_), channel_id=1, source_target_pairs={{0,2},{1,3},{2,6},{3,7},{6,4},{7,5},{4,0},{5,1},{8,10},{9,11},{10,... | collective-permute-start | bytes 3538952 | tf_op jit(solution)/shard_map/ppermute | solution.py:423
  106.7 24.1 %collective-permute-start.13 = (bf16[128,4608]{1,0:T(8,128)(2,1)S(1)}, bf16[128,4608]{1,0:T(8,128)(2,1)S(1)}, u32[]{:S(2)}, u32[]{:S(2)}) collective-permute-start(bf16[128,4608]{1,0:T(8,128)(2,1)S(1)} %get-tuple-element.110), channel_id=1, source_target_pairs={{0,8},{1,17},{2,10},{3,19},{4,12},{5,21},{6,14},{7,23},{8,0},{9,25... | collective-permute-start | bytes 3538952 | tf_op jit(solution)/shard_map/ppermute | solution.py:431
  114.3 4.8 %collective-permute-start.15 = (bf16[512,256]{1,0:T(8,128)(2,1)S(1)}, bf16[512,256]{1,0:T(8,128)(2,1)S(1)}, u32[]{:S(2)}, u32[]{:S(2)}) collective-permute-start(bf16[512,256]{1,0:T(8,128)(2,1)S(1)} %get-tuple-element.114), channel_id=1, source_target_pairs={{0,1},{1,0},{2,3},{3,2},{4,5},{5,4},{6,7},{7,6},{8,9},{9,8},{10,11... | collective-permute-start | bytes 786440 | tf_op jit(solution)/shard_map/ppermute | solution.py:416
  115.0 19.1 %collective-permute-start.18 = (bf16[64,4608]{1,0:T(8,128)(2,1)S(1)}, bf16[64,4608]{1,0:T(8,128)(2,1)S(1)}, u32[]{:S(2)}, u32[]{:S(2)}) collective-permute-start(bf16[64,4608]{1,0:T(8,128)(2,1)S(1)} %get-tuple-element.121), channel_id=1, source_target_pairs={{0,16},{1,9},{2,18},{3,11},{4,20},{5,13},{6,22},{7,15},{8,24},{9,1... | collective-permute-start | bytes 1769480 | tf_op jit(solution)/shard_map/ppermute | solution.py:431
  116.5 26.1 %collective-permute-start.19 = (bf16[64,4608]{1,0:T(8,128)(2,1)S(1)}, bf16[64,4608]{1,0:T(8,128)(2,1)S(1)}, u32[]{:S(2)}, u32[]{:S(2)}) collective-permute-start(bf16[64,4608]{1,0:T(8,128)(2,1)S(1)} %get-tuple-element.122), channel_id=1, source_target_pairs={{0,2},{1,3},{2,6},{3,7},{6,4},{7,5},{4,0},{5,1},{8,10},{9,11},{10,... | collective-permute-start | bytes 1769480 | tf_op jit(solution)/shard_map/ppermute | solution.py:423
  131.5 21.4 %collective-permute-start.17 = (bf16[256,2304]{1,0:T(8,128)(2,1)S(1)}, bf16[256,2304]{1,0:T(8,128)(2,1)S(1)}, u32[]{:S(2)}, u32[]{:S(2)}) collective-permute-start(bf16[256,2304]{1,0:T(8,128)(2,1)S(1)} %get-tuple-element.120.refs_2_), channel_id=1, source_target_pairs={{0,8},{1,17},{2,10},{3,19},{4,12},{5,21},{6,14},{7,23},{8,0},{9,25... | collective-permute-start | bytes 3538952 | tf_op jit(solution)/shard_map/ppermute | solution.py:431
  132.6 26.8 %collective-permute-start.21 = (bf16[64,4608]{1,0:T(8,128)(2,1)S(1)}, bf16[64,4608]{1,0:T(8,128)(2,1)S(1)}, u32[]{:S(2)}, u32[]{:S(2)}) collective-permute-start(bf16[64,4608]{1,0:T(8,128)(2,1)S(1)} %get-tuple-element.130), channel_id=1, source_target_pairs={{0,16},{1,9},{2,18},{3,11},{4,20},{5,13},{6,22},{7,15},{8,24},{9,1... | collective-permute-start | bytes 1769480 | tf_op jit(solution)/shard_map/ppermute | solution.py:431
  143.4 15.9 %collective-permute-start.22 = (bf16[64,4608]{1,0:T(8,128)(2,1)S(1)}, bf16[64,4608]{1,0:T(8,128)(2,1)S(1)}, u32[]{:S(2)}, u32[]{:S(2)}) collective-permute-start(bf16[64,4608]{1,0:T(8,128)(2,1)S(1)} %get-tuple-element.131), channel_id=1, source_target_pairs={{0,2},{1,3},{2,6},{3,7},{6,4},{7,5},{4,0},{5,1},{8,10},{9,11},{10,... | collective-permute-start | bytes 1769480 | tf_op jit(solution)/shard_map/ppermute | solution.py:423
  160.2 24.4 %copy-start.8 = (bf16[64,4608]{1,0:T(8,128)(2,1)}, bf16[64,4608]{1,0:T(8,128)(2,1)S(1)}, u32[]{:S(2)}) copy-start(bf16[64,4608]{1,0:T(8,128)(2,1)S(1)} %get-tuple-element.137.refs_2_) | copy-start | bytes 1769476
  160.2 15.6 %collective-permute-start.23 = (bf16[64,4608]{1,0:T(8,128)(2,1)S(1)}, bf16[64,4608]{1,0:T(8,128)(2,1)}, u32[]{:S(2)}, u32[]{:S(2)}) collective-permute-start(bf16[64,4608]{1,0:T(8,128)(2,1)S(1)} %get-tuple-element.137.refs_2_), channel_id=1, source_target_pairs={{0,16},{1,9},{2,18},{3,11},{4,20},{5,13},{6,22},{7,15},{8,24},{9,1... | collective-permute-start | bytes 1769480 | tf_op jit(solution)/shard_map/ppermute | solution.py:431
  161.6 23.6 %collective-permute-start.25 = (bf16[64,4608]{1,0:T(8,128)(2,1)S(1)}, bf16[64,4608]{1,0:T(8,128)(2,1)S(1)}, u32[]{:S(2)}, u32[]{:S(2)}) collective-permute-start(bf16[64,4608]{1,0:T(8,128)(2,1)S(1)} %get-tuple-element.137.refs_2_), channel_id=1, source_target_pairs={{0,8},{1,17},{2,10},{3,19},{4,12},{5,21},{6,14},{7,23},{8,0},{9,25... | collective-permute-start | bytes 1769480 | tf_op jit(solution)/shard_map/ppermute | solution.py:431
  175.9 17.9 %collective-permute-start.24 = (bf16[64,4608]{1,0:T(8,128)(2,1)}, bf16[64,4608]{1,0:T(8,128)(2,1)S(1)}, u32[]{:S(2)}, u32[]{:S(2)}) collective-permute-start(bf16[64,4608]{1,0:T(8,128)(2,1)} %collective-permute-done.23.refs_3_), channel_id=1, source_target_pairs={{0,8},{1,17},{2,10},{3,19},{4,12},{5,21},{6,14},{7,23},{8,0},{9,25... | collective-permute-start | bytes 1769480 | tf_op jit(solution)/shard_map/ppermute | solution.py:431
  176.7 1.5 collective-permute-start.20
  184.6 0.6 copy-start.7
  185.2 0.8 copy-start.13
  193.8 0.8 copy-start.12

commit v6 on v5

--- a/solution.py
+++ b/solution.py
@@ -97,6 +97,14 @@
         [(weight, block, lambda n, sc: (0, sc[lay.at_bit(0)]))],
         [(block, BF16, block, first), ((8, 128), F32, (8, 128), first)],
     )
+
+
+def relay_body(sc_ref):
+    pass
+
+
+def relay(sc, through):
+    return call(relay_body, sc, (1,), [], [], through=through)
 
 
 def forward_body(heads, sc_ref, q_ref, k_ref, v_ref, seg_row_ref, seg_col_ref, out_ref, mask_ref):
@@ -505,37 +513,37 @@
     contexts = {}
     (both_sides,) = run(forward, sc, [1], [0, 1], block, lay)
     contexts[1] = (both_sides, 1), (lay.sibling(both_sides[:rows]), 0)
-    (away,) = run(forward, sc, late, [0], block, lay)
-    away = lay.sibling(away)
     do_product(1)
     send(1)
-    (stay,) = run(forward, sc, late, [1], block, lay)
-    for n, k in enumerate(late):
-        contexts[k] = (stay, n), (away, n)
-    do_product(2)
-    send(2)
-    do_halve(1, held=[("ring", 1)])
+    (both_sides,) = run(forward, sc, late, [0, 1], block, lay)
+    box["context"] = lay.sibling(both_sides[: len(late) * rows])
+    do_halve(1, held=[("ring", 1), "context"])
+    send(1)
     pass_weights(1)
     cross_weights(1)
-    send(1)
+    for n, k in enumerate(late):
+        contexts[k] = (both_sides, len(late) + n), (box["context"], n)
+    do_product(2)
+    do_sum(1)
+    pass_sum(1)
+    send(2)
     do_product(3)
     send(3)
+    do_grad_context([0, 1])
+    swap_grad_context(0)
+    run(relay, sc, held=[("ring", 2)])
+    pass_weights(2)
+    cross_weights(2)
     do_halve(2)
     send(2)
+    do_backward(0)
     do_product(0)
-    do_grad_context([0, 1])
-    swap_grad_context(0)
-    do_sum(1, held=[("ring", 2), ("gc", 0)])
-    pass_sum(1)
-    pass_weights(2)
-    cross_weights(2)
-    do_backward(0)
     do_halve(3)
     send(3)
-    do_backward(1)
-    do_sum(2, held=[("send", 0)])
+    do_backward(1, held=[("send", 0)])
+    send(0)
+    do_sum(2)
     pass_sum(2)
-    send(0)
     for k in range(4, lay.z):
         do_product(k, held=[("ring", k - 1)])
         pass_weights(k - 1)
@@ -544,16 +552,21 @@
         do_halve(k)
         send(k)
     last = lay.z - 1
-    for k in range(2, last):
+    do_grad_context([2])
+    swap_grad_context(2)
+    do_sum(3, held=[("ring", last)])
+    pass_sum(3)
+    cross_weights(last)
+    do_backward(2)
+    for k in range(4, lay.z):
+        do_sum(k)
+        pass_sum(k)
+    for k in range(3, last):
         do_grad_context([k])
         swap_grad_context(k)
         do_backward(k)
-    do_halve(0, held=[("ring", last)])
+    do_halve(0)
     send(0)
-    cross_weights(last)
-    for k in range(3, lay.z):
-        do_sum(k)
-        pass_sum(k)
     do_grad_context([last])
     swap_grad_context(last)
     do_sum(0)
@@ -567,6 +580,9 @@
     moments = first_moment, second_moment, tokens, lay
     direct = [spread(n, have[0]) for n in range(lay.bits - 1, -1, -1)]
     do_backward(last)
+    box["got"] = direct[0][0]
+    step = run(adam, sc, have, *moments, before=(), held=["got"])
+    direct[0] = (box["got"], direct[0][1])
     near = [have[0], *direct]
     have = [have[0], direct[0]]
     done = {flips for _, flips in near}
@@ -581,7 +597,7 @@
                 more.append((lay.across(x, n), flips))
                 far.append(more[-1])
         have += more
-    step = run(adam, sc, near, *moments, before=())
+    step = run(adam, sc, direct, *moments, before=step)
     step = run(adam, sc, far, *moments, before=step)
     return (*grads, *step)
 

time: 200 us -> 198 us (0.990)
  starting transfers between devices: 32.1 us -> 29.6 us
  Pallas kernels: 106 us -> 108 us
    ppermute x6, waiting for transfers between devices: 15.6 us -> 21.1 us  [onward(): return lax.ppermute(x, 'shard', perm)]
    ppermute x14, waiting for transfers between devices: 32.9 us -> 28.4 us  [across(): return lax.ppermute(x, ('replica', 'shard'), perm)]
    ppermute x6, starting transfers between devices: 13.2 us -> 9.03 us  [onward(): return lax.ppermute(x, 'shard', perm)]
    ppermute x14, starting transfers between devices: 17.5 us -> 19.7 us  [across(): return lax.ppermute(x, ('replica', 'shard'), perm)]
    pallas_call x25 -> x26, Pallas kernels: 106 us -> 108 us  [call(): pl.pallas_call(kernel, grid_spec=pltpu.PrefetchScalarGridSpec(num_scalar_...]
    unnamed x32 -> x30, local copies, waits for them, and re-layouts: 7.42 us -> 7.38 us
  transfers between devices with their start and end apart: 26 -> 26, of which waited for: 10 -> 8; matrix products, arithmetic and copies ran while one was open for 1% -> 0% of each run, Pallas kernels for 51% -> 52%
where the time goes in v6:
time: 198 us; the launch traced here: 197 us
  Pallas kernels  108 us (55%)
  waiting for transfers between devices  50.3 us (25%)
  starting transfers between devices  29.6 us (15%)
  local copies, waits for them, and re-layouts  8.29 us (4%)
    pallas_call x26, Pallas kernels, call(): pl.pallas_call(kernel, grid_spec=pltpu.PrefetchScalarGridSpec(num_scalar_...  108 us
    ppermute x14, waiting for transfers between devices, across(): return lax.ppermute(x, ('replica', 'shard'), perm)  28.4 us
    ppermute x6, waiting for transfers between devices, onward(): return lax.ppermute(x, 'shard', perm)  21.1 us
    ppermute x14, starting transfers between devices, across(): return lax.ppermute(x, ('replica', 'shard'), perm)  19.7 us
    ppermute x6, starting transfers between devices, onward(): return lax.ppermute(x, 'shard', perm)  9.03 us
    unnamed x30, local copies, waits for them, and re-layouts  7.38 us
  transfers between devices with their start and end apart: 26, of which 8 were waited for; matrix products, arithmetic and copies ran while one was open for 0% of the time, Pallas kernels for 52%

profile of v6, /device:TPU:0, one launch (start us, length us, event | category | flops | bytes accessed | tf_op | source)
XLA Modules:
  0.0 196.9 jit_solution(6972266770266107159)
XLA Ops:
  0.6 0.5 collective-permute-start
  1.1 0.7 dynamic-slice_bitcast_fusion.sc_ref
  1.8 1.7 copy-done.6
  3.5 0.6 shard_map.120
  4.2 1.0 copy-done.12
  5.2 0.1 copy.60.refs_4_
  5.3 1.2 copy-done.2
  6.5 1.2 copy-done.4
  7.8 3.7 %shard_map.121 = (bf16[512,512]{1,0:T(8,128)(2,1)S(1)}, f32[8,128]{1,0:T(8,128)S(1)}) custom-call(s32[15]{0:T(128)S(1)} %dynamic-slice_bitcast_fusion.sc_ref, bf16[512,2048]{1,0:T(8,128)(2,1)S(1)} %copy-done.1, bf16[512,1024]{1,0:T(8,128)(2,1)S(1)} %copy-done.2, bf16[512,1024]{1,0:T(8,128)(2,1)S(1)} %copy-done.4, ...), custom_call_target="tpu_custom_call", output_to_operand_aliasing={{1}: (6, {})} | custom-call | flops 1 | bytes 1 | tf_op jit(solution)/shard_map/pallas_call | solution.py:41
  11.5 0.1 collective-permute-start.1
  11.6 3.0 %collective-permute-start.3 = (bf16[256,2304]{1,0:T(8,128)(2,1)}, bf16[256,2304]{1,0:T(8,128)(2,1)S(1)}, u32[]{:S(2)}, u32[]{:S(2)}) collective-permute-start(bf16[256,2304]{1,0:T(8,128)(2,1)} %copy-done.12), channel_id=1, source_target_pairs={{0,2},{1,3},{2,6},{3,7},{6,4},{7,5},{4,0},{5,1},{8,10},{9,11},{10,... | collective-permute-start | bytes 3538952 | tf_op jit(solution)/shard_map/ppermute | solution.py:431
  14.6 6.3 %shard_map.122 = (bf16[128,4608]{1,0:T(8,128)(2,1)S(1)}, bf16[128,4608]{1,0:T(8,128)(2,1)S(1)}, f32[8,128]{1,0:T(8,128)S(1)}) custom-call(s32[15]{0:T(128)S(1)} %dynamic-slice_bitcast_fusion.sc_ref, bf16[512,512]{1,0:T(8,128)(2,1)S(1)} %get-tuple-element.76.refs_0_, ...), custom_call_target="tpu_custom_call", output_to_operand_aliasing={{2}: (5, {})} | custom-call | flops 1 | bytes 1 | tf_op jit(solution)/shard_map/pallas_call | solution.py:41
  20.9 1.6 collective-permute-start.2
  22.5 9.6 %shard_map.123 = (bf16[1536,512]{1,0:T(8,128)(2,1)S(1)}, f32[8,128]{1,0:T(8,128)S(1)}) custom-call(s32[15]{0:T(128)S(1)} %dynamic-slice_bitcast_fusion.sc_ref, bf16[512,2048]{1,0:T(8,128)(2,1)S(1)} %copy-done.1, bf16[512,1024]{1,0:T(8,128)(2,1)S(1)} %copy-done.3, bf16[512,1024]{1,0:T(8,128)(2,1)S(1)} %copy-done.4, ...), custom_call_target="tpu_custom_call", output_to_operand_aliasing={{1}: (6, {})} | custom-call | flops 1 | bytes 1 | tf_op jit(solution)/shard_map/pallas_call | solution.py:41
  32.3 9.7 %collective-permute-done.3.refs_3_ = bf16[256,2304]{1,0:T(8,128)(2,1)S(1)} collective-permute-done((bf16[256,2304]{1,0:T(8,128)(2,1)}, bf16[256,2304]{1,0:T(8,128)(2,1)S(1)}, u32[]{:S(2)}, u32[]{:S(2)}) %collective-permute-start.3) | collective-permute-done | bytes 1179680 | tf_op jit(solution)/shard_map/ppermute | solution.py:431
  42.0 0.7 shard_map.124
  42.7 1.6 collective-permute-start.7
  44.3 1.5 collective-permute-start.5
  45.9 0.9 collective-permute-start.10
  46.8 6.3 %shard_map.125 = (bf16[128,4608]{1,0:T(8,128)(2,1)S(1)}, bf16[128,4608]{1,0:T(8,128)(2,1)S(1)}, f32[8,128]{1,0:T(8,128)S(1)}) custom-call(s32[15]{0:T(128)S(1)} %dynamic-slice_bitcast_fusion.sc_ref, bf16[1536,512]{1,0:T(8,128)(2,1)S(1)} %get-tuple-element.79.refs_0_, ...), custom_call_target="tpu_custom_call", output_to_operand_aliasing={{2}: (5, {})} | custom-call | flops 1 | bytes 1 | tf_op jit(solution)/shard_map/pallas_call | solution.py:41
  53.0 0.6 collective-permute-start.9
  53.6 7.0 %collective-permute-done.5.refs_2_ = bf16[64,4608]{1,0:T(8,128)(2,1)S(1)} collective-permute-done((bf16[64,4608]{1,0:T(8,128)(2,1)S(1)}, bf16[64,4608]{1,0:T(8,128)(2,1)S(1)}, u32[]{:S(2)}, u32[]{:S(2)}) %collective-permute-start.5) | collective-permute-done | bytes 589856 | tf_op jit(solution)/shard_map/ppermute | solution.py:439
  60.6 0.8 shard_map.126
  61.4 6.3 %shard_map.127 = (bf16[128,4608]{1,0:T(8,128)(2,1)S(1)}, bf16[128,4608]{1,0:T(8,128)(2,1)S(1)}, f32[8,128]{1,0:T(8,128)S(1)}) custom-call(s32[15]{0:T(128)S(1)} %dynamic-slice_bitcast_fusion.sc_ref, bf16[1536,512]{1,0:T(8,128)(2,1)S(1)} %get-tuple-element.79.refs_0_, ...), custom_call_target="tpu_custom_call", output_to_operand_aliasing={{2}: (5, {})} | custom-call | flops 1 | bytes 1 | tf_op jit(solution)/shard_map/pallas_call | solution.py:41
  67.7 0.5 collective-permute-start.6
  68.3 10.4 %shard_map.128 = (bf16[512,512]{1,0:T(8,128)(2,1)S(1)}, bf16[512,512]{1,0:T(8,128)(2,1)S(1)}, f32[8,128]{1,0:T(8,128)S(1)}) custom-call(s32[15]{0:T(128)S(1)} %dynamic-slice_bitcast_fusion.sc_ref, bf16[512,4608]{1,0:T(8,128)(2,1)S(1)} %copy-done, bf16[512,4608]{1,0:T(8,128)(2,1)} %collective-permute-done.refs_3_.refs_1_, ...), custom_call_target="tpu_custom_call", output_to_operand_aliasing={{2}: (6, {})} | custom-call | flops 1 | bytes 1 | tf_op jit(solution)/shard_map/pallas_call | solution.py:41
  78.8 1.0 collective-permute-start.13
  79.8 0.5 shard_map.129
  80.3 1.6 collective-permute-start.15
  81.9 0.7 shard_map.130
  82.6 1.6 collective-permute-start.12
  84.2 3.3 %collective-permute-start.16 = (bf16[256,2304]{1,0:T(8,128)(2,1)S(1)}, bf16[256,2304]{1,0:T(8,128)(2,1)S(1)}, u32[]{:S(2)}, u32[]{:S(2)}) collective-permute-start(bf16[256,2304]{1,0:T(8,128)(2,1)S(1)} %get-tuple-element.112.refs_2_), channel_id=1, source_target_pairs={{0,2},{1,3},{2,6},{3,7},{6,4},{7,5},{4,0},{5,1},{8,10},{9,11},{10,... | collective-permute-start | bytes 3538952 | tf_op jit(solution)/shard_map/ppermute | solution.py:431
  87.5 6.3 %shard_map.131 = (bf16[512,2048]{1,0:T(8,128)(2,1)}, bf16[512,1024]{1,0:T(8,128)(2,1)}, bf16[512,1024]{1,0:T(8,128)(2,1)}, f32[8,128]{1,0:T(8,128)S(1)}) custom-call(s32[15]{0:T(128)S(1)} %dynamic-slice_bitcast_fusion.sc_ref, bf16[512,2048]{1,0:T(8,128)(2,1)S(1)} %copy-done.1, bf16[512,1024]{1,0:T(8,128)(2,1)S(1)} %copy-done.3, ...), custom_call_target="tpu_custom_call", output_to_operand_aliasing={{3}: (8, {})} | custom-call | flops 1 | bytes 1 | tf_op jit(solution)/shard_map/pallas_call | solution.py:41
  93.8 6.3 %shard_map.132 = (bf16[128,4608]{1,0:T(8,128)(2,1)S(1)}, bf16[128,4608]{1,0:T(8,128)(2,1)S(1)}, f32[8,128]{1,0:T(8,128)S(1)}) custom-call(s32[15]{0:T(128)S(1)} %dynamic-slice_bitcast_fusion.sc_ref, bf16[1536,512]{1,0:T(8,128)(2,1)S(1)} %get-tuple-element.79.refs_0_, ...), custom_call_target="tpu_custom_call", output_to_operand_aliasing={{2}: (5, {})} | custom-call | flops 1 | bytes 1 | tf_op jit(solution)/shard_map/pallas_call | solution.py:41
  100.0 0.7 shard_map.133
  100.7 0.6 collective-permute-start.11
  101.3 6.3 %shard_map.134 = (bf16[512,2048]{1,0:T(8,128)(2,1)}, bf16[512,1024]{1,0:T(8,128)(2,1)}, bf16[512,1024]{1,0:T(8,128)(2,1)}, f32[8,128]{1,0:T(8,128)S(1)}, bf16[128,4608]{1,0:T(8,128)(2,1)S(1)}) custom-call(s32[15]{0:T(128)S(1)} %dynamic-slice_bitcast_fusion.sc_ref, ...), custom_call_target="tpu_custom_call", output_to_operand_aliasing={{0}: (8, {}), {1}: (9, {}), {2}: (10, {}), {3}: (11, {}), {... | custom-call | flops 1 | bytes 1 | tf_op jit(solution)/shard_map/pallas_call | solution.py:41
  107.6 0.8 shard_map.135
  108.5 0.6 collective-permute-start.18
  109.1 6.3 %collective-permute-done.15.refs_3_ = bf16[256,2304]{1,0:T(8,128)(2,1)S(1)} collective-permute-done((bf16[256,2304]{1,0:T(8,128)(2,1)S(1)}, bf16[256,2304]{1,0:T(8,128)(2,1)S(1)}, u32[]{:S(2)}, u32[]{:S(2)}) %collective-permute-start.15) | collective-permute-done | bytes 1179680 | tf_op jit(solution)/shard_map/ppermute | solution.py:439
  115.4 6.5 %shard_map.136 = (bf16[512,256]{1,0:T(8,128)(2,1)S(1)}, bf16[512,256]{1,0:T(8,128)(2,1)S(1)}, f32[8,128]{1,0:T(8,128)S(1)}) custom-call(s32[15]{0:T(128)S(1)} %dynamic-slice_bitcast_fusion.sc_ref, bf16[512,4608]{1,0:T(8,128)(2,1)S(1)} %copy-done, bf16[512,4608]{1,0:T(8,128)(2,1)} %collective-permute-done.refs_3_.refs_1_, ...), custom_call_target="tpu_custom_call", output_to_operand_aliasing={{2}: (5, {})} | custom-call | flops 1 | bytes 1 | tf_op jit(solution)/shard_map/pallas_call | solution.py:41
  122.0 11.4 %collective-permute-done.14.refs_3_ = bf16[64,4608]{1,0:T(8,128)(2,1)S(1)} collective-permute-done((bf16[64,4608]{1,0:T(8,128)(2,1)S(1)}, bf16[64,4608]{1,0:T(8,128)(2,1)S(1)}, u32[]{:S(2)}, u32[]{:S(2)}) %collective-permute-start.14) | collective-permute-done | bytes 589856 | tf_op jit(solution)/shard_map/ppermute | solution.py:431
  133.3 0.8 shard_map.137
  134.2 1.6 collective-permute-start.17
  135.8 0.8 collective-permute-start.22
  136.6 0.7 collective-permute-done.19.refs_6_
  137.3 6.3 %shard_map.138 = (bf16[512,2048]{1,0:T(8,128)(2,1)}, bf16[512,1024]{1,0:T(8,128)(2,1)}, bf16[512,1024]{1,0:T(8,128)(2,1)}, f32[8,128]{1,0:T(8,128)S(1)}) custom-call(s32[15]{0:T(128)S(1)} %dynamic-slice_bitcast_fusion.sc_ref, bf16[512,2048]{1,0:T(8,128)(2,1)S(1)} %copy-done.1, ...), custom_call_target="tpu_custom_call", output_to_operand_aliasing={{0}: (8, {}), {1}: (9, {}), {2}: (10, {}), {3}: (11, {})} | custom-call | flops 1 | bytes 1 | tf_op jit(solution)/shard_map/pallas_call | solution.py:41
  143.6 0.7 shard_map.139
  144.3 1.6 collective-permute-start.21
  145.9 7.9 %collective-permute-done.17.refs_3_ = bf16[256,2304]{1,0:T(8,128)(2,1)S(1)} collective-permute-done((bf16[256,2304]{1,0:T(8,128)(2,1)S(1)}, bf16[256,2304]{1,0:T(8,128)(2,1)S(1)}, u32[]{:S(2)}, u32[]{:S(2)}) %collective-permute-start.17) | collective-permute-done | bytes 1179680 | tf_op jit(solution)/shard_map/ppermute | solution.py:439
  153.7 6.5 %shard_map.140 = (bf16[512,256]{1,0:T(8,128)(2,1)S(1)}, bf16[512,256]{1,0:T(8,128)(2,1)S(1)}, f32[8,128]{1,0:T(8,128)S(1)}) custom-call(s32[15]{0:T(128)S(1)} %dynamic-slice_bitcast_fusion.sc_ref, bf16[512,4608]{1,0:T(8,128)(2,1)S(1)} %copy-done, bf16[512,4608]{1,0:T(8,128)(2,1)} %collective-permute-done.refs_3_.refs_1_, ...), custom_call_target="tpu_custom_call", output_to_operand_aliasing={{2}: (5, {})} | custom-call | flops 1 | bytes 1 | tf_op jit(solution)/shard_map/pallas_call | solution.py:41
  160.3 0.8 shard_map.141
  161.1 1.7 collective-permute-start.23
  162.8 2.4 %collective-permute-start.25 = (bf16[64,4608]{1,0:T(8,128)(2,1)S(1)}, bf16[64,4608]{1,0:T(8,128)(2,1)}, u32[]{:S(2)}, u32[]{:S(2)}) collective-permute-start(bf16[64,4608]{1,0:T(8,128)(2,1)S(1)} %get-tuple-element.138.refs_2_), channel_id=1, source_target_pairs={{0,8},{1,17},{2,10},{3,19},{4,12},{5,21},{6,14},{7,23},{8,0},{9,25... | collective-permute-start | bytes 1769480 | tf_op jit(solution)/shard_map/ppermute | solution.py:439
  165.2 6.3 %shard_map.142 = (bf16[512,2048]{1,0:T(8,128)(2,1)}, bf16[512,1024]{1,0:T(8,128)(2,1)}, bf16[512,1024]{1,0:T(8,128)(2,1)}, f32[8,128]{1,0:T(8,128)S(1)}) custom-call(s32[15]{0:T(128)S(1)} %dynamic-slice_bitcast_fusion.sc_ref, bf16[512,2048]{1,0:T(8,128)(2,1)S(1)} %copy-done.1, ...), custom_call_target="tpu_custom_call", output_to_operand_aliasing={{0}: (8, {}), {1}: (9, {}), {2}: (10, {}), {3}: (11, {})} | custom-call | flops 1 | bytes 1 | tf_op jit(solution)/shard_map/pallas_call | solution.py:41
  171.5 0.6 copy-done.8
  172.1 4.4 %collective-permute-done.23.refs_4_ = bf16[64,4608]{1,0:T(8,128)(2,1)S(1)} collective-permute-done((bf16[64,4608]{1,0:T(8,128)(2,1)S(1)}, bf16[64,4608]{1,0:T(8,128)(2,1)S(1)}, u32[]{:S(2)}, u32[]{:S(2)}) %collective-permute-start.23) | collective-permute-done | bytes 589856 | tf_op jit(solution)/shard_map/ppermute | solution.py:439
  176.5 0.8 copy-done.13
  177.3 4.2 %shard_map.143 = (f32[256,4608]{1,0:T(8,128)}, f32[8,128]{1,0:T(8,128)}, bf16[64,4608]{1,0:T(8,128)(2,1)}) custom-call(s32[15]{0:T(128)} %copy-done.10, f32[256,4608]{1,0:T(8,128)} %refs_0_.25, f32[256,4608]{1,0:T(8,128)} %refs_1_.17, bf16[64,4608]{1,0:T(8,128)(2,1)} %copy-done.9, f32[8,128]{1,0:T(8,128)} %copy-done.8, ...), custom_call_target="tpu_custom_call", output_to_operand_aliasing={{1}: (4, {}), {2}: (5, {})} | custom-call | flops 1 | bytes 1 | tf_op jit(solution)/shard_map/pallas_call | solution.py:41
  181.5 2.3 %collective-permute-start.24 = (bf16[64,4608]{1,0:T(8,128)(2,1)}, bf16[64,4608]{1,0:T(8,128)(2,1)S(1)}, u32[]{:S(2)}, u32[]{:S(2)}) collective-permute-start(bf16[64,4608]{1,0:T(8,128)(2,1)} %get-tuple-element.140.refs_2_), channel_id=1, source_target_pairs={{0,8},{1,17},{2,10},{3,19},{4,12},{5,21},{6,14},{7,23},{8,0},{9,25... | collective-permute-start | bytes 1769480 | tf_op jit(solution)/shard_map/ppermute | solution.py:439
  183.8 5.2 %shard_map.144 = (f32[256,4608]{1,0:T(8,128)}, f32[8,128]{1,0:T(8,128)}) custom-call(s32[15]{0:T(128)} %copy-done.10, f32[256,4608]{1,0:T(8,128)} %refs_0_.25, f32[256,4608]{1,0:T(8,128)} %refs_1_.17, bf16[64,4608]{1,0:T(8,128)(2,1)} %get-tuple-element.140.refs_2_, ...), custom_call_target="tpu_custom_call", output_to_operand_aliasing={{0}: (5, {}), {1}: (6, {})} | custom-call | flops 1 | bytes 1 | tf_op jit(solution)/shard_map/pallas_call | solution.py:41
  189.0 2.9 %collective-permute-done.24.refs_2_ = bf16[64,4608]{1,0:T(8,128)(2,1)S(1)} collective-permute-done((bf16[64,4608]{1,0:T(8,128)(2,1)}, bf16[64,4608]{1,0:T(8,128)(2,1)S(1)}, u32[]{:S(2)}, u32[]{:S(2)}) %collective-permute-start.24) | collective-permute-done | bytes 589856 | tf_op jit(solution)/shard_map/ppermute | solution.py:439
  191.9 0.8 copy-done.14
  192.7 4.2 %shard_map.145 = (f32[256,4608]{1,0:T(8,128)}, f32[8,128]{1,0:T(8,128)}) custom-call(s32[15]{0:T(128)} %copy-done.10, f32[256,4608]{1,0:T(8,128)} %refs_0_.25, f32[256,4608]{1,0:T(8,128)} %refs_1_.17, bf16[64,4608]{1,0:T(8,128)(2,1)} %copy-done.14, f32[256,4608]{1,0:T(8,128)} %get-tuple-element.143.refs_3_, ...), custom_call_target="tpu_custom_call", output_to_operand_aliasing={{0}: (4, {}), {1}: (5, {})} | custom-call | flops 1 | bytes 1 | tf_op jit(solution)/shard_map/pallas_call | solution.py:41
  (48 shorter events, 0.4 us)
Async XLA Ops:
  0.6 14.0 %collective-permute-start = (bf16[512,4608]{1,0:T(8,128)(2,1)}, bf16[512,4608]{1,0:T(8,128)(2,1)}, u32[]{:S(2)}, u32[]{:S(2)}) collective-permute-start(bf16[512,4608]{1,0:T(8,128)(2,1)} %refs_0_.21), channel_id=1, source_target_pairs={{0,1},{1,0},{2,3},{3,2},{4,5},{5,4},{6,7},{7,6},{8,9},{9,8},{10,11... | collective-permute-start | bytes 14155784 | tf_op jit(solution)/shard_map/ppermute | solution.py:424
  1.8 1.7 copy-start.6
  3.5 161.7 %copy-start.10 = (s32[15]{0:T(128)}, s32[15]{0:T(128)S(1)}, u32[]{:S(2)}) copy-start(s32[15]{0:T(128)S(1)} %dynamic-slice_bitcast_fusion.sc_ref) | copy-start | bytes 184
  3.5 1.6 copy-start.11
  3.5 1.8 copy-start.1
  4.1 1.0 copy-start.12
  5.3 1.2 copy-start.2
  6.5 1.2 copy-start.4
  7.8 6.9 %copy-start = (bf16[512,4608]{1,0:T(8,128)(2,1)S(1)}, bf16[512,4608]{1,0:T(8,128)(2,1)}, u32[]{:S(2)}) copy-start(bf16[512,4608]{1,0:T(8,128)(2,1)} %refs_0_.21) | copy-start | bytes 14155780
  11.5 3.1 %collective-permute-start.1 = (bf16[256,512]{1,0:T(8,128)(2,1)S(1)}, bf16[256,512]{1,0:T(8,128)(2,1)S(1)}, u32[]{:S(2)}, u32[]{:S(2)}) collective-permute-start(bf16[256,512]{1,0:T(8,128)(2,1)S(1)} %slice.6), channel_id=1, source_target_pairs={{0,1},{1,0},{2,3},{3,2},{4,5},{5,4},{6,7},{7,6},{8,9},{9,8},{10,11... | collective-permute-start | bytes 786440 | tf_op jit(solution)/shard_map/ppermute | solution.py:424
  11.6 30.4 %collective-permute-start.3 = (bf16[256,2304]{1,0:T(8,128)(2,1)}, bf16[256,2304]{1,0:T(8,128)(2,1)S(1)}, u32[]{:S(2)}, u32[]{:S(2)}) collective-permute-start(bf16[256,2304]{1,0:T(8,128)(2,1)} %copy-done.12), channel_id=1, source_target_pairs={{0,2},{1,3},{2,6},{3,7},{6,4},{7,5},{4,0},{5,1},{8,10},{9,11},{10,... | collective-permute-start | bytes 3538952 | tf_op jit(solution)/shard_map/ppermute | solution.py:431
  14.6 7.9 %copy-start.3 = (bf16[512,1024]{1,0:T(8,128)(2,1)S(1)}, bf16[512,1024]{1,0:T(8,128)(2,1)}, u32[]{:S(2)}) copy-start(bf16[512,1024]{1,0:T(8,128)(2,1)} %refs_1_.14) | copy-start | bytes 3145732
  20.9 21.1 %collective-permute-start.2 = (bf16[128,4608]{1,0:T(8,128)(2,1)S(1)}, bf16[128,4608]{1,0:T(8,128)(2,1)S(1)}, u32[]{:S(2)}, u32[]{:S(2)}) collective-permute-start(bf16[128,4608]{1,0:T(8,128)(2,1)S(1)} %get-tuple-element.81), channel_id=1, source_target_pairs={{0,8},{1,17},{2,10},{3,19},{4,12},{5,21},{6,14},{7,23},{8,0},{9,25... | collective-permute-start | bytes 3538952 | tf_op jit(solution)/shard_map/ppermute | solution.py:439
  32.2 9.8 %collective-permute-start.4 = (bf16[768,512]{1,0:T(8,128)(2,1)S(1)}, bf16[768,512]{1,0:T(8,128)(2,1)S(1)}, u32[]{:S(2)}, u32[]{:S(2)}) collective-permute-start(bf16[768,512]{1,0:T(8,128)(2,1)S(1)} %slice.7), channel_id=1, source_target_pairs={{0,1},{1,0},{2,3},{3,2},{4,5},{5,4},{6,7},{7,6},{8,9},{9,8},{10,11... | collective-permute-start | bytes 2359304 | tf_op jit(solution)/shard_map/ppermute | solution.py:424
  42.7 25.5 %collective-permute-start.7 = (bf16[256,2304]{1,0:T(8,128)(2,1)S(1)}, bf16[256,2304]{1,0:T(8,128)(2,1)S(1)}, u32[]{:S(2)}, u32[]{:S(2)}) collective-permute-start(bf16[256,2304]{1,0:T(8,128)(2,1)S(1)} %get-tuple-element.91.refs_3_), channel_id=1, source_target_pairs={{0,8},{1,17},{2,10},{3,19},{4,12},{5,21},{6,14},{7,23},{8,0},{9,25... | collective-permute-start | bytes 3538952 | tf_op jit(solution)/shard_map/ppermute | solution.py:439
  44.3 16.3 %collective-permute-start.5 = (bf16[64,4608]{1,0:T(8,128)(2,1)S(1)}, bf16[64,4608]{1,0:T(8,128)(2,1)S(1)}, u32[]{:S(2)}, u32[]{:S(2)}) collective-permute-start(bf16[64,4608]{1,0:T(8,128)(2,1)S(1)} %get-tuple-element.85), channel_id=1, source_target_pairs={{0,16},{1,9},{2,18},{3,11},{4,20},{5,13},{6,22},{7,15},{8,24},{9,1... | collective-permute-start | bytes 1769480 | tf_op jit(solution)/shard_map/ppermute | solution.py:439
  45.9 33.9 %collective-permute-start.10 = (bf16[256,2304]{1,0:T(8,128)(2,1)S(1)}, bf16[256,2304]{1,0:T(8,128)(2,1)S(1)}, u32[]{:S(2)}, u32[]{:S(2)}) collective-permute-start(bf16[256,2304]{1,0:T(8,128)(2,1)S(1)} %get-tuple-element.91.refs_3_), channel_id=1, source_target_pairs={{0,2},{1,3},{2,6},{3,7},{6,4},{7,5},{4,0},{5,1},{8,10},{9,11},{10,... | collective-permute-start | bytes 3538952 | tf_op jit(solution)/shard_map/ppermute | solution.py:431
  53.0 28.9 %collective-permute-start.9 = (bf16[128,4608]{1,0:T(8,128)(2,1)S(1)}, bf16[128,4608]{1,0:T(8,128)(2,1)S(1)}, u32[]{:S(2)}, u32[]{:S(2)}) collective-permute-start(bf16[128,4608]{1,0:T(8,128)(2,1)S(1)} %get-tuple-element.96), channel_id=1, source_target_pairs={{0,8},{1,17},{2,10},{3,19},{4,12},{5,21},{6,14},{7,23},{8,0},{9,25... | collective-permute-start | bytes 3538952 | tf_op jit(solution)/shard_map/ppermute | solution.py:439
  61.4 6.9 %copy-start.7 = (bf16[256,4608]{1,0:T(8,128)(2,1)S(1)}, bf16[256,4608]{1,0:T(8,128)(2,1)}, u32[]{:S(2)}) copy-start(bf16[256,4608]{1,0:T(8,128)(2,1)} %refs_2_.16) | copy-start | bytes 7077892
  67.7 32.3 %collective-permute-start.6 = (bf16[128,4608]{1,0:T(8,128)(2,1)S(1)}, bf16[128,4608]{1,0:T(8,128)(2,1)S(1)}, u32[]{:S(2)}, u32[]{:S(2)}) collective-permute-start(bf16[128,4608]{1,0:T(8,128)(2,1)S(1)} %get-tuple-element.90), channel_id=1, source_target_pairs={{0,8},{1,17},{2,10},{3,19},{4,12},{5,21},{6,14},{7,23},{8,0},{9,25... | collective-permute-start | bytes 3538952 | tf_op jit(solution)/shard_map/ppermute | solution.py:439
  78.7 5.5 %collective-permute-start.8 = (bf16[512,512]{1,0:T(8,128)(2,1)S(1)}, bf16[512,512]{1,0:T(8,128)(2,1)S(1)}, u32[]{:S(2)}, u32[]{:S(2)}) collective-permute-start(bf16[512,512]{1,0:T(8,128)(2,1)S(1)} %get-tuple-element.94), channel_id=1, source_target_pairs={{0,1},{1,0},{2,3},{3,2},{4,5},{5,4},{6,7},{7,6},{8,9},{9,8},{10,11... | collective-permute-start | bytes 1572872 | tf_op jit(solution)/shard_map/ppermute | solution.py:424
  78.8 28.8 %collective-permute-start.13 = (bf16[64,4608]{1,0:T(8,128)(2,1)S(1)}, bf16[64,4608]{1,0:T(8,128)(2,1)S(1)}, u32[]{:S(2)}, u32[]{:S(2)}) collective-permute-start(bf16[64,4608]{1,0:T(8,128)(2,1)S(1)} %get-tuple-element.104), channel_id=1, source_target_pairs={{0,2},{1,3},{2,6},{3,7},{6,4},{7,5},{4,0},{5,1},{8,10},{9,11},{10,... | collective-permute-start | bytes 1769480 | tf_op jit(solution)/shard_map/ppermute | solution.py:431
  80.3 35.1 %collective-permute-start.15 = (bf16[256,2304]{1,0:T(8,128)(2,1)S(1)}, bf16[256,2304]{1,0:T(8,128)(2,1)S(1)}, u32[]{:S(2)}, u32[]{:S(2)}) collective-permute-start(bf16[256,2304]{1,0:T(8,128)(2,1)S(1)} %get-tuple-element.112.refs_2_), channel_id=1, source_target_pairs={{0,8},{1,17},{2,10},{3,19},{4,12},{5,21},{6,14},{7,23},{8,0},{9,25... | collective-permute-start | bytes 3538952 | tf_op jit(solution)/shard_map/ppermute | solution.py:439
  81.9 5.6 %copy-start.5 = (bf16[512,1024]{1,0:T(8,128)(2,1)S(1)}, bf16[512,1024]{1,0:T(8,128)(2,1)}, u32[]{:S(2)}) copy-start(bf16[512,1024]{1,0:T(8,128)(2,1)} %refs_2_.21) | copy-start | bytes 3145732
  82.6 25.0 %collective-permute-start.12 = (bf16[64,4608]{1,0:T(8,128)(2,1)S(1)}, bf16[64,4608]{1,0:T(8,128)(2,1)S(1)}, u32[]{:S(2)}, u32[]{:S(2)}) collective-permute-start(bf16[64,4608]{1,0:T(8,128)(2,1)S(1)} %get-tuple-element.103), channel_id=1, source_target_pairs={{0,16},{1,9},{2,18},{3,11},{4,20},{5,13},{6,22},{7,15},{8,24},{9,1... | collective-permute-start | bytes 1769480 | tf_op jit(solution)/shard_map/ppermute | solution.py:439
  84.2 37.8 %collective-permute-start.16 = (bf16[256,2304]{1,0:T(8,128)(2,1)S(1)}, bf16[256,2304]{1,0:T(8,128)(2,1)S(1)}, u32[]{:S(2)}, u32[]{:S(2)}) collective-permute-start(bf16[256,2304]{1,0:T(8,128)(2,1)S(1)} %get-tuple-element.112.refs_2_), channel_id=1, source_target_pairs={{0,2},{1,3},{2,6},{3,7},{6,4},{7,5},{4,0},{5,1},{8,10},{9,11},{10,... | collective-permute-start | bytes 3538952 | tf_op jit(solution)/shard_map/ppermute | solution.py:431
  100.7 21.2 %collective-permute-start.11 = (bf16[64,4608]{1,0:T(8,128)(2,1)S(1)}, bf16[64,4608]{1,0:T(8,128)(2,1)S(1)}, u32[]{:S(2)}, u32[]{:S(2)}) collective-permute-start(bf16[64,4608]{1,0:T(8,128)(2,1)S(1)} %get-tuple-element.102), channel_id=1, source_target_pairs={{0,16},{1,9},{2,18},{3,11},{4,20},{5,13},{6,22},{7,15},{8,24},{9,1... | collective-permute-start | bytes 1769480 | tf_op jit(solution)/shard_map/ppermute | solution.py:439
  108.5 24.9 %collective-permute-start.14 = (bf16[64,4608]{1,0:T(8,128)(2,1)S(1)}, bf16[64,4608]{1,0:T(8,128)(2,1)S(1)}, u32[]{:S(2)}, u32[]{:S(2)}) collective-permute-start(bf16[64,4608]{1,0:T(8,128)(2,1)S(1)} %get-tuple-element.111), channel_id=1, source_target_pairs={{0,2},{1,3},{2,6},{3,7},{6,4},{7,5},{4,0},{5,1},{8,10},{9,11},{10,... | collective-permute-start | bytes 1769480 | tf_op jit(solution)/shard_map/ppermute | solution.py:431
  108.5 35.1 %collective-permute-start.18 = (bf16[128,4608]{1,0:T(8,128)(2,1)S(1)}, bf16[128,4608]{1,0:T(8,128)(2,1)S(1)}, u32[]{:S(2)}, u32[]{:S(2)}) collective-permute-start(bf16[128,4608]{1,0:T(8,128)(2,1)S(1)} %get-tuple-element.117), channel_id=1, source_target_pairs={{0,8},{1,17},{2,10},{3,19},{4,12},{5,21},{6,14},{7,23},{8,0},{9,25... | collective-permute-start | bytes 3538952 | tf_op jit(solution)/shard_map/ppermute | solution.py:439
  134.2 19.6 %collective-permute-start.17 = (bf16[256,2304]{1,0:T(8,128)(2,1)S(1)}, bf16[256,2304]{1,0:T(8,128)(2,1)S(1)}, u32[]{:S(2)}, u32[]{:S(2)}) collective-permute-start(bf16[256,2304]{1,0:T(8,128)(2,1)S(1)} %get-tuple-element.115.refs_2_), channel_id=1, source_target_pairs={{0,8},{1,17},{2,10},{3,19},{4,12},{5,21},{6,14},{7,23},{8,0},{9,25... | collective-permute-start | bytes 3538952 | tf_op jit(solution)/shard_map/ppermute | solution.py:439
  135.8 1.5 collective-permute-start.19
  135.8 24.5 %collective-permute-start.22 = (bf16[64,4608]{1,0:T(8,128)(2,1)S(1)}, bf16[64,4608]{1,0:T(8,128)(2,1)S(1)}, u32[]{:S(2)}, u32[]{:S(2)}) collective-permute-start(bf16[64,4608]{1,0:T(8,128)(2,1)S(1)} %get-tuple-element.132), channel_id=1, source_target_pairs={{0,2},{1,3},{2,6},{3,7},{6,4},{7,5},{4,0},{5,1},{8,10},{9,11},{10,... | collective-permute-start | bytes 1769480 | tf_op jit(solution)/shard_map/ppermute | solution.py:431
  144.3 16.0 %collective-permute-start.21 = (bf16[64,4608]{1,0:T(8,128)(2,1)S(1)}, bf16[64,4608]{1,0:T(8,128)(2,1)S(1)}, u32[]{:S(2)}, u32[]{:S(2)}) collective-permute-start(bf16[64,4608]{1,0:T(8,128)(2,1)S(1)} %get-tuple-element.131), channel_id=1, source_target_pairs={{0,16},{1,9},{2,18},{3,11},{4,20},{5,13},{6,22},{7,15},{8,24},{9,1... | collective-permute-start | bytes 1769480 | tf_op jit(solution)/shard_map/ppermute | solution.py:439
  161.1 10.4 %copy-start.9 = (bf16[64,4608]{1,0:T(8,128)(2,1)}, bf16[64,4608]{1,0:T(8,128)(2,1)S(1)}, u32[]{:S(2)}) copy-start(bf16[64,4608]{1,0:T(8,128)(2,1)S(1)} %get-tuple-element.138.refs_2_) | copy-start | bytes 1769476
  161.1 15.4 %collective-permute-start.23 = (bf16[64,4608]{1,0:T(8,128)(2,1)S(1)}, bf16[64,4608]{1,0:T(8,128)(2,1)S(1)}, u32[]{:S(2)}, u32[]{:S(2)}) collective-permute-start(bf16[64,4608]{1,0:T(8,128)(2,1)S(1)} %get-tuple-element.138.refs_2_), channel_id=1, source_target_pairs={{0,16},{1,9},{2,18},{3,11},{4,20},{5,13},{6,22},{7,15},{8,24},{9,1... | collective-permute-start | bytes 1769480 | tf_op jit(solution)/shard_map/ppermute | solution.py:439
  162.8 2.4 %collective-permute-start.20 = (bf16[512,256]{1,0:T(8,128)(2,1)S(1)}, bf16[512,256]{1,0:T(8,128)(2,1)S(1)}, u32[]{:S(2)}, u32[]{:S(2)}) collective-permute-start(bf16[512,256]{1,0:T(8,128)(2,1)S(1)} %get-tuple-element.127), channel_id=1, source_target_pairs={{0,1},{1,0},{2,3},{3,2},{4,5},{5,4},{6,7},{7,6},{8,9},{9,8},{10,11... | collective-permute-start | bytes 786440 | tf_op jit(solution)/shard_map/ppermute | solution.py:424
  162.8 21.0 %collective-permute-start.25 = (bf16[64,4608]{1,0:T(8,128)(2,1)S(1)}, bf16[64,4608]{1,0:T(8,128)(2,1)}, u32[]{:S(2)}, u32[]{:S(2)}) collective-permute-start(bf16[64,4608]{1,0:T(8,128)(2,1)S(1)} %get-tuple-element.138.refs_2_), channel_id=1, source_target_pairs={{0,8},{1,17},{2,10},{3,19},{4,12},{5,21},{6,14},{7,23},{8,0},{9,25... | collective-permute-start | bytes 1769480 | tf_op jit(solution)/shard_map/ppermute | solution.py:439
  171.5 0.6 copy-start.8
  176.5 0.8 copy-start.13
  181.5 10.4 %collective-permute-start.24 = (bf16[64,4608]{1,0:T(8,128)(2,1)}, bf16[64,4608]{1,0:T(8,128)(2,1)S(1)}, u32[]{:S(2)}, u32[]{:S(2)}) collective-permute-start(bf16[64,4608]{1,0:T(8,128)(2,1)} %get-tuple-element.140.refs_2_), channel_id=1, source_target_pairs={{0,8},{1,17},{2,10},{3,19},{4,12},{5,21},{6,14},{7,23},{8,0},{9,25... | collective-permute-start | bytes 1769480 | tf_op jit(solution)/shard_map/ppermute | solution.py:439
  191.9 0.8 copy-start.14

commit v7 on v6

--- a/solution.py
+++ b/solution.py
@@ -368,19 +368,22 @@
     count = len(pieces)
     columns = [lay.at_place(flips) for _, flips in pieces]
 
-    def at(n, sc):
+    def at(n, m, sc):
         row = sc[columns[0]]
         for p in range(1, count):
             row = jnp.where(n == p, sc[columns[p]], row)
-        return (row, 0)
-
-    block = (rows, width)
+        return (row, m)
+
+    def of(p):
+        return lambda n, m, sc: (0, jnp.where(n == p, m, jnp.where(n < p, 0, 1)))
+
+    block = (rows, width // 2)
     return call(
         functools.partial(adam_body, count, tokens),
         sc,
-        (count,),
+        (count, 2),
         [(first_moment, block, at), (second_moment, block, at)]
-        + [(x, block, first) for x, _ in pieces],
+        + [(x, block, of(p)) for p, (x, _) in enumerate(pieces)],
         [(first_moment.shape, F32, block, at)],
         before=before,
         through=through,
@@ -430,6 +433,13 @@
             perm += [(2 * a + core, 2 * b + core) for core in range(2)]
         return lax.ppermute(x, "shard", perm)
 
+    def backward(self, x):
+        perm = []
+        for p in range(self.z):
+            a, b = self.order[p], self.order[p - 1]
+            perm += [(2 * a + core, 2 * b + core) for core in range(2)]
+        return lax.ppermute(x, "shard", perm)
+
     def across(self, x, n):
         perm = []
         for r in range(self.replicas):
@@ -482,8 +492,10 @@
         box["part", (k + 1) % lay.z] = lay.onward(box["sum", k])
 
     def pass_weights(k):
-        if k + 1 < lay.z:
+        if k < middle:
             box["ring", k + 1] = lay.onward(box["ring", k])
+        elif k > middle + 1:
+            box["ring", k - 1] = lay.backward(box["ring", k])
 
     def cross_weights(k):
         box["cross", k] = lay.across(box["ring", k], 0)
@@ -505,8 +517,10 @@
         grads = run(backward, sc, k, block, own, box["gc", base], column, grads, lay, held=held)
 
     upstream_other = lay.sibling(upstream)
-    box["ring", 1], box["token"] = cut(sc, out_weight, lay)[0]
-    box["ring", 1] = lay.onward(box["ring", 1])
+    middle, last = lay.z // 2, lay.z - 1
+    half, box["token"] = cut(sc, out_weight, lay)[0]
+    box["ring", 1] = lay.onward(half)
+    box["ring", last] = lay.backward(half)
 
     late = [*range(2, lay.z), 0]
     rows = lay.rows
@@ -524,51 +538,54 @@
     for n, k in enumerate(late):
         contexts[k] = (both_sides, len(late) + n), (box["context"], n)
     do_product(2)
-    do_sum(1)
-    pass_sum(1)
     send(2)
     do_product(3)
     send(3)
+    do_sum(1)
+    pass_sum(1)
     do_grad_context([0, 1])
     swap_grad_context(0)
-    run(relay, sc, held=[("ring", 2)])
-    pass_weights(2)
-    cross_weights(2)
-    do_halve(2)
+    do_halve(2, held=[("ring", last)])
     send(2)
+    pass_weights(last)
+    cross_weights(last)
     do_backward(0)
     do_product(0)
     do_halve(3)
     send(3)
     do_backward(1, held=[("send", 0)])
     send(0)
-    do_sum(2)
+    for j in range(2, middle):
+        run(relay, sc, held=[("ring", j), ("ring", lay.z - j)])
+        pass_weights(j)
+        pass_weights(lay.z - j)
+        cross_weights(j)
+        cross_weights(lay.z - j)
+    do_sum(2, held=[("ring", middle)])
     pass_sum(2)
+    cross_weights(middle)
     for k in range(4, lay.z):
-        do_product(k, held=[("ring", k - 1)])
-        pass_weights(k - 1)
-        cross_weights(k - 1)
+        do_product(k)
         send(k)
         do_halve(k)
         send(k)
-    last = lay.z - 1
-    do_grad_context([2])
-    swap_grad_context(2)
-    do_sum(3, held=[("ring", last)])
+    do_grad_context([last])
+    swap_grad_context(last)
+    do_sum(3)
     pass_sum(3)
-    cross_weights(last)
-    do_backward(2)
+    do_backward(last)
     for k in range(4, lay.z):
         do_sum(k)
         pass_sum(k)
-    for k in range(3, last):
-        do_grad_context([k])
-        swap_grad_context(k)
-        do_backward(k)
+    for k in range(2, last):
+        if k != middle:
+            do_grad_context([k])
+            swap_grad_context(k)
+            do_backward(k)
     do_halve(0)
     send(0)
-    do_grad_context([last])
-    swap_grad_context(last)
+    do_grad_context([middle])
+    swap_grad_context(middle)
     do_sum(0)
 
     have = [(box["sum", 0], (False,) * lay.bits)]
@@ -579,9 +596,10 @@
 
     moments = first_moment, second_moment, tokens, lay
     direct = [spread(n, have[0]) for n in range(lay.bits - 1, -1, -1)]
-    do_backward(last)
+    do_backward(middle)
+    step = run(adam, sc, have, *moments, before=())
     box["got"] = direct[0][0]
-    step = run(adam, sc, have, *moments, before=(), held=["got"])
+    run(relay, sc, held=["got"])
     direct[0] = (box["got"], direct[0][1])
     near = [have[0], *direct]
     have = [have[0], direct[0]]

time: 198 us -> 202 us (1.020)
  the two profiles are of different devices: /device:TPU:0 before, /device:TPU:12 now
where the time goes in v7:
time: 202 us; the launch traced here: 201 us
  Pallas kernels  108 us (53%)
  starting transfers between devices  41.5 us (21%)
  waiting for transfers between devices  40.9 us (20%)
  local copies, waits for them, and re-layouts  9.74 us (5%)
    pallas_call x26, Pallas kernels, call(): pl.pallas_call(kernel, grid_spec=pltpu.PrefetchScalarGridSpec(num_scalar_...  108 us
    ppermute x14, starting transfers between devices, across(): return lax.ppermute(x, ('replica', 'shard'), perm)  32.3 us
    ppermute x14, waiting for transfers between devices, across(): return lax.ppermute(x, ('replica', 'shard'), perm)  32.2 us
    unnamed x34, local copies, waits for them, and re-layouts  8.83 us
    ppermute x5, waiting for transfers between devices, onward(): return lax.ppermute(x, 'shard', perm)  7.81 us
    ppermute x5, starting transfers between devices, onward(): return lax.ppermute(x, 'shard', perm)  7.08 us
  transfers between devices with their start and end apart: 26, of which 7 were waited for; matrix products, arithmetic and copies ran while one was open for 0% of the time, Pallas kernels for 51%

profile of v7, /device:TPU:12, one launch (start us, length us, event | category | flops | bytes accessed | tf_op | source)
XLA Modules:
  0.0 200.7 jit_solution(7352660724644320410)
XLA Ops:
  0.6 0.1 collective-permute-start
  0.7 0.7 dynamic-slice_bitcast_fusion.sc_ref
  1.4 1.7 copy-done.6
  3.1 0.6 shard_map.120
  3.8 0.1 copy.60.refs_4_
  3.9 0.8 copy-done.1
  4.7 1.2 copy-done.2
  5.9 1.2 copy-done.4
  7.1 3.7 %shard_map.121 = (bf16[512,512]{1,0:T(8,128)(2,1)S(1)}, f32[8,128]{1,0:T(8,128)S(1)}) custom-call(s32[15]{0:T(128)S(1)} %dynamic-slice_bitcast_fusion.sc_ref, bf16[512,2048]{1,0:T(8,128)(2,1)S(1)} %copy-done.1, bf16[512,1024]{1,0:T(8,128)(2,1)S(1)} %copy-done.2, bf16[512,1024]{1,0:T(8,128)(2,1)S(1)} %copy-done.4, ...), custom_call_target="tpu_custom_call", output_to_operand_aliasing={{1}: (6, {})} | custom-call | flops 1 | bytes 1 | tf_op jit(solution)/shard_map/pallas_call | solution.py:41
  10.8 0.5 collective-permute-start.1
  11.4 2.6 %collective-permute-start.3 = (bf16[256,2304]{1,0:T(8,128)(2,1)S(1)}, bf16[256,2304]{1,0:T(8,128)(2,1)S(1)}, u32[]{:S(2)}, u32[]{:S(2)}) collective-permute-start(bf16[256,2304]{1,0:T(8,128)(2,1)S(1)} %get-tuple-element.83), channel_id=1, source_target_pairs={{0,2},{1,3},{2,6},{3,7},{6,4},{7,5},{4,0},{5,1},{8,10},{9,11},{10,... | collective-permute-start | bytes 3538952 | tf_op jit(solution)/shard_map/ppermute | solution.py:434
  14.0 6.3 %shard_map.122 = (bf16[128,4608]{1,0:T(8,128)(2,1)S(1)}, bf16[128,4608]{1,0:T(8,128)(2,1)S(1)}, f32[8,128]{1,0:T(8,128)S(1)}) custom-call(s32[15]{0:T(128)S(1)} %dynamic-slice_bitcast_fusion.sc_ref, bf16[512,512]{1,0:T(8,128)(2,1)S(1)} %get-tuple-element.76.refs_0_, ...), custom_call_target="tpu_custom_call", output_to_operand_aliasing={{2}: (5, {})} | custom-call | flops 1 | bytes 1 | tf_op jit(solution)/shard_map/pallas_call | solution.py:41
  20.3 1.6 collective-permute-start.2
  21.8 9.6 %shard_map.123 = (bf16[1536,512]{1,0:T(8,128)(2,1)S(1)}, f32[8,128]{1,0:T(8,128)S(1)}) custom-call(s32[15]{0:T(128)S(1)} %dynamic-slice_bitcast_fusion.sc_ref, bf16[512,2048]{1,0:T(8,128)(2,1)S(1)} %copy-done.1, bf16[512,1024]{1,0:T(8,128)(2,1)S(1)} %copy-done.3, bf16[512,1024]{1,0:T(8,128)(2,1)S(1)} %copy-done.4, ...), custom_call_target="tpu_custom_call", output_to_operand_aliasing={{1}: (6, {})} | custom-call | flops 1 | bytes 1 | tf_op jit(solution)/shard_map/pallas_call | solution.py:41
  31.6 7.8 %collective-permute-done.3.refs_3_ = bf16[256,2304]{1,0:T(8,128)(2,1)S(1)} collective-permute-done((bf16[256,2304]{1,0:T(8,128)(2,1)S(1)}, bf16[256,2304]{1,0:T(8,128)(2,1)S(1)}, u32[]{:S(2)}, u32[]{:S(2)}) %collective-permute-start.3) | collective-permute-done | bytes 1179680 | tf_op jit(solution)/shard_map/ppermute | solution.py:434
  39.4 0.7 shard_map.124
  40.1 1.6 collective-permute-start.6
  41.7 1.2 collective-permute-start.8
  42.9 6.3 %shard_map.125 = (bf16[128,4608]{1,0:T(8,128)(2,1)S(1)}, bf16[128,4608]{1,0:T(8,128)(2,1)S(1)}, f32[8,128]{1,0:T(8,128)S(1)}) custom-call(s32[15]{0:T(128)S(1)} %dynamic-slice_bitcast_fusion.sc_ref, bf16[1536,512]{1,0:T(8,128)(2,1)S(1)} %get-tuple-element.79.refs_0_, ...), custom_call_target="tpu_custom_call", output_to_operand_aliasing={{2}: (5, {})} | custom-call | flops 1 | bytes 1 | tf_op jit(solution)/shard_map/pallas_call | solution.py:41
  49.2 0.6 collective-permute-start.5
  49.8 0.5 collective-permute-start.7
  50.3 6.3 %shard_map.126 = (bf16[128,4608]{1,0:T(8,128)(2,1)S(1)}, bf16[128,4608]{1,0:T(8,128)(2,1)S(1)}, f32[8,128]{1,0:T(8,128)S(1)}) custom-call(s32[15]{0:T(128)S(1)} %dynamic-slice_bitcast_fusion.sc_ref, bf16[1536,512]{1,0:T(8,128)(2,1)S(1)} %get-tuple-element.79.refs_0_, ...), custom_call_target="tpu_custom_call", output_to_operand_aliasing={{2}: (5, {})} | custom-call | flops 1 | bytes 1 | tf_op jit(solution)/shard_map/pallas_call | solution.py:41
  56.5 1.6 collective-permute-start.12
  58.2 7.9 %collective-permute-done.7.refs_2_ = bf16[64,4608]{1,0:T(8,128)(2,1)S(1)} collective-permute-done((bf16[64,4608]{1,0:T(8,128)(2,1)S(1)}, bf16[64,4608]{1,0:T(8,128)(2,1)S(1)}, u32[]{:S(2)}, u32[]{:S(2)}) %collective-permute-start.7) | collective-permute-done | bytes 589856 | tf_op jit(solution)/shard_map/ppermute | solution.py:449
  66.1 2.1 %collective-permute-start.13 = (bf16[256,2304]{1,0:T(8,128)(2,1)S(1)}, bf16[256,2304]{1,0:T(8,128)(2,1)S(1)}, u32[]{:S(2)}, u32[]{:S(2)}) collective-permute-start(bf16[256,2304]{1,0:T(8,128)(2,1)S(1)} %get-tuple-element.88.refs_3_), channel_id=1, source_target_pairs={{0,2},{1,3},{2,6},{3,7},{6,4},{7,5},{4,0},{5,1},{8,10},{9,11},{10,... | collective-permute-start | bytes 3538952 | tf_op jit(solution)/shard_map/ppermute | solution.py:434
  68.2 0.8 shard_map.127
  69.0 0.9 copy-done.7
  69.9 10.4 %shard_map.128 = (bf16[512,512]{1,0:T(8,128)(2,1)S(1)}, bf16[512,512]{1,0:T(8,128)(2,1)S(1)}, f32[8,128]{1,0:T(8,128)S(1)}) custom-call(s32[15]{0:T(128)S(1)} %dynamic-slice_bitcast_fusion.sc_ref, bf16[512,4608]{1,0:T(8,128)(2,1)S(1)} %copy-done, bf16[512,4608]{1,0:T(8,128)(2,1)} %collective-permute-done.refs_3_.refs_1_, ...), custom_call_target="tpu_custom_call", output_to_operand_aliasing={{2}: (6, {})} | custom-call | flops 1 | bytes 1 | tf_op jit(solution)/shard_map/pallas_call | solution.py:41
  80.4 0.7 shard_map.129
  81.1 1.5 collective-permute-start.16
  82.7 2.0 collective-permute-start.10
  84.7 21.6 %collective-permute-start.9 = (bf16[64,4608]{1,0:T(8,128)(2,1)S(1)}, bf16[64,4608]{1,0:T(8,128)(2,1)S(1)}, u32[]{:S(2)}, u32[]{:S(2)}) collective-permute-start(bf16[64,4608]{1,0:T(8,128)(2,1)S(1)} %get-tuple-element.94), channel_id=1, source_target_pairs={{0,16},{1,9},{2,18},{3,11},{4,20},{5,13},{6,22},{7,15},{8,24},{9,1... | collective-permute-start | bytes 1769480 | tf_op jit(solution)/shard_map/ppermute | solution.py:449
  106.3 6.3 %shard_map.130 = (bf16[512,2048]{1,0:T(8,128)(2,1)}, bf16[512,1024]{1,0:T(8,128)(2,1)}, bf16[512,1024]{1,0:T(8,128)(2,1)}, f32[8,128]{1,0:T(8,128)S(1)}) custom-call(s32[15]{0:T(128)S(1)} %dynamic-slice_bitcast_fusion.sc_ref, bf16[512,2048]{1,0:T(8,128)(2,1)S(1)} %copy-done.1, bf16[512,1024]{1,0:T(8,128)(2,1)S(1)} %copy-done.3, ...), custom_call_target="tpu_custom_call", output_to_operand_aliasing={{3}: (8, {})} | custom-call | flops 1 | bytes 1 | tf_op jit(solution)/shard_map/pallas_call | solution.py:41
  112.6 6.3 %shard_map.131 = (bf16[128,4608]{1,0:T(8,128)(2,1)S(1)}, bf16[128,4608]{1,0:T(8,128)(2,1)S(1)}, f32[8,128]{1,0:T(8,128)S(1)}) custom-call(s32[15]{0:T(128)S(1)} %dynamic-slice_bitcast_fusion.sc_ref, bf16[1536,512]{1,0:T(8,128)(2,1)S(1)} %get-tuple-element.79.refs_0_, ...), custom_call_target="tpu_custom_call", output_to_operand_aliasing={{2}: (5, {})} | custom-call | flops 1 | bytes 1 | tf_op jit(solution)/shard_map/pallas_call | solution.py:41
  118.9 0.7 shard_map.132
  119.6 6.3 %shard_map.133 = (bf16[512,2048]{1,0:T(8,128)(2,1)}, bf16[512,1024]{1,0:T(8,128)(2,1)}, bf16[512,1024]{1,0:T(8,128)(2,1)}, f32[8,128]{1,0:T(8,128)S(1)}, bf16[128,4608]{1,0:T(8,128)(2,1)S(1)}) custom-call(s32[15]{0:T(128)S(1)} %dynamic-slice_bitcast_fusion.sc_ref, ...), custom_call_target="tpu_custom_call", output_to_operand_aliasing={{0}: (8, {}), {1}: (9, {}), {2}: (10, {}), {3}: (11, {}), {... | custom-call | flops 1 | bytes 1 | tf_op jit(solution)/shard_map/pallas_call | solution.py:41
  125.9 0.5 collective-permute-start.15
  126.4 0.8 shard_map.134
  127.3 1.6 collective-permute-start.14
  128.9 6.5 %shard_map.135 = (bf16[512,256]{1,0:T(8,128)(2,1)S(1)}, bf16[512,256]{1,0:T(8,128)(2,1)S(1)}, f32[8,128]{1,0:T(8,128)S(1)}) custom-call(s32[15]{0:T(128)S(1)} %dynamic-slice_bitcast_fusion.sc_ref, bf16[512,4608]{1,0:T(8,128)(2,1)S(1)} %copy-done, bf16[512,4608]{1,0:T(8,128)(2,1)} %collective-permute-done.refs_3_.refs_1_, ...), custom_call_target="tpu_custom_call", output_to_operand_aliasing={{2}: (5, {})} | custom-call | flops 1 | bytes 1 | tf_op jit(solution)/shard_map/pallas_call | solution.py:41
  135.5 7.2 %collective-permute-done.18.refs_2_ = bf16[64,4608]{1,0:T(8,128)(2,1)S(1)} collective-permute-done((bf16[64,4608]{1,0:T(8,128)(2,1)S(1)}, bf16[64,4608]{1,0:T(8,128)(2,1)S(1)}, u32[]{:S(2)}, u32[]{:S(2)}) %collective-permute-start.18) | collective-permute-done | bytes 589856 | tf_op jit(solution)/shard_map/ppermute | solution.py:449
  142.7 0.8 shard_map.136
  143.5 0.3 collective-permute-start.22
  143.8 6.3 %shard_map.137 = (bf16[512,2048]{1,0:T(8,128)(2,1)}, bf16[512,1024]{1,0:T(8,128)(2,1)}, bf16[512,1024]{1,0:T(8,128)(2,1)}, f32[8,128]{1,0:T(8,128)S(1)}) custom-call(s32[15]{0:T(128)S(1)} %dynamic-slice_bitcast_fusion.sc_ref, bf16[512,2048]{1,0:T(8,128)(2,1)S(1)} %copy-done.1, ...), custom_call_target="tpu_custom_call", output_to_operand_aliasing={{0}: (8, {}), {1}: (9, {}), {2}: (10, {}), {3}: (11, {})} | custom-call | flops 1 | bytes 1 | tf_op jit(solution)/shard_map/pallas_call | solution.py:41
  150.1 0.7 shard_map.138
  150.8 0.1 collective-permute-start.21
  150.9 10.1 %collective-permute-done.14.refs_3_ = bf16[256,2304]{1,0:T(8,128)(2,1)S(1)} collective-permute-done((bf16[256,2304]{1,0:T(8,128)(2,1)S(1)}, bf16[256,2304]{1,0:T(8,128)(2,1)S(1)}, u32[]{:S(2)}, u32[]{:S(2)}) %collective-permute-start.14) | collective-permute-done | bytes 1179680 | tf_op jit(solution)/shard_map/ppermute | solution.py:449
  161.0 6.5 %shard_map.139 = (bf16[512,256]{1,0:T(8,128)(2,1)S(1)}, bf16[512,256]{1,0:T(8,128)(2,1)S(1)}, f32[8,128]{1,0:T(8,128)S(1)}) custom-call(s32[15]{0:T(128)S(1)} %dynamic-slice_bitcast_fusion.sc_ref, bf16[512,4608]{1,0:T(8,128)(2,1)S(1)} %copy-done, bf16[512,4608]{1,0:T(8,128)(2,1)} %collective-permute-done.refs_3_.refs_1_, ...), custom_call_target="tpu_custom_call", output_to_operand_aliasing={{2}: (5, {})} | custom-call | flops 1 | bytes 1 | tf_op jit(solution)/shard_map/pallas_call | solution.py:41
  167.6 0.8 shard_map.140
  168.6 0.6 collective-permute-start.25
  169.2 0.9 collective-permute-done.20.refs_6_
  170.1 6.3 %shard_map.141 = (bf16[512,2048]{1,0:T(8,128)(2,1)}, bf16[512,1024]{1,0:T(8,128)(2,1)}, bf16[512,1024]{1,0:T(8,128)(2,1)}, f32[8,128]{1,0:T(8,128)S(1)}) custom-call(s32[15]{0:T(128)S(1)} %dynamic-slice_bitcast_fusion.sc_ref, bf16[512,2048]{1,0:T(8,128)(2,1)S(1)} %copy-done.1, ...), custom_call_target="tpu_custom_call", output_to_operand_aliasing={{0}: (8, {}), {1}: (9, {}), {2}: (10, {}), {3}: (11, {})} | custom-call | flops 1 | bytes 1 | tf_op jit(solution)/shard_map/pallas_call | solution.py:41
  176.4 0.6 copy-done.8
  177.0 3.8 %shard_map.142 = (f32[256,4608]{1,0:T(8,128)}, f32[8,128]{1,0:T(8,128)}) custom-call(s32[15]{0:T(128)} %copy-done.13, f32[256,4608]{1,0:T(8,128)} %refs_0_.25, f32[256,4608]{1,0:T(8,128)} %refs_1_.17, bf16[64,4608]{1,0:T(8,128)(2,1)} %copy-done.12, f32[8,128]{1,0:T(8,128)} %copy-done.8), custom_call_target="tpu_custom_call", output_to_operand_aliasing={{1}: (4, {})} | custom-call | flops 1 | bytes 1 | tf_op jit(solution)/shard_map/pallas_call | solution.py:41
  180.8 3.8 %collective-permute-done.23.refs_1_ = bf16[64,4608]{1,0:T(8,128)(2,1)S(1)} collective-permute-done((bf16[64,4608]{1,0:T(8,128)(2,1)S(1)}, bf16[64,4608]{1,0:T(8,128)(2,1)S(1)}, u32[]{:S(2)}, u32[]{:S(2)}) %collective-permute-start.23) | collective-permute-done | bytes 589856 | tf_op jit(solution)/shard_map/ppermute | solution.py:449
  184.5 0.7 copy-done.9
  185.2 0.5 shard_map.143
  185.8 0.6 copy-done.10
  186.3 0.5 collective-permute-start.24
  186.9 0.3 copy-done.11
  187.2 5.9 %shard_map.144 = (f32[256,4608]{1,0:T(8,128)}, f32[8,128]{1,0:T(8,128)}) custom-call(s32[15]{0:T(128)} %copy-done.13, f32[256,4608]{1,0:T(8,128)} %refs_0_.25, f32[256,4608]{1,0:T(8,128)} %refs_1_.17, bf16[64,4608]{1,0:T(8,128)(2,1)} %copy-done.11, bf16[64,4608]{1,0:T(8,128)(2,1)} %collective-permute-done.25.refs_3_, ...), custom_call_target="tpu_custom_call", output_to_operand_aliasing={{0}: (5, {}), {1}: (6, {})} | custom-call | flops 1 | bytes 1 | tf_op jit(solution)/shard_map/pallas_call | solution.py:41
  193.1 3.2 %collective-permute-done.24.refs_2_ = bf16[64,4608]{1,0:T(8,128)(2,1)S(1)} collective-permute-done((bf16[64,4608]{1,0:T(8,128)(2,1)S(1)}, bf16[64,4608]{1,0:T(8,128)(2,1)S(1)}, u32[]{:S(2)}, u32[]{:S(2)}) %collective-permute-start.24) | collective-permute-done | bytes 589856 | tf_op jit(solution)/shard_map/ppermute | solution.py:449
  196.2 0.8 copy-done.16
  197.1 3.6 %shard_map.145 = (f32[256,4608]{1,0:T(8,128)}, f32[8,128]{1,0:T(8,128)}) custom-call(s32[15]{0:T(128)} %copy-done.13, f32[256,4608]{1,0:T(8,128)} %refs_0_.25, f32[256,4608]{1,0:T(8,128)} %refs_1_.17, bf16[64,4608]{1,0:T(8,128)(2,1)} %copy-done.16, f32[256,4608]{1,0:T(8,128)} %get-tuple-element.143.refs_3_, ...), custom_call_target="tpu_custom_call", output_to_operand_aliasing={{0}: (4, {}), {1}: (5, {})} | custom-call | flops 1 | bytes 1 | tf_op jit(solution)/shard_map/pallas_call | solution.py:41
  (52 shorter events, 0.7 us)
Async XLA Ops:
  0.6 13.4 %collective-permute-start = (bf16[512,4608]{1,0:T(8,128)(2,1)}, bf16[512,4608]{1,0:T(8,128)(2,1)}, u32[]{:S(2)}, u32[]{:S(2)}) collective-permute-start(bf16[512,4608]{1,0:T(8,128)(2,1)} %refs_0_.21), channel_id=1, source_target_pairs={{0,1},{1,0},{2,3},{3,2},{4,5},{5,4},{6,7},{7,6},{8,9},{9,8},{10,11... | collective-permute-start | bytes 14155784 | tf_op jit(solution)/shard_map/ppermute | solution.py:427
  1.4 1.7 copy-start.6
  3.1 167.0 %copy-start.13 = (s32[15]{0:T(128)}, s32[15]{0:T(128)S(1)}, u32[]{:S(2)}) copy-start(s32[15]{0:T(128)S(1)} %dynamic-slice_bitcast_fusion.sc_ref) | copy-start | bytes 184
  3.1 0.7 copy-start.15
  3.1 1.6 copy-start.1
  4.7 1.2 copy-start.2
  5.9 1.2 copy-start.4
  7.1 6.8 %copy-start = (bf16[512,4608]{1,0:T(8,128)(2,1)S(1)}, bf16[512,4608]{1,0:T(8,128)(2,1)}, u32[]{:S(2)}) copy-start(bf16[512,4608]{1,0:T(8,128)(2,1)} %refs_0_.21) | copy-start | bytes 14155780
  10.8 3.1 %collective-permute-start.1 = (bf16[256,512]{1,0:T(8,128)(2,1)S(1)}, bf16[256,512]{1,0:T(8,128)(2,1)S(1)}, u32[]{:S(2)}, u32[]{:S(2)}) collective-permute-start(bf16[256,512]{1,0:T(8,128)(2,1)S(1)} %slice.6), channel_id=1, source_target_pairs={{0,1},{1,0},{2,3},{3,2},{4,5},{5,4},{6,7},{7,6},{8,9},{9,8},{10,11... | collective-permute-start | bytes 786440 | tf_op jit(solution)/shard_map/ppermute | solution.py:427
  11.4 28.0 %collective-permute-start.3 = (bf16[256,2304]{1,0:T(8,128)(2,1)S(1)}, bf16[256,2304]{1,0:T(8,128)(2,1)S(1)}, u32[]{:S(2)}, u32[]{:S(2)}) collective-permute-start(bf16[256,2304]{1,0:T(8,128)(2,1)S(1)} %get-tuple-element.83), channel_id=1, source_target_pairs={{0,2},{1,3},{2,6},{3,7},{6,4},{7,5},{4,0},{5,1},{8,10},{9,11},{10,... | collective-permute-start | bytes 3538952 | tf_op jit(solution)/shard_map/ppermute | solution.py:434
  14.0 7.9 %copy-start.3 = (bf16[512,1024]{1,0:T(8,128)(2,1)S(1)}, bf16[512,1024]{1,0:T(8,128)(2,1)}, u32[]{:S(2)}) copy-start(bf16[512,1024]{1,0:T(8,128)(2,1)} %refs_1_.14) | copy-start | bytes 3145732
  20.3 19.1 %collective-permute-start.2 = (bf16[128,4608]{1,0:T(8,128)(2,1)S(1)}, bf16[128,4608]{1,0:T(8,128)(2,1)S(1)}, u32[]{:S(2)}, u32[]{:S(2)}) collective-permute-start(bf16[128,4608]{1,0:T(8,128)(2,1)S(1)} %get-tuple-element.81), channel_id=1, source_target_pairs={{0,8},{1,17},{2,10},{3,19},{4,12},{5,21},{6,14},{7,23},{8,0},{9,25... | collective-permute-start | bytes 3538952 | tf_op jit(solution)/shard_map/ppermute | solution.py:449
  31.6 7.9 %collective-permute-start.4 = (bf16[768,512]{1,0:T(8,128)(2,1)S(1)}, bf16[768,512]{1,0:T(8,128)(2,1)S(1)}, u32[]{:S(2)}, u32[]{:S(2)}) collective-permute-start(bf16[768,512]{1,0:T(8,128)(2,1)S(1)} %slice.7), channel_id=1, source_target_pairs={{0,1},{1,0},{2,3},{3,2},{4,5},{5,4},{6,7},{7,6},{8,9},{9,8},{10,11... | collective-permute-start | bytes 2359304 | tf_op jit(solution)/shard_map/ppermute | solution.py:427
  40.1 28.9 %collective-permute-start.6 = (bf16[256,2304]{1,0:T(8,128)(2,1)S(1)}, bf16[256,2304]{1,0:T(8,128)(2,1)S(1)}, u32[]{:S(2)}, u32[]{:S(2)}) collective-permute-start(bf16[256,2304]{1,0:T(8,128)(2,1)S(1)} %get-tuple-element.88.refs_3_), channel_id=1, source_target_pairs={{0,8},{1,17},{2,10},{3,19},{4,12},{5,21},{6,14},{7,23},{8,0},{9,25... | collective-permute-start | bytes 3538952 | tf_op jit(solution)/shard_map/ppermute | solution.py:449
  41.7 38.7 %collective-permute-start.8 = (bf16[256,2304]{1,0:T(8,128)(2,1)S(1)}, bf16[256,2304]{1,0:T(8,128)(2,1)S(1)}, u32[]{:S(2)}, u32[]{:S(2)}) collective-permute-start(bf16[256,2304]{1,0:T(8,128)(2,1)S(1)} %get-tuple-element.83), channel_id=1, source_target_pairs={{0,4},{1,5},{2,0},{3,1},{6,2},{7,3},{4,6},{5,7},{8,12},{9,13},{10,... | collective-permute-start | bytes 3538952 | tf_op jit(solution)/shard_map/ppermute | solution.py:441
  49.2 31.2 %collective-permute-start.5 = (bf16[128,4608]{1,0:T(8,128)(2,1)S(1)}, bf16[128,4608]{1,0:T(8,128)(2,1)S(1)}, u32[]{:S(2)}, u32[]{:S(2)}) collective-permute-start(bf16[128,4608]{1,0:T(8,128)(2,1)S(1)} %get-tuple-element.87), channel_id=1, source_target_pairs={{0,8},{1,17},{2,10},{3,19},{4,12},{5,21},{6,14},{7,23},{8,0},{9,25... | collective-permute-start | bytes 3538952 | tf_op jit(solution)/shard_map/ppermute | solution.py:449
  49.8 16.3 %collective-permute-start.7 = (bf16[64,4608]{1,0:T(8,128)(2,1)S(1)}, bf16[64,4608]{1,0:T(8,128)(2,1)S(1)}, u32[]{:S(2)}, u32[]{:S(2)}) collective-permute-start(bf16[64,4608]{1,0:T(8,128)(2,1)S(1)} %get-tuple-element.89), channel_id=1, source_target_pairs={{0,16},{1,9},{2,18},{3,11},{4,20},{5,13},{6,22},{7,15},{8,24},{9,1... | collective-permute-start | bytes 1769480 | tf_op jit(solution)/shard_map/ppermute | solution.py:449
  56.5 62.3 %collective-permute-start.12 = (bf16[128,4608]{1,0:T(8,128)(2,1)S(1)}, bf16[128,4608]{1,0:T(8,128)(2,1)S(1)}, u32[]{:S(2)}, u32[]{:S(2)}) collective-permute-start(bf16[128,4608]{1,0:T(8,128)(2,1)S(1)} %get-tuple-element.103), channel_id=1, source_target_pairs={{0,8},{1,17},{2,10},{3,19},{4,12},{5,21},{6,14},{7,23},{8,0},{9,25... | collective-permute-start | bytes 3538952 | tf_op jit(solution)/shard_map/ppermute | solution.py:449
  66.1 60.3 %collective-permute-start.13 = (bf16[256,2304]{1,0:T(8,128)(2,1)S(1)}, bf16[256,2304]{1,0:T(8,128)(2,1)S(1)}, u32[]{:S(2)}, u32[]{:S(2)}) collective-permute-start(bf16[256,2304]{1,0:T(8,128)(2,1)S(1)} %get-tuple-element.88.refs_3_), channel_id=1, source_target_pairs={{0,2},{1,3},{2,6},{3,7},{6,4},{7,5},{4,0},{5,1},{8,10},{9,11},{10,... | collective-permute-start | bytes 3538952 | tf_op jit(solution)/shard_map/ppermute | solution.py:434
  68.2 1.7 copy-start.7
  80.3 4.4 %collective-permute-start.11 = (bf16[512,512]{1,0:T(8,128)(2,1)S(1)}, bf16[512,512]{1,0:T(8,128)(2,1)S(1)}, u32[]{:S(2)}, u32[]{:S(2)}) collective-permute-start(bf16[512,512]{1,0:T(8,128)(2,1)S(1)} %get-tuple-element.97), channel_id=1, source_target_pairs={{0,1},{1,0},{2,3},{3,2},{4,5},{5,4},{6,7},{7,6},{8,9},{9,8},{10,11... | collective-permute-start | bytes 1572872 | tf_op jit(solution)/shard_map/ppermute | solution.py:427
  80.4 25.8 %copy-start.5 = (bf16[512,1024]{1,0:T(8,128)(2,1)S(1)}, bf16[512,1024]{1,0:T(8,128)(2,1)}, u32[]{:S(2)}) copy-start(bf16[512,1024]{1,0:T(8,128)(2,1)} %refs_2_.21) | copy-start | bytes 3145732
  81.1 47.8 %collective-permute-start.16 = (bf16[256,2304]{1,0:T(8,128)(2,1)S(1)}, bf16[256,2304]{1,0:T(8,128)(2,1)S(1)}, u32[]{:S(2)}, u32[]{:S(2)}) collective-permute-start(bf16[256,2304]{1,0:T(8,128)(2,1)S(1)} %get-tuple-element.112.refs_2_), channel_id=1, source_target_pairs={{0,8},{1,17},{2,10},{3,19},{4,12},{5,21},{6,14},{7,23},{8,0},{9,25... | collective-permute-start | bytes 3538952 | tf_op jit(solution)/shard_map/ppermute | solution.py:449
  82.7 43.8 %collective-permute-start.10 = (bf16[64,4608]{1,0:T(8,128)(2,1)S(1)}, bf16[64,4608]{1,0:T(8,128)(2,1)S(1)}, u32[]{:S(2)}, u32[]{:S(2)}) collective-permute-start(bf16[64,4608]{1,0:T(8,128)(2,1)S(1)} %get-tuple-element.95), channel_id=1, source_target_pairs={{0,2},{1,3},{2,6},{3,7},{6,4},{7,5},{4,0},{5,1},{8,10},{9,11},{10,... | collective-permute-start | bytes 1769480 | tf_op jit(solution)/shard_map/ppermute | solution.py:434
  84.7 41.7 %collective-permute-start.9 = (bf16[64,4608]{1,0:T(8,128)(2,1)S(1)}, bf16[64,4608]{1,0:T(8,128)(2,1)S(1)}, u32[]{:S(2)}, u32[]{:S(2)}) collective-permute-start(bf16[64,4608]{1,0:T(8,128)(2,1)S(1)} %get-tuple-element.94), channel_id=1, source_target_pairs={{0,16},{1,9},{2,18},{3,11},{4,20},{5,13},{6,22},{7,15},{8,24},{9,1... | collective-permute-start | bytes 1769480 | tf_op jit(solution)/shard_map/ppermute | solution.py:449
  125.9 24.2 %collective-permute-start.15 = (bf16[128,4608]{1,0:T(8,128)(2,1)S(1)}, bf16[128,4608]{1,0:T(8,128)(2,1)S(1)}, u32[]{:S(2)}, u32[]{:S(2)}) collective-permute-start(bf16[128,4608]{1,0:T(8,128)(2,1)S(1)} %get-tuple-element.111), channel_id=1, source_target_pairs={{0,8},{1,17},{2,10},{3,19},{4,12},{5,21},{6,14},{7,23},{8,0},{9,25... | collective-permute-start | bytes 3538952 | tf_op jit(solution)/shard_map/ppermute | solution.py:449
  126.4 16.3 %collective-permute-start.18 = (bf16[64,4608]{1,0:T(8,128)(2,1)S(1)}, bf16[64,4608]{1,0:T(8,128)(2,1)S(1)}, u32[]{:S(2)}, u32[]{:S(2)}) collective-permute-start(bf16[64,4608]{1,0:T(8,128)(2,1)S(1)} %get-tuple-element.119), channel_id=1, source_target_pairs={{0,16},{1,9},{2,18},{3,11},{4,20},{5,13},{6,22},{7,15},{8,24},{9,1... | collective-permute-start | bytes 1769480 | tf_op jit(solution)/shard_map/ppermute | solution.py:449
  127.3 15.4 %collective-permute-start.19 = (bf16[64,4608]{1,0:T(8,128)(2,1)S(1)}, bf16[64,4608]{1,0:T(8,128)(2,1)S(1)}, u32[]{:S(2)}, u32[]{:S(2)}) collective-permute-start(bf16[64,4608]{1,0:T(8,128)(2,1)S(1)} %get-tuple-element.120), channel_id=1, source_target_pairs={{0,2},{1,3},{2,6},{3,7},{6,4},{7,5},{4,0},{5,1},{8,10},{9,11},{10,... | collective-permute-start | bytes 1769480 | tf_op jit(solution)/shard_map/ppermute | solution.py:434
  127.3 33.7 %collective-permute-start.14 = (bf16[256,2304]{1,0:T(8,128)(2,1)S(1)}, bf16[256,2304]{1,0:T(8,128)(2,1)S(1)}, u32[]{:S(2)}, u32[]{:S(2)}) collective-permute-start(bf16[256,2304]{1,0:T(8,128)(2,1)S(1)} %get-tuple-element.109.refs_2_), channel_id=1, source_target_pairs={{0,8},{1,17},{2,10},{3,19},{4,12},{5,21},{6,14},{7,23},{8,0},{9,25... | collective-permute-start | bytes 3538952 | tf_op jit(solution)/shard_map/ppermute | solution.py:449
  135.4 8.4 %collective-permute-start.17 = (bf16[512,256]{1,0:T(8,128)(2,1)S(1)}, bf16[512,256]{1,0:T(8,128)(2,1)S(1)}, u32[]{:S(2)}, u32[]{:S(2)}) collective-permute-start(bf16[512,256]{1,0:T(8,128)(2,1)S(1)} %get-tuple-element.115), channel_id=1, source_target_pairs={{0,1},{1,0},{2,3},{3,2},{4,5},{5,4},{6,7},{7,6},{8,9},{9,8},{10,11... | collective-permute-start | bytes 786440 | tf_op jit(solution)/shard_map/ppermute | solution.py:427
  143.5 24.0 %collective-permute-start.22 = (bf16[64,4608]{1,0:T(8,128)(2,1)S(1)}, bf16[64,4608]{1,0:T(8,128)(2,1)S(1)}, u32[]{:S(2)}, u32[]{:S(2)}) collective-permute-start(bf16[64,4608]{1,0:T(8,128)(2,1)S(1)} %get-tuple-element.131), channel_id=1, source_target_pairs={{0,2},{1,3},{2,6},{3,7},{6,4},{7,5},{4,0},{5,1},{8,10},{9,11},{10,... | collective-permute-start | bytes 1769480 | tf_op jit(solution)/shard_map/ppermute | solution.py:434
  150.8 16.8 %collective-permute-start.21 = (bf16[64,4608]{1,0:T(8,128)(2,1)S(1)}, bf16[64,4608]{1,0:T(8,128)(2,1)S(1)}, u32[]{:S(2)}, u32[]{:S(2)}) collective-permute-start(bf16[64,4608]{1,0:T(8,128)(2,1)S(1)} %get-tuple-element.130), channel_id=1, source_target_pairs={{0,16},{1,9},{2,18},{3,11},{4,20},{5,13},{6,22},{7,15},{8,24},{9,1... | collective-permute-start | bytes 1769480 | tf_op jit(solution)/shard_map/ppermute | solution.py:449
  168.4 8.0 %copy-start.12 = (bf16[64,4608]{1,0:T(8,128)(2,1)}, bf16[64,4608]{1,0:T(8,128)(2,1)S(1)}, u32[]{:S(2)}) copy-start(bf16[64,4608]{1,0:T(8,128)(2,1)S(1)} %get-tuple-element.137.refs_2_) | copy-start | bytes 1769476
  168.4 16.1 %collective-permute-start.23 = (bf16[64,4608]{1,0:T(8,128)(2,1)S(1)}, bf16[64,4608]{1,0:T(8,128)(2,1)S(1)}, u32[]{:S(2)}, u32[]{:S(2)}) collective-permute-start(bf16[64,4608]{1,0:T(8,128)(2,1)S(1)} %get-tuple-element.137.refs_2_), channel_id=1, source_target_pairs={{0,16},{1,9},{2,18},{3,11},{4,20},{5,13},{6,22},{7,15},{8,24},{9,1... | collective-permute-start | bytes 1769480 | tf_op jit(solution)/shard_map/ppermute | solution.py:449
  168.5 1.6 collective-permute-start.20
  168.6 18.3 %collective-permute-start.25 = (bf16[64,4608]{1,0:T(8,128)(2,1)S(1)}, bf16[64,4608]{1,0:T(8,128)(2,1)}, u32[]{:S(2)}, u32[]{:S(2)}) collective-permute-start(bf16[64,4608]{1,0:T(8,128)(2,1)S(1)} %get-tuple-element.137.refs_2_), channel_id=1, source_target_pairs={{0,8},{1,17},{2,10},{3,19},{4,12},{5,21},{6,14},{7,23},{8,0},{9,25... | collective-permute-start | bytes 1769480 | tf_op jit(solution)/shard_map/ppermute | solution.py:449
  176.4 0.6 copy-start.8
  177.0 7.5 %copy-start.14 = (s32[15]{0:T(128)S(1)}, s32[15]{0:T(128)}, u32[]{:S(2)}) copy-start(s32[15]{0:T(128)} %copy-done.13) | copy-start | bytes 184
  184.5 0.7 copy-start.9
  185.8 0.6 copy-start.10
  186.3 0.8 copy-start.11
  186.3 9.9 %collective-permute-start.24 = (bf16[64,4608]{1,0:T(8,128)(2,1)S(1)}, bf16[64,4608]{1,0:T(8,128)(2,1)S(1)}, u32[]{:S(2)}, u32[]{:S(2)}) collective-permute-start(bf16[64,4608]{1,0:T(8,128)(2,1)S(1)} %get-tuple-element.140.refs_2_), channel_id=1, source_target_pairs={{0,8},{1,17},{2,10},{3,19},{4,12},{5,21},{6,14},{7,23},{8,0},{9,25... | collective-permute-start | bytes 1769480 | tf_op jit(solution)/shard_map/ppermute | solution.py:449
  196.2 0.8 copy-start.16

commit v8 on v6

--- a/solution.py
+++ b/solution.py
@@ -368,19 +368,22 @@
     count = len(pieces)
     columns = [lay.at_place(flips) for _, flips in pieces]
 
-    def at(n, sc):
+    def at(n, m, sc):
         row = sc[columns[0]]
         for p in range(1, count):
             row = jnp.where(n == p, sc[columns[p]], row)
-        return (row, 0)
-
-    block = (rows, width)
+        return (row, m)
+
+    def of(p):
+        return lambda n, m, sc: (0, jnp.where(n == p, m, jnp.where(n < p, 0, 1)))
+
+    block = (rows, width // 2)
     return call(
         functools.partial(adam_body, count, tokens),
         sc,
-        (count,),
+        (count, 2),
         [(first_moment, block, at), (second_moment, block, at)]
-        + [(x, block, first) for x, _ in pieces],
+        + [(x, block, of(p)) for p, (x, _) in enumerate(pieces)],
         [(first_moment.shape, F32, block, at)],
         before=before,
         through=through,
@@ -580,8 +583,9 @@
     moments = first_moment, second_moment, tokens, lay
     direct = [spread(n, have[0]) for n in range(lay.bits - 1, -1, -1)]
     do_backward(last)
+    step = run(adam, sc, have, *moments, before=())
     box["got"] = direct[0][0]
-    step = run(adam, sc, have, *moments, before=(), held=["got"])
+    run(relay, sc, held=["got"])
     direct[0] = (box["got"], direct[0][1])
     near = [have[0], *direct]
     have = [have[0], direct[0]]

time: 198 us -> 194 us (0.980)
  waiting for transfers between devices: 50.3 us -> 45.4 us
    ppermute x14, waiting for transfers between devices: 28.4 us -> 23.7 us  [across(): return lax.ppermute(x, ('replica', 'shard'), perm)]
    unnamed x30 -> x34, local copies, waits for them, and re-layouts: 7.38 us -> 7.67 us
    pallas_call x26 -> x27, Pallas kernels: 108 us -> 108 us  [call(): pl.pallas_call(kernel, grid_spec=pltpu.PrefetchScalarGridSpec(num_scalar_...]
  transfers between devices with their start and end apart: 26 -> 26, of which waited for: 8 -> 8; matrix products, arithmetic and copies ran while one was open for 0% -> 0% of each run, Pallas kernels for 52% -> 53%
where the time goes in v8:
time: 194 us; the launch traced here: 193 us
  Pallas kernels  108 us (56%)
  waiting for transfers between devices  45.4 us (23%)
  starting transfers between devices  29.6 us (15%)
  local copies, waits for them, and re-layouts  8.57 us (4%)
    pallas_call x27, Pallas kernels, call(): pl.pallas_call(kernel, grid_spec=pltpu.PrefetchScalarGridSpec(num_scalar_...  108 us
    ppermute x14, waiting for transfers between devices, across(): return lax.ppermute(x, ('replica', 'shard'), perm)  23.7 us
    ppermute x6, waiting for transfers between devices, onward(): return lax.ppermute(x, 'shard', perm)  20.9 us
    ppermute x14, starting transfers between devices, across(): return lax.ppermute(x, ('replica', 'shard'), perm)  19.9 us
    ppermute x6, starting transfers between devices, onward(): return lax.ppermute(x, 'shard', perm)  8.92 us
    unnamed x34, local copies, waits for them, and re-layouts  7.67 us
  transfers between devices with their start and end apart: 26, of which 8 were waited for; matrix products, arithmetic and copies ran while one was open for 0% of the time, Pallas kernels for 53%

profile of v8, /device:TPU:0, one launch (start us, length us, event | category | flops | bytes accessed | tf_op | source)
XLA Modules:
  0.0 192.6 jit_solution(2251702849981141682)
XLA Ops:
  0.6 0.5 collective-permute-start
  1.1 0.7 dynamic-slice_bitcast_fusion.sc_ref
  1.8 1.7 copy-done.6
  3.5 0.6 shard_map.120
  4.3 0.8 copy-done.1
  5.1 1.2 copy-done.2
  6.3 1.2 copy-done.4
  7.6 3.7 %shard_map.121 = (bf16[512,512]{1,0:T(8,128)(2,1)S(1)}, f32[8,128]{1,0:T(8,128)S(1)}) custom-call(s32[15]{0:T(128)S(1)} %dynamic-slice_bitcast_fusion.sc_ref, bf16[512,2048]{1,0:T(8,128)(2,1)S(1)} %copy-done.1, bf16[512,1024]{1,0:T(8,128)(2,1)S(1)} %copy-done.2, bf16[512,1024]{1,0:T(8,128)(2,1)S(1)} %copy-done.4, ...), custom_call_target="tpu_custom_call", output_to_operand_aliasing={{1}: (6, {})} | custom-call | flops 1 | bytes 1 | tf_op jit(solution)/shard_map/pallas_call | solution.py:41
  11.4 3.0 %collective-permute-start.3 = (bf16[256,2304]{1,0:T(8,128)(2,1)S(1)}, bf16[256,2304]{1,0:T(8,128)(2,1)S(1)}, u32[]{:S(2)}, u32[]{:S(2)}) collective-permute-start(bf16[256,2304]{1,0:T(8,128)(2,1)S(1)} %get-tuple-element.84), channel_id=1, source_target_pairs={{0,2},{1,3},{2,6},{3,7},{6,4},{7,5},{4,0},{5,1},{8,10},{9,11},{10,... | collective-permute-start | bytes 3538952 | tf_op jit(solution)/shard_map/ppermute | solution.py:434
  14.4 6.3 %shard_map.122 = (bf16[128,4608]{1,0:T(8,128)(2,1)S(1)}, bf16[128,4608]{1,0:T(8,128)(2,1)S(1)}, f32[8,128]{1,0:T(8,128)S(1)}) custom-call(s32[15]{0:T(128)S(1)} %dynamic-slice_bitcast_fusion.sc_ref, bf16[512,512]{1,0:T(8,128)(2,1)S(1)} %get-tuple-element.77.refs_0_, ...), custom_call_target="tpu_custom_call", output_to_operand_aliasing={{2}: (5, {})} | custom-call | flops 1 | bytes 1 | tf_op jit(solution)/shard_map/pallas_call | solution.py:41
  20.7 1.6 collective-permute-start.2
  22.3 9.6 %shard_map.123 = (bf16[1536,512]{1,0:T(8,128)(2,1)S(1)}, f32[8,128]{1,0:T(8,128)S(1)}) custom-call(s32[15]{0:T(128)S(1)} %dynamic-slice_bitcast_fusion.sc_ref, bf16[512,2048]{1,0:T(8,128)(2,1)S(1)} %copy-done.1, bf16[512,1024]{1,0:T(8,128)(2,1)S(1)} %copy-done.3, bf16[512,1024]{1,0:T(8,128)(2,1)S(1)} %copy-done.4, ...), custom_call_target="tpu_custom_call", output_to_operand_aliasing={{1}: (6, {})} | custom-call | flops 1 | bytes 1 | tf_op jit(solution)/shard_map/pallas_call | solution.py:41
  32.1 9.5 %collective-permute-done.3.refs_3_ = bf16[256,2304]{1,0:T(8,128)(2,1)S(1)} collective-permute-done((bf16[256,2304]{1,0:T(8,128)(2,1)S(1)}, bf16[256,2304]{1,0:T(8,128)(2,1)S(1)}, u32[]{:S(2)}, u32[]{:S(2)}) %collective-permute-start.3) | collective-permute-done | bytes 1179680 | tf_op jit(solution)/shard_map/ppermute | solution.py:434
  41.6 0.7 shard_map.124
  42.3 1.6 collective-permute-start.7
  43.9 1.5 collective-permute-start.5
  45.4 0.8 collective-permute-start.10
  46.2 6.3 %shard_map.125 = (bf16[128,4608]{1,0:T(8,128)(2,1)S(1)}, bf16[128,4608]{1,0:T(8,128)(2,1)S(1)}, f32[8,128]{1,0:T(8,128)S(1)}) custom-call(s32[15]{0:T(128)S(1)} %dynamic-slice_bitcast_fusion.sc_ref, bf16[1536,512]{1,0:T(8,128)(2,1)S(1)} %get-tuple-element.80.refs_0_, ...), custom_call_target="tpu_custom_call", output_to_operand_aliasing={{2}: (5, {})} | custom-call | flops 1 | bytes 1 | tf_op jit(solution)/shard_map/pallas_call | solution.py:41
  52.5 0.6 collective-permute-start.9
  53.1 7.1 %collective-permute-done.5.refs_2_ = bf16[64,4608]{1,0:T(8,128)(2,1)S(1)} collective-permute-done((bf16[64,4608]{1,0:T(8,128)(2,1)S(1)}, bf16[64,4608]{1,0:T(8,128)(2,1)S(1)}, u32[]{:S(2)}, u32[]{:S(2)}) %collective-permute-start.5) | collective-permute-done | bytes 589856 | tf_op jit(solution)/shard_map/ppermute | solution.py:442
  60.2 0.8 shard_map.126
  61.0 6.3 %shard_map.127 = (bf16[128,4608]{1,0:T(8,128)(2,1)S(1)}, bf16[128,4608]{1,0:T(8,128)(2,1)S(1)}, f32[8,128]{1,0:T(8,128)S(1)}) custom-call(s32[15]{0:T(128)S(1)} %dynamic-slice_bitcast_fusion.sc_ref, bf16[1536,512]{1,0:T(8,128)(2,1)S(1)} %get-tuple-element.80.refs_0_, ...), custom_call_target="tpu_custom_call", output_to_operand_aliasing={{2}: (5, {})} | custom-call | flops 1 | bytes 1 | tf_op jit(solution)/shard_map/pallas_call | solution.py:41
  67.3 0.5 collective-permute-start.6
  67.9 10.4 %shard_map.128 = (bf16[512,512]{1,0:T(8,128)(2,1)S(1)}, bf16[512,512]{1,0:T(8,128)(2,1)S(1)}, f32[8,128]{1,0:T(8,128)S(1)}) custom-call(s32[15]{0:T(128)S(1)} %dynamic-slice_bitcast_fusion.sc_ref, bf16[512,4608]{1,0:T(8,128)(2,1)S(1)} %copy-done, bf16[512,4608]{1,0:T(8,128)(2,1)} %collective-permute-done.refs_3_.refs_1_, ...), custom_call_target="tpu_custom_call", output_to_operand_aliasing={{2}: (6, {})} | custom-call | flops 1 | bytes 1 | tf_op jit(solution)/shard_map/pallas_call | solution.py:41
  78.4 0.9 collective-permute-start.13
  79.3 0.5 shard_map.129
  79.8 1.6 collective-permute-start.15
  81.4 0.7 shard_map.130
  82.1 1.6 collective-permute-start.12
  83.7 3.4 %collective-permute-start.16 = (bf16[256,2304]{1,0:T(8,128)(2,1)S(1)}, bf16[256,2304]{1,0:T(8,128)(2,1)S(1)}, u32[]{:S(2)}, u32[]{:S(2)}) collective-permute-start(bf16[256,2304]{1,0:T(8,128)(2,1)S(1)} %get-tuple-element.113.refs_2_), channel_id=1, source_target_pairs={{0,2},{1,3},{2,6},{3,7},{6,4},{7,5},{4,0},{5,1},{8,10},{9,11},{10,... | collective-permute-start | bytes 3538952 | tf_op jit(solution)/shard_map/ppermute | solution.py:434
  87.0 6.3 %shard_map.131 = (bf16[512,2048]{1,0:T(8,128)(2,1)}, bf16[512,1024]{1,0:T(8,128)(2,1)}, bf16[512,1024]{1,0:T(8,128)(2,1)}, f32[8,128]{1,0:T(8,128)S(1)}) custom-call(s32[15]{0:T(128)S(1)} %dynamic-slice_bitcast_fusion.sc_ref, bf16[512,2048]{1,0:T(8,128)(2,1)S(1)} %copy-done.1, bf16[512,1024]{1,0:T(8,128)(2,1)S(1)} %copy-done.3, ...), custom_call_target="tpu_custom_call", output_to_operand_aliasing={{3}: (8, {})} | custom-call | flops 1 | bytes 1 | tf_op jit(solution)/shard_map/pallas_call | solution.py:41
  93.3 6.3 %shard_map.132 = (bf16[128,4608]{1,0:T(8,128)(2,1)S(1)}, bf16[128,4608]{1,0:T(8,128)(2,1)S(1)}, f32[8,128]{1,0:T(8,128)S(1)}) custom-call(s32[15]{0:T(128)S(1)} %dynamic-slice_bitcast_fusion.sc_ref, bf16[1536,512]{1,0:T(8,128)(2,1)S(1)} %get-tuple-element.80.refs_0_, ...), custom_call_target="tpu_custom_call", output_to_operand_aliasing={{2}: (5, {})} | custom-call | flops 1 | bytes 1 | tf_op jit(solution)/shard_map/pallas_call | solution.py:41
  99.6 0.7 shard_map.133
  100.3 0.6 collective-permute-start.11
  100.9 6.3 %shard_map.134 = (bf16[512,2048]{1,0:T(8,128)(2,1)}, bf16[512,1024]{1,0:T(8,128)(2,1)}, bf16[512,1024]{1,0:T(8,128)(2,1)}, f32[8,128]{1,0:T(8,128)S(1)}, bf16[128,4608]{1,0:T(8,128)(2,1)S(1)}) custom-call(s32[15]{0:T(128)S(1)} %dynamic-slice_bitcast_fusion.sc_ref, ...), custom_call_target="tpu_custom_call", output_to_operand_aliasing={{0}: (8, {}), {1}: (9, {}), {2}: (10, {}), {3}: (11, {}), {... | custom-call | flops 1 | bytes 1 | tf_op jit(solution)/shard_map/pallas_call | solution.py:41
  107.2 0.8 shard_map.135
  108.1 0.6 collective-permute-start.18
  108.7 6.3 %collective-permute-done.15.refs_3_ = bf16[256,2304]{1,0:T(8,128)(2,1)S(1)} collective-permute-done((bf16[256,2304]{1,0:T(8,128)(2,1)S(1)}, bf16[256,2304]{1,0:T(8,128)(2,1)S(1)}, u32[]{:S(2)}, u32[]{:S(2)}) %collective-permute-start.15) | collective-permute-done | bytes 1179680 | tf_op jit(solution)/shard_map/ppermute | solution.py:442
  115.0 6.5 %shard_map.136 = (bf16[512,256]{1,0:T(8,128)(2,1)S(1)}, bf16[512,256]{1,0:T(8,128)(2,1)S(1)}, f32[8,128]{1,0:T(8,128)S(1)}) custom-call(s32[15]{0:T(128)S(1)} %dynamic-slice_bitcast_fusion.sc_ref, bf16[512,4608]{1,0:T(8,128)(2,1)S(1)} %copy-done, bf16[512,4608]{1,0:T(8,128)(2,1)} %collective-permute-done.refs_3_.refs_1_, ...), custom_call_target="tpu_custom_call", output_to_operand_aliasing={{2}: (5, {})} | custom-call | flops 1 | bytes 1 | tf_op jit(solution)/shard_map/pallas_call | solution.py:41
  121.5 11.4 %collective-permute-done.14.refs_3_ = bf16[64,4608]{1,0:T(8,128)(2,1)S(1)} collective-permute-done((bf16[64,4608]{1,0:T(8,128)(2,1)S(1)}, bf16[64,4608]{1,0:T(8,128)(2,1)S(1)}, u32[]{:S(2)}, u32[]{:S(2)}) %collective-permute-start.14) | collective-permute-done | bytes 589856 | tf_op jit(solution)/shard_map/ppermute | solution.py:434
  132.9 0.8 shard_map.137
  133.8 1.6 collective-permute-start.17
  135.4 0.8 collective-permute-start.22
  136.2 0.8 collective-permute-done.19.refs_6_
  136.9 6.3 %shard_map.138 = (bf16[512,2048]{1,0:T(8,128)(2,1)}, bf16[512,1024]{1,0:T(8,128)(2,1)}, bf16[512,1024]{1,0:T(8,128)(2,1)}, f32[8,128]{1,0:T(8,128)S(1)}) custom-call(s32[15]{0:T(128)S(1)} %dynamic-slice_bitcast_fusion.sc_ref, bf16[512,2048]{1,0:T(8,128)(2,1)S(1)} %copy-done.1, ...), custom_call_target="tpu_custom_call", output_to_operand_aliasing={{0}: (8, {}), {1}: (9, {}), {2}: (10, {}), {3}: (11, {})} | custom-call | flops 1 | bytes 1 | tf_op jit(solution)/shard_map/pallas_call | solution.py:41
  143.2 0.7 shard_map.139
  143.9 1.6 collective-permute-start.21
  145.5 7.8 %collective-permute-done.17.refs_3_ = bf16[256,2304]{1,0:T(8,128)(2,1)S(1)} collective-permute-done((bf16[256,2304]{1,0:T(8,128)(2,1)S(1)}, bf16[256,2304]{1,0:T(8,128)(2,1)S(1)}, u32[]{:S(2)}, u32[]{:S(2)}) %collective-permute-start.17) | collective-permute-done | bytes 1179680 | tf_op jit(solution)/shard_map/ppermute | solution.py:442
  153.3 6.5 %shard_map.140 = (bf16[512,256]{1,0:T(8,128)(2,1)S(1)}, bf16[512,256]{1,0:T(8,128)(2,1)S(1)}, f32[8,128]{1,0:T(8,128)S(1)}) custom-call(s32[15]{0:T(128)S(1)} %dynamic-slice_bitcast_fusion.sc_ref, bf16[512,4608]{1,0:T(8,128)(2,1)S(1)} %copy-done, bf16[512,4608]{1,0:T(8,128)(2,1)} %collective-permute-done.refs_3_.refs_1_, ...), custom_call_target="tpu_custom_call", output_to_operand_aliasing={{2}: (5, {})} | custom-call | flops 1 | bytes 1 | tf_op jit(solution)/shard_map/pallas_call | solution.py:41
  159.8 0.8 shard_map.141
  160.7 1.7 collective-permute-start.23
  162.4 2.5 %collective-permute-start.25 = (bf16[64,4608]{1,0:T(8,128)(2,1)S(1)}, bf16[64,4608]{1,0:T(8,128)(2,1)}, u32[]{:S(2)}, u32[]{:S(2)}) collective-permute-start(bf16[64,4608]{1,0:T(8,128)(2,1)S(1)} %get-tuple-element.139.refs_2_), channel_id=1, source_target_pairs={{0,8},{1,17},{2,10},{3,19},{4,12},{5,21},{6,14},{7,23},{8,0},{9,25... | collective-permute-start | bytes 1769480 | tf_op jit(solution)/shard_map/ppermute | solution.py:442
  164.9 6.3 %shard_map.142 = (bf16[512,2048]{1,0:T(8,128)(2,1)}, bf16[512,1024]{1,0:T(8,128)(2,1)}, bf16[512,1024]{1,0:T(8,128)(2,1)}, f32[8,128]{1,0:T(8,128)S(1)}) custom-call(s32[15]{0:T(128)S(1)} %dynamic-slice_bitcast_fusion.sc_ref, bf16[512,2048]{1,0:T(8,128)(2,1)S(1)} %copy-done.1, ...), custom_call_target="tpu_custom_call", output_to_operand_aliasing={{0}: (8, {}), {1}: (9, {}), {2}: (10, {}), {3}: (11, {})} | custom-call | flops 1 | bytes 1 | tf_op jit(solution)/shard_map/pallas_call | solution.py:41
  171.2 0.6 copy-done.8
  171.8 3.8 %shard_map.143 = (f32[256,4608]{1,0:T(8,128)}, f32[8,128]{1,0:T(8,128)}) custom-call(s32[15]{0:T(128)} %copy-done.13, f32[256,4608]{1,0:T(8,128)} %refs_0_.25, f32[256,4608]{1,0:T(8,128)} %refs_1_.17, bf16[64,4608]{1,0:T(8,128)(2,1)} %copy-done.12, f32[8,128]{1,0:T(8,128)} %copy-done.8), custom_call_target="tpu_custom_call", output_to_operand_aliasing={{1}: (4, {})} | custom-call | flops 1 | bytes 1 | tf_op jit(solution)/shard_map/pallas_call | solution.py:41
  175.5 0.5 collective-permute-done.23.refs_1_
  176.1 0.7 copy-done.9
  176.7 0.5 shard_map.144
  177.3 0.6 copy-done.10
  177.9 2.3 %collective-permute-start.24 = (bf16[64,4608]{1,0:T(8,128)(2,1)S(1)}, bf16[64,4608]{1,0:T(8,128)(2,1)S(1)}, u32[]{:S(2)}, u32[]{:S(2)}) collective-permute-start(bf16[64,4608]{1,0:T(8,128)(2,1)S(1)} %get-tuple-element.142.refs_2_), channel_id=1, source_target_pairs={{0,8},{1,17},{2,10},{3,19},{4,12},{5,21},{6,14},{7,23},{8,0},{9,25... | collective-permute-start | bytes 1769480 | tf_op jit(solution)/shard_map/ppermute | solution.py:442
  180.2 5.9 %shard_map.145 = (f32[256,4608]{1,0:T(8,128)}, f32[8,128]{1,0:T(8,128)}) custom-call(s32[15]{0:T(128)} %copy-done.13, f32[256,4608]{1,0:T(8,128)} %refs_0_.25, f32[256,4608]{1,0:T(8,128)} %refs_1_.17, bf16[64,4608]{1,0:T(8,128)(2,1)} %copy-done.11, bf16[64,4608]{1,0:T(8,128)(2,1)} %collective-permute-done.25.refs_3_, ...), custom_call_target="tpu_custom_call", output_to_operand_aliasing={{0}: (5, {}), {1}: (6, {})} | custom-call | flops 1 | bytes 1 | tf_op jit(solution)/shard_map/pallas_call | solution.py:41
  186.1 2.0 %collective-permute-done.24.refs_2_ = bf16[64,4608]{1,0:T(8,128)(2,1)S(1)} collective-permute-done((bf16[64,4608]{1,0:T(8,128)(2,1)S(1)}, bf16[64,4608]{1,0:T(8,128)(2,1)S(1)}, u32[]{:S(2)}, u32[]{:S(2)}) %collective-permute-start.24) | collective-permute-done | bytes 589856 | tf_op jit(solution)/shard_map/ppermute | solution.py:442
  188.1 0.8 copy-done.16
  188.9 3.6 %shard_map.146 = (f32[256,4608]{1,0:T(8,128)}, f32[8,128]{1,0:T(8,128)}) custom-call(s32[15]{0:T(128)} %copy-done.13, f32[256,4608]{1,0:T(8,128)} %refs_0_.25, f32[256,4608]{1,0:T(8,128)} %refs_1_.17, bf16[64,4608]{1,0:T(8,128)(2,1)} %copy-done.16, f32[256,4608]{1,0:T(8,128)} %get-tuple-element.145.refs_3_, ...), custom_call_target="tpu_custom_call", output_to_operand_aliasing={{0}: (4, {}), {1}: (5, {})} | custom-call | flops 1 | bytes 1 | tf_op jit(solution)/shard_map/pallas_call | solution.py:41
  (53 shorter events, 0.7 us)
Async XLA Ops:
  0.6 13.8 %collective-permute-start = (bf16[512,4608]{1,0:T(8,128)(2,1)}, bf16[512,4608]{1,0:T(8,128)(2,1)}, u32[]{:S(2)}, u32[]{:S(2)}) collective-permute-start(bf16[512,4608]{1,0:T(8,128)(2,1)} %refs_0_.21), channel_id=1, source_target_pairs={{0,1},{1,0},{2,3},{3,2},{4,5},{5,4},{6,7},{7,6},{8,9},{9,8},{10,11... | collective-permute-start | bytes 14155784 | tf_op jit(solution)/shard_map/ppermute | solution.py:427
  1.8 1.7 copy-start.6
  3.5 161.4 %copy-start.13 = (s32[15]{0:T(128)}, s32[15]{0:T(128)S(1)}, u32[]{:S(2)}) copy-start(s32[15]{0:T(128)S(1)} %dynamic-slice_bitcast_fusion.sc_ref) | copy-start | bytes 184
  3.5 0.7 copy-start.15
  3.5 1.6 copy-start.1
  5.1 1.2 copy-start.2
  6.3 1.2 copy-start.4
  7.6 6.9 %copy-start = (bf16[512,4608]{1,0:T(8,128)(2,1)S(1)}, bf16[512,4608]{1,0:T(8,128)(2,1)}, u32[]{:S(2)}) copy-start(bf16[512,4608]{1,0:T(8,128)(2,1)} %refs_0_.21) | copy-start | bytes 14155780
  11.3 3.2 %collective-permute-start.1 = (bf16[256,512]{1,0:T(8,128)(2,1)S(1)}, bf16[256,512]{1,0:T(8,128)(2,1)S(1)}, u32[]{:S(2)}, u32[]{:S(2)}) collective-permute-start(bf16[256,512]{1,0:T(8,128)(2,1)S(1)} %slice.6), channel_id=1, source_target_pairs={{0,1},{1,0},{2,3},{3,2},{4,5},{5,4},{6,7},{7,6},{8,9},{9,8},{10,11... | collective-permute-start | bytes 786440 | tf_op jit(solution)/shard_map/ppermute | solution.py:427
  11.4 30.2 %collective-permute-start.3 = (bf16[256,2304]{1,0:T(8,128)(2,1)S(1)}, bf16[256,2304]{1,0:T(8,128)(2,1)S(1)}, u32[]{:S(2)}, u32[]{:S(2)}) collective-permute-start(bf16[256,2304]{1,0:T(8,128)(2,1)S(1)} %get-tuple-element.84), channel_id=1, source_target_pairs={{0,2},{1,3},{2,6},{3,7},{6,4},{7,5},{4,0},{5,1},{8,10},{9,11},{10,... | collective-permute-start | bytes 3538952 | tf_op jit(solution)/shard_map/ppermute | solution.py:434
  14.4 7.9 %copy-start.3 = (bf16[512,1024]{1,0:T(8,128)(2,1)S(1)}, bf16[512,1024]{1,0:T(8,128)(2,1)}, u32[]{:S(2)}) copy-start(bf16[512,1024]{1,0:T(8,128)(2,1)} %refs_1_.14) | copy-start | bytes 3145732
  20.7 20.9 %collective-permute-start.2 = (bf16[128,4608]{1,0:T(8,128)(2,1)S(1)}, bf16[128,4608]{1,0:T(8,128)(2,1)S(1)}, u32[]{:S(2)}, u32[]{:S(2)}) collective-permute-start(bf16[128,4608]{1,0:T(8,128)(2,1)S(1)} %get-tuple-element.82), channel_id=1, source_target_pairs={{0,8},{1,17},{2,10},{3,19},{4,12},{5,21},{6,14},{7,23},{8,0},{9,25... | collective-permute-start | bytes 3538952 | tf_op jit(solution)/shard_map/ppermute | solution.py:442
  32.0 9.6 %collective-permute-start.4 = (bf16[768,512]{1,0:T(8,128)(2,1)S(1)}, bf16[768,512]{1,0:T(8,128)(2,1)S(1)}, u32[]{:S(2)}, u32[]{:S(2)}) collective-permute-start(bf16[768,512]{1,0:T(8,128)(2,1)S(1)} %slice.7), channel_id=1, source_target_pairs={{0,1},{1,0},{2,3},{3,2},{4,5},{5,4},{6,7},{7,6},{8,9},{9,8},{10,11... | collective-permute-start | bytes 2359304 | tf_op jit(solution)/shard_map/ppermute | solution.py:427
  42.3 25.5 %collective-permute-start.7 = (bf16[256,2304]{1,0:T(8,128)(2,1)S(1)}, bf16[256,2304]{1,0:T(8,128)(2,1)S(1)}, u32[]{:S(2)}, u32[]{:S(2)}) collective-permute-start(bf16[256,2304]{1,0:T(8,128)(2,1)S(1)} %get-tuple-element.92.refs_3_), channel_id=1, source_target_pairs={{0,8},{1,17},{2,10},{3,19},{4,12},{5,21},{6,14},{7,23},{8,0},{9,25... | collective-permute-start | bytes 3538952 | tf_op jit(solution)/shard_map/ppermute | solution.py:442
  43.9 16.3 %collective-permute-start.5 = (bf16[64,4608]{1,0:T(8,128)(2,1)S(1)}, bf16[64,4608]{1,0:T(8,128)(2,1)S(1)}, u32[]{:S(2)}, u32[]{:S(2)}) collective-permute-start(bf16[64,4608]{1,0:T(8,128)(2,1)S(1)} %get-tuple-element.86), channel_id=1, source_target_pairs={{0,16},{1,9},{2,18},{3,11},{4,20},{5,13},{6,22},{7,15},{8,24},{9,1... | collective-permute-start | bytes 1769480 | tf_op jit(solution)/shard_map/ppermute | solution.py:442
  45.4 33.8 %collective-permute-start.10 = (bf16[256,2304]{1,0:T(8,128)(2,1)S(1)}, bf16[256,2304]{1,0:T(8,128)(2,1)S(1)}, u32[]{:S(2)}, u32[]{:S(2)}) collective-permute-start(bf16[256,2304]{1,0:T(8,128)(2,1)S(1)} %get-tuple-element.92.refs_3_), channel_id=1, source_target_pairs={{0,2},{1,3},{2,6},{3,7},{6,4},{7,5},{4,0},{5,1},{8,10},{9,11},{10,... | collective-permute-start | bytes 3538952 | tf_op jit(solution)/shard_map/ppermute | solution.py:434
  52.5 28.9 %collective-permute-start.9 = (bf16[128,4608]{1,0:T(8,128)(2,1)S(1)}, bf16[128,4608]{1,0:T(8,128)(2,1)S(1)}, u32[]{:S(2)}, u32[]{:S(2)}) collective-permute-start(bf16[128,4608]{1,0:T(8,128)(2,1)S(1)} %get-tuple-element.97), channel_id=1, source_target_pairs={{0,8},{1,17},{2,10},{3,19},{4,12},{5,21},{6,14},{7,23},{8,0},{9,25... | collective-permute-start | bytes 3538952 | tf_op jit(solution)/shard_map/ppermute | solution.py:442
  61.0 6.9 %copy-start.7 = (bf16[256,4608]{1,0:T(8,128)(2,1)S(1)}, bf16[256,4608]{1,0:T(8,128)(2,1)}, u32[]{:S(2)}) copy-start(bf16[256,4608]{1,0:T(8,128)(2,1)} %refs_2_.16) | copy-start | bytes 7077892
  67.3 32.3 %collective-permute-start.6 = (bf16[128,4608]{1,0:T(8,128)(2,1)S(1)}, bf16[128,4608]{1,0:T(8,128)(2,1)S(1)}, u32[]{:S(2)}, u32[]{:S(2)}) collective-permute-start(bf16[128,4608]{1,0:T(8,128)(2,1)S(1)} %get-tuple-element.91), channel_id=1, source_target_pairs={{0,8},{1,17},{2,10},{3,19},{4,12},{5,21},{6,14},{7,23},{8,0},{9,25... | collective-permute-start | bytes 3538952 | tf_op jit(solution)/shard_map/ppermute | solution.py:442
  78.3 5.4 %collective-permute-start.8 = (bf16[512,512]{1,0:T(8,128)(2,1)S(1)}, bf16[512,512]{1,0:T(8,128)(2,1)S(1)}, u32[]{:S(2)}, u32[]{:S(2)}) collective-permute-start(bf16[512,512]{1,0:T(8,128)(2,1)S(1)} %get-tuple-element.95), channel_id=1, source_target_pairs={{0,1},{1,0},{2,3},{3,2},{4,5},{5,4},{6,7},{7,6},{8,9},{9,8},{10,11... | collective-permute-start | bytes 1572872 | tf_op jit(solution)/shard_map/ppermute | solution.py:427
  78.4 28.8 %collective-permute-start.13 = (bf16[64,4608]{1,0:T(8,128)(2,1)S(1)}, bf16[64,4608]{1,0:T(8,128)(2,1)S(1)}, u32[]{:S(2)}, u32[]{:S(2)}) collective-permute-start(bf16[64,4608]{1,0:T(8,128)(2,1)S(1)} %get-tuple-element.105), channel_id=1, source_target_pairs={{0,2},{1,3},{2,6},{3,7},{6,4},{7,5},{4,0},{5,1},{8,10},{9,11},{10,... | collective-permute-start | bytes 1769480 | tf_op jit(solution)/shard_map/ppermute | solution.py:434
  79.8 35.2 %collective-permute-start.15 = (bf16[256,2304]{1,0:T(8,128)(2,1)S(1)}, bf16[256,2304]{1,0:T(8,128)(2,1)S(1)}, u32[]{:S(2)}, u32[]{:S(2)}) collective-permute-start(bf16[256,2304]{1,0:T(8,128)(2,1)S(1)} %get-tuple-element.113.refs_2_), channel_id=1, source_target_pairs={{0,8},{1,17},{2,10},{3,19},{4,12},{5,21},{6,14},{7,23},{8,0},{9,25... | collective-permute-start | bytes 3538952 | tf_op jit(solution)/shard_map/ppermute | solution.py:442
  81.4 5.6 %copy-start.5 = (bf16[512,1024]{1,0:T(8,128)(2,1)S(1)}, bf16[512,1024]{1,0:T(8,128)(2,1)}, u32[]{:S(2)}) copy-start(bf16[512,1024]{1,0:T(8,128)(2,1)} %refs_2_.21) | copy-start | bytes 3145732
  82.1 25.1 %collective-permute-start.12 = (bf16[64,4608]{1,0:T(8,128)(2,1)S(1)}, bf16[64,4608]{1,0:T(8,128)(2,1)S(1)}, u32[]{:S(2)}, u32[]{:S(2)}) collective-permute-start(bf16[64,4608]{1,0:T(8,128)(2,1)S(1)} %get-tuple-element.104), channel_id=1, source_target_pairs={{0,16},{1,9},{2,18},{3,11},{4,20},{5,13},{6,22},{7,15},{8,24},{9,1... | collective-permute-start | bytes 1769480 | tf_op jit(solution)/shard_map/ppermute | solution.py:442
  83.7 37.9 %collective-permute-start.16 = (bf16[256,2304]{1,0:T(8,128)(2,1)S(1)}, bf16[256,2304]{1,0:T(8,128)(2,1)S(1)}, u32[]{:S(2)}, u32[]{:S(2)}) collective-permute-start(bf16[256,2304]{1,0:T(8,128)(2,1)S(1)} %get-tuple-element.113.refs_2_), channel_id=1, source_target_pairs={{0,2},{1,3},{2,6},{3,7},{6,4},{7,5},{4,0},{5,1},{8,10},{9,11},{10,... | collective-permute-start | bytes 3538952 | tf_op jit(solution)/shard_map/ppermute | solution.py:434
  100.3 21.2 %collective-permute-start.11 = (bf16[64,4608]{1,0:T(8,128)(2,1)S(1)}, bf16[64,4608]{1,0:T(8,128)(2,1)S(1)}, u32[]{:S(2)}, u32[]{:S(2)}) collective-permute-start(bf16[64,4608]{1,0:T(8,128)(2,1)S(1)} %get-tuple-element.103), channel_id=1, source_target_pairs={{0,16},{1,9},{2,18},{3,11},{4,20},{5,13},{6,22},{7,15},{8,24},{9,1... | collective-permute-start | bytes 1769480 | tf_op jit(solution)/shard_map/ppermute | solution.py:442
  108.0 24.9 %collective-permute-start.14 = (bf16[64,4608]{1,0:T(8,128)(2,1)S(1)}, bf16[64,4608]{1,0:T(8,128)(2,1)S(1)}, u32[]{:S(2)}, u32[]{:S(2)}) collective-permute-start(bf16[64,4608]{1,0:T(8,128)(2,1)S(1)} %get-tuple-element.112), channel_id=1, source_target_pairs={{0,2},{1,3},{2,6},{3,7},{6,4},{7,5},{4,0},{5,1},{8,10},{9,11},{10,... | collective-permute-start | bytes 1769480 | tf_op jit(solution)/shard_map/ppermute | solution.py:434
  108.1 35.1 %collective-permute-start.18 = (bf16[128,4608]{1,0:T(8,128)(2,1)S(1)}, bf16[128,4608]{1,0:T(8,128)(2,1)S(1)}, u32[]{:S(2)}, u32[]{:S(2)}) collective-permute-start(bf16[128,4608]{1,0:T(8,128)(2,1)S(1)} %get-tuple-element.118), channel_id=1, source_target_pairs={{0,8},{1,17},{2,10},{3,19},{4,12},{5,21},{6,14},{7,23},{8,0},{9,25... | collective-permute-start | bytes 3538952 | tf_op jit(solution)/shard_map/ppermute | solution.py:442
  133.8 19.5 %collective-permute-start.17 = (bf16[256,2304]{1,0:T(8,128)(2,1)S(1)}, bf16[256,2304]{1,0:T(8,128)(2,1)S(1)}, u32[]{:S(2)}, u32[]{:S(2)}) collective-permute-start(bf16[256,2304]{1,0:T(8,128)(2,1)S(1)} %get-tuple-element.116.refs_2_), channel_id=1, source_target_pairs={{0,8},{1,17},{2,10},{3,19},{4,12},{5,21},{6,14},{7,23},{8,0},{9,25... | collective-permute-start | bytes 3538952 | tf_op jit(solution)/shard_map/ppermute | solution.py:442
  135.4 1.5 collective-permute-start.19
  135.4 24.4 %collective-permute-start.22 = (bf16[64,4608]{1,0:T(8,128)(2,1)S(1)}, bf16[64,4608]{1,0:T(8,128)(2,1)S(1)}, u32[]{:S(2)}, u32[]{:S(2)}) collective-permute-start(bf16[64,4608]{1,0:T(8,128)(2,1)S(1)} %get-tuple-element.133), channel_id=1, source_target_pairs={{0,2},{1,3},{2,6},{3,7},{6,4},{7,5},{4,0},{5,1},{8,10},{9,11},{10,... | collective-permute-start | bytes 1769480 | tf_op jit(solution)/shard_map/ppermute | solution.py:434
  143.9 15.9 %collective-permute-start.21 = (bf16[64,4608]{1,0:T(8,128)(2,1)S(1)}, bf16[64,4608]{1,0:T(8,128)(2,1)S(1)}, u32[]{:S(2)}, u32[]{:S(2)}) collective-permute-start(bf16[64,4608]{1,0:T(8,128)(2,1)S(1)} %get-tuple-element.132), channel_id=1, source_target_pairs={{0,16},{1,9},{2,18},{3,11},{4,20},{5,13},{6,22},{7,15},{8,24},{9,1... | collective-permute-start | bytes 1769480 | tf_op jit(solution)/shard_map/ppermute | solution.py:442
  160.7 10.5 %copy-start.12 = (bf16[64,4608]{1,0:T(8,128)(2,1)}, bf16[64,4608]{1,0:T(8,128)(2,1)S(1)}, u32[]{:S(2)}) copy-start(bf16[64,4608]{1,0:T(8,128)(2,1)S(1)} %get-tuple-element.139.refs_2_) | copy-start | bytes 1769476
  160.7 15.4 %collective-permute-start.23 = (bf16[64,4608]{1,0:T(8,128)(2,1)S(1)}, bf16[64,4608]{1,0:T(8,128)(2,1)S(1)}, u32[]{:S(2)}, u32[]{:S(2)}) collective-permute-start(bf16[64,4608]{1,0:T(8,128)(2,1)S(1)} %get-tuple-element.139.refs_2_), channel_id=1, source_target_pairs={{0,16},{1,9},{2,18},{3,11},{4,20},{5,13},{6,22},{7,15},{8,24},{9,1... | collective-permute-start | bytes 1769480 | tf_op jit(solution)/shard_map/ppermute | solution.py:442
  162.4 2.5 %collective-permute-start.20 = (bf16[512,256]{1,0:T(8,128)(2,1)S(1)}, bf16[512,256]{1,0:T(8,128)(2,1)S(1)}, u32[]{:S(2)}, u32[]{:S(2)}) collective-permute-start(bf16[512,256]{1,0:T(8,128)(2,1)S(1)} %get-tuple-element.128), channel_id=1, source_target_pairs={{0,1},{1,0},{2,3},{3,2},{4,5},{5,4},{6,7},{7,6},{8,9},{9,8},{10,11... | collective-permute-start | bytes 786440 | tf_op jit(solution)/shard_map/ppermute | solution.py:427
  162.4 17.8 %collective-permute-start.25 = (bf16[64,4608]{1,0:T(8,128)(2,1)S(1)}, bf16[64,4608]{1,0:T(8,128)(2,1)}, u32[]{:S(2)}, u32[]{:S(2)}) collective-permute-start(bf16[64,4608]{1,0:T(8,128)(2,1)S(1)} %get-tuple-element.139.refs_2_), channel_id=1, source_target_pairs={{0,8},{1,17},{2,10},{3,19},{4,12},{5,21},{6,14},{7,23},{8,0},{9,25... | collective-permute-start | bytes 1769480 | tf_op jit(solution)/shard_map/ppermute | solution.py:442
  171.2 0.6 copy-start.8
  171.8 4.3 %copy-start.14 = (s32[15]{0:T(128)S(1)}, s32[15]{0:T(128)}, u32[]{:S(2)}) copy-start(s32[15]{0:T(128)} %copy-done.13) | copy-start | bytes 184
  176.1 0.7 copy-start.9
  177.3 0.6 copy-start.10
  177.9 2.4 %copy-start.11 = (bf16[64,4608]{1,0:T(8,128)(2,1)}, bf16[64,4608]{1,0:T(8,128)(2,1)S(1)}, u32[]{:S(2)}) copy-start(bf16[64,4608]{1,0:T(8,128)(2,1)S(1)} %get-tuple-element.142.refs_2_) | copy-start | bytes 1769476
  177.9 10.2 %collective-permute-start.24 = (bf16[64,4608]{1,0:T(8,128)(2,1)S(1)}, bf16[64,4608]{1,0:T(8,128)(2,1)S(1)}, u32[]{:S(2)}, u32[]{:S(2)}) collective-permute-start(bf16[64,4608]{1,0:T(8,128)(2,1)S(1)} %get-tuple-element.142.refs_2_), channel_id=1, source_target_pairs={{0,8},{1,17},{2,10},{3,19},{4,12},{5,21},{6,14},{7,23},{8,0},{9,25... | collective-permute-start | bytes 1769480 | tf_op jit(solution)/shard_map/ppermute | solution.py:442
  188.1 0.8 copy-start.16

commit v9 on v8

--- a/solution.py
+++ b/solution.py
@@ -557,10 +557,13 @@
     last = lay.z - 1
     do_grad_context([2])
     swap_grad_context(2)
-    do_sum(3, held=[("ring", last)])
-    pass_sum(3)
+    run(relay, sc, held=[("ring", last)])
     cross_weights(last)
     do_backward(2)
+    do_halve(0)
+    send(0)
+    do_sum(3)
+    pass_sum(3)
     for k in range(4, lay.z):
         do_sum(k)
         pass_sum(k)
@@ -568,8 +571,6 @@
         do_grad_context([k])
         swap_grad_context(k)
         do_backward(k)
-    do_halve(0)
-    send(0)
     do_grad_context([last])
     swap_grad_context(last)
     do_sum(0)

time: 194 us -> 188 us (0.969)
  waiting for transfers between devices: 45.4 us -> 39.5 us
    ppermute x14, waiting for transfers between devices: 23.7 us -> 12.3 us  [across(): return lax.ppermute(x, ('replica', 'shard'), perm)]
    ppermute x6, waiting for transfers between devices: 20.9 us -> 25.6 us  [onward(): return lax.ppermute(x, 'shard', perm)]
    ppermute x14, starting transfers between devices: 19.9 us -> 16.1 us  [across(): return lax.ppermute(x, ('replica', 'shard'), perm)]
    ppermute x6, starting transfers between devices: 8.92 us -> 12.5 us  [onward(): return lax.ppermute(x, 'shard', perm)]
    pallas_call x27 -> x28, Pallas kernels: 108 us -> 109 us  [call(): pl.pallas_call(kernel, grid_spec=pltpu.PrefetchScalarGridSpec(num_scalar_...]
  transfers between devices with their start and end apart: 26 -> 26, of which waited for: 8 -> 8; matrix products, arithmetic and copies ran while one was open for 0% -> 0% of each run, Pallas kernels for 53% -> 55%
where the time goes in v9:
time: 188 us
  Pallas kernels  109 us (58%)
  waiting for transfers between devices  39.5 us (21%)
  starting transfers between devices  29.4 us (16%)
  local copies, waits for them, and re-layouts  9.04 us (5%)
    pallas_call x28, Pallas kernels, call(): pl.pallas_call(kernel, grid_spec=pltpu.PrefetchScalarGridSpec(num_scalar_...  109 us
    ppermute x6, waiting for transfers between devices, onward(): return lax.ppermute(x, 'shard', perm)  25.6 us
    ppermute x14, starting transfers between devices, across(): return lax.ppermute(x, ('replica', 'shard'), perm)  16.1 us
    ppermute x6, starting transfers between devices, onward(): return lax.ppermute(x, 'shard', perm)  12.5 us
    ppermute x14, waiting for transfers between devices, across(): return lax.ppermute(x, ('replica', 'shard'), perm)  12.3 us
    unnamed x34, local copies, waits for them, and re-layouts  8.14 us
  transfers between devices with their start and end apart: 26, of which 8 were waited for; matrix products, arithmetic and copies ran while one was open for 0% of the time, Pallas kernels for 55%

profile of v9, /device:TPU:0, one launch (start us, length us, event | category | flops | bytes accessed | tf_op | source)
XLA Modules:
  0.0 187.5 jit_solution(11333569308707323375)
XLA Ops:
  0.6 0.5 collective-permute-start
  1.1 0.7 dynamic-slice_bitcast_fusion.sc_ref
  1.8 1.7 copy-done.6
  3.5 0.6 shard_map.120
  4.3 0.8 copy-done.1
  5.1 1.2 copy-done.2
  6.3 1.2 copy-done.4
  7.6 3.7 %shard_map.121 = (bf16[512,512]{1,0:T(8,128)(2,1)S(1)}, f32[8,128]{1,0:T(8,128)S(1)}) custom-call(s32[15]{0:T(128)S(1)} %dynamic-slice_bitcast_fusion.sc_ref, bf16[512,2048]{1,0:T(8,128)(2,1)S(1)} %copy-done.1, bf16[512,1024]{1,0:T(8,128)(2,1)S(1)} %copy-done.2, bf16[512,1024]{1,0:T(8,128)(2,1)S(1)} %copy-done.4, ...), custom_call_target="tpu_custom_call", output_to_operand_aliasing={{1}: (6, {})} | custom-call | flops 1 | bytes 1 | tf_op jit(solution)/shard_map/pallas_call | solution.py:41
  11.4 3.0 %collective-permute-start.3 = (bf16[256,2304]{1,0:T(8,128)(2,1)S(1)}, bf16[256,2304]{1,0:T(8,128)(2,1)S(1)}, u32[]{:S(2)}, u32[]{:S(2)}) collective-permute-start(bf16[256,2304]{1,0:T(8,128)(2,1)S(1)} %get-tuple-element.84), channel_id=1, source_target_pairs={{0,2},{1,3},{2,6},{3,7},{6,4},{7,5},{4,0},{5,1},{8,10},{9,11},{10,... | collective-permute-start | bytes 3538952 | tf_op jit(solution)/shard_map/ppermute | solution.py:434
  14.4 6.3 %shard_map.122 = (bf16[128,4608]{1,0:T(8,128)(2,1)S(1)}, bf16[128,4608]{1,0:T(8,128)(2,1)S(1)}, f32[8,128]{1,0:T(8,128)S(1)}) custom-call(s32[15]{0:T(128)S(1)} %dynamic-slice_bitcast_fusion.sc_ref, bf16[512,512]{1,0:T(8,128)(2,1)S(1)} %get-tuple-element.78.refs_0_, ...), custom_call_target="tpu_custom_call", output_to_operand_aliasing={{2}: (5, {})} | custom-call | flops 1 | bytes 1 | tf_op jit(solution)/shard_map/pallas_call | solution.py:41
  20.7 1.6 collective-permute-start.2
  22.3 9.6 %shard_map.123 = (bf16[1536,512]{1,0:T(8,128)(2,1)S(1)}, f32[8,128]{1,0:T(8,128)S(1)}) custom-call(s32[15]{0:T(128)S(1)} %dynamic-slice_bitcast_fusion.sc_ref, bf16[512,2048]{1,0:T(8,128)(2,1)S(1)} %copy-done.1, bf16[512,1024]{1,0:T(8,128)(2,1)S(1)} %copy-done.3, bf16[512,1024]{1,0:T(8,128)(2,1)S(1)} %copy-done.4, ...), custom_call_target="tpu_custom_call", output_to_operand_aliasing={{1}: (6, {})} | custom-call | flops 1 | bytes 1 | tf_op jit(solution)/shard_map/pallas_call | solution.py:41
  32.1 9.5 %collective-permute-done.3.refs_3_ = bf16[256,2304]{1,0:T(8,128)(2,1)S(1)} collective-permute-done((bf16[256,2304]{1,0:T(8,128)(2,1)S(1)}, bf16[256,2304]{1,0:T(8,128)(2,1)S(1)}, u32[]{:S(2)}, u32[]{:S(2)}) %collective-permute-start.3) | collective-permute-done | bytes 1179680 | tf_op jit(solution)/shard_map/ppermute | solution.py:434
  41.6 0.7 shard_map.124
  42.3 1.6 collective-permute-start.6
  44.0 1.5 collective-permute-start.5
  45.4 0.8 collective-permute-start.7
  46.2 6.3 %shard_map.125 = (bf16[128,4608]{1,0:T(8,128)(2,1)S(1)}, bf16[128,4608]{1,0:T(8,128)(2,1)S(1)}, f32[8,128]{1,0:T(8,128)S(1)}) custom-call(s32[15]{0:T(128)S(1)} %dynamic-slice_bitcast_fusion.sc_ref, bf16[1536,512]{1,0:T(8,128)(2,1)S(1)} %get-tuple-element.85.refs_0_, ...), custom_call_target="tpu_custom_call", output_to_operand_aliasing={{2}: (5, {})} | custom-call | flops 1 | bytes 1 | tf_op jit(solution)/shard_map/pallas_call | solution.py:41
  52.5 0.6 collective-permute-start.9
  53.1 5.4 %collective-permute-done.6.refs_2_ = bf16[64,4608]{1,0:T(8,128)(2,1)S(1)} collective-permute-done((bf16[64,4608]{1,0:T(8,128)(2,1)S(1)}, bf16[64,4608]{1,0:T(8,128)(2,1)S(1)}, u32[]{:S(2)}, u32[]{:S(2)}) %collective-permute-start.6) | collective-permute-done | bytes 589856 | tf_op jit(solution)/shard_map/ppermute | solution.py:442
  58.5 0.8 shard_map.126
  59.3 6.3 %shard_map.127 = (bf16[128,4608]{1,0:T(8,128)(2,1)S(1)}, bf16[128,4608]{1,0:T(8,128)(2,1)S(1)}, f32[8,128]{1,0:T(8,128)S(1)}) custom-call(s32[15]{0:T(128)S(1)} %dynamic-slice_bitcast_fusion.sc_ref, bf16[1536,512]{1,0:T(8,128)(2,1)S(1)} %get-tuple-element.85.refs_0_, ...), custom_call_target="tpu_custom_call", output_to_operand_aliasing={{2}: (5, {})} | custom-call | flops 1 | bytes 1 | tf_op jit(solution)/shard_map/pallas_call | solution.py:41
  65.6 1.7 collective-permute-start.13
  67.3 10.4 %shard_map.128 = (bf16[512,512]{1,0:T(8,128)(2,1)S(1)}, bf16[512,512]{1,0:T(8,128)(2,1)S(1)}, f32[8,128]{1,0:T(8,128)S(1)}) custom-call(s32[15]{0:T(128)S(1)} %dynamic-slice_bitcast_fusion.sc_ref, bf16[512,4608]{1,0:T(8,128)(2,1)S(1)} %copy-done, bf16[512,4608]{1,0:T(8,128)(2,1)} %collective-permute-done.refs_3_.refs_1_, ...), custom_call_target="tpu_custom_call", output_to_operand_aliasing={{2}: (6, {})} | custom-call | flops 1 | bytes 1 | tf_op jit(solution)/shard_map/pallas_call | solution.py:41
  77.8 0.5 shard_map.129
  78.8 0.9 collective-permute-start.14
  79.6 3.4 %collective-permute-start.11 = (bf16[64,4608]{1,0:T(8,128)(2,1)S(1)}, bf16[64,4608]{1,0:T(8,128)(2,1)S(1)}, u32[]{:S(2)}, u32[]{:S(2)}) collective-permute-start(bf16[64,4608]{1,0:T(8,128)(2,1)S(1)} %get-tuple-element.99), channel_id=1, source_target_pairs={{0,2},{1,3},{2,6},{3,7},{6,4},{7,5},{4,0},{5,1},{8,10},{9,11},{10,... | collective-permute-start | bytes 1769480 | tf_op jit(solution)/shard_map/ppermute | solution.py:434
  83.0 0.7 shard_map.130
  83.7 1.6 collective-permute-start.10
  85.3 6.3 %shard_map.131 = (bf16[512,2048]{1,0:T(8,128)(2,1)}, bf16[512,1024]{1,0:T(8,128)(2,1)}, bf16[512,1024]{1,0:T(8,128)(2,1)}, f32[8,128]{1,0:T(8,128)S(1)}) custom-call(s32[15]{0:T(128)S(1)} %dynamic-slice_bitcast_fusion.sc_ref, bf16[512,2048]{1,0:T(8,128)(2,1)S(1)} %copy-done.1, bf16[512,1024]{1,0:T(8,128)(2,1)S(1)} %copy-done.3, ...), custom_call_target="tpu_custom_call", output_to_operand_aliasing={{3}: (8, {})} | custom-call | flops 1 | bytes 1 | tf_op jit(solution)/shard_map/pallas_call | solution.py:41
  91.6 6.3 %shard_map.132 = (bf16[128,4608]{1,0:T(8,128)(2,1)S(1)}, bf16[128,4608]{1,0:T(8,128)(2,1)S(1)}, f32[8,128]{1,0:T(8,128)S(1)}) custom-call(s32[15]{0:T(128)S(1)} %dynamic-slice_bitcast_fusion.sc_ref, bf16[1536,512]{1,0:T(8,128)(2,1)S(1)} %get-tuple-element.85.refs_0_, ...), custom_call_target="tpu_custom_call", output_to_operand_aliasing={{2}: (5, {})} | custom-call | flops 1 | bytes 1 | tf_op jit(solution)/shard_map/pallas_call | solution.py:41
  97.9 0.7 shard_map.133
  98.6 6.3 %shard_map.134 = (bf16[512,2048]{1,0:T(8,128)(2,1)}, bf16[512,1024]{1,0:T(8,128)(2,1)}, bf16[512,1024]{1,0:T(8,128)(2,1)}, f32[8,128]{1,0:T(8,128)S(1)}, bf16[128,4608]{1,0:T(8,128)(2,1)S(1)}) custom-call(s32[15]{0:T(128)S(1)} %dynamic-slice_bitcast_fusion.sc_ref, ...), custom_call_target="tpu_custom_call", output_to_operand_aliasing={{0}: (8, {}), {1}: (9, {}), {2}: (10, {}), {3}: (11, {}), {... | custom-call | flops 1 | bytes 1 | tf_op jit(solution)/shard_map/pallas_call | solution.py:41
  104.9 1.6 collective-permute-start.18
  106.5 11.7 %collective-permute-done.11.refs_3_ = bf16[64,4608]{1,0:T(8,128)(2,1)S(1)} collective-permute-done((bf16[64,4608]{1,0:T(8,128)(2,1)S(1)}, bf16[64,4608]{1,0:T(8,128)(2,1)S(1)}, u32[]{:S(2)}, u32[]{:S(2)}) %collective-permute-start.11) | collective-permute-done | bytes 589856 | tf_op jit(solution)/shard_map/ppermute | solution.py:434
  118.3 0.8 shard_map.135
  119.1 0.8 collective-permute-start.17
  119.9 0.5 collective-permute-start.16
  120.4 6.5 %shard_map.136 = (bf16[512,256]{1,0:T(8,128)(2,1)S(1)}, bf16[512,256]{1,0:T(8,128)(2,1)S(1)}, f32[8,128]{1,0:T(8,128)S(1)}) custom-call(s32[15]{0:T(128)S(1)} %dynamic-slice_bitcast_fusion.sc_ref, bf16[512,4608]{1,0:T(8,128)(2,1)S(1)} %copy-done, bf16[512,4608]{1,0:T(8,128)(2,1)} %collective-permute-done.refs_3_.refs_1_, ...), custom_call_target="tpu_custom_call", output_to_operand_aliasing={{2}: (5, {})} | custom-call | flops 1 | bytes 1 | tf_op jit(solution)/shard_map/pallas_call | solution.py:41
  127.0 0.5 shard_map.137
  127.5 1.2 collective-permute-start.15
  128.7 1.5 collective-permute-done.19.refs_6_
  130.2 6.3 %shard_map.138 = (bf16[512,2048]{1,0:T(8,128)(2,1)}, bf16[512,1024]{1,0:T(8,128)(2,1)}, bf16[512,1024]{1,0:T(8,128)(2,1)}, f32[8,128]{1,0:T(8,128)S(1)}) custom-call(s32[15]{0:T(128)S(1)} %dynamic-slice_bitcast_fusion.sc_ref, bf16[512,2048]{1,0:T(8,128)(2,1)S(1)} %copy-done.1, ...), custom_call_target="tpu_custom_call", output_to_operand_aliasing={{0}: (8, {}), {1}: (9, {}), {2}: (10, {}), {3}: (11, {})} | custom-call | flops 1 | bytes 1 | tf_op jit(solution)/shard_map/pallas_call | solution.py:41
  136.5 0.7 shard_map.139
  137.2 0.8 shard_map.140
  138.1 3.7 %collective-permute-start.22 = (bf16[64,4608]{1,0:T(8,128)(2,1)S(1)}, bf16[64,4608]{1,0:T(8,128)(2,1)S(1)}, u32[]{:S(2)}, u32[]{:S(2)}) collective-permute-start(bf16[64,4608]{1,0:T(8,128)(2,1)S(1)} %get-tuple-element.135), channel_id=1, source_target_pairs={{0,2},{1,3},{2,6},{3,7},{6,4},{7,5},{4,0},{5,1},{8,10},{9,11},{10,... | collective-permute-start | bytes 1769480 | tf_op jit(solution)/shard_map/ppermute | solution.py:434
  141.7 1.0 collective-permute-start.21
  142.7 1.1 collective-permute-done.15.refs_3_
  143.8 6.5 %shard_map.141 = (bf16[512,256]{1,0:T(8,128)(2,1)S(1)}, bf16[512,256]{1,0:T(8,128)(2,1)S(1)}, f32[8,128]{1,0:T(8,128)S(1)}) custom-call(s32[15]{0:T(128)S(1)} %dynamic-slice_bitcast_fusion.sc_ref, bf16[512,4608]{1,0:T(8,128)(2,1)S(1)} %copy-done, bf16[512,4608]{1,0:T(8,128)(2,1)} %collective-permute-done.refs_3_.refs_1_, ...), custom_call_target="tpu_custom_call", output_to_operand_aliasing={{2}: (5, {})} | custom-call | flops 1 | bytes 1 | tf_op jit(solution)/shard_map/pallas_call | solution.py:41
  150.3 4.3 %collective-permute-done.22.refs_3_ = bf16[64,4608]{1,0:T(8,128)(2,1)S(1)} collective-permute-done((bf16[64,4608]{1,0:T(8,128)(2,1)S(1)}, bf16[64,4608]{1,0:T(8,128)(2,1)S(1)}, u32[]{:S(2)}, u32[]{:S(2)}) %collective-permute-start.22) | collective-permute-done | bytes 589856 | tf_op jit(solution)/shard_map/ppermute | solution.py:434
  154.6 0.8 shard_map.142
  155.5 1.0 collective-permute-start.23
  156.5 1.5 collective-permute-start.25
  158.0 6.3 %shard_map.143 = (bf16[512,2048]{1,0:T(8,128)(2,1)}, bf16[512,1024]{1,0:T(8,128)(2,1)}, bf16[512,1024]{1,0:T(8,128)(2,1)}, f32[8,128]{1,0:T(8,128)S(1)}) custom-call(s32[15]{0:T(128)S(1)} %dynamic-slice_bitcast_fusion.sc_ref, bf16[512,2048]{1,0:T(8,128)(2,1)S(1)} %copy-done.1, ...), custom_call_target="tpu_custom_call", output_to_operand_aliasing={{0}: (8, {}), {1}: (9, {}), {2}: (10, {}), {3}: (11, {})} | custom-call | flops 1 | bytes 1 | tf_op jit(solution)/shard_map/pallas_call | solution.py:41
  164.3 0.6 copy-done.8
  164.9 3.8 %shard_map.144 = (f32[256,4608]{1,0:T(8,128)}, f32[8,128]{1,0:T(8,128)}) custom-call(s32[15]{0:T(128)} %copy-done.13, f32[256,4608]{1,0:T(8,128)} %refs_0_.25, f32[256,4608]{1,0:T(8,128)} %refs_1_.17, bf16[64,4608]{1,0:T(8,128)(2,1)} %copy-done.12, f32[8,128]{1,0:T(8,128)} %copy-done.8), custom_call_target="tpu_custom_call", output_to_operand_aliasing={{1}: (4, {})} | custom-call | flops 1 | bytes 1 | tf_op jit(solution)/shard_map/pallas_call | solution.py:41
  168.7 2.6 %collective-permute-done.23.refs_1_ = bf16[64,4608]{1,0:T(8,128)(2,1)S(1)} collective-permute-done((bf16[64,4608]{1,0:T(8,128)(2,1)S(1)}, bf16[64,4608]{1,0:T(8,128)(2,1)S(1)}, u32[]{:S(2)}, u32[]{:S(2)}) %collective-permute-start.23) | collective-permute-done | bytes 589856 | tf_op jit(solution)/shard_map/ppermute | solution.py:442
  171.3 0.7 copy-done.9
  172.0 0.5 shard_map.145
  172.5 0.6 copy-done.10
  173.9 5.9 %shard_map.146 = (f32[256,4608]{1,0:T(8,128)}, f32[8,128]{1,0:T(8,128)}) custom-call(s32[15]{0:T(128)} %copy-done.13, f32[256,4608]{1,0:T(8,128)} %refs_0_.25, f32[256,4608]{1,0:T(8,128)} %refs_1_.17, bf16[64,4608]{1,0:T(8,128)(2,1)} %copy-done.11, bf16[64,4608]{1,0:T(8,128)(2,1)} %collective-permute-done.25.refs_3_, ...), custom_call_target="tpu_custom_call", output_to_operand_aliasing={{0}: (5, {}), {1}: (6, {})} | custom-call | flops 1 | bytes 1 | tf_op jit(solution)/shard_map/pallas_call | solution.py:41
  179.8 3.2 %collective-permute-done.24.refs_2_ = bf16[64,4608]{1,0:T(8,128)(2,1)S(1)} collective-permute-done((bf16[64,4608]{1,0:T(8,128)(2,1)S(1)}, bf16[64,4608]{1,0:T(8,128)(2,1)S(1)}, u32[]{:S(2)}, u32[]{:S(2)}) %collective-permute-start.24) | collective-permute-done | bytes 589856 | tf_op jit(solution)/shard_map/ppermute | solution.py:442
  183.0 0.9 copy-done.16
  183.9 3.6 %shard_map.147 = (f32[256,4608]{1,0:T(8,128)}, f32[8,128]{1,0:T(8,128)}) custom-call(s32[15]{0:T(128)} %copy-done.13, f32[256,4608]{1,0:T(8,128)} %refs_0_.25, f32[256,4608]{1,0:T(8,128)} %refs_1_.17, bf16[64,4608]{1,0:T(8,128)(2,1)} %copy-done.16, f32[256,4608]{1,0:T(8,128)} %get-tuple-element.147.refs_3_, ...), custom_call_target="tpu_custom_call", output_to_operand_aliasing={{0}: (4, {}), {1}: (5, {})} | custom-call | flops 1 | bytes 1 | tf_op jit(solution)/shard_map/pallas_call | solution.py:41
  (54 shorter events, 1.9 us)
Async XLA Ops:
  0.6 13.8 %collective-permute-start = (bf16[512,4608]{1,0:T(8,128)(2,1)}, bf16[512,4608]{1,0:T(8,128)(2,1)}, u32[]{:S(2)}, u32[]{:S(2)}) collective-permute-start(bf16[512,4608]{1,0:T(8,128)(2,1)} %refs_0_.21), channel_id=1, source_target_pairs={{0,1},{1,0},{2,3},{3,2},{4,5},{5,4},{6,7},{7,6},{8,9},{9,8},{10,11... | collective-permute-start | bytes 14155784 | tf_op jit(solution)/shard_map/ppermute | solution.py:427
  1.8 1.7 copy-start.6
  3.5 154.5 %copy-start.13 = (s32[15]{0:T(128)}, s32[15]{0:T(128)S(1)}, u32[]{:S(2)}) copy-start(s32[15]{0:T(128)S(1)} %dynamic-slice_bitcast_fusion.sc_ref) | copy-start | bytes 184
  3.5 0.7 copy-start.15
  3.5 1.6 copy-start.1
  5.1 1.2 copy-start.2
  6.3 1.2 copy-start.4
  7.6 6.9 %copy-start = (bf16[512,4608]{1,0:T(8,128)(2,1)S(1)}, bf16[512,4608]{1,0:T(8,128)(2,1)}, u32[]{:S(2)}) copy-start(bf16[512,4608]{1,0:T(8,128)(2,1)} %refs_0_.21) | copy-start | bytes 14155780
  11.3 3.2 %collective-permute-start.1 = (bf16[256,512]{1,0:T(8,128)(2,1)S(1)}, bf16[256,512]{1,0:T(8,128)(2,1)S(1)}, u32[]{:S(2)}, u32[]{:S(2)}) collective-permute-start(bf16[256,512]{1,0:T(8,128)(2,1)S(1)} %slice.6), channel_id=1, source_target_pairs={{0,1},{1,0},{2,3},{3,2},{4,5},{5,4},{6,7},{7,6},{8,9},{9,8},{10,11... | collective-permute-start | bytes 786440 | tf_op jit(solution)/shard_map/ppermute | solution.py:427
  11.4 30.2 %collective-permute-start.3 = (bf16[256,2304]{1,0:T(8,128)(2,1)S(1)}, bf16[256,2304]{1,0:T(8,128)(2,1)S(1)}, u32[]{:S(2)}, u32[]{:S(2)}) collective-permute-start(bf16[256,2304]{1,0:T(8,128)(2,1)S(1)} %get-tuple-element.84), channel_id=1, source_target_pairs={{0,2},{1,3},{2,6},{3,7},{6,4},{7,5},{4,0},{5,1},{8,10},{9,11},{10,... | collective-permute-start | bytes 3538952 | tf_op jit(solution)/shard_map/ppermute | solution.py:434
  14.4 7.9 %copy-start.3 = (bf16[512,1024]{1,0:T(8,128)(2,1)S(1)}, bf16[512,1024]{1,0:T(8,128)(2,1)}, u32[]{:S(2)}) copy-start(bf16[512,1024]{1,0:T(8,128)(2,1)} %refs_1_.14) | copy-start | bytes 3145732
  20.7 20.9 %collective-permute-start.2 = (bf16[128,4608]{1,0:T(8,128)(2,1)S(1)}, bf16[128,4608]{1,0:T(8,128)(2,1)S(1)}, u32[]{:S(2)}, u32[]{:S(2)}) collective-permute-start(bf16[128,4608]{1,0:T(8,128)(2,1)S(1)} %get-tuple-element.81), channel_id=1, source_target_pairs={{0,8},{1,17},{2,10},{3,19},{4,12},{5,21},{6,14},{7,23},{8,0},{9,25... | collective-permute-start | bytes 3538952 | tf_op jit(solution)/shard_map/ppermute | solution.py:442
  32.0 9.6 %collective-permute-start.4 = (bf16[768,512]{1,0:T(8,128)(2,1)S(1)}, bf16[768,512]{1,0:T(8,128)(2,1)S(1)}, u32[]{:S(2)}, u32[]{:S(2)}) collective-permute-start(bf16[768,512]{1,0:T(8,128)(2,1)S(1)} %slice.7), channel_id=1, source_target_pairs={{0,1},{1,0},{2,3},{3,2},{4,5},{5,4},{6,7},{7,6},{8,9},{9,8},{10,11... | collective-permute-start | bytes 2359304 | tf_op jit(solution)/shard_map/ppermute | solution.py:427
  42.3 16.2 %collective-permute-start.6 = (bf16[64,4608]{1,0:T(8,128)(2,1)S(1)}, bf16[64,4608]{1,0:T(8,128)(2,1)S(1)}, u32[]{:S(2)}, u32[]{:S(2)}) collective-permute-start(bf16[64,4608]{1,0:T(8,128)(2,1)S(1)} %get-tuple-element.88), channel_id=1, source_target_pairs={{0,16},{1,9},{2,18},{3,11},{4,20},{5,13},{6,22},{7,15},{8,24},{9,1... | collective-permute-start | bytes 1769480 | tf_op jit(solution)/shard_map/ppermute | solution.py:442
  44.0 23.4 %collective-permute-start.5 = (bf16[256,2304]{1,0:T(8,128)(2,1)S(1)}, bf16[256,2304]{1,0:T(8,128)(2,1)S(1)}, u32[]{:S(2)}, u32[]{:S(2)}) collective-permute-start(bf16[256,2304]{1,0:T(8,128)(2,1)S(1)} %get-tuple-element.86.refs_3_), channel_id=1, source_target_pairs={{0,8},{1,17},{2,10},{3,19},{4,12},{5,21},{6,14},{7,23},{8,0},{9,25... | collective-permute-start | bytes 3538952 | tf_op jit(solution)/shard_map/ppermute | solution.py:442
  45.4 32.3 %collective-permute-start.7 = (bf16[256,2304]{1,0:T(8,128)(2,1)S(1)}, bf16[256,2304]{1,0:T(8,128)(2,1)S(1)}, u32[]{:S(2)}, u32[]{:S(2)}) collective-permute-start(bf16[256,2304]{1,0:T(8,128)(2,1)S(1)} %get-tuple-element.86.refs_3_), channel_id=1, source_target_pairs={{0,2},{1,3},{2,6},{3,7},{6,4},{7,5},{4,0},{5,1},{8,10},{9,11},{10,... | collective-permute-start | bytes 3538952 | tf_op jit(solution)/shard_map/ppermute | solution.py:434
  52.5 27.1 %collective-permute-start.9 = (bf16[128,4608]{1,0:T(8,128)(2,1)S(1)}, bf16[128,4608]{1,0:T(8,128)(2,1)S(1)}, u32[]{:S(2)}, u32[]{:S(2)}) collective-permute-start(bf16[128,4608]{1,0:T(8,128)(2,1)S(1)} %get-tuple-element.96), channel_id=1, source_target_pairs={{0,8},{1,17},{2,10},{3,19},{4,12},{5,21},{6,14},{7,23},{8,0},{9,25... | collective-permute-start | bytes 3538952 | tf_op jit(solution)/shard_map/ppermute | solution.py:442
  59.3 8.1 %copy-start.7 = (bf16[256,4608]{1,0:T(8,128)(2,1)S(1)}, bf16[256,4608]{1,0:T(8,128)(2,1)}, u32[]{:S(2)}) copy-start(bf16[256,4608]{1,0:T(8,128)(2,1)} %refs_2_.16) | copy-start | bytes 7077892
  65.6 32.3 %collective-permute-start.13 = (bf16[128,4608]{1,0:T(8,128)(2,1)S(1)}, bf16[128,4608]{1,0:T(8,128)(2,1)S(1)}, u32[]{:S(2)}, u32[]{:S(2)}) collective-permute-start(bf16[128,4608]{1,0:T(8,128)(2,1)S(1)} %get-tuple-element.107), channel_id=1, source_target_pairs={{0,8},{1,17},{2,10},{3,19},{4,12},{5,21},{6,14},{7,23},{8,0},{9,25... | collective-permute-start | bytes 3538952 | tf_op jit(solution)/shard_map/ppermute | solution.py:442
  78.3 42.1 %collective-permute-start.8 = (bf16[256,2304]{1,0:T(8,128)(2,1)S(1)}, bf16[256,2304]{1,0:T(8,128)(2,1)S(1)}, u32[]{:S(2)}, u32[]{:S(2)}) collective-permute-start(bf16[256,2304]{1,0:T(8,128)(2,1)S(1)} %get-tuple-element.94.refs_2_), channel_id=1, source_target_pairs={{0,8},{1,17},{2,10},{3,19},{4,12},{5,21},{6,14},{7,23},{8,0},{9,25... | collective-permute-start | bytes 3538952 | tf_op jit(solution)/shard_map/ppermute | solution.py:442
  78.8 48.2 %collective-permute-start.14 = (bf16[256,2304]{1,0:T(8,128)(2,1)S(1)}, bf16[256,2304]{1,0:T(8,128)(2,1)S(1)}, u32[]{:S(2)}, u32[]{:S(2)}) collective-permute-start(bf16[256,2304]{1,0:T(8,128)(2,1)S(1)} %get-tuple-element.94.refs_2_), channel_id=1, source_target_pairs={{0,2},{1,3},{2,6},{3,7},{6,4},{7,5},{4,0},{5,1},{8,10},{9,11},{10,... | collective-permute-start | bytes 3538952 | tf_op jit(solution)/shard_map/ppermute | solution.py:434
  79.6 4.1 %collective-permute-start.12 = (bf16[512,512]{1,0:T(8,128)(2,1)S(1)}, bf16[512,512]{1,0:T(8,128)(2,1)S(1)}, u32[]{:S(2)}, u32[]{:S(2)}) collective-permute-start(bf16[512,512]{1,0:T(8,128)(2,1)S(1)} %get-tuple-element.101), channel_id=1, source_target_pairs={{0,1},{1,0},{2,3},{3,2},{4,5},{5,4},{6,7},{7,6},{8,9},{9,8},{10,11... | collective-permute-start | bytes 1572872 | tf_op jit(solution)/shard_map/ppermute | solution.py:427
  79.6 38.6 %collective-permute-start.11 = (bf16[64,4608]{1,0:T(8,128)(2,1)S(1)}, bf16[64,4608]{1,0:T(8,128)(2,1)S(1)}, u32[]{:S(2)}, u32[]{:S(2)}) collective-permute-start(bf16[64,4608]{1,0:T(8,128)(2,1)S(1)} %get-tuple-element.99), channel_id=1, source_target_pairs={{0,2},{1,3},{2,6},{3,7},{6,4},{7,5},{4,0},{5,1},{8,10},{9,11},{10,... | collective-permute-start | bytes 1769480 | tf_op jit(solution)/shard_map/ppermute | solution.py:434
  83.0 2.3 %copy-start.5 = (bf16[512,1024]{1,0:T(8,128)(2,1)S(1)}, bf16[512,1024]{1,0:T(8,128)(2,1)}, u32[]{:S(2)}) copy-start(bf16[512,1024]{1,0:T(8,128)(2,1)} %refs_2_.21) | copy-start | bytes 3145732
  83.7 34.5 %collective-permute-start.10 = (bf16[64,4608]{1,0:T(8,128)(2,1)S(1)}, bf16[64,4608]{1,0:T(8,128)(2,1)S(1)}, u32[]{:S(2)}, u32[]{:S(2)}) collective-permute-start(bf16[64,4608]{1,0:T(8,128)(2,1)S(1)} %get-tuple-element.98), channel_id=1, source_target_pairs={{0,16},{1,9},{2,18},{3,11},{4,20},{5,13},{6,22},{7,15},{8,24},{9,1... | collective-permute-start | bytes 1769480 | tf_op jit(solution)/shard_map/ppermute | solution.py:442
  104.9 31.6 %collective-permute-start.18 = (bf16[128,4608]{1,0:T(8,128)(2,1)S(1)}, bf16[128,4608]{1,0:T(8,128)(2,1)S(1)}, u32[]{:S(2)}, u32[]{:S(2)}) collective-permute-start(bf16[128,4608]{1,0:T(8,128)(2,1)S(1)} %get-tuple-element.119), channel_id=1, source_target_pairs={{0,8},{1,17},{2,10},{3,19},{4,12},{5,21},{6,14},{7,23},{8,0},{9,25... | collective-permute-start | bytes 3538952 | tf_op jit(solution)/shard_map/ppermute | solution.py:442
  119.1 18.1 %collective-permute-start.17 = (bf16[64,4608]{1,0:T(8,128)(2,1)S(1)}, bf16[64,4608]{1,0:T(8,128)(2,1)S(1)}, u32[]{:S(2)}, u32[]{:S(2)}) collective-permute-start(bf16[64,4608]{1,0:T(8,128)(2,1)S(1)} %get-tuple-element.117), channel_id=1, source_target_pairs={{0,2},{1,3},{2,6},{3,7},{6,4},{7,5},{4,0},{5,1},{8,10},{9,11},{10,... | collective-permute-start | bytes 1769480 | tf_op jit(solution)/shard_map/ppermute | solution.py:434
  119.9 17.3 %collective-permute-start.16 = (bf16[64,4608]{1,0:T(8,128)(2,1)S(1)}, bf16[64,4608]{1,0:T(8,128)(2,1)S(1)}, u32[]{:S(2)}, u32[]{:S(2)}) collective-permute-start(bf16[64,4608]{1,0:T(8,128)(2,1)S(1)} %get-tuple-element.116), channel_id=1, source_target_pairs={{0,16},{1,9},{2,18},{3,11},{4,20},{5,13},{6,22},{7,15},{8,24},{9,1... | collective-permute-start | bytes 1769480 | tf_op jit(solution)/shard_map/ppermute | solution.py:442
  127.5 16.3 %collective-permute-start.15 = (bf16[256,2304]{1,0:T(8,128)(2,1)S(1)}, bf16[256,2304]{1,0:T(8,128)(2,1)S(1)}, u32[]{:S(2)}, u32[]{:S(2)}) collective-permute-start(bf16[256,2304]{1,0:T(8,128)(2,1)S(1)} %get-tuple-element.115.refs_2_), channel_id=1, source_target_pairs={{0,8},{1,17},{2,10},{3,19},{4,12},{5,21},{6,14},{7,23},{8,0},{9,25... | collective-permute-start | bytes 3538952 | tf_op jit(solution)/shard_map/ppermute | solution.py:442
  128.7 1.5 collective-permute-start.19
  138.1 16.5 %collective-permute-start.22 = (bf16[64,4608]{1,0:T(8,128)(2,1)S(1)}, bf16[64,4608]{1,0:T(8,128)(2,1)S(1)}, u32[]{:S(2)}, u32[]{:S(2)}) collective-permute-start(bf16[64,4608]{1,0:T(8,128)(2,1)S(1)} %get-tuple-element.135), channel_id=1, source_target_pairs={{0,2},{1,3},{2,6},{3,7},{6,4},{7,5},{4,0},{5,1},{8,10},{9,11},{10,... | collective-permute-start | bytes 1769480 | tf_op jit(solution)/shard_map/ppermute | solution.py:434
  141.7 12.9 %collective-permute-start.21 = (bf16[64,4608]{1,0:T(8,128)(2,1)S(1)}, bf16[64,4608]{1,0:T(8,128)(2,1)S(1)}, u32[]{:S(2)}, u32[]{:S(2)}) collective-permute-start(bf16[64,4608]{1,0:T(8,128)(2,1)S(1)} %get-tuple-element.134), channel_id=1, source_target_pairs={{0,16},{1,9},{2,18},{3,11},{4,20},{5,13},{6,22},{7,15},{8,24},{9,1... | collective-permute-start | bytes 1769480 | tf_op jit(solution)/shard_map/ppermute | solution.py:442
  155.5 8.9 %copy-start.12 = (bf16[64,4608]{1,0:T(8,128)(2,1)}, bf16[64,4608]{1,0:T(8,128)(2,1)S(1)}, u32[]{:S(2)}) copy-start(bf16[64,4608]{1,0:T(8,128)(2,1)S(1)} %get-tuple-element.141.refs_2_) | copy-start | bytes 1769476
  155.5 15.8 %collective-permute-start.23 = (bf16[64,4608]{1,0:T(8,128)(2,1)S(1)}, bf16[64,4608]{1,0:T(8,128)(2,1)S(1)}, u32[]{:S(2)}, u32[]{:S(2)}) collective-permute-start(bf16[64,4608]{1,0:T(8,128)(2,1)S(1)} %get-tuple-element.141.refs_2_), channel_id=1, source_target_pairs={{0,16},{1,9},{2,18},{3,11},{4,20},{5,13},{6,22},{7,15},{8,24},{9,1... | collective-permute-start | bytes 1769480 | tf_op jit(solution)/shard_map/ppermute | solution.py:442
  156.5 1.5 collective-permute-start.20
  156.5 17.0 %collective-permute-start.25 = (bf16[64,4608]{1,0:T(8,128)(2,1)S(1)}, bf16[64,4608]{1,0:T(8,128)(2,1)}, u32[]{:S(2)}, u32[]{:S(2)}) collective-permute-start(bf16[64,4608]{1,0:T(8,128)(2,1)S(1)} %get-tuple-element.141.refs_2_), channel_id=1, source_target_pairs={{0,8},{1,17},{2,10},{3,19},{4,12},{5,21},{6,14},{7,23},{8,0},{9,25... | collective-permute-start | bytes 1769480 | tf_op jit(solution)/shard_map/ppermute | solution.py:442
  164.3 0.6 copy-start.8
  164.9 6.4 %copy-start.14 = (s32[15]{0:T(128)S(1)}, s32[15]{0:T(128)}, u32[]{:S(2)}) copy-start(s32[15]{0:T(128)} %copy-done.13) | copy-start | bytes 184
  171.3 0.7 copy-start.9
  172.5 0.6 copy-start.10
  173.1 0.8 copy-start.11
  173.1 9.9 %collective-permute-start.24 = (bf16[64,4608]{1,0:T(8,128)(2,1)S(1)}, bf16[64,4608]{1,0:T(8,128)(2,1)S(1)}, u32[]{:S(2)}, u32[]{:S(2)}) collective-permute-start(bf16[64,4608]{1,0:T(8,128)(2,1)S(1)} %get-tuple-element.144.refs_2_), channel_id=1, source_target_pairs={{0,8},{1,17},{2,10},{3,19},{4,12},{5,21},{6,14},{7,23},{8,0},{9,25... | collective-permute-start | bytes 1769480 | tf_op jit(solution)/shard_map/ppermute | solution.py:442
  183.0 0.9 copy-start.16

commit v10 on v9

--- a/solution.py
+++ b/solution.py
@@ -545,8 +545,6 @@
     send(3)
     do_backward(1, held=[("send", 0)])
     send(0)
-    do_sum(2)
-    pass_sum(2)
     for k in range(4, lay.z):
         do_product(k, held=[("ring", k - 1)])
         pass_weights(k - 1)
@@ -557,7 +555,8 @@
     last = lay.z - 1
     do_grad_context([2])
     swap_grad_context(2)
-    run(relay, sc, held=[("ring", last)])
+    do_sum(2, held=[("ring", last)])
+    pass_sum(2)
     cross_weights(last)
     do_backward(2)
     do_halve(0)

time: 188 us -> 185 us (0.984)
    ppermute x6, waiting for transfers between devices: 25.6 us -> 16.2 us  [onward(): return lax.ppermute(x, 'shard', perm)]
    ppermute x14, waiting for transfers between devices: 12.3 us -> 20.6 us  [across(): return lax.ppermute(x, ('replica', 'shard'), perm)]
    ppermute x6, starting transfers between devices: 12.5 us -> 9.68 us  [onward(): return lax.ppermute(x, 'shard', perm)]
    pallas_call x28 -> x27, Pallas kernels: 109 us -> 108 us  [call(): pl.pallas_call(kernel, grid_spec=pltpu.PrefetchScalarGridSpec(num_scalar_...]
  transfers between devices with their start and end apart: 26 -> 26, of which waited for: 8 -> 10; matrix products, arithmetic and copies ran while one was open for 0% -> 0% of each run, Pallas kernels for 55% -> 56%
where the time goes in v10:
time: 185 us; the launch traced here: 184 us
  Pallas kernels  108 us (58%)
  waiting for transfers between devices  38.4 us (21%)
  starting transfers between devices  27.9 us (15%)
  local copies, waits for them, and re-layouts  8.58 us (5%)
    pallas_call x27, Pallas kernels, call(): pl.pallas_call(kernel, grid_spec=pltpu.PrefetchScalarGridSpec(num_scalar_...  108 us
    ppermute x14, waiting for transfers between devices, across(): return lax.ppermute(x, ('replica', 'shard'), perm)  20.6 us
    ppermute x14, starting transfers between devices, across(): return lax.ppermute(x, ('replica', 'shard'), perm)  17.5 us
    ppermute x6, waiting for transfers between devices, onward(): return lax.ppermute(x, 'shard', perm)  16.2 us
    ppermute x6, starting transfers between devices, onward(): return lax.ppermute(x, 'shard', perm)  9.68 us
    unnamed x34, local copies, waits for them, and re-layouts  7.67 us
  transfers between devices with their start and end apart: 26, of which 10 were waited for; matrix products, arithmetic and copies ran while one was open for 0% of the time, Pallas kernels for 56%

profile of v10, /device:TPU:0, one launch (start us, length us, event | category | flops | bytes accessed | tf_op | source)
XLA Modules:
  0.0 183.9 jit_solution(2267140586095480834)
XLA Ops:
  1.1 0.7 dynamic-slice_bitcast_fusion.sc_ref
  1.8 1.7 copy-done.6
  3.5 0.6 shard_map.120
  4.3 0.8 copy-done.1
  5.1 1.2 copy-done.2
  6.3 1.2 copy-done.4
  7.6 3.7 %shard_map.121 = (bf16[512,512]{1,0:T(8,128)(2,1)S(1)}, f32[8,128]{1,0:T(8,128)S(1)}) custom-call(s32[15]{0:T(128)S(1)} %dynamic-slice_bitcast_fusion.sc_ref, bf16[512,2048]{1,0:T(8,128)(2,1)S(1)} %copy-done.1, bf16[512,1024]{1,0:T(8,128)(2,1)S(1)} %copy-done.2, bf16[512,1024]{1,0:T(8,128)(2,1)S(1)} %copy-done.4, ...), custom_call_target="tpu_custom_call", output_to_operand_aliasing={{1}: (6, {})} | custom-call | flops 1 | bytes 1 | tf_op jit(solution)/shard_map/pallas_call | solution.py:41
  11.4 3.0 %collective-permute-start.3 = (bf16[256,2304]{1,0:T(8,128)(2,1)S(1)}, bf16[256,2304]{1,0:T(8,128)(2,1)S(1)}, u32[]{:S(2)}, u32[]{:S(2)}) collective-permute-start(bf16[256,2304]{1,0:T(8,128)(2,1)S(1)} %get-tuple-element.84), channel_id=1, source_target_pairs={{0,2},{1,3},{2,6},{3,7},{6,4},{7,5},{4,0},{5,1},{8,10},{9,11},{10,... | collective-permute-start | bytes 3538952 | tf_op jit(solution)/shard_map/ppermute | solution.py:434
  14.4 6.3 %shard_map.122 = (bf16[128,4608]{1,0:T(8,128)(2,1)S(1)}, bf16[128,4608]{1,0:T(8,128)(2,1)S(1)}, f32[8,128]{1,0:T(8,128)S(1)}) custom-call(s32[15]{0:T(128)S(1)} %dynamic-slice_bitcast_fusion.sc_ref, bf16[512,512]{1,0:T(8,128)(2,1)S(1)} %get-tuple-element.77.refs_0_, ...), custom_call_target="tpu_custom_call", output_to_operand_aliasing={{2}: (5, {})} | custom-call | flops 1 | bytes 1 | tf_op jit(solution)/shard_map/pallas_call | solution.py:41
  20.7 1.6 collective-permute-start.2
  22.3 9.6 %shard_map.123 = (bf16[1536,512]{1,0:T(8,128)(2,1)S(1)}, f32[8,128]{1,0:T(8,128)S(1)}) custom-call(s32[15]{0:T(128)S(1)} %dynamic-slice_bitcast_fusion.sc_ref, bf16[512,2048]{1,0:T(8,128)(2,1)S(1)} %copy-done.1, bf16[512,1024]{1,0:T(8,128)(2,1)S(1)} %copy-done.3, bf16[512,1024]{1,0:T(8,128)(2,1)S(1)} %copy-done.4, ...), custom_call_target="tpu_custom_call", output_to_operand_aliasing={{1}: (6, {})} | custom-call | flops 1 | bytes 1 | tf_op jit(solution)/shard_map/pallas_call | solution.py:41
  32.1 9.6 %collective-permute-done.3.refs_3_ = bf16[256,2304]{1,0:T(8,128)(2,1)S(1)} collective-permute-done((bf16[256,2304]{1,0:T(8,128)(2,1)S(1)}, bf16[256,2304]{1,0:T(8,128)(2,1)S(1)}, u32[]{:S(2)}, u32[]{:S(2)}) %collective-permute-start.3) | collective-permute-done | bytes 1179680 | tf_op jit(solution)/shard_map/ppermute | solution.py:434
  41.6 0.7 shard_map.124
  42.3 1.6 collective-permute-start.7
  44.0 1.5 collective-permute-start.6
  45.4 0.8 collective-permute-start.8
  46.2 6.3 %shard_map.125 = (bf16[128,4608]{1,0:T(8,128)(2,1)S(1)}, bf16[128,4608]{1,0:T(8,128)(2,1)S(1)}, f32[8,128]{1,0:T(8,128)S(1)}) custom-call(s32[15]{0:T(128)S(1)} %dynamic-slice_bitcast_fusion.sc_ref, bf16[1536,512]{1,0:T(8,128)(2,1)S(1)} %get-tuple-element.80.refs_0_, ...), custom_call_target="tpu_custom_call", output_to_operand_aliasing={{2}: (5, {})} | custom-call | flops 1 | bytes 1 | tf_op jit(solution)/shard_map/pallas_call | solution.py:41
  52.5 0.6 collective-permute-start.5
  53.1 5.4 %collective-permute-done.7.refs_2_ = bf16[64,4608]{1,0:T(8,128)(2,1)S(1)} collective-permute-done((bf16[64,4608]{1,0:T(8,128)(2,1)S(1)}, bf16[64,4608]{1,0:T(8,128)(2,1)S(1)}, u32[]{:S(2)}, u32[]{:S(2)}) %collective-permute-start.7) | collective-permute-done | bytes 589856 | tf_op jit(solution)/shard_map/ppermute | solution.py:442
  58.5 0.8 shard_map.126
  59.3 6.3 %shard_map.127 = (bf16[128,4608]{1,0:T(8,128)(2,1)S(1)}, bf16[128,4608]{1,0:T(8,128)(2,1)S(1)}, f32[8,128]{1,0:T(8,128)S(1)}) custom-call(s32[15]{0:T(128)S(1)} %dynamic-slice_bitcast_fusion.sc_ref, bf16[1536,512]{1,0:T(8,128)(2,1)S(1)} %get-tuple-element.80.refs_0_, ...), custom_call_target="tpu_custom_call", output_to_operand_aliasing={{2}: (5, {})} | custom-call | flops 1 | bytes 1 | tf_op jit(solution)/shard_map/pallas_call | solution.py:41
  65.6 1.7 collective-permute-start.13
  67.3 10.4 %shard_map.128 = (bf16[512,512]{1,0:T(8,128)(2,1)S(1)}, bf16[512,512]{1,0:T(8,128)(2,1)S(1)}, f32[8,128]{1,0:T(8,128)S(1)}) custom-call(s32[15]{0:T(128)S(1)} %dynamic-slice_bitcast_fusion.sc_ref, bf16[512,4608]{1,0:T(8,128)(2,1)S(1)} %copy-done, bf16[512,4608]{1,0:T(8,128)(2,1)} %collective-permute-done.refs_3_.refs_1_, ...), custom_call_target="tpu_custom_call", output_to_operand_aliasing={{2}: (6, {})} | custom-call | flops 1 | bytes 1 | tf_op jit(solution)/shard_map/pallas_call | solution.py:41
  77.8 0.5 shard_map.129
  78.8 0.9 collective-permute-start.14
  79.6 3.4 %collective-permute-start.10 = (bf16[64,4608]{1,0:T(8,128)(2,1)S(1)}, bf16[64,4608]{1,0:T(8,128)(2,1)S(1)}, u32[]{:S(2)}, u32[]{:S(2)}) collective-permute-start(bf16[64,4608]{1,0:T(8,128)(2,1)S(1)} %get-tuple-element.97), channel_id=1, source_target_pairs={{0,2},{1,3},{2,6},{3,7},{6,4},{7,5},{4,0},{5,1},{8,10},{9,11},{10,... | collective-permute-start | bytes 1769480 | tf_op jit(solution)/shard_map/ppermute | solution.py:434
  83.0 0.7 shard_map.130
  83.7 1.6 collective-permute-start.9
  85.3 6.3 %shard_map.131 = (bf16[512,2048]{1,0:T(8,128)(2,1)}, bf16[512,1024]{1,0:T(8,128)(2,1)}, bf16[512,1024]{1,0:T(8,128)(2,1)}, f32[8,128]{1,0:T(8,128)S(1)}) custom-call(s32[15]{0:T(128)S(1)} %dynamic-slice_bitcast_fusion.sc_ref, bf16[512,2048]{1,0:T(8,128)(2,1)S(1)} %copy-done.1, bf16[512,1024]{1,0:T(8,128)(2,1)S(1)} %copy-done.3, ...), custom_call_target="tpu_custom_call", output_to_operand_aliasing={{3}: (8, {})} | custom-call | flops 1 | bytes 1 | tf_op jit(solution)/shard_map/pallas_call | solution.py:41
  91.6 6.3 %shard_map.132 = (bf16[128,4608]{1,0:T(8,128)(2,1)S(1)}, bf16[128,4608]{1,0:T(8,128)(2,1)S(1)}, f32[8,128]{1,0:T(8,128)S(1)}) custom-call(s32[15]{0:T(128)S(1)} %dynamic-slice_bitcast_fusion.sc_ref, bf16[1536,512]{1,0:T(8,128)(2,1)S(1)} %get-tuple-element.80.refs_0_, ...), custom_call_target="tpu_custom_call", output_to_operand_aliasing={{2}: (5, {})} | custom-call | flops 1 | bytes 1 | tf_op jit(solution)/shard_map/pallas_call | solution.py:41
  97.9 0.7 shard_map.133
  98.6 6.3 %shard_map.134 = (bf16[512,2048]{1,0:T(8,128)(2,1)}, bf16[512,1024]{1,0:T(8,128)(2,1)}, bf16[512,1024]{1,0:T(8,128)(2,1)}, f32[8,128]{1,0:T(8,128)S(1)}, bf16[128,4608]{1,0:T(8,128)(2,1)S(1)}) custom-call(s32[15]{0:T(128)S(1)} %dynamic-slice_bitcast_fusion.sc_ref, ...), custom_call_target="tpu_custom_call", output_to_operand_aliasing={{0}: (8, {}), {1}: (9, {}), {2}: (10, {}), {3}: (11, {}), {... | custom-call | flops 1 | bytes 1 | tf_op jit(solution)/shard_map/pallas_call | solution.py:41
  104.9 1.6 collective-permute-start.18
  106.5 1.2 collective-permute-done.11.refs_3_
  107.7 1.2 collective-permute-start.16
  109.0 6.5 %shard_map.135 = (bf16[512,256]{1,0:T(8,128)(2,1)S(1)}, bf16[512,256]{1,0:T(8,128)(2,1)S(1)}, f32[8,128]{1,0:T(8,128)S(1)}) custom-call(s32[15]{0:T(128)S(1)} %dynamic-slice_bitcast_fusion.sc_ref, bf16[512,4608]{1,0:T(8,128)(2,1)S(1)} %copy-done, bf16[512,4608]{1,0:T(8,128)(2,1)} %collective-permute-done.refs_3_.refs_1_, ...), custom_call_target="tpu_custom_call", output_to_operand_aliasing={{2}: (5, {})} | custom-call | flops 1 | bytes 1 | tf_op jit(solution)/shard_map/pallas_call | solution.py:41
  115.5 2.8 %collective-permute-done.10.refs_3_ = bf16[64,4608]{1,0:T(8,128)(2,1)S(1)} collective-permute-done((bf16[64,4608]{1,0:T(8,128)(2,1)S(1)}, bf16[64,4608]{1,0:T(8,128)(2,1)S(1)}, u32[]{:S(2)}, u32[]{:S(2)}) %collective-permute-start.10) | collective-permute-done | bytes 589856 | tf_op jit(solution)/shard_map/ppermute | solution.py:434
  118.3 0.8 shard_map.136
  119.1 0.8 collective-permute-start.17
  119.9 0.5 collective-permute-start.15
  120.5 1.5 collective-permute-done.19.refs_6_
  122.0 6.3 %shard_map.137 = (bf16[512,2048]{1,0:T(8,128)(2,1)}, bf16[512,1024]{1,0:T(8,128)(2,1)}, bf16[512,1024]{1,0:T(8,128)(2,1)}, f32[8,128]{1,0:T(8,128)S(1)}) custom-call(s32[15]{0:T(128)S(1)} %dynamic-slice_bitcast_fusion.sc_ref, bf16[512,2048]{1,0:T(8,128)(2,1)S(1)} %copy-done.1, ...), custom_call_target="tpu_custom_call", output_to_operand_aliasing={{0}: (8, {}), {1}: (9, {}), {2}: (10, {}), {3}: (11, {})} | custom-call | flops 1 | bytes 1 | tf_op jit(solution)/shard_map/pallas_call | solution.py:41
  128.3 0.7 shard_map.138
  129.0 3.9 %collective-permute-done.17.refs_3_ = bf16[64,4608]{1,0:T(8,128)(2,1)S(1)} collective-permute-done((bf16[64,4608]{1,0:T(8,128)(2,1)S(1)}, bf16[64,4608]{1,0:T(8,128)(2,1)S(1)}, u32[]{:S(2)}, u32[]{:S(2)}) %collective-permute-start.17) | collective-permute-done | bytes 589856 | tf_op jit(solution)/shard_map/ppermute | solution.py:434
  132.9 0.8 shard_map.139
  133.7 0.8 collective-permute-start.22
  134.5 1.5 collective-permute-start.21
  136.0 8.1 %collective-permute-done.15.refs_3_ = bf16[256,2304]{1,0:T(8,128)(2,1)S(1)} collective-permute-done((bf16[256,2304]{1,0:T(8,128)(2,1)S(1)}, bf16[256,2304]{1,0:T(8,128)(2,1)S(1)}, u32[]{:S(2)}, u32[]{:S(2)}) %collective-permute-start.15) | collective-permute-done | bytes 1179680 | tf_op jit(solution)/shard_map/ppermute | solution.py:442
  144.1 6.5 %shard_map.140 = (bf16[512,256]{1,0:T(8,128)(2,1)S(1)}, bf16[512,256]{1,0:T(8,128)(2,1)S(1)}, f32[8,128]{1,0:T(8,128)S(1)}) custom-call(s32[15]{0:T(128)S(1)} %dynamic-slice_bitcast_fusion.sc_ref, bf16[512,4608]{1,0:T(8,128)(2,1)S(1)} %copy-done, bf16[512,4608]{1,0:T(8,128)(2,1)} %collective-permute-done.refs_3_.refs_1_, ...), custom_call_target="tpu_custom_call", output_to_operand_aliasing={{2}: (5, {})} | custom-call | flops 1 | bytes 1 | tf_op jit(solution)/shard_map/pallas_call | solution.py:41
  150.7 0.8 shard_map.141
  151.5 0.6 collective-permute-start.23
  152.1 1.4 collective-permute-start.25
  153.6 6.3 %shard_map.142 = (bf16[512,2048]{1,0:T(8,128)(2,1)}, bf16[512,1024]{1,0:T(8,128)(2,1)}, bf16[512,1024]{1,0:T(8,128)(2,1)}, f32[8,128]{1,0:T(8,128)S(1)}) custom-call(s32[15]{0:T(128)S(1)} %dynamic-slice_bitcast_fusion.sc_ref, bf16[512,2048]{1,0:T(8,128)(2,1)S(1)} %copy-done.1, ...), custom_call_target="tpu_custom_call", output_to_operand_aliasing={{0}: (8, {}), {1}: (9, {}), {2}: (10, {}), {3}: (11, {})} | custom-call | flops 1 | bytes 1 | tf_op jit(solution)/shard_map/pallas_call | solution.py:41
  159.9 0.6 copy-done.8
  160.5 3.8 %shard_map.143 = (f32[256,4608]{1,0:T(8,128)}, f32[8,128]{1,0:T(8,128)}) custom-call(s32[15]{0:T(128)} %copy-done.13, f32[256,4608]{1,0:T(8,128)} %refs_0_.25, f32[256,4608]{1,0:T(8,128)} %refs_1_.17, bf16[64,4608]{1,0:T(8,128)(2,1)} %copy-done.12, f32[8,128]{1,0:T(8,128)} %copy-done.8), custom_call_target="tpu_custom_call", output_to_operand_aliasing={{1}: (4, {})} | custom-call | flops 1 | bytes 1 | tf_op jit(solution)/shard_map/pallas_call | solution.py:41
  164.3 3.4 %collective-permute-done.23.refs_1_ = bf16[64,4608]{1,0:T(8,128)(2,1)S(1)} collective-permute-done((bf16[64,4608]{1,0:T(8,128)(2,1)S(1)}, bf16[64,4608]{1,0:T(8,128)(2,1)S(1)}, u32[]{:S(2)}, u32[]{:S(2)}) %collective-permute-start.23) | collective-permute-done | bytes 589856 | tf_op jit(solution)/shard_map/ppermute | solution.py:442
  167.8 0.7 copy-done.9
  168.4 0.5 shard_map.144
  169.0 0.6 copy-done.10
  169.6 1.6 collective-permute-start.24
  171.2 5.9 %shard_map.145 = (f32[256,4608]{1,0:T(8,128)}, f32[8,128]{1,0:T(8,128)}) custom-call(s32[15]{0:T(128)} %copy-done.13, f32[256,4608]{1,0:T(8,128)} %refs_0_.25, f32[256,4608]{1,0:T(8,128)} %refs_1_.17, bf16[64,4608]{1,0:T(8,128)(2,1)} %copy-done.11, bf16[64,4608]{1,0:T(8,128)(2,1)} %collective-permute-done.25.refs_3_, ...), custom_call_target="tpu_custom_call", output_to_operand_aliasing={{0}: (5, {}), {1}: (6, {})} | custom-call | flops 1 | bytes 1 | tf_op jit(solution)/shard_map/pallas_call | solution.py:41
  177.0 2.4 %collective-permute-done.24.refs_2_ = bf16[64,4608]{1,0:T(8,128)(2,1)S(1)} collective-permute-done((bf16[64,4608]{1,0:T(8,128)(2,1)S(1)}, bf16[64,4608]{1,0:T(8,128)(2,1)S(1)}, u32[]{:S(2)}, u32[]{:S(2)}) %collective-permute-start.24) | collective-permute-done | bytes 589856 | tf_op jit(solution)/shard_map/ppermute | solution.py:442
  179.5 0.8 copy-done.16
  180.3 3.6 %shard_map.146 = (f32[256,4608]{1,0:T(8,128)}, f32[8,128]{1,0:T(8,128)}) custom-call(s32[15]{0:T(128)} %copy-done.13, f32[256,4608]{1,0:T(8,128)} %refs_0_.25, f32[256,4608]{1,0:T(8,128)} %refs_1_.17, bf16[64,4608]{1,0:T(8,128)(2,1)} %copy-done.16, f32[256,4608]{1,0:T(8,128)} %get-tuple-element.145.refs_3_, ...), custom_call_target="tpu_custom_call", output_to_operand_aliasing={{0}: (4, {}), {1}: (5, {})} | custom-call | flops 1 | bytes 1 | tf_op jit(solution)/shard_map/pallas_call | solution.py:41
  (53 shorter events, 1.6 us)
Async XLA Ops:
  0.6 13.8 %collective-permute-start = (bf16[512,4608]{1,0:T(8,128)(2,1)}, bf16[512,4608]{1,0:T(8,128)(2,1)}, u32[]{:S(2)}, u32[]{:S(2)}) collective-permute-start(bf16[512,4608]{1,0:T(8,128)(2,1)} %refs_0_.21), channel_id=1, source_target_pairs={{0,1},{1,0},{2,3},{3,2},{4,5},{5,4},{6,7},{7,6},{8,9},{9,8},{10,11... | collective-permute-start | bytes 14155784 | tf_op jit(solution)/shard_map/ppermute | solution.py:427
  1.8 1.7 copy-start.6
  3.5 150.1 %copy-start.13 = (s32[15]{0:T(128)}, s32[15]{0:T(128)S(1)}, u32[]{:S(2)}) copy-start(s32[15]{0:T(128)S(1)} %dynamic-slice_bitcast_fusion.sc_ref) | copy-start | bytes 184
  3.5 0.7 copy-start.15
  3.5 1.6 copy-start.1
  5.1 1.2 copy-start.2
  6.3 1.2 copy-start.4
  7.6 6.9 %copy-start = (bf16[512,4608]{1,0:T(8,128)(2,1)S(1)}, bf16[512,4608]{1,0:T(8,128)(2,1)}, u32[]{:S(2)}) copy-start(bf16[512,4608]{1,0:T(8,128)(2,1)} %refs_0_.21) | copy-start | bytes 14155780
  11.3 3.2 %collective-permute-start.1 = (bf16[256,512]{1,0:T(8,128)(2,1)S(1)}, bf16[256,512]{1,0:T(8,128)(2,1)S(1)}, u32[]{:S(2)}, u32[]{:S(2)}) collective-permute-start(bf16[256,512]{1,0:T(8,128)(2,1)S(1)} %slice.6), channel_id=1, source_target_pairs={{0,1},{1,0},{2,3},{3,2},{4,5},{5,4},{6,7},{7,6},{8,9},{9,8},{10,11... | collective-permute-start | bytes 786440 | tf_op jit(solution)/shard_map/ppermute | solution.py:427
  11.4 30.2 %collective-permute-start.3 = (bf16[256,2304]{1,0:T(8,128)(2,1)S(1)}, bf16[256,2304]{1,0:T(8,128)(2,1)S(1)}, u32[]{:S(2)}, u32[]{:S(2)}) collective-permute-start(bf16[256,2304]{1,0:T(8,128)(2,1)S(1)} %get-tuple-element.84), channel_id=1, source_target_pairs={{0,2},{1,3},{2,6},{3,7},{6,4},{7,5},{4,0},{5,1},{8,10},{9,11},{10,... | collective-permute-start | bytes 3538952 | tf_op jit(solution)/shard_map/ppermute | solution.py:434
  14.4 7.9 %copy-start.3 = (bf16[512,1024]{1,0:T(8,128)(2,1)S(1)}, bf16[512,1024]{1,0:T(8,128)(2,1)}, u32[]{:S(2)}) copy-start(bf16[512,1024]{1,0:T(8,128)(2,1)} %refs_1_.14) | copy-start | bytes 3145732
  20.7 20.9 %collective-permute-start.2 = (bf16[128,4608]{1,0:T(8,128)(2,1)S(1)}, bf16[128,4608]{1,0:T(8,128)(2,1)S(1)}, u32[]{:S(2)}, u32[]{:S(2)}) collective-permute-start(bf16[128,4608]{1,0:T(8,128)(2,1)S(1)} %get-tuple-element.82), channel_id=1, source_target_pairs={{0,8},{1,17},{2,10},{3,19},{4,12},{5,21},{6,14},{7,23},{8,0},{9,25... | collective-permute-start | bytes 3538952 | tf_op jit(solution)/shard_map/ppermute | solution.py:442
  32.0 9.6 %collective-permute-start.4 = (bf16[768,512]{1,0:T(8,128)(2,1)S(1)}, bf16[768,512]{1,0:T(8,128)(2,1)S(1)}, u32[]{:S(2)}, u32[]{:S(2)}) collective-permute-start(bf16[768,512]{1,0:T(8,128)(2,1)S(1)} %slice.7), channel_id=1, source_target_pairs={{0,1},{1,0},{2,3},{3,2},{4,5},{5,4},{6,7},{7,6},{8,9},{9,8},{10,11... | collective-permute-start | bytes 2359304 | tf_op jit(solution)/shard_map/ppermute | solution.py:427
  42.3 16.2 %collective-permute-start.7 = (bf16[64,4608]{1,0:T(8,128)(2,1)S(1)}, bf16[64,4608]{1,0:T(8,128)(2,1)S(1)}, u32[]{:S(2)}, u32[]{:S(2)}) collective-permute-start(bf16[64,4608]{1,0:T(8,128)(2,1)S(1)} %get-tuple-element.90), channel_id=1, source_target_pairs={{0,16},{1,9},{2,18},{3,11},{4,20},{5,13},{6,22},{7,15},{8,24},{9,1... | collective-permute-start | bytes 1769480 | tf_op jit(solution)/shard_map/ppermute | solution.py:442
  44.0 23.4 %collective-permute-start.6 = (bf16[256,2304]{1,0:T(8,128)(2,1)S(1)}, bf16[256,2304]{1,0:T(8,128)(2,1)S(1)}, u32[]{:S(2)}, u32[]{:S(2)}) collective-permute-start(bf16[256,2304]{1,0:T(8,128)(2,1)S(1)} %get-tuple-element.89.refs_3_), channel_id=1, source_target_pairs={{0,8},{1,17},{2,10},{3,19},{4,12},{5,21},{6,14},{7,23},{8,0},{9,25... | collective-permute-start | bytes 3538952 | tf_op jit(solution)/shard_map/ppermute | solution.py:442
  45.4 32.3 %collective-permute-start.8 = (bf16[256,2304]{1,0:T(8,128)(2,1)S(1)}, bf16[256,2304]{1,0:T(8,128)(2,1)S(1)}, u32[]{:S(2)}, u32[]{:S(2)}) collective-permute-start(bf16[256,2304]{1,0:T(8,128)(2,1)S(1)} %get-tuple-element.89.refs_3_), channel_id=1, source_target_pairs={{0,2},{1,3},{2,6},{3,7},{6,4},{7,5},{4,0},{5,1},{8,10},{9,11},{10,... | collective-permute-start | bytes 3538952 | tf_op jit(solution)/shard_map/ppermute | solution.py:434
  52.5 27.1 %collective-permute-start.5 = (bf16[128,4608]{1,0:T(8,128)(2,1)S(1)}, bf16[128,4608]{1,0:T(8,128)(2,1)S(1)}, u32[]{:S(2)}, u32[]{:S(2)}) collective-permute-start(bf16[128,4608]{1,0:T(8,128)(2,1)S(1)} %get-tuple-element.88), channel_id=1, source_target_pairs={{0,8},{1,17},{2,10},{3,19},{4,12},{5,21},{6,14},{7,23},{8,0},{9,25... | collective-permute-start | bytes 3538952 | tf_op jit(solution)/shard_map/ppermute | solution.py:442
  59.3 8.1 %copy-start.7 = (bf16[256,4608]{1,0:T(8,128)(2,1)S(1)}, bf16[256,4608]{1,0:T(8,128)(2,1)}, u32[]{:S(2)}) copy-start(bf16[256,4608]{1,0:T(8,128)(2,1)} %refs_2_.16) | copy-start | bytes 7077892
  65.6 32.3 %collective-permute-start.13 = (bf16[128,4608]{1,0:T(8,128)(2,1)S(1)}, bf16[128,4608]{1,0:T(8,128)(2,1)S(1)}, u32[]{:S(2)}, u32[]{:S(2)}) collective-permute-start(bf16[128,4608]{1,0:T(8,128)(2,1)S(1)} %get-tuple-element.106), channel_id=1, source_target_pairs={{0,8},{1,17},{2,10},{3,19},{4,12},{5,21},{6,14},{7,23},{8,0},{9,25... | collective-permute-start | bytes 3538952 | tf_op jit(solution)/shard_map/ppermute | solution.py:442
  78.3 29.4 %collective-permute-start.11 = (bf16[256,2304]{1,0:T(8,128)(2,1)S(1)}, bf16[256,2304]{1,0:T(8,128)(2,1)S(1)}, u32[]{:S(2)}, u32[]{:S(2)}) collective-permute-start(bf16[256,2304]{1,0:T(8,128)(2,1)S(1)} %get-tuple-element.98.refs_2_), channel_id=1, source_target_pairs={{0,8},{1,17},{2,10},{3,19},{4,12},{5,21},{6,14},{7,23},{8,0},{9,25... | collective-permute-start | bytes 3538952 | tf_op jit(solution)/shard_map/ppermute | solution.py:442
  78.8 39.5 %collective-permute-start.14 = (bf16[256,2304]{1,0:T(8,128)(2,1)S(1)}, bf16[256,2304]{1,0:T(8,128)(2,1)S(1)}, u32[]{:S(2)}, u32[]{:S(2)}) collective-permute-start(bf16[256,2304]{1,0:T(8,128)(2,1)S(1)} %get-tuple-element.98.refs_2_), channel_id=1, source_target_pairs={{0,2},{1,3},{2,6},{3,7},{6,4},{7,5},{4,0},{5,1},{8,10},{9,11},{10,... | collective-permute-start | bytes 3538952 | tf_op jit(solution)/shard_map/ppermute | solution.py:434
  79.6 4.1 %collective-permute-start.12 = (bf16[512,512]{1,0:T(8,128)(2,1)S(1)}, bf16[512,512]{1,0:T(8,128)(2,1)S(1)}, u32[]{:S(2)}, u32[]{:S(2)}) collective-permute-start(bf16[512,512]{1,0:T(8,128)(2,1)S(1)} %get-tuple-element.100), channel_id=1, source_target_pairs={{0,1},{1,0},{2,3},{3,2},{4,5},{5,4},{6,7},{7,6},{8,9},{9,8},{10,11... | collective-permute-start | bytes 1572872 | tf_op jit(solution)/shard_map/ppermute | solution.py:427
  79.6 38.6 %collective-permute-start.10 = (bf16[64,4608]{1,0:T(8,128)(2,1)S(1)}, bf16[64,4608]{1,0:T(8,128)(2,1)S(1)}, u32[]{:S(2)}, u32[]{:S(2)}) collective-permute-start(bf16[64,4608]{1,0:T(8,128)(2,1)S(1)} %get-tuple-element.97), channel_id=1, source_target_pairs={{0,2},{1,3},{2,6},{3,7},{6,4},{7,5},{4,0},{5,1},{8,10},{9,11},{10,... | collective-permute-start | bytes 1769480 | tf_op jit(solution)/shard_map/ppermute | solution.py:434
  83.0 2.3 %copy-start.5 = (bf16[512,1024]{1,0:T(8,128)(2,1)S(1)}, bf16[512,1024]{1,0:T(8,128)(2,1)}, u32[]{:S(2)}) copy-start(bf16[512,1024]{1,0:T(8,128)(2,1)} %refs_2_.21) | copy-start | bytes 3145732
  83.7 34.5 %collective-permute-start.9 = (bf16[64,4608]{1,0:T(8,128)(2,1)S(1)}, bf16[64,4608]{1,0:T(8,128)(2,1)S(1)}, u32[]{:S(2)}, u32[]{:S(2)}) collective-permute-start(bf16[64,4608]{1,0:T(8,128)(2,1)S(1)} %get-tuple-element.96), channel_id=1, source_target_pairs={{0,16},{1,9},{2,18},{3,11},{4,20},{5,13},{6,22},{7,15},{8,24},{9,1... | collective-permute-start | bytes 1769480 | tf_op jit(solution)/shard_map/ppermute | solution.py:442
  104.9 23.4 %collective-permute-start.18 = (bf16[128,4608]{1,0:T(8,128)(2,1)S(1)}, bf16[128,4608]{1,0:T(8,128)(2,1)S(1)}, u32[]{:S(2)}, u32[]{:S(2)}) collective-permute-start(bf16[128,4608]{1,0:T(8,128)(2,1)S(1)} %get-tuple-element.117), channel_id=1, source_target_pairs={{0,8},{1,17},{2,10},{3,19},{4,12},{5,21},{6,14},{7,23},{8,0},{9,25... | collective-permute-start | bytes 3538952 | tf_op jit(solution)/shard_map/ppermute | solution.py:442
  107.7 21.3 %collective-permute-start.16 = (bf16[64,4608]{1,0:T(8,128)(2,1)S(1)}, bf16[64,4608]{1,0:T(8,128)(2,1)S(1)}, u32[]{:S(2)}, u32[]{:S(2)}) collective-permute-start(bf16[64,4608]{1,0:T(8,128)(2,1)S(1)} %get-tuple-element.114), channel_id=1, source_target_pairs={{0,16},{1,9},{2,18},{3,11},{4,20},{5,13},{6,22},{7,15},{8,24},{9,1... | collective-permute-start | bytes 1769480 | tf_op jit(solution)/shard_map/ppermute | solution.py:442
  119.1 13.8 %collective-permute-start.17 = (bf16[64,4608]{1,0:T(8,128)(2,1)S(1)}, bf16[64,4608]{1,0:T(8,128)(2,1)S(1)}, u32[]{:S(2)}, u32[]{:S(2)}) collective-permute-start(bf16[64,4608]{1,0:T(8,128)(2,1)S(1)} %get-tuple-element.115), channel_id=1, source_target_pairs={{0,2},{1,3},{2,6},{3,7},{6,4},{7,5},{4,0},{5,1},{8,10},{9,11},{10,... | collective-permute-start | bytes 1769480 | tf_op jit(solution)/shard_map/ppermute | solution.py:434
  119.9 24.2 %collective-permute-start.15 = (bf16[256,2304]{1,0:T(8,128)(2,1)S(1)}, bf16[256,2304]{1,0:T(8,128)(2,1)S(1)}, u32[]{:S(2)}, u32[]{:S(2)}) collective-permute-start(bf16[256,2304]{1,0:T(8,128)(2,1)S(1)} %get-tuple-element.113.refs_2_), channel_id=1, source_target_pairs={{0,8},{1,17},{2,10},{3,19},{4,12},{5,21},{6,14},{7,23},{8,0},{9,25... | collective-permute-start | bytes 3538952 | tf_op jit(solution)/shard_map/ppermute | solution.py:442
  120.5 1.5 collective-permute-start.19
  133.7 16.9 %collective-permute-start.22 = (bf16[64,4608]{1,0:T(8,128)(2,1)S(1)}, bf16[64,4608]{1,0:T(8,128)(2,1)S(1)}, u32[]{:S(2)}, u32[]{:S(2)}) collective-permute-start(bf16[64,4608]{1,0:T(8,128)(2,1)S(1)} %get-tuple-element.133), channel_id=1, source_target_pairs={{0,2},{1,3},{2,6},{3,7},{6,4},{7,5},{4,0},{5,1},{8,10},{9,11},{10,... | collective-permute-start | bytes 1769480 | tf_op jit(solution)/shard_map/ppermute | solution.py:434
  134.5 16.2 %collective-permute-start.21 = (bf16[64,4608]{1,0:T(8,128)(2,1)S(1)}, bf16[64,4608]{1,0:T(8,128)(2,1)S(1)}, u32[]{:S(2)}, u32[]{:S(2)}) collective-permute-start(bf16[64,4608]{1,0:T(8,128)(2,1)S(1)} %get-tuple-element.132), channel_id=1, source_target_pairs={{0,16},{1,9},{2,18},{3,11},{4,20},{5,13},{6,22},{7,15},{8,24},{9,1... | collective-permute-start | bytes 1769480 | tf_op jit(solution)/shard_map/ppermute | solution.py:442
  151.5 8.4 %copy-start.12 = (bf16[64,4608]{1,0:T(8,128)(2,1)}, bf16[64,4608]{1,0:T(8,128)(2,1)S(1)}, u32[]{:S(2)}) copy-start(bf16[64,4608]{1,0:T(8,128)(2,1)S(1)} %get-tuple-element.139.refs_2_) | copy-start | bytes 1769476
  151.5 16.2 %collective-permute-start.23 = (bf16[64,4608]{1,0:T(8,128)(2,1)S(1)}, bf16[64,4608]{1,0:T(8,128)(2,1)S(1)}, u32[]{:S(2)}, u32[]{:S(2)}) collective-permute-start(bf16[64,4608]{1,0:T(8,128)(2,1)S(1)} %get-tuple-element.139.refs_2_), channel_id=1, source_target_pairs={{0,16},{1,9},{2,18},{3,11},{4,20},{5,13},{6,22},{7,15},{8,24},{9,1... | collective-permute-start | bytes 1769480 | tf_op jit(solution)/shard_map/ppermute | solution.py:442
  152.1 1.5 collective-permute-start.20
  152.1 19.1 %collective-permute-start.25 = (bf16[64,4608]{1,0:T(8,128)(2,1)S(1)}, bf16[64,4608]{1,0:T(8,128)(2,1)}, u32[]{:S(2)}, u32[]{:S(2)}) collective-permute-start(bf16[64,4608]{1,0:T(8,128)(2,1)S(1)} %get-tuple-element.139.refs_2_), channel_id=1, source_target_pairs={{0,8},{1,17},{2,10},{3,19},{4,12},{5,21},{6,14},{7,23},{8,0},{9,25... | collective-permute-start | bytes 1769480 | tf_op jit(solution)/shard_map/ppermute | solution.py:442
  159.9 0.6 copy-start.8
  160.5 7.2 %copy-start.14 = (s32[15]{0:T(128)S(1)}, s32[15]{0:T(128)}, u32[]{:S(2)}) copy-start(s32[15]{0:T(128)} %copy-done.13) | copy-start | bytes 184
  167.8 0.7 copy-start.9
  169.0 0.6 copy-start.10
  169.6 1.6 copy-start.11
  169.6 9.9 %collective-permute-start.24 = (bf16[64,4608]{1,0:T(8,128)(2,1)S(1)}, bf16[64,4608]{1,0:T(8,128)(2,1)S(1)}, u32[]{:S(2)}, u32[]{:S(2)}) collective-permute-start(bf16[64,4608]{1,0:T(8,128)(2,1)S(1)} %get-tuple-element.142.refs_2_), channel_id=1, source_target_pairs={{0,8},{1,17},{2,10},{3,19},{4,12},{5,21},{6,14},{7,23},{8,0},{9,25... | collective-permute-start | bytes 1769480 | tf_op jit(solution)/shard_map/ppermute | solution.py:442
  179.5 0.8 copy-start.16
